TPU v7x, 32 devices: a whole 2x2x4 slice. The times are simulated.
32 devices in a mesh: cuts: 2 (over y), idx: 8 (over z, x), half: 2 (over core).
Axes of the slice: x: 2, y: 2, z: 4, core: 2. Of those that a mesh axis runs over, the one named last changes fastest.
Arguments:
- left_factor: float32 [2, 4, 64, 1024, 256], P('half', 'cuts', 'idx'), parts along dimension 1, may hold values from -6 to 6
- right_factor: float32 [2, 4, 64, 256, 1024], P('half', 'cuts', None, 'idx'), parts along dimension 1, may hold values from -0.25 to 0.25
Outputs:
- amplitudes: float32 [1024, 4, 1024], P(('idx', 'half'), 'cuts'), parts along dimension 1
There are 2 independent parts, one for each index of `cuts`. A program takes and returns all parts, laid end to end along the dimension named above; each array names one. Nothing has to cross between parts.
All inputs are finite; a program needn't handle non-finite values.
Results may differ from a plain program's by a relative error of at most 0.0003.
Values sent between devices are 32-bit elements; how exact they have to be, the bound alone decides.
No kernel may reach another device: no remote copies, remote signals or barrier semaphores. Data moves between devices by JAX's collectives and lax.ppermute only.
A program may use at most 256 MiB of HBM per device.

v0:
```python
import math

import jax
import jax.numpy as jnp
from jax import lax
from jax.sharding import PartitionSpec as P

BATCH = 64
N = 1024


def swapped(x, axis, bit):
    return lax.ppermute(x, axis, [(i, i ^ 1 << bit) for i in range(lax.axis_size(axis))])


def complex_product(left_real, left_imag, right_real, right_imag, pattern):
    highest = lax.Precision.HIGHEST
    first_term = jnp.einsum(pattern, left_real, right_real, precision=highest)
    second_term = jnp.einsum(pattern, left_imag, right_imag, precision=highest)
    mixed_term = jnp.einsum(
        pattern, left_real + left_imag, right_real + right_imag, precision=highest
    )
    return (first_term - second_term, mixed_term - first_term - second_term)


def on_device(left_factor, right_factor):
    left_local = left_factor[0]
    right_local = right_factor[0]
    columns = lax.all_to_all(right_local, "idx", split_axis=1, concat_axis=2, tiled=True)
    real_part, imag_part = complex_product(
        left_local[0], left_local[1], columns[0], columns[1], "bmk,bkn->bmn"
    )
    merged = jnp.stack([real_part, imag_part])
    half_cols = merged.shape[3] // 2
    half_index = lax.axis_index("half")
    outgoing = lax.dynamic_slice_in_dim(merged, (1 - half_index) * half_cols, half_cols, 3)
    own_slab = lax.dynamic_slice_in_dim(merged, half_index * half_cols, half_cols, 3)
    other_slab = swapped(outgoing, "half", 0)
    is_lower = half_index == 0
    first_pair = jnp.where(is_lower, own_slab, other_slab)
    second_pair = jnp.where(is_lower, other_slab, own_slab)
    norm_scale = 1.0 / math.sqrt(2.0 * BATCH * N)
    real_part, imag_part = complex_product(
        first_pair[0], first_pair[1], second_pair[0], second_pair[1], "bmn,bon->mo"
    )
    return lax.psum_scatter(
        jnp.stack([real_part, imag_part], axis=1) * norm_scale,
        ("idx", "half"),
        scatter_dimension=0,
        tiled=True,
    )


def solution(mesh):
    return jax.shard_map(
        on_device,
        mesh=mesh,
        in_specs=(P("half", "cuts", "idx", None, None), P("half", "cuts", None, "idx", None)),
        out_specs=P(("idx", "half"), "cuts", None),
        check_vma=False,
    )
```

profile of v0, /device:TPU:0, one launch (start us, length us, event | category | flops | bytes accessed | tf_op | source)
XLA Modules:
  0.0 991.2 jit_solution(9931853911004770356)
XLA Ops:
  6.5 11.8 %copy.11 = f32[1,2,64,32,1024]{4,3,1,2,0:T(8,128)} copy(f32[1,2,64,32,1024]{4,3,2,1,0:T(8,128)} %param.3) | data formatting | bytes 33554432 | tf_op args[1]
  18.3 7.3 all-to-all-start
  25.6 0.0 reduce-scatter.2.cloned.1.call-start
  25.7 363.0 %all-to-all-done = f32[2,64,32,1024]{3,2,0,1:T(8,128)} async-done(((f32[2,64,32,1024]{3,2,0,1:T(8,128)}), f32[2,64,32,1024]{3,2,0,1:T(8,128)}, u32[]{:S(2)}, u32[]{:S(2)}) %all-to-all-start) | async-done | bytes 16777248 | tf_op jit(solution)/shard_map/all_to_all | solution.py:29
  388.6 11.8 %copy.10 = f32[2,8,8,32,1024]{4,3,1,2,0:T(8,128)} copy(f32[2,8,8,32,1024]{4,3,0,2,1:T(8,128)} %bitcast.2) | data formatting | bytes 33554432 | tf_op jit(solution)/shard_map/all_to_all | solution.py:29
  400.5 6.7 fusion.38
  407.2 0.0 copy-start.1
  407.2 0.0 copy-start
  407.2 34.2 %fusion.24 = f32[8,1024,1024]{2,1,0:T(8,128)} fusion(f32[8,256,1024]{2,1,0:T(8,128)S(1)} %bitcast.103, f32[1,2,8,1024,256]{4,3,2,1,0:T(8,128)} %param.2), kind=kOutput, calls=%fused_computation.36 | convolution fusion | flops 25769803776 | bytes 50331648 | tf_op jit(solution)/shard_map/bmk,bkn->bmn/dot_general | solution.py:18
  441.5 0.0 copy-done.1
  441.5 0.0 copy-done
  441.5 32.8 %fusion.21 = f32[8,1024,1024]{2,1,0:T(8,128)} fusion(f32[8,256,1024]{2,1,0:T(8,128)S(1)} %bitcast.101, f32[1,2,8,1024,256]{4,3,2,1,0:T(8,128)} %param.2), kind=kOutput, calls=%fused_computation.33 | convolution fusion | flops 25769803776 | bytes 50331648 | tf_op jit(solution)/shard_map/bmk,bkn->bmn/dot_general | solution.py:19
  474.2 55.7 %subtract_bitcast_fusion = f32[1,8,1024,1024]{3,2,1,0:T(8,128)} fusion(f32[8,1024,1024]{2,1,0:T(8,128)} %fusion.21, f32[8,1024,1024]{2,1,0:T(8,128)} %fusion.24, f32[8,256,1024]{2,1,0:T(8,128)} %bitcast.104, f32[8,256,1024]{2,1,0:T(8,128)} %bitcast.102, f32[1,2,8,1024,256]{4,3,2,1,0:T(8,128)} %param.2), kind=kOutput, calls=%fused_computation.6 | convolution fusion | flops 25790775296 | bytes 134217728 | tf_op jit(solution)/shard_map/bmk,bkn->bmn/dot_general | solution.py:20
  529.9 33.0 %subtract_bitcast_fusion.1 = f32[1,8,1024,1024]{3,2,1,0:T(8,128)} fusion(f32[8,1024,1024]{2,1,0:T(8,128)} %fusion.24, f32[8,1024,1024]{2,1,0:T(8,128)} %fusion.21), kind=kLoop, calls=%fused_computation.7 | loop fusion | flops 8388608 | bytes 100663296 | tf_op jit(solution)/shard_map/stack | solution.py:33
  562.9 23.0 %fusion = f32[2,8,1024,512]{3,2,1,0:T(8,128)} fusion(s32[]{:T(128)S(6)} %select_n.20, f32[1,8,1024,1024]{3,2,1,0:T(8,128)} %subtract_bitcast_fusion.1, f32[1,8,1024,1024]{3,2,1,0:T(8,128)} %subtract_bitcast_fusion), kind=kLoop, calls=%fused_computation.4 | loop fusion | flops 8388608 | bytes 100663296 | tf_op jit(solution)/shard_map/stack | solution.py:33
  586.0 0.0 collective-permute-start
  586.0 49.5 %collective-permute-done = f32[2,8,1024,512]{3,2,1,0:T(8,128)} collective-permute-done((f32[2,8,1024,512]{3,2,1,0:T(8,128)}, f32[2,8,1024,512]{3,2,1,0:T(8,128)}, u32[]{:S(2)}, u32[]{:S(2)}) %collective-permute-start) | collective-permute-done | bytes 33554464 | tf_op jit(solution)/shard_map/ppermute | solution.py:13
  635.4 54.2 %broadcast_select_fusion.1 = (f32[2,8,1024,512]{3,2,1,0:T(8,128)}, f32[2,8,1024,512]{3,2,1,0:T(8,128)}) fusion(f32[2,8,1024,512]{3,2,1,0:T(8,128)} %collective-permute-done, pred[]{:T(512)S(6)} %eq.3, s32[]{:T(128)S(6)} %select_n.19, f32[1,8,1024,1024]{3,2,1,0:T(8,128)} %subtract_bitcast_fusion, f32[1,8,1024,1024]{3,2,1,0:T(8,128)} %subtract_bitcast_fusion.1), kind=kLoop, calls=%fused_computation.22 | loop fusion | flops 33554432 | bytes 167772160 | tf_op jit(solution)/shard_map/jit(_where)/select_n | solution.py:40
  689.6 59.4 %fusion.5 = f32[1024,1024,1]{1,0,2:T(8,128)S(1)} fusion(f32[2,8,1024,512]{3,2,1,0:T(8,128)} %get-tuple-element.6, f32[2,8,1024,512]{3,2,1,0:T(8,128)} %get-tuple-element.5), kind=kOutput, calls=%fused_computation.11 | convolution fusion | flops 51539607552 | bytes 37748736 | tf_op jit(solution)/shard_map/bmn,bon->mo/dot_general | solution.py:19
  749.1 59.3 %fusion.8 = f32[1024,1024,1]{1,0,2:T(8,128)S(1)} fusion(f32[2,8,1024,512]{3,2,1,0:T(8,128)} %get-tuple-element.6, f32[2,8,1024,512]{3,2,1,0:T(8,128)} %get-tuple-element.5), kind=kOutput, calls=%fused_computation.14 | convolution fusion | flops 51539607552 | bytes 37748736 | tf_op jit(solution)/shard_map/bmn,bon->mo/dot_general | solution.py:18
  808.4 63.7 %fusion.32 = f32[1024,1,1024]{2,0,1:T(8,128)S(1)} fusion(f32[1024,1024,1]{1,0,2:T(8,128)S(1)} %fusion.5, f32[1024,1024,1]{1,0,2:T(8,128)S(1)} %fusion.8, f32[2,8,1024,512]{3,2,1,0:T(8,128)} %get-tuple-element.6, f32[2,8,1024,512]{3,2,1,0:T(8,128)} %get-tuple-element.5), kind=kOutput, calls=%fused_computation.45 | convolution fusion | flops 51550093312 | bytes 79691776 | tf_op jit(solution)/shard_map/bmn,bon->mo/dot_general | solution.py:20
  872.1 1.4 fusion.33
  873.4 4.3 maximum_multiply_fusion
  877.7 0.0 reduce-scatter.2.cloned.1.call-update
  877.7 103.9 %reduce-scatter.2.cloned.1.call-done = f32[64,2,1024]{2,0,1:T(8,128)} async-done(((f32[1024,2,1024]{2,0,1:T(8,128)}), f32[64,2,1024]{2,0,1:T(8,128)}) %reduce-scatter.2.cloned.1.call-update) | async-done | bytes 524304 | tf_op jit(solution)/shard_map/reduce_scatter | solution.py:46
  981.7 2.2 copy.7
Async XLA Ops:
  18.3 370.3 %all-to-all-start = ((f32[2,64,32,1024]{3,2,0,1:T(8,128)}), f32[2,64,32,1024]{3,2,0,1:T(8,128)}, u32[]{:S(2)}, u32[]{:S(2)}) async-start(f32[2,64,32,1024]{3,2,0,1:T(8,128)} %bitcast.105), calls=%async_computation | async-start | bytes 33554432 | tf_op jit(solution)/shard_map/all_to_all | solution.py:29
  25.6 956.1 %reduce-scatter.2.cloned.1.call-start = ((), (), s32[]{:S(2)}) async-start(), calls=%async_computation.2 | async-start | bytes 8912896 | tf_op jit(solution)/shard_map/reduce_scatter | solution.py:46
  407.2 34.3 %copy-start.1 = (f32[1,8,8,32,1024]{4,3,2,1,0:T(8,128)}, f32[1,8,8,32,1024]{4,3,2,1,0:T(8,128)S(1)}, u32[]{:S(2)}) copy-start(f32[1,8,8,32,1024]{4,3,2,1,0:T(8,128)S(1)} %get-tuple-element.8) | copy-start | bytes 25165828
  407.2 34.3 %copy-start = (f32[1,8,8,32,1024]{4,3,2,1,0:T(8,128)}, f32[1,8,8,32,1024]{4,3,2,1,0:T(8,128)S(1)}, u32[]{:S(2)}) copy-start(f32[1,8,8,32,1024]{4,3,2,1,0:T(8,128)S(1)} %get-tuple-element.7) | copy-start | bytes 25165828
  586.0 49.5 %collective-permute-start = (f32[2,8,1024,512]{3,2,1,0:T(8,128)}, f32[2,8,1024,512]{3,2,1,0:T(8,128)}, u32[]{:S(2)}, u32[]{:S(2)}) collective-permute-start(f32[2,8,1024,512]{3,2,1,0:T(8,128)} %fusion), channel_id=1, source_target_pairs={{0,1},{1,0},{2,3},{3,2},{4,5},{5,4},{6,7},{7,6},{8,9},{9,8},{10,11... | collective-permute-start | bytes 100663304 | tf_op jit(solution)/shard_map/ppermute | solution.py:13
Sparse Core Ops, SparseCore 0:
  877.8 103.7 reduce-scatter.1
where the time goes:
time: 998 us; the launch traced here: 991 us
  waiting for transfers between devices  516 us (52%)
  matrix products  305 us (31%)
  other arithmetic  116 us (12%)
  local copies, waits for them, and re-layouts  32.6 us (3%)
  between operations  13.9 us (1%)
    all_to_all x1, waiting for transfers between devices, on_device(): lax.all_to_all(right_local, 'idx', split_axis=1, concat_axis=2, tiled=True)  363 us
    dot_general x2, matrix products, complex_product(): jnp.einsum(pattern, left_real + left_imag, right_real + right_imag, preci...  119 us
    reduce_scatter x1, waiting for transfers between devices, on_device(): lax.psum_scatter(jnp.stack([real_part, imag_part], axis=1) * norm_scale,...  104 us
    dot_general x2, matrix products, complex_product(): first_term = jnp.einsum(pattern, left_real, right_real, precision=highest)  93.6 us
    dot_general x2, matrix products, complex_product(): second_term = jnp.einsum(pattern, left_imag, right_imag, precision=highest)  92.2 us
    another operation x2, other arithmetic, on_device(): merged = jnp.stack([real_part, imag_part])  56 us
    select_n x1, other arithmetic, on_device(): first_pair = jnp.where(is_lower, own_slab, other_slab)  54.2 us
    ppermute x1, waiting for transfers between devices, swapped(): lax.ppermute(x, axis, [(i, i ^ 1 << bit) for i in range(lax.axis_size(axi...  49.5 us
  transfers between devices with their start and end apart: 3, of which 3 were waited for; matrix products, arithmetic and copies ran while one was open for 0% of the time, Pallas kernels for 0%

commit v1 on v0

v1 whole, which is shorter than its diff:
```python
import math

import jax
import jax.numpy as jnp
from jax import lax
from jax.sharding import PartitionSpec as P

HIGH = lax.Precision.HIGH


def swapped(x, axis):
    return lax.ppermute(x, axis, [(i, i ^ 1) for i in range(lax.axis_size(axis))])


def complex_terms(left_real, left_imag, right_real, right_imag, pattern):
    first = jnp.einsum(pattern, left_real, right_real, precision=HIGH)
    second = jnp.einsum(pattern, left_imag, right_imag, precision=HIGH)
    mixed = jnp.einsum(pattern, left_real + left_imag, right_real + right_imag, precision=HIGH)
    return first, second, mixed


def on_device(left_factor, right_factor):
    idx_size = lax.axis_size("idx")
    half_size = lax.axis_size("half")
    left = left_factor[0]
    right = right_factor[0]
    _, local_batch, rows, inner = left.shape
    _, batch, inner_part, between = right.shape
    own_rows = rows // (idx_size * half_size)
    half_rows = rows // half_size
    half_cols = between // half_size
    is_lower = lax.axis_index("half") == 0
    scale = 1.0 / math.sqrt(2.0 * batch * between)

    pieces = right.reshape(2, idx_size, local_batch, inner_part, half_size, half_cols)

    split_rows = left.reshape(2, local_batch, idx_size, half_size, own_rows, inner)
    upper_rows = lax.ppermute(split_rows[:, :, :, 1], "half", [(0, 1)])
    other_whole = lax.ppermute(left, "half", [(1, 0)])
    first_left = jnp.where(is_lower, split_rows[:, :, :, 0], upper_rows)
    first_left = first_left.reshape(2, local_batch, half_rows, inner)
    second_left = jnp.where(is_lower, other_whole, left)

    totals = None
    for b in range(local_batch):
        outgoing = jnp.transpose(pieces[:, :, b], (1, 3, 0, 2, 4))
        outgoing = outgoing.reshape(idx_size * half_size, 2, inner_part, half_cols)
        arrived = lax.all_to_all(outgoing, ("idx", "half"), 0, 0, tiled=True)
        arrived = arrived.reshape(idx_size, half_size, 2, inner_part, half_cols)
        factors = jnp.transpose(arrived, (1, 2, 0, 3, 4)).reshape(2, 2, inner, half_cols)
        first, second, mixed = complex_terms(
            factors[0, 0], factors[0, 1], factors[1, 0], factors[1, 1], "kn,ln->kl"
        )
        core = jnp.stack([first - second, mixed - first - second]) * scale
        core = core + swapped(core, "half")
        first, second, mixed = complex_terms(
            first_left[0, b], first_left[1, b], core[0], core[1], "mk,kl->ml"
        )
        terms = complex_terms(
            first - second, mixed - first - second, second_left[0, b], second_left[1, b], "ml,ol->mo"
        )
        totals = terms if totals is None else [t + u for t, u in zip(totals, terms)]
    first, second, mixed = totals
    partial = jnp.stack([first - second, mixed - first - second], axis=1)
    return lax.psum_scatter(partial, "idx", scatter_dimension=0, tiled=True)


def solution(mesh):
    return jax.shard_map(
        on_device,
        mesh=mesh,
        in_specs=(P("half", "cuts", "idx", None, None), P("half", "cuts", None, "idx", None)),
        out_specs=P(("idx", "half"), "cuts", None),
        check_vma=False,
    )
```

time: 998 us -> 697 us (0.70)
  matrix products: 305 us -> 87.7 us
  waiting for transfers between devices: 516 us -> 358 us
  starting transfers between devices: 7.29 us -> 102 us
  other arithmetic: 116 us -> 32.6 us
  local copies, waits for them, and re-layouts: 32.6 us -> 91.6 us
    dot_general x6 -> x72, matrix products: 305 us -> 87.7 us  [the longest x24 33.4 us: complex_terms(): jnp.einsum(pattern, left_real + left_imag, right_real + right_imag, preci...]
    all_to_all x1 -> x8, waiting for transfers between devices: 363 us -> 266 us  [on_device(): arrived = lax.all_to_all(outgoing, ('idx', 'half'), 0, 0, tiled=True)]
    all_to_all x1 -> x8, starting transfers between devices: 7.25 us -> 86.3 us  [on_device(): arrived = lax.all_to_all(outgoing, ('idx', 'half'), 0, 0, tiled=True)]
    another operation x3 -> x10, other arithmetic: 57.4 us -> 4.98 us  [the longest x2 4.69 us: on_device(): partial = jnp.stack([first - second, mixed - first - second], axis=1)]
    ppermute x1 -> x10, waiting for transfers between devices: 49.5 us -> 1.87 us  [the longest x8 1.86 us: swapped(): lax.ppermute(x, axis, [(i, i ^ 1) for i in range(lax.axis_size(axis))])]
    transpose x0 -> x9, local copies, waits for them, and re-layouts: none -> 36.8 us  [on_device(): outgoing = jnp.transpose(pieces[:, :, b], (1, 3, 0, 2, 4))]
    select_n x1 -> x2, other arithmetic: 54.2 us -> 21.1 us  [the longest x1 11.6 us: on_device(): second_left = jnp.where(is_lower, other_whole, left)]
    another operation x0 -> x1, local copies, waits for them, and re-layouts: none -> 22.1 us  [on_device(): right.reshape(2, idx_size, local_batch, inner_part, half_size, half_cols)]
  transfers between devices with their start and end apart: 3 -> 19, of which waited for: 3 -> 10; matrix products, arithmetic and copies ran while one was open for 0% -> 14% of each run, Pallas kernels for 0% -> 0%
where the time goes in v1:
time: 697 us; the launch traced here: 687 us
  waiting for transfers between devices  358 us (51%)
  starting transfers between devices  102 us (15%)
  local copies, waits for them, and re-layouts  91.6 us (13%)
  matrix products  87.7 us (13%)
  other arithmetic  32.6 us (5%)
  between operations  15.1 us (2%)
    all_to_all x8, waiting for transfers between devices, on_device(): arrived = lax.all_to_all(outgoing, ('idx', 'half'), 0, 0, tiled=True)  266 us
    reduce_scatter x1, waiting for transfers between devices, on_device(): return lax.psum_scatter(partial, 'idx', scatter_dimension=0, tiled=True)  89.8 us
    all_to_all x8, starting transfers between devices, on_device(): arrived = lax.all_to_all(outgoing, ('idx', 'half'), 0, 0, tiled=True)  86.3 us
    transpose x9, local copies, waits for them, and re-layouts, on_device(): outgoing = jnp.transpose(pieces[:, :, b], (1, 3, 0, 2, 4))  36.8 us
    dot_general x24, matrix products, complex_terms(): jnp.einsum(pattern, left_real + left_imag, right_real + right_imag, preci...  33.4 us
    dot_general x24, matrix products, complex_terms(): first = jnp.einsum(pattern, left_real, right_real, precision=HIGH)  32.6 us
    another operation x1, local copies, waits for them, and re-layouts, on_device(): right.reshape(2, idx_size, local_batch, inner_part, half_size, half_cols)  22.1 us
    dot_general x24, matrix products, complex_terms(): second = jnp.einsum(pattern, left_imag, right_imag, precision=HIGH)  21.7 us
  transfers between devices with their start and end apart: 19, of which 10 were waited for; matrix products, arithmetic and copies ran while one was open for 14% of the time, Pallas kernels for 0%

profile of v1, /device:TPU:0, one launch (start us, length us, event | category | flops | bytes accessed | tf_op | source)
XLA Modules:
  0.0 687.1 jit_solution(12261873322110644962)
XLA Ops:
  6.5 22.1 %reshape_squeeze.7 = f32[2,8,8,32,2,512]{5,4,3,2,1,0:T(2,128)} reshape(f32[1,2,64,32,1024]{4,3,2,1,0:T(8,128)} %param.3) | data formatting | bytes 33554432 | tf_op jit(solution)/shard_map/reshape;squeeze | solution.py:35
  28.6 13.3 %slice_bitcast_fusion.2 = (f32[8,2,2,32,512]{4,1,3,0,2:T(2,128)S(1)}, f32[8,2,2,32,512]{4,1,3,0,2:T(2,128)}, f32[8,2,2,32,512]{4,1,3,0,2:T(2,128)}, f32[8,2,2,32...) fusion(f32[2,8,8,32,2,512]{5,4,3,2,1,0:T(2,128)} %reshape_squeeze.7), kind=kLoop, calls=%fused_computation.5 | loop fusion | bytes 33554432 | tf_op jit(solution)/shard_map/transpose | solution.py:46
  43.6 7.4 %all-to-all-start.1 = ((f32[16,2,32,512]{3,2,1,0:T(8,128)}), f32[16,2,32,512]{3,2,1,0:T(8,128)}, u32[]{:S(2)}, u32[]{:S(2)}) async-start(f32[16,2,32,512]{3,2,1,0:T(8,128)} %bitcast.576), calls=%async_computation.1 | async-start | bytes 4194304 | tf_op jit(solution)/shard_map/all_to_all | solution.py:48
  51.0 3.3 copy.16
  54.3 37.9 %all-to-all-done.1 = f32[16,2,32,512]{3,2,1,0:T(8,128)} async-done(((f32[16,2,32,512]{3,2,1,0:T(8,128)}), f32[16,2,32,512]{3,2,1,0:T(8,128)}, u32[]{:S(2)}, u32[]{:S(2)}) %all-to-all-start.1) | async-done | bytes 2097184 | tf_op jit(solution)/shard_map/all_to_all | solution.py:48
  92.2 11.3 %all-to-all-start = ((f32[16,2,32,512]{3,2,1,0:T(8,128)}), f32[16,2,32,512]{3,2,1,0:T(8,128)}, u32[]{:S(2)}, u32[]{:S(2)}) async-start(f32[16,2,32,512]{3,2,1,0:T(8,128)} %bitcast.571), calls=%async_computation | async-start | bytes 4194304 | tf_op jit(solution)/shard_map/all_to_all | solution.py:48
  103.5 3.4 copy.20
  106.8 37.8 %all-to-all-done = f32[16,2,32,512]{3,2,1,0:T(8,128)} async-done(((f32[16,2,32,512]{3,2,1,0:T(8,128)}), f32[16,2,32,512]{3,2,1,0:T(8,128)}, u32[]{:S(2)}, u32[]{:S(2)}) %all-to-all-start) | async-done | bytes 2097184 | tf_op jit(solution)/shard_map/all_to_all | solution.py:48
  144.6 11.3 %all-to-all-start.2 = ((f32[16,2,32,512]{3,2,1,0:T(8,128)}), f32[16,2,32,512]{3,2,1,0:T(8,128)}, u32[]{:S(2)}, u32[]{:S(2)}) async-start(f32[16,2,32,512]{3,2,1,0:T(8,128)} %bitcast.572), calls=%async_computation.2 | async-start | bytes 4194304 | tf_op jit(solution)/shard_map/all_to_all | solution.py:48
  155.9 3.4 copy.22
  159.3 37.8 %all-to-all-done.2 = f32[16,2,32,512]{3,2,1,0:T(8,128)} async-done(((f32[16,2,32,512]{3,2,1,0:T(8,128)}), f32[16,2,32,512]{3,2,1,0:T(8,128)}, u32[]{:S(2)}, u32[]{:S(2)}) %all-to-all-start.2) | async-done | bytes 2097184 | tf_op jit(solution)/shard_map/all_to_all | solution.py:48
  197.1 11.3 %all-to-all-start.3 = ((f32[16,2,32,512]{3,2,1,0:T(8,128)}), f32[16,2,32,512]{3,2,1,0:T(8,128)}, u32[]{:S(2)}, u32[]{:S(2)}) async-start(f32[16,2,32,512]{3,2,1,0:T(8,128)} %bitcast.573), calls=%async_computation.3 | async-start | bytes 4194304 | tf_op jit(solution)/shard_map/all_to_all | solution.py:48
  208.3 3.4 copy.24
  211.7 37.8 %all-to-all-done.3 = f32[16,2,32,512]{3,2,1,0:T(8,128)} async-done(((f32[16,2,32,512]{3,2,1,0:T(8,128)}), f32[16,2,32,512]{3,2,1,0:T(8,128)}, u32[]{:S(2)}, u32[]{:S(2)}) %all-to-all-start.3) | async-done | bytes 2097184 | tf_op jit(solution)/shard_map/all_to_all | solution.py:48
  249.5 11.3 %all-to-all-start.4 = ((f32[16,2,32,512]{3,2,1,0:T(8,128)}), f32[16,2,32,512]{3,2,1,0:T(8,128)}, u32[]{:S(2)}, u32[]{:S(2)}) async-start(f32[16,2,32,512]{3,2,1,0:T(8,128)} %bitcast.574), calls=%async_computation.4 | async-start | bytes 4194304 | tf_op jit(solution)/shard_map/all_to_all | solution.py:48
  260.8 3.4 copy.26
  264.1 37.8 %all-to-all-done.4 = f32[16,2,32,512]{3,2,1,0:T(8,128)} async-done(((f32[16,2,32,512]{3,2,1,0:T(8,128)}), f32[16,2,32,512]{3,2,1,0:T(8,128)}, u32[]{:S(2)}, u32[]{:S(2)}) %all-to-all-start.4) | async-done | bytes 2097184 | tf_op jit(solution)/shard_map/all_to_all | solution.py:48
  301.9 11.3 %all-to-all-start.5 = ((f32[16,2,32,512]{3,2,1,0:T(8,128)}), f32[16,2,32,512]{3,2,1,0:T(8,128)}, u32[]{:S(2)}, u32[]{:S(2)}) async-start(f32[16,2,32,512]{3,2,1,0:T(8,128)} %bitcast.575), calls=%async_computation.5 | async-start | bytes 4194304 | tf_op jit(solution)/shard_map/all_to_all | solution.py:48
  313.2 3.3 copy.28
  316.5 37.8 %all-to-all-done.5 = f32[16,2,32,512]{3,2,1,0:T(8,128)} async-done(((f32[16,2,32,512]{3,2,1,0:T(8,128)}), f32[16,2,32,512]{3,2,1,0:T(8,128)}, u32[]{:S(2)}, u32[]{:S(2)}) %all-to-all-start.5) | async-done | bytes 2097184 | tf_op jit(solution)/shard_map/all_to_all | solution.py:48
  354.4 11.3 %all-to-all-start.6 = ((f32[16,2,32,512]{3,2,1,0:T(8,128)}), f32[16,2,32,512]{3,2,1,0:T(8,128)}, u32[]{:S(2)}, u32[]{:S(2)}) async-start(f32[16,2,32,512]{3,2,1,0:T(8,128)} %bitcast.570), calls=%async_computation.6 | async-start | bytes 4194304 | tf_op jit(solution)/shard_map/all_to_all | solution.py:48
  367.4 39.4 %all-to-all-done.6 = f32[16,2,32,512]{3,2,1,0:T(8,128)} async-done(((f32[16,2,32,512]{3,2,1,0:T(8,128)}), f32[16,2,32,512]{3,2,1,0:T(8,128)}, u32[]{:S(2)}, u32[]{:S(2)}) %all-to-all-start.6) | async-done | bytes 2097184 | tf_op jit(solution)/shard_map/all_to_all | solution.py:48
  406.8 11.3 %all-to-all-start.7 = ((f32[16,2,32,512]{3,2,1,0:T(8,128)}), f32[16,2,32,512]{3,2,1,0:T(8,128)}, u32[]{:S(2)}, u32[]{:S(2)}) async-start(f32[16,2,32,512]{3,2,1,0:T(8,128)} %bitcast.569), calls=%async_computation.7 | async-start | bytes 4194304 | tf_op jit(solution)/shard_map/all_to_all | solution.py:48
  418.1 7.8 %slice_bitcast_fusion = f32[2,8,8,64,256]{4,3,2,1,0:T(8,128)} fusion(f32[2,8,8,2,64,256]{5,4,3,2,1,0:T(8,128)} %bitcast.518), kind=kLoop, calls=%fused_computation | loop fusion | bytes 16777216 | tf_op jit(solution)/shard_map/squeeze | solution.py:38
  425.9 5.5 collective-permute-start
  436.9 6.9 collective-permute-start.3
  452.9 3.2 copy.23
  456.1 3.2 copy.25
  459.2 3.2 copy.27
  481.4 9.5 %fusion = f32[2,8,8,64,256]{4,3,2,1,0:T(8,128)} fusion(f32[2,8,8,64,256]{4,3,2,1,0:T(8,128)} %collective-permute-done, f32[2,8,8,2,64,256]{5,4,3,2,1,0:T(8,128)} %bitcast.520, pred[]{:T(512)S(6)} %eq.3), kind=kLoop, calls=%fused_computation.2 | loop fusion | flops 2097152 | bytes 25165824 | tf_op jit(solution)/shard_map/jit(_where)/select_n | solution.py:40
  512.0 11.6 %broadcast_select_fusion = f32[2,8,1024,256]{3,2,1,0:T(8,128)S(1)} fusion(f32[2,8,1024,256]{3,2,1,0:T(8,128)} %collective-permute-done.2, pred[]{:T(512)S(6)} %eq.3, f32[1,2,8,1024,256]{4,3,2,1,0:T(8,128)} %param.2), kind=kLoop, calls=%fused_computation.3 | loop fusion | flops 4194304 | bytes 50331648 | tf_op jit(solution)/shard_map/jit(_where)/select_n | solution.py:42
  524.6 2.4 fusion.40
  527.1 2.4 fusion.42
  531.8 2.4 fusion.44
  534.2 2.4 fusion.45
  536.6 2.4 fusion.46
  540.1 2.4 fusion.36
  543.6 2.5 fusion.38
  547.3 2.4 fusion.34
  550.8 2.5 fusion.32
  554.3 2.4 fusion.30
  557.8 2.4 fusion.28
  561.3 2.4 fusion.26
  563.7 6.5 add_add_fusion.1
  570.2 3.3 add_add_fusion
  576.3 7.3 %subtract_bitcast_fusion = f32[512,1,1024]{2,0,1:T(8,128)} fusion(f32[512,1024]{1,0:T(8,128)S(1)} %add_add_fusion, f32[512,1024]{1,0:T(8,128)S(1)} %add_add_fusion.1, f32[512,1024]{1,0:T(8,128)} %fusion.26, f32[512,1024]{1,0:T(8,128)} %fusion.28, f32[512,1024]{1,0:T(8,128)} %fusion.30, f32[512,1024]{1,0:T(8,128)} %fusion.32, f32[512,1024]{1,0:T(8,128)S(1)} %copy-done.6, ...), kind=kOutput, calls=%fused_computation.13 | convolution fusion | flops 810549248 | bytes 24641536 | tf_op jit(solution)/shard_map/ml,ol->mo/dot_general | solution.py:18
  583.7 4.1 pad_maximum_fusion
  587.8 89.8 %reduce-scatter.2.cloned.1.call-done = f32[64,2,1024]{2,0,1:T(8,128)} async-done(((f32[512,2,1024]{2,0,1:T(8,128)}), f32[64,2,1024]{2,0,1:T(8,128)}) %reduce-scatter.2.cloned.1.call-update) | async-done | bytes 524304 | tf_op jit(solution)/shard_map/reduce_scatter | solution.py:65
  (137 shorter events, 73.2 us)
Async XLA Ops:
  43.6 48.6 %all-to-all-start.1 = ((f32[16,2,32,512]{3,2,1,0:T(8,128)}), f32[16,2,32,512]{3,2,1,0:T(8,128)}, u32[]{:S(2)}, u32[]{:S(2)}) async-start(f32[16,2,32,512]{3,2,1,0:T(8,128)} %bitcast.576), calls=%async_computation.1 | async-start | bytes 4194304 | tf_op jit(solution)/shard_map/all_to_all | solution.py:48
  92.2 52.4 %all-to-all-start = ((f32[16,2,32,512]{3,2,1,0:T(8,128)}), f32[16,2,32,512]{3,2,1,0:T(8,128)}, u32[]{:S(2)}, u32[]{:S(2)}) async-start(f32[16,2,32,512]{3,2,1,0:T(8,128)} %bitcast.571), calls=%async_computation | async-start | bytes 4194304 | tf_op jit(solution)/shard_map/all_to_all | solution.py:48
  144.6 52.4 %all-to-all-start.2 = ((f32[16,2,32,512]{3,2,1,0:T(8,128)}), f32[16,2,32,512]{3,2,1,0:T(8,128)}, u32[]{:S(2)}, u32[]{:S(2)}) async-start(f32[16,2,32,512]{3,2,1,0:T(8,128)} %bitcast.572), calls=%async_computation.2 | async-start | bytes 4194304 | tf_op jit(solution)/shard_map/all_to_all | solution.py:48
  197.1 52.4 %all-to-all-start.3 = ((f32[16,2,32,512]{3,2,1,0:T(8,128)}), f32[16,2,32,512]{3,2,1,0:T(8,128)}, u32[]{:S(2)}, u32[]{:S(2)}) async-start(f32[16,2,32,512]{3,2,1,0:T(8,128)} %bitcast.573), calls=%async_computation.3 | async-start | bytes 4194304 | tf_op jit(solution)/shard_map/all_to_all | solution.py:48
  249.5 52.4 %all-to-all-start.4 = ((f32[16,2,32,512]{3,2,1,0:T(8,128)}), f32[16,2,32,512]{3,2,1,0:T(8,128)}, u32[]{:S(2)}, u32[]{:S(2)}) async-start(f32[16,2,32,512]{3,2,1,0:T(8,128)} %bitcast.574), calls=%async_computation.4 | async-start | bytes 4194304 | tf_op jit(solution)/shard_map/all_to_all | solution.py:48
  301.9 52.4 %all-to-all-start.5 = ((f32[16,2,32,512]{3,2,1,0:T(8,128)}), f32[16,2,32,512]{3,2,1,0:T(8,128)}, u32[]{:S(2)}, u32[]{:S(2)}) async-start(f32[16,2,32,512]{3,2,1,0:T(8,128)} %bitcast.575), calls=%async_computation.5 | async-start | bytes 4194304 | tf_op jit(solution)/shard_map/all_to_all | solution.py:48
  354.4 52.4 %all-to-all-start.6 = ((f32[16,2,32,512]{3,2,1,0:T(8,128)}), f32[16,2,32,512]{3,2,1,0:T(8,128)}, u32[]{:S(2)}, u32[]{:S(2)}) async-start(f32[16,2,32,512]{3,2,1,0:T(8,128)} %bitcast.570), calls=%async_computation.6 | async-start | bytes 4194304 | tf_op jit(solution)/shard_map/all_to_all | solution.py:48
  406.8 57.4 %all-to-all-start.7 = ((f32[16,2,32,512]{3,2,1,0:T(8,128)}), f32[16,2,32,512]{3,2,1,0:T(8,128)}, u32[]{:S(2)}, u32[]{:S(2)}) async-start(f32[16,2,32,512]{3,2,1,0:T(8,128)} %bitcast.569), calls=%async_computation.7 | async-start | bytes 4194304 | tf_op jit(solution)/shard_map/all_to_all | solution.py:48
  418.1 259.5 %reduce-scatter.2.cloned.1.call-start = ((), (), s32[]{:S(2)}) async-start(), calls=%async_computation.9 | async-start | bytes 4718592 | tf_op jit(solution)/shard_map/reduce_scatter | solution.py:65
  425.9 55.6 %collective-permute-start = (f32[2,8,8,64,256]{4,3,2,1,0:T(8,128)}, f32[2,8,8,64,256]{4,3,2,1,0:T(8,128)}, u32[]{:S(2)}, u32[]{:S(2)}) collective-permute-start(f32[2,8,8,64,256]{4,3,2,1,0:T(8,128)} %slice_bitcast_fusion), channel_id=1, source_target_pairs={{0,1},{2,3},{4,5},{6,7},{8,9},{10,11},{12,13},{14,15},{16,17},{18,... | collective-permute-start | bytes 25165832 | tf_op jit(solution)/shard_map/ppermute | solution.py:38
  431.4 80.6 %collective-permute-start.2 = (f32[2,8,1024,256]{3,2,1,0:T(8,128)}, f32[2,8,1024,256]{3,2,1,0:T(8,128)}, u32[]{:S(2)}, u32[]{:S(2)}) collective-permute-start(f32[2,8,1024,256]{3,2,1,0:T(8,128)} %bitcast.519), channel_id=1, source_target_pairs={{1,0},{3,2},{5,4},{7,6},{9,8},{11,10},{13,12},{15,14},{17,16},{19,... | collective-permute-start | bytes 50331656 | tf_op jit(solution)/shard_map/ppermute | solution.py:39
  436.9 37.1 %collective-permute-start.3 = (f32[2,256,256]{2,1,0:T(8,128)}, f32[2,256,256]{2,1,0:T(8,128)}, u32[]{:S(2)}, u32[]{:S(2)}) collective-permute-start(f32[2,256,256]{2,1,0:T(8,128)} %maximum_multiply_fusion.1), channel_id=1, source_target_pairs={{0,1},{1,0},{2,3},{3,2},{4,5},{5,4},{6,7},{7,6},{8,9},{9,8},{10,11... | collective-permute-start | bytes 1572872 | tf_op jit(solution)/shard_map/ppermute | solution.py:12
  447.7 27.5 %collective-permute-start.1 = (f32[2,256,256]{2,1,0:T(8,128)}, f32[2,256,256]{2,1,0:T(8,128)}, u32[]{:S(2)}, u32[]{:S(2)}) collective-permute-start(f32[2,256,256]{2,1,0:T(8,128)} %maximum_multiply_fusion), channel_id=1, source_target_pairs={{0,1},{1,0},{2,3},{3,2},{4,5},{5,4},{6,7},{7,6},{8,9},{9,8},{10,11... | collective-permute-start | bytes 1572872 | tf_op jit(solution)/shard_map/ppermute | solution.py:12
  450.8 0.7 copy-start.11
  452.4 24.5 %collective-permute-start.4 = (f32[2,256,256]{2,1,0:T(8,128)}, f32[2,256,256]{2,1,0:T(8,128)}, u32[]{:S(2)}, u32[]{:S(2)}) collective-permute-start(f32[2,256,256]{2,1,0:T(8,128)} %maximum_multiply_fusion.2), channel_id=1, source_target_pairs={{0,1},{1,0},{2,3},{3,2},{4,5},{5,4},{6,7},{7,6},{8,9},{9,8},{10,11... | collective-permute-start | bytes 1572872 | tf_op jit(solution)/shard_map/ppermute | solution.py:12
  464.2 2.2 copy-start.3
  466.5 1.6 copy-start.2
  468.1 1.6 copy-start.1
  473.9 3.0 copy-start.12
  474.0 4.1 collective-permute-start.5
  475.2 3.5 collective-permute-start.6
  476.9 2.0 collective-permute-start.7
  478.1 2.1 collective-permute-start.8
  478.8 2.2 collective-permute-start.9
  480.3 23.6 %copy-start.8 = (f32[2,256,256]{2,1,0:T(8,128)}, f32[2,256,256]{2,1,0:T(8,128)S(1)}, u32[]{:S(2)}) copy-start(f32[2,256,256]{2,1,0:T(8,128)S(1)} %fusion.369) | copy-start | bytes 1572868
  481.4 22.8 %copy-start.10 = (f32[2,256,256]{2,1,0:T(8,128)}, f32[2,256,256]{2,1,0:T(8,128)S(1)}, u32[]{:S(2)}) copy-start(f32[2,256,256]{2,1,0:T(8,128)S(1)} %fusion.368) | copy-start | bytes 1572868
  491.0 10.6 %copy-start = (f32[2,8,8,64,256]{4,3,2,1,0:T(8,128)S(1)}, f32[2,8,8,64,256]{4,3,2,1,0:T(8,128)}, u32[]{:S(2)}) copy-start(f32[2,8,8,64,256]{4,3,2,1,0:T(8,128)} %fusion) | copy-start | bytes 25165828
  509.8 1.0 copy-start.9
  557.8 2.4 copy-start.7
  573.5 1.6 copy-start.4
  573.5 2.2 copy-start.5
  573.5 2.8 copy-start.6
Sparse Core Ops, SparseCore 0:
  587.9 89.6 reduce-scatter.1

commit v2 on v1

--- a/solution.py
+++ b/solution.py
@@ -1,11 +1,19 @@
+import functools
 import math
 
 import jax
 import jax.numpy as jnp
 from jax import lax
+from jax.experimental import pallas as pl
+from jax.experimental.pallas import tpu as pltpu
 from jax.sharding import PartitionSpec as P
 
 HIGH = lax.Precision.HIGH
+MIB = 1 << 20
+WINDOW = 4
+ANYWHERE = pl.BlockSpec(memory_space=pl.ANY)
+IN_VMEM = pl.BlockSpec(memory_space=pltpu.VMEM)
+IN_SMEM = pl.BlockSpec(memory_space=pltpu.SMEM)
 
 
 def swapped(x, axis):
@@ -19,7 +27,7 @@
     return first, second, mixed
 
 
-def on_device(left_factor, right_factor):
+def general(left_factor, right_factor):
     idx_size = lax.axis_size("idx")
     half_size = lax.axis_size("half")
     left = left_factor[0]
@@ -31,16 +39,13 @@
     half_cols = between // half_size
     is_lower = lax.axis_index("half") == 0
     scale = 1.0 / math.sqrt(2.0 * batch * between)
-
     pieces = right.reshape(2, idx_size, local_batch, inner_part, half_size, half_cols)
-
     split_rows = left.reshape(2, local_batch, idx_size, half_size, own_rows, inner)
     upper_rows = lax.ppermute(split_rows[:, :, :, 1], "half", [(0, 1)])
     other_whole = lax.ppermute(left, "half", [(1, 0)])
     first_left = jnp.where(is_lower, split_rows[:, :, :, 0], upper_rows)
     first_left = first_left.reshape(2, local_batch, half_rows, inner)
     second_left = jnp.where(is_lower, other_whole, left)
-
     totals = None
     for b in range(local_batch):
         outgoing = jnp.transpose(pieces[:, :, b], (1, 3, 0, 2, 4))
@@ -65,6 +70,285 @@
     return lax.psum_scatter(partial, "idx", scatter_dimension=0, tiled=True)
 
 
+def split_float(x):
+    high = x.astype(jnp.bfloat16)
+    return high, (x - high.astype(jnp.float32)).astype(jnp.bfloat16)
+
+
+def dot_parts(left, right, dims):
+    def dot(a, b):
+        return lax.dot_general(a, b, (dims, ((), ())), preferred_element_type=jnp.float32)
+
+    return dot(left[0], right[0]) + (dot(left[0], right[1]) + dot(left[1], right[0]))
+
+
+def complex_dot(left_real, left_imag, right_real, right_imag, dims):
+    first = dot_parts(split_float(left_real), split_float(right_real), dims)
+    second = dot_parts(split_float(left_imag), split_float(right_imag), dims)
+    mixed = dot_parts(
+        split_float(left_real + left_imag), split_float(right_real + right_imag), dims
+    )
+    return first - second, mixed - first - second
+
+
+NT = ((1,), (1,))
+NN = ((1,), (0,))
+
+
+def deal_kernel(start, count, half_cols, place, right, *refs):
+    outs, sems = refs[:-1], refs[-1]
+    idx, half = place[0], place[1]
+    copies = []
+    for slot, out in enumerate(outs):
+        far, side = slot // 2, slot % 2
+        column = pl.multiple_of((half ^ side) * half_cols, half_cols)
+        source = right.at[:, idx ^ far, pl.ds(start, count), :, pl.ds(column, half_cols)]
+        copy = pltpu.make_async_copy(source, out, sems.at[slot])
+        copy.start()
+        copies.append(copy)
+    for copy in copies:
+        copy.wait()
+
+
+def core_kernel(count, inner_part, scale, place, *refs):
+    pieces, core, factors, sems = refs[:-3], refs[-3], refs[-2], refs[-1]
+    idx, half = place[0], place[1]
+    copies = []
+    for slot, piece in enumerate(pieces):
+        far, side = slot // 2, slot % 2
+        row = pl.multiple_of((idx ^ far) * inner_part, inner_part)
+        target = factors.at[half ^ side, :, :, pl.ds(row, inner_part), :]
+        copy = pltpu.make_async_copy(piece, target, sems.at[slot])
+        copy.start()
+        copies.append(copy)
+    for copy in copies:
+        copy.wait()
+    for b in range(count):
+        real, imag = complex_dot(
+            factors[0, 0, b], factors[0, 1, b], factors[1, 0, b], factors[1, 1, b], NT
+        )
+        core[b, 0] = real * scale
+        core[b, 1] = imag * scale
+
+
+def amplitude_kernel(start, count, tile, fresh, place, own_core, other_core, own_left, other_left, *refs):
+    before = None if fresh else refs[0]
+    total, first, second, product, sems, sum_sem = refs[-6:]
+    half = place[1]
+
+    def copies(lower):
+        pairs = (own_left, other_left) if lower else (other_left, own_left)
+        side = 0 if lower else 1
+        return [
+            pltpu.make_async_copy(pairs[0].at[:, pl.ds(start, count), :, side], first, sems.at[0]),
+            pltpu.make_async_copy(pairs[1].at[:, pl.ds(start, count)], second, sems.at[1]),
+        ]
+
+    for lower in (True, False):
+
+        @pl.when(half == (0 if lower else 1))
+        def _():
+            for copy in copies(lower):
+                copy.start()
+
+    if not fresh:
+        loading = pltpu.make_async_copy(before, total, sum_sem)
+        loading.start()
+    for lower in (True, False):
+
+        @pl.when(half == (0 if lower else 1))
+        def _():
+            for copy in copies(lower):
+                copy.wait()
+
+    if not fresh:
+        loading.wait()
+    _, _, groups, own_rows, inner = first.shape
+    rows = groups * own_rows
+    columns = second.shape[2] * second.shape[3] * second.shape[4]
+    for b in range(count):
+        real, imag = complex_dot(
+            first[0, b].reshape(rows, inner),
+            first[1, b].reshape(rows, inner),
+            own_core[b, 0] + other_core[b, 0],
+            own_core[b, 1] + other_core[b, 1],
+            NN,
+        )
+        for place_in, part in enumerate((real, imag, real + imag)):
+            product[2 * place_in], product[2 * place_in + 1] = split_float(part)
+
+        def column_tile(step, carry):
+            at = pl.multiple_of(step * tile, tile)
+            per = second.shape[3] * second.shape[4]
+            right_real = second[0, b, pl.ds(step * (tile // per), tile // per)].reshape(tile, inner)
+            right_imag = second[1, b, pl.ds(step * (tile // per), tile // per)].reshape(tile, inner)
+            one = dot_parts((product[0], product[1]), split_float(right_real), NT)
+            two = dot_parts((product[2], product[3]), split_float(right_imag), NT)
+            three = dot_parts((product[4], product[5]), split_float(right_real + right_imag), NT)
+            spot = pl.ds(at, tile)
+            if fresh and b == 0:
+                total[0, :, spot] = one - two
+                total[1, :, spot] = three - one - two
+            else:
+                total[0, :, spot] += one - two
+                total[1, :, spot] += three - one - two
+            return carry
+
+        lax.fori_loop(0, columns // tile, column_tile, 0)
+
+
+def sending_order(devices):
+    far = list(range(devices // 2, devices))
+    near = list(range(1, devices // 2))
+    order = []
+    for i, slot in enumerate(far):
+        order.append(slot)
+        order += near[i : i + 1]
+    return order
+
+
+def pieces_of(arrived, pieces, q):
+    return arrived[q] if q < len(arrived) else pieces
+
+
+def chunks_of(count):
+    sizes = []
+    left = count
+    while left:
+        size = 2 if left > 2 else 1
+        sizes.append(size)
+        left -= size
+    return sizes
+
+
+def overlapped(left_factor, right_factor):
+    idx_size = lax.axis_size("idx")
+    _, _, local_batch, rows, inner = left_factor.shape
+    _, _, batch, inner_part, between = right_factor.shape
+    own_rows = rows // (idx_size * 2)
+    half_rows = rows // 2
+    half_cols = between // 2
+    scale = 1.0 / math.sqrt(2.0 * batch * between)
+    place = jnp.stack([lax.axis_index("idx"), lax.axis_index("half")]).astype(jnp.int32)
+    right = right_factor.reshape(2, idx_size, local_batch, inner_part, between)
+    devices = idx_size * 2
+    params = pltpu.CompilerParams(vmem_limit_bytes=40 * MIB)
+
+    sizes = chunks_of(local_batch)
+    starts = [sum(sizes[:q]) for q in range(len(sizes))]
+    shape = (2, local_batch, idx_size, 2, own_rows, inner)
+    own_left = left_factor.reshape(shape)
+    other_left = None
+
+    def dealt(start, count, source):
+        pieces = pl.pallas_call(
+            functools.partial(deal_kernel, start, count, half_cols),
+            out_shape=[jax.ShapeDtypeStruct((2, count, inner_part, half_cols), jnp.float32)] * devices,
+            in_specs=[IN_SMEM, ANYWHERE],
+            out_specs=[ANYWHERE] * devices,
+            scratch_shapes=[pltpu.SemaphoreType.DMA((devices,))],
+            cost_estimate=pl.CostEstimate(
+                flops=0, bytes_accessed=2 * devices * 8 * count * inner_part * half_cols, transcendentals=0
+            ),
+            compiler_params=params,
+        )(place, source)
+        return list(pieces)
+
+    def core_of(count, pieces):
+        return pl.pallas_call(
+            functools.partial(core_kernel, count, inner_part, scale),
+            out_shape=jax.ShapeDtypeStruct((count, 2, inner, inner), jnp.float32),
+            in_specs=[IN_SMEM] + [ANYWHERE] * devices,
+            out_specs=IN_VMEM,
+            scratch_shapes=[
+                pltpu.VMEM((2, 2, count, inner, half_cols), jnp.float32),
+                pltpu.SemaphoreType.DMA((devices,)),
+            ],
+            cost_estimate=pl.CostEstimate(
+                flops=18 * count * inner * inner * half_cols,
+                bytes_accessed=16 * count * inner * (inner + half_cols),
+                transcendentals=0,
+            ),
+            compiler_params=params,
+        )(place, *pieces)
+
+    def added(start, count, core, other_core, total):
+        fresh = total is None
+        return pl.pallas_call(
+            functools.partial(amplitude_kernel, start, count, 256, fresh),
+            out_shape=jax.ShapeDtypeStruct((2, half_rows, rows), jnp.float32),
+            in_specs=[IN_SMEM, IN_VMEM, IN_VMEM, ANYWHERE, ANYWHERE] + [ANYWHERE] * (not fresh),
+            out_specs=IN_VMEM,
+            scratch_shapes=[
+                pltpu.VMEM((2, count, idx_size, own_rows, inner), jnp.float32),
+                pltpu.VMEM((2, count, idx_size, 2, own_rows, inner), jnp.float32),
+                pltpu.VMEM((6, half_rows, inner), jnp.bfloat16),
+                pltpu.SemaphoreType.DMA((2,)),
+                pltpu.SemaphoreType.DMA,
+            ],
+            cost_estimate=pl.CostEstimate(
+                flops=18 * count * half_rows * inner * (inner + rows),
+                bytes_accessed=count * 12 * rows * inner + 16 * half_rows * rows,
+                transcendentals=0,
+            ),
+            compiler_params=params,
+        )(place, core, other_core, own_left, other_left, *([] if fresh else [total]))
+
+    order = sending_order(devices)
+    other_left = None
+    total = None
+    landed = []
+    arrived = []
+
+    def finish(q):
+        core = core_of(sizes[q], arrived[q])
+        return added(starts[q], sizes[q], core, swapped(core, "half"), total)
+
+    upcoming = dealt(starts[0], sizes[0], right)
+    for q in range(len(sizes)):
+        pieces = upcoming
+        for turn, slot in enumerate(order):
+            piece = pieces[slot]
+            if len(landed) >= WINDOW:
+                old_q, old_slot = landed[-WINDOW]
+                piece, arrived_piece = lax.optimization_barrier((piece, pieces_of(arrived, pieces, old_q)[old_slot]))
+                pieces_of(arrived, pieces, old_q)[old_slot] = arrived_piece
+            if q and turn == WINDOW + 1:
+                arrived[q - 1], pieces[order[1]] = lax.optimization_barrier((arrived[q - 1], pieces[order[1]]))
+                total = finish(q - 1)
+            if q and turn == len(order) - 4:
+                piece, total = lax.optimization_barrier((piece, total))
+            if q + 1 < len(sizes) and turn == WINDOW + 3:
+                piece, upcoming = lax.optimization_barrier((piece, upcoming))
+            pairs = [(i, i ^ slot) for i in range(devices)]
+            pieces[slot] = lax.ppermute(piece, ("idx", "half"), pairs)
+            landed.append((q, slot))
+            if q == 0 and turn == 1:
+                other_left = swapped(left_factor, "half").reshape(shape)
+            if q + 1 < len(sizes) and turn == 4:
+                source, pieces[order[0]] = lax.optimization_barrier((right, pieces[order[0]]))
+                upcoming = dealt(starts[q + 1], sizes[q + 1], source)
+        arrived.append(pieces)
+    total = finish(len(sizes) - 1)
+
+    return lax.psum_scatter(jnp.moveaxis(total, 0, 1), "idx", scatter_dimension=0, tiled=True)
+
+
+def on_device(left_factor, right_factor):
+    idx_size = lax.axis_size("idx")
+    rows, inner_part, between = left_factor.shape[3], right_factor.shape[3], right_factor.shape[4]
+    aligned = (
+        lax.axis_size("half") == 2
+        and idx_size in (2, 4, 8)
+        and inner_part % 8 == 0
+        and between % 256 == 0
+        and rows % 256 == 0
+        and rows % (16 * idx_size) == 0
+        and 256 % (rows // idx_size) == 0
+    )
+    return (overlapped if aligned else general)(left_factor, right_factor)
+
+
 def solution(mesh):
     return jax.shard_map(
         on_device,

time: 697 us -> 562 us (0.81); the launches traced: 687 us -> 562 us
  matrix products: 87.7 us -> 0 us
  local copies, waits for them, and re-layouts: 91.6 us -> 4.24 us
  Pallas kernels: 0 us -> 77.3 us
  starting transfers between devices: 102 us -> 165 us
  waiting for transfers between devices: 358 us -> 301 us
  other arithmetic: 32.6 us -> 0.07 us
    all_to_all x8 -> x0, waiting for transfers between devices: 266 us -> none  [on_device(): arrived = lax.all_to_all(outgoing, ('idx', 'half'), 0, 0, tiled=True)]
    ppermute x2 -> x75, waiting for transfers between devices: 0.01 us -> 211 us  [overlapped(): pieces[slot] = lax.ppermute(piece, ('idx', 'half'), pairs)]
    ppermute x2 -> x75, starting transfers between devices: 7.03 us -> 163 us  [overlapped(): pieces[slot] = lax.ppermute(piece, ('idx', 'half'), pairs)]
    dot_general x72 -> x0, matrix products: 87.7 us -> none  [the longest x24 33.4 us: complex_terms(): jnp.einsum(pattern, left_real + left_imag, right_real + right_imag, preci...]
    all_to_all x8 -> x0, starting transfers between devices: 86.3 us -> none  [on_device(): arrived = lax.all_to_all(outgoing, ('idx', 'half'), 0, 0, tiled=True)]
    pallas_call x0 -> x15, Pallas kernels: none -> 77.3 us  [the longest x5 50.1 us: added(): pl.pallas_call(functools.partial(amplitude_kernel, start, count, 256, fre...]
    transpose x9 -> x0, local copies, waits for them, and re-layouts: 36.8 us -> none  [on_device(): outgoing = jnp.transpose(pieces[:, :, b], (1, 3, 0, 2, 4))]
    another operation x1 -> x0, local copies, waits for them, and re-layouts: 22.1 us -> none  [on_device(): right.reshape(2, idx_size, local_batch, inner_part, half_size, half_cols)]
  transfers between devices with their start and end apart: 19 -> 82, of which waited for: 10 -> 41; matrix products, arithmetic and copies ran while one was open for 14% -> 0% of each run, Pallas kernels for 0% -> 11%
where the time goes in v2:
time: 562 us
  waiting for transfers between devices  301 us (54%)
  starting transfers between devices  165 us (29%)
  Pallas kernels  77.3 us (14%)
  between operations  13.7 us (2%)
    ppermute x75, waiting for transfers between devices, overlapped(): pieces[slot] = lax.ppermute(piece, ('idx', 'half'), pairs)  211 us
    ppermute x75, starting transfers between devices, overlapped(): pieces[slot] = lax.ppermute(piece, ('idx', 'half'), pairs)  163 us
    reduce_scatter x1, waiting for transfers between devices, overlapped(): lax.psum_scatter(jnp.moveaxis(total, 0, 1), 'idx', scatter_dimension=0, t...  88.3 us
    pallas_call x5, Pallas kernels, added(): pl.pallas_call(functools.partial(amplitude_kernel, start, count, 256, fre...  50.1 us
    pallas_call x5, Pallas kernels, core_of(): pl.pallas_call(functools.partial(core_kernel, count, inner_part, scale),...  14.1 us
    pallas_call x5, Pallas kernels, dealt(): pl.pallas_call(functools.partial(deal_kernel, start, count, half_cols), o...  13.2 us
  transfers between devices with their start and end apart: 82, of which 41 were waited for; matrix products, arithmetic and copies ran while one was open for 0% of the time, Pallas kernels for 11%

profile of v2, /device:TPU:0, one launch (start us, length us, event | category | flops | bytes accessed | tf_op | source)
XLA Modules:
  0.0 561.6 jit_solution(2135437835220726036)
XLA Ops:
  9.9 3.7 collective-permute-start.1
  13.8 18.1 %collective-permute-done.1.refs_8_ = f32[2,2,32,512]{3,2,1,0:T(8,128)S(1)} collective-permute-done((f32[2,2,32,512]{3,2,1,0:T(8,128)S(1)}, f32[2,2,32,512]{3,2,1,0:T(8,128)S(1)}, u32[]{:S(2)}, u32[]{:S(2)}) %collective-permute-start.1) | collective-permute-done | bytes 262176 | tf_op jit(solution)/shard_map/ppermute | solution.py:324
  33.7 9.1 %collective-permute-done.2.refs_9_ = f32[2,2,32,512]{3,2,1,0:T(8,128)S(1)} collective-permute-done((f32[2,2,32,512]{3,2,1,0:T(8,128)S(1)}, f32[2,2,32,512]{3,2,1,0:T(8,128)S(1)}, u32[]{:S(2)}, u32[]{:S(2)}) %collective-permute-start.2) | collective-permute-done | bytes 262176 | tf_op jit(solution)/shard_map/ppermute | solution.py:324
  44.7 10.9 %collective-permute-done.20.refs_10_ = f32[2,2,32,512]{3,2,1,0:T(8,128)S(1)} collective-permute-done((f32[2,2,32,512]{3,2,1,0:T(8,128)S(1)}, f32[2,2,32,512]{3,2,1,0:T(8,128)S(1)}, u32[]{:S(2)}, u32[]{:S(2)}) %collective-permute-start.20) | collective-permute-done | bytes 262176 | tf_op jit(solution)/shard_map/ppermute | solution.py:324
  55.6 3.2 collective-permute-start.21
  61.8 4.2 collective-permute-done.3.refs_11_
  66.0 3.8 collective-permute-start.4
  70.0 6.1 %collective-permute-done.7.refs_4_ = f32[2,2,32,512]{3,2,1,0:T(8,128)S(1)} collective-permute-done((f32[2,2,32,512]{3,2,1,0:T(8,128)S(1)}, f32[2,2,32,512]{3,2,1,0:T(8,128)S(1)}, u32[]{:S(2)}, u32[]{:S(2)}) %collective-permute-start.7) | collective-permute-done | bytes 262176 | tf_op jit(solution)/shard_map/ppermute | solution.py:324
  81.3 6.2 %collective-permute-done.12.refs_5_ = f32[2,2,32,512]{3,2,1,0:T(8,128)S(1)} collective-permute-done((f32[2,2,32,512]{3,2,1,0:T(8,128)S(1)}, f32[2,2,32,512]{3,2,1,0:T(8,128)S(1)}, u32[]{:S(2)}, u32[]{:S(2)}) %collective-permute-start.12) | collective-permute-done | bytes 262176 | tf_op jit(solution)/shard_map/ppermute | solution.py:324
  89.9 10.2 %collective-permute-done.8.refs_6_ = f32[2,2,32,512]{3,2,1,0:T(8,128)S(1)} collective-permute-done((f32[2,2,32,512]{3,2,1,0:T(8,128)S(1)}, f32[2,2,32,512]{3,2,1,0:T(8,128)S(1)}, u32[]{:S(2)}, u32[]{:S(2)}) %collective-permute-start.8) | collective-permute-done | bytes 262176 | tf_op jit(solution)/shard_map/ppermute | solution.py:324
  100.0 5.2 collective-permute-start.9
  105.2 4.6 collective-permute-done.13.refs_7_
  117.4 7.0 %collective-permute-done.9.refs_8_ = f32[2,2,32,512]{3,2,1,0:T(8,128)S(1)} collective-permute-done((f32[2,2,32,512]{3,2,1,0:T(8,128)S(1)}, f32[2,2,32,512]{3,2,1,0:T(8,128)S(1)}, u32[]{:S(2)}, u32[]{:S(2)}) %collective-permute-start.9) | collective-permute-done | bytes 262176 | tf_op jit(solution)/shard_map/ppermute | solution.py:324
  125.2 4.4 collective-permute-done.14.refs_9_
  129.6 4.8 collective-permute-start.28
  137.3 4.9 collective-permute-done.37.refs_10_
  142.2 10.0 %collective-permute-start.38 = (f32[2,2,32,512]{3,2,1,0:T(8,128)S(1)}, f32[2,2,32,512]{3,2,1,0:T(8,128)S(1)}, u32[]{:S(2)}, u32[]{:S(2)}) collective-permute-start(f32[2,2,32,512]{3,2,1,0:T(8,128)S(1)} %get-tuple-element.559), channel_id=1, source_target_pairs={{0,12},{1,13},{2,14},{3,15},{4,8},{5,9},{6,10},{7,11},{8,4},{9,5},... | collective-permute-start | bytes 786440 | tf_op jit(solution)/shard_map/ppermute | solution.py:324
  153.3 5.9 %collective-permute-start.29 = (f32[2,2,32,512]{3,2,1,0:T(8,128)S(1)}, f32[2,2,32,512]{3,2,1,0:T(8,128)S(1)}, u32[]{:S(2)}, u32[]{:S(2)}) collective-permute-start(f32[2,2,32,512]{3,2,1,0:T(8,128)S(1)} %get-tuple-element.531), channel_id=1, source_target_pairs={{0,5},{1,4},{2,7},{3,6},{4,1},{5,0},{6,3},{7,2},{8,13},{9,12},{10,... | collective-permute-start | bytes 786440 | tf_op jit(solution)/shard_map/ppermute | solution.py:324
  159.3 3.2 collective-permute-start.16
  164.5 4.5 collective-permute-start.39
  173.0 3.7 collective-permute-done.16.refs_13_
  176.7 8.8 %collective-permute-start.17 = (f32[2,2,32,512]{3,2,1,0:T(8,128)S(1)}, f32[2,2,32,512]{3,2,1,0:T(8,128)S(1)}, u32[]{:S(2)}, u32[]{:S(2)}) collective-permute-start(f32[2,2,32,512]{3,2,1,0:T(8,128)S(1)} %get-tuple-element.453), channel_id=1, source_target_pairs={{0,15},{1,14},{2,13},{3,12},{4,11},{5,10},{6,9},{7,8},{8,7},{9,6},... | collective-permute-start | bytes 786440 | tf_op jit(solution)/shard_map/ppermute | solution.py:324
  185.5 12.0 %shard_map.32.refs_0_ = f32[2,512,1024]{2,1,0:T(8,128)S(1)} custom-call(s32[2]{0:T(128)S(1)} %pad_add_fusion.place, f32[2,2,256,256]{3,2,1,0:T(8,128)S(1)} %shard_map.31.own_core, f32[2,2,256,256]{3,2,1,0:T(8,128)S(1)} %collective-permute-done.24.other_core, f32[2,8,8,2,64,256]{5,4,3,2,1,0:T(8,128)} %bitcast.12, f32[2,8,8,2,64,256]{5,4,3,2,1,0:T(8,128)} %bitcast.4.other_left), custom_call_target="tpu_custom_call" | custom-call | flops 6039797760 | bytes 14680064 | tf_op jit(solution)/shard_map/pallas_call | solution.py:277
  197.6 12.7 %collective-permute-start.26 = (f32[2,2,32,512]{3,2,1,0:T(8,128)S(1)}, f32[2,2,32,512]{3,2,1,0:T(8,128)S(1)}, u32[]{:S(2)}, u32[]{:S(2)}) collective-permute-start(f32[2,2,32,512]{3,2,1,0:T(8,128)S(1)} %get-tuple-element.502), channel_id=1, source_target_pairs={{0,6},{1,7},{2,4},{3,5},{4,2},{5,3},{6,0},{7,1},{8,14},{9,15},{10,... | collective-permute-start | bytes 786440 | tf_op jit(solution)/shard_map/ppermute | solution.py:324
  210.3 7.0 %collective-permute-done.26.refs_6_ = f32[2,2,32,512]{3,2,1,0:T(8,128)S(1)} collective-permute-done((f32[2,2,32,512]{3,2,1,0:T(8,128)S(1)}, f32[2,2,32,512]{3,2,1,0:T(8,128)S(1)}, u32[]{:S(2)}, u32[]{:S(2)}) %collective-permute-start.26) | collective-permute-done | bytes 262176 | tf_op jit(solution)/shard_map/ppermute | solution.py:324
  220.0 4.7 collective-permute-start.31
  226.5 15.9 %collective-permute-done.31.refs_9_ = f32[2,2,32,512]{3,2,1,0:T(8,128)S(1)} collective-permute-done((f32[2,2,32,512]{3,2,1,0:T(8,128)S(1)}, f32[2,2,32,512]{3,2,1,0:T(8,128)S(1)}, u32[]{:S(2)}, u32[]{:S(2)}) %collective-permute-start.31) | collective-permute-done | bytes 262176 | tf_op jit(solution)/shard_map/ppermute | solution.py:324
  242.3 11.3 %collective-permute-done.27.refs_8_ = f32[2,2,32,512]{3,2,1,0:T(8,128)S(1)} collective-permute-done((f32[2,2,32,512]{3,2,1,0:T(8,128)S(1)}, f32[2,2,32,512]{3,2,1,0:T(8,128)S(1)}, u32[]{:S(2)}, u32[]{:S(2)}) %collective-permute-start.27) | collective-permute-done | bytes 262176 | tf_op jit(solution)/shard_map/ppermute | solution.py:324
  255.8 9.7 %collective-permute-done.32.refs_11_ = f32[2,2,32,512]{3,2,1,0:T(8,128)S(1)} collective-permute-done((f32[2,2,32,512]{3,2,1,0:T(8,128)S(1)}, f32[2,2,32,512]{3,2,1,0:T(8,128)S(1)}, u32[]{:S(2)}, u32[]{:S(2)}) %collective-permute-start.32) | collective-permute-done | bytes 262176 | tf_op jit(solution)/shard_map/ppermute | solution.py:324
  270.1 6.7 %collective-permute-done.47.refs_10_ = f32[2,2,32,512]{3,2,1,0:T(8,128)S(1)} collective-permute-done((f32[2,2,32,512]{3,2,1,0:T(8,128)S(1)}, f32[2,2,32,512]{3,2,1,0:T(8,128)S(1)}, u32[]{:S(2)}, u32[]{:S(2)}) %collective-permute-start.47) | collective-permute-done | bytes 262176 | tf_op jit(solution)/shard_map/ppermute | solution.py:324
  280.2 8.4 %collective-permute-done.36.refs_4_ = f32[2,2,32,512]{3,2,1,0:T(8,128)S(1)} collective-permute-done((f32[2,2,32,512]{3,2,1,0:T(8,128)S(1)}, f32[2,2,32,512]{3,2,1,0:T(8,128)S(1)}, u32[]{:S(2)}, u32[]{:S(2)}) %collective-permute-start.36) | collective-permute-done | bytes 262176 | tf_op jit(solution)/shard_map/ppermute | solution.py:324
  291.4 12.3 %shard_map.35.refs_0_ = f32[2,512,1024]{2,1,0:T(8,128)S(1)} custom-call(s32[2]{0:T(128)S(1)} %pad_add_fusion.place, f32[2,2,256,256]{3,2,1,0:T(8,128)S(1)} %shard_map.34.own_core, f32[2,2,256,256]{3,2,1,0:T(8,128)S(1)} %collective-permute-done.41.other_core, f32[2,8,8,2,64,256]{5,4,3,2,1,0:T(8,128)} %bitcast.13, ...), custom_call_target="tpu_custom_call" | custom-call | flops 6039797760 | bytes 14680064 | tf_op jit(solution)/shard_map/pallas_call | solution.py:277
  303.7 16.2 %collective-permute-start.42 = (f32[2,2,32,512]{3,2,1,0:T(8,128)S(1)}, f32[2,2,32,512]{3,2,1,0:T(8,128)S(1)}, u32[]{:S(2)}, u32[]{:S(2)}) collective-permute-start(f32[2,2,32,512]{3,2,1,0:T(8,128)S(1)} %get-tuple-element.586), channel_id=1, source_target_pairs={{0,6},{1,7},{2,4},{3,5},{4,2},{5,3},{6,0},{7,1},{8,14},{9,15},{10,... | collective-permute-start | bytes 786440 | tf_op jit(solution)/shard_map/ppermute | solution.py:324
  321.2 3.8 collective-permute-done.42.refs_6_
  327.8 3.1 collective-permute-start.43
  330.9 9.9 %collective-permute-done.43.refs_8_ = f32[2,1,32,512]{3,2,1,0:T(8,128)S(1)} collective-permute-done((f32[2,1,32,512]{3,2,1,0:T(8,128)S(1)}, f32[2,1,32,512]{3,2,1,0:T(8,128)S(1)}, u32[]{:S(2)}, u32[]{:S(2)}) %collective-permute-start.43) | collective-permute-done | bytes 131104 | tf_op jit(solution)/shard_map/ppermute | solution.py:324
  341.8 4.1 collective-permute-done.57.refs_9_
  347.0 5.3 collective-permute-done.58.refs_10_
  368.2 3.8 collective-permute-done.62.refs_14_
  371.9 12.1 %shard_map.38.refs_0_ = f32[2,512,1024]{2,1,0:T(8,128)S(1)} custom-call(s32[2]{0:T(128)S(1)} %pad_add_fusion.place, f32[2,2,256,256]{3,2,1,0:T(8,128)S(1)} %shard_map.37.own_core, f32[2,2,256,256]{3,2,1,0:T(8,128)S(1)} %collective-permute-done.54.other_core, f32[2,8,8,2,64,256]{5,4,3,2,1,0:T(8,128)} %bitcast.14, ...), custom_call_target="tpu_custom_call" | custom-call | flops 6039797760 | bytes 14680064 | tf_op jit(solution)/shard_map/pallas_call | solution.py:277
  384.0 5.4 collective-permute-start.55
  389.4 4.2 collective-permute-done.55.refs_6_
  400.9 7.9 %collective-permute-done.73.refs_9_ = f32[2,1,32,512]{3,2,1,0:T(8,128)S(1)} collective-permute-done((f32[2,1,32,512]{3,2,1,0:T(8,128)S(1)}, f32[2,1,32,512]{3,2,1,0:T(8,128)S(1)}, u32[]{:S(2)}, u32[]{:S(2)}) %collective-permute-start.73) | collective-permute-done | bytes 131104 | tf_op jit(solution)/shard_map/ppermute | solution.py:324
  414.9 5.9 %collective-permute-done.75.refs_11_ = f32[2,1,32,512]{3,2,1,0:T(8,128)S(1)} collective-permute-done((f32[2,1,32,512]{3,2,1,0:T(8,128)S(1)}, f32[2,1,32,512]{3,2,1,0:T(8,128)S(1)}, u32[]{:S(2)}, u32[]{:S(2)}) %collective-permute-start.75) | collective-permute-done | bytes 131104 | tf_op jit(solution)/shard_map/ppermute | solution.py:324
  437.1 6.9 %shard_map.40.refs_0_ = f32[2,512,1024]{2,1,0:T(8,128)S(1)} custom-call(s32[2]{0:T(128)S(1)} %pad_add_fusion.place, f32[1,2,256,256]{3,2,1,0:T(8,128)S(1)} %shard_map.39.own_core, f32[1,2,256,256]{3,2,1,0:T(8,128)S(1)} %collective-permute-done.69.other_core, f32[2,8,8,2,64,256]{5,4,3,2,1,0:T(8,128)} %bitcast.15, ...), custom_call_target="tpu_custom_call" | custom-call | flops 3019898880 | bytes 11534336 | tf_op jit(solution)/shard_map/pallas_call | solution.py:277
  447.0 3.3 collective-permute-done.70.refs_6_
  455.4 6.8 %shard_map.42 = f32[2,512,1024]{2,1,0:T(8,128)S(1)} custom-call(s32[2]{0:T(128)S(1)} %pad_add_fusion.place, f32[1,2,256,256]{3,2,1,0:T(8,128)S(1)} %shard_map.41.own_core, f32[1,2,256,256]{3,2,1,0:T(8,128)S(1)} %collective-permute-done.80.other_core, f32[2,8,8,2,64,256]{5,4,3,2,1,0:T(8,128)} %bitcast.16, f32[2,8,8,2,64,256]{5,4,3,2,1,0:T(8,128)} %bitcast.4.other_left, ...), custom_call_target="tpu_custom_call" | custom-call | flops 3019898880 | bytes 11534336 | tf_op jit(solution)/shard_map/pallas_call | solution.py:277
  464.3 88.3 %reduce-scatter.2.cloned.1.call-done = f32[64,2,1024]{2,0,1:T(8,128)} async-done(((f32[512,2,1024]{2,0,1:T(8,128)}), f32[64,2,1024]{2,0,1:T(8,128)}) %reduce-scatter.2.cloned.1.call-update) | async-done | bytes 524304 | tf_op jit(solution)/shard_map/reduce_scatter | solution.py:334
  (136 shorter events, 118.0 us)
Async XLA Ops:
  6.5 546.0 %reduce-scatter.2.cloned.1.call-start = ((), (), s32[]{:S(2)}) async-start(), calls=%async_computation.1 | async-start | bytes 4718592 | tf_op jit(solution)/shard_map/reduce_scatter | solution.py:334
  6.5 179.0 %collective-permute-start.25 = (f32[1,2,8,1024,256]{4,3,2,1,0:T(8,128)}, f32[1,2,8,1024,256]{4,3,2,1,0:T(8,128)}, u32[]{:S(2)}, u32[]{:S(2)}) collective-permute-start(f32[1,2,8,1024,256]{4,3,2,1,0:T(8,128)} %param.2), channel_id=1, source_target_pairs={{0,1},{1,0},{2,3},{3,2},{4,5},{5,4},{6,7},{7,6},{8,9},{9,8},{10,11... | collective-permute-start | bytes 50331656 | tf_op jit(solution)/shard_map/ppermute | solution.py:20
  9.9 22.0 %collective-permute-start.1 = (f32[2,2,32,512]{3,2,1,0:T(8,128)S(1)}, f32[2,2,32,512]{3,2,1,0:T(8,128)S(1)}, u32[]{:S(2)}, u32[]{:S(2)}) collective-permute-start(f32[2,2,32,512]{3,2,1,0:T(8,128)S(1)} %get-tuple-element.383), channel_id=1, source_target_pairs={{0,8},{1,9},{2,10},{3,11},{4,12},{5,13},{6,14},{7,15},{8,0},{9,1},... | collective-permute-start | bytes 786440 | tf_op jit(solution)/shard_map/ppermute | solution.py:324
  13.6 29.3 %collective-permute-start.2 = (f32[2,2,32,512]{3,2,1,0:T(8,128)S(1)}, f32[2,2,32,512]{3,2,1,0:T(8,128)S(1)}, u32[]{:S(2)}, u32[]{:S(2)}) collective-permute-start(f32[2,2,32,512]{3,2,1,0:T(8,128)S(1)} %get-tuple-element.407), channel_id=1, source_target_pairs={{0,9},{1,8},{2,11},{3,10},{4,13},{5,12},{6,15},{7,14},{8,1},{9,0},... | collective-permute-start | bytes 786440 | tf_op jit(solution)/shard_map/ppermute | solution.py:324
  13.8 29.1 %collective-permute-start.10 = (f32[2,2,32,512]{3,2,1,0:T(8,128)S(1)}, f32[2,2,32,512]{3,2,1,0:T(8,128)S(1)}, u32[]{:S(2)}, u32[]{:S(2)}) collective-permute-start(f32[2,2,32,512]{3,2,1,0:T(8,128)S(1)} %get-tuple-element.446), channel_id=1, source_target_pairs={{0,1},{1,0},{2,3},{3,2},{4,5},{5,4},{6,7},{7,6},{8,9},{9,8},{10,11... | collective-permute-start | bytes 786440 | tf_op jit(solution)/shard_map/ppermute | solution.py:324
  32.0 23.7 %collective-permute-start.20 = (f32[2,2,32,512]{3,2,1,0:T(8,128)S(1)}, f32[2,2,32,512]{3,2,1,0:T(8,128)S(1)}, u32[]{:S(2)}, u32[]{:S(2)}) collective-permute-start(f32[2,2,32,512]{3,2,1,0:T(8,128)S(1)} %get-tuple-element.472), channel_id=1, source_target_pairs={{0,10},{1,11},{2,8},{3,9},{4,14},{5,15},{6,12},{7,13},{8,2},{9,3},... | collective-permute-start | bytes 786440 | tf_op jit(solution)/shard_map/ppermute | solution.py:324
  32.7 26.2 %collective-permute-start = (f32[2,2,32,512]{3,2,1,0:T(8,128)S(1)}, f32[2,2,32,512]{3,2,1,0:T(8,128)S(1)}, u32[]{:S(2)}, u32[]{:S(2)}) collective-permute-start(f32[2,2,32,512]{3,2,1,0:T(8,128)S(1)} %get-tuple-element.380), channel_id=1, source_target_pairs={{0,2},{1,3},{2,0},{3,1},{4,6},{5,7},{6,4},{7,5},{8,10},{9,11},{10,... | collective-permute-start | bytes 786440 | tf_op jit(solution)/shard_map/ppermute | solution.py:324
  42.8 23.1 %collective-permute-start.3 = (f32[2,2,32,512]{3,2,1,0:T(8,128)S(1)}, f32[2,2,32,512]{3,2,1,0:T(8,128)S(1)}, u32[]{:S(2)}, u32[]{:S(2)}) collective-permute-start(f32[2,2,32,512]{3,2,1,0:T(8,128)S(1)} %get-tuple-element.408), channel_id=1, source_target_pairs={{0,11},{1,10},{2,9},{3,8},{4,15},{5,14},{6,13},{7,12},{8,3},{9,2},... | collective-permute-start | bytes 786440 | tf_op jit(solution)/shard_map/ppermute | solution.py:324
  42.8 26.9 %collective-permute-start.11 = (f32[2,2,32,512]{3,2,1,0:T(8,128)S(1)}, f32[2,2,32,512]{3,2,1,0:T(8,128)S(1)}, u32[]{:S(2)}, u32[]{:S(2)}) collective-permute-start(f32[2,2,32,512]{3,2,1,0:T(8,128)S(1)} %get-tuple-element.447), channel_id=1, source_target_pairs={{0,3},{1,2},{2,1},{3,0},{4,7},{5,6},{6,5},{7,4},{8,11},{9,10},{10,... | collective-permute-start | bytes 786440 | tf_op jit(solution)/shard_map/ppermute | solution.py:324
  69.7 17.7 %collective-permute-start.12 = (f32[2,2,32,512]{3,2,1,0:T(8,128)S(1)}, f32[2,2,32,512]{3,2,1,0:T(8,128)S(1)}, u32[]{:S(2)}, u32[]{:S(2)}) collective-permute-start(f32[2,2,32,512]{3,2,1,0:T(8,128)S(1)} %get-tuple-element.448), channel_id=1, source_target_pairs={{0,5},{1,4},{2,7},{3,6},{4,1},{5,0},{6,3},{7,2},{8,13},{9,12},{10,... | collective-permute-start | bytes 786440 | tf_op jit(solution)/shard_map/ppermute | solution.py:324
  69.7 19.9 %collective-permute-start.22 = (f32[2,2,32,512]{3,2,1,0:T(8,128)S(1)}, f32[2,2,32,512]{3,2,1,0:T(8,128)S(1)}, u32[]{:S(2)}, u32[]{:S(2)}) collective-permute-start(f32[2,2,32,512]{3,2,1,0:T(8,128)S(1)} %get-tuple-element.480), channel_id=1, source_target_pairs={{0,14},{1,15},{2,12},{3,13},{4,10},{5,11},{6,8},{7,9},{8,6},{9,7},... | collective-permute-start | bytes 786440 | tf_op jit(solution)/shard_map/ppermute | solution.py:324
  76.1 23.9 %collective-permute-start.8 = (f32[2,2,32,512]{3,2,1,0:T(8,128)S(1)}, f32[2,2,32,512]{3,2,1,0:T(8,128)S(1)}, u32[]{:S(2)}, u32[]{:S(2)}) collective-permute-start(f32[2,2,32,512]{3,2,1,0:T(8,128)S(1)} %get-tuple-element.417), channel_id=1, source_target_pairs={{0,6},{1,7},{2,4},{3,5},{4,2},{5,3},{6,0},{7,1},{8,14},{9,15},{10,... | collective-permute-start | bytes 786440 | tf_op jit(solution)/shard_map/ppermute | solution.py:324
  78.7 26.5 %collective-permute-start.5 = (f32[2,2,32,512]{3,2,1,0:T(8,128)S(1)}, f32[2,2,32,512]{3,2,1,0:T(8,128)S(1)}, u32[]{:S(2)}, u32[]{:S(2)}) collective-permute-start(f32[2,2,32,512]{3,2,1,0:T(8,128)S(1)} %get-tuple-element.410), channel_id=1, source_target_pairs={{0,15},{1,14},{2,13},{3,12},{4,11},{5,10},{6,9},{7,8},{8,7},{9,6},... | collective-permute-start | bytes 786440 | tf_op jit(solution)/shard_map/ppermute | solution.py:324
  87.5 22.3 %collective-permute-start.13 = (f32[2,2,32,512]{3,2,1,0:T(8,128)S(1)}, f32[2,2,32,512]{3,2,1,0:T(8,128)S(1)}, u32[]{:S(2)}, u32[]{:S(2)}) collective-permute-start(f32[2,2,32,512]{3,2,1,0:T(8,128)S(1)} %get-tuple-element.449), channel_id=1, source_target_pairs={{0,7},{1,6},{2,5},{3,4},{4,3},{5,2},{6,1},{7,0},{8,15},{9,14},{10,... | collective-permute-start | bytes 786440 | tf_op jit(solution)/shard_map/ppermute | solution.py:324
  89.7 22.2 %collective-permute-start.23 = (f32[2,2,32,512]{3,2,1,0:T(8,128)S(1)}, f32[2,2,32,512]{3,2,1,0:T(8,128)S(1)}, u32[]{:S(2)}, u32[]{:S(2)}) collective-permute-start(f32[2,2,32,512]{3,2,1,0:T(8,128)S(1)} %get-tuple-element.484), channel_id=1, source_target_pairs={{0,1},{1,0},{2,3},{3,2},{4,5},{5,4},{6,7},{7,6},{8,9},{9,8},{10,11... | collective-permute-start | bytes 786440 | tf_op jit(solution)/shard_map/ppermute | solution.py:324
  100.0 24.3 %collective-permute-start.9 = (f32[2,2,32,512]{3,2,1,0:T(8,128)S(1)}, f32[2,2,32,512]{3,2,1,0:T(8,128)S(1)}, u32[]{:S(2)}, u32[]{:S(2)}) collective-permute-start(f32[2,2,32,512]{3,2,1,0:T(8,128)S(1)} %get-tuple-element.418), channel_id=1, source_target_pairs={{0,8},{1,9},{2,10},{3,11},{4,12},{5,13},{6,14},{7,15},{8,0},{9,1},... | collective-permute-start | bytes 786440 | tf_op jit(solution)/shard_map/ppermute | solution.py:324
  109.8 19.8 %collective-permute-start.14 = (f32[2,2,32,512]{3,2,1,0:T(8,128)S(1)}, f32[2,2,32,512]{3,2,1,0:T(8,128)S(1)}, u32[]{:S(2)}, u32[]{:S(2)}) collective-permute-start(f32[2,2,32,512]{3,2,1,0:T(8,128)S(1)} %get-tuple-element.450), channel_id=1, source_target_pairs={{0,9},{1,8},{2,11},{3,10},{4,13},{5,12},{6,15},{7,14},{8,1},{9,0},... | collective-permute-start | bytes 786440 | tf_op jit(solution)/shard_map/ppermute | solution.py:324
  114.5 71.0 %collective-permute-start.24 = (f32[2,2,256,256]{3,2,1,0:T(8,128)S(1)}, f32[2,2,256,256]{3,2,1,0:T(8,128)S(1)}, u32[]{:S(2)}, u32[]{:S(2)}) collective-permute-start(f32[2,2,256,256]{3,2,1,0:T(8,128)S(1)} %shard_map.31.own_core), channel_id=1, source_target_pairs={{0,1},{1,0},{2,3},{3,2},{4,5},{5,4},{6,7},{7,6},{8,9},{9,8},{10,11... | collective-permute-start | bytes 3145736 | tf_op jit(solution)/shard_map/ppermute | solution.py:20
  115.5 21.7 %collective-permute-start.6 = (f32[2,2,32,512]{3,2,1,0:T(8,128)S(1)}, f32[2,2,32,512]{3,2,1,0:T(8,128)S(1)}, u32[]{:S(2)}, u32[]{:S(2)}) collective-permute-start(f32[2,2,32,512]{3,2,1,0:T(8,128)S(1)} %get-tuple-element.411), channel_id=1, source_target_pairs={{0,2},{1,3},{2,0},{3,1},{4,6},{5,7},{6,4},{7,5},{8,10},{9,11},{10,... | collective-permute-start | bytes 786440 | tf_op jit(solution)/shard_map/ppermute | solution.py:324
  124.3 17.9 %collective-permute-start.37 = (f32[2,2,32,512]{3,2,1,0:T(8,128)S(1)}, f32[2,2,32,512]{3,2,1,0:T(8,128)S(1)}, u32[]{:S(2)}, u32[]{:S(2)}) collective-permute-start(f32[2,2,32,512]{3,2,1,0:T(8,128)S(1)} %get-tuple-element.555), channel_id=1, source_target_pairs={{0,10},{1,11},{2,8},{3,9},{4,14},{5,15},{6,12},{7,13},{8,2},{9,3},... | collective-permute-start | bytes 786440 | tf_op jit(solution)/shard_map/ppermute | solution.py:324
  129.6 22.6 %collective-permute-start.28 = (f32[2,2,32,512]{3,2,1,0:T(8,128)S(1)}, f32[2,2,32,512]{3,2,1,0:T(8,128)S(1)}, u32[]{:S(2)}, u32[]{:S(2)}) collective-permute-start(f32[2,2,32,512]{3,2,1,0:T(8,128)S(1)} %get-tuple-element.530), channel_id=1, source_target_pairs={{0,3},{1,2},{2,1},{3,0},{4,7},{5,6},{6,5},{7,4},{8,11},{9,10},{10,... | collective-permute-start | bytes 786440 | tf_op jit(solution)/shard_map/ppermute | solution.py:324
  142.2 17.1 %collective-permute-start.38 = (f32[2,2,32,512]{3,2,1,0:T(8,128)S(1)}, f32[2,2,32,512]{3,2,1,0:T(8,128)S(1)}, u32[]{:S(2)}, u32[]{:S(2)}) collective-permute-start(f32[2,2,32,512]{3,2,1,0:T(8,128)S(1)} %get-tuple-element.559), channel_id=1, source_target_pairs={{0,12},{1,13},{2,14},{3,15},{4,8},{5,9},{6,10},{7,11},{8,4},{9,5},... | collective-permute-start | bytes 786440 | tf_op jit(solution)/shard_map/ppermute | solution.py:324
  153.3 16.8 %collective-permute-start.29 = (f32[2,2,32,512]{3,2,1,0:T(8,128)S(1)}, f32[2,2,32,512]{3,2,1,0:T(8,128)S(1)}, u32[]{:S(2)}, u32[]{:S(2)}) collective-permute-start(f32[2,2,32,512]{3,2,1,0:T(8,128)S(1)} %get-tuple-element.531), channel_id=1, source_target_pairs={{0,5},{1,4},{2,7},{3,6},{4,1},{5,0},{6,3},{7,2},{8,13},{9,12},{10,... | collective-permute-start | bytes 786440 | tf_op jit(solution)/shard_map/ppermute | solution.py:324
  159.3 17.4 %collective-permute-start.16 = (f32[2,2,32,512]{3,2,1,0:T(8,128)S(1)}, f32[2,2,32,512]{3,2,1,0:T(8,128)S(1)}, u32[]{:S(2)}, u32[]{:S(2)}) collective-permute-start(f32[2,2,32,512]{3,2,1,0:T(8,128)S(1)} %get-tuple-element.452), channel_id=1, source_target_pairs={{0,13},{1,12},{2,15},{3,14},{4,9},{5,8},{6,11},{7,10},{8,5},{9,4},... | collective-permute-start | bytes 786440 | tf_op jit(solution)/shard_map/ppermute | solution.py:324
  164.5 21.0 %collective-permute-start.39 = (f32[2,2,32,512]{3,2,1,0:T(8,128)S(1)}, f32[2,2,32,512]{3,2,1,0:T(8,128)S(1)}, u32[]{:S(2)}, u32[]{:S(2)}) collective-permute-start(f32[2,2,32,512]{3,2,1,0:T(8,128)S(1)} %get-tuple-element.563), channel_id=1, source_target_pairs={{0,14},{1,15},{2,12},{3,13},{4,10},{5,11},{6,8},{7,9},{8,6},{9,7},... | collective-permute-start | bytes 786440 | tf_op jit(solution)/shard_map/ppermute | solution.py:324
  170.1 40.2 %collective-permute-start.30 = (f32[2,2,32,512]{3,2,1,0:T(8,128)S(1)}, f32[2,2,32,512]{3,2,1,0:T(8,128)S(1)}, u32[]{:S(2)}, u32[]{:S(2)}) collective-permute-start(f32[2,2,32,512]{3,2,1,0:T(8,128)S(1)} %get-tuple-element.532), channel_id=1, source_target_pairs={{0,7},{1,6},{2,5},{3,4},{4,3},{5,2},{6,1},{7,0},{8,15},{9,14},{10,... | collective-permute-start | bytes 786440 | tf_op jit(solution)/shard_map/ppermute | solution.py:324
  176.7 33.6 %collective-permute-start.17 = (f32[2,2,32,512]{3,2,1,0:T(8,128)S(1)}, f32[2,2,32,512]{3,2,1,0:T(8,128)S(1)}, u32[]{:S(2)}, u32[]{:S(2)}) collective-permute-start(f32[2,2,32,512]{3,2,1,0:T(8,128)S(1)} %get-tuple-element.453), channel_id=1, source_target_pairs={{0,15},{1,14},{2,13},{3,12},{4,11},{5,10},{6,9},{7,8},{8,7},{9,6},... | collective-permute-start | bytes 786440 | tf_op jit(solution)/shard_map/ppermute | solution.py:324
  185.5 24.8 %collective-permute-start.40 = (f32[2,2,32,512]{3,2,1,0:T(8,128)S(1)}, f32[2,2,32,512]{3,2,1,0:T(8,128)S(1)}, u32[]{:S(2)}, u32[]{:S(2)}) collective-permute-start(f32[2,2,32,512]{3,2,1,0:T(8,128)S(1)} %get-tuple-element.567), channel_id=1, source_target_pairs={{0,1},{1,0},{2,3},{3,2},{4,5},{5,4},{6,7},{7,6},{8,9},{9,8},{10,11... | collective-permute-start | bytes 786440 | tf_op jit(solution)/shard_map/ppermute | solution.py:324
  197.6 19.7 %collective-permute-start.26 = (f32[2,2,32,512]{3,2,1,0:T(8,128)S(1)}, f32[2,2,32,512]{3,2,1,0:T(8,128)S(1)}, u32[]{:S(2)}, u32[]{:S(2)}) collective-permute-start(f32[2,2,32,512]{3,2,1,0:T(8,128)S(1)} %get-tuple-element.502), channel_id=1, source_target_pairs={{0,6},{1,7},{2,4},{3,5},{4,2},{5,3},{6,0},{7,1},{8,14},{9,15},{10,... | collective-permute-start | bytes 786440 | tf_op jit(solution)/shard_map/ppermute | solution.py:324
  220.0 71.4 %collective-permute-start.41 = (f32[2,2,256,256]{3,2,1,0:T(8,128)S(1)}, f32[2,2,256,256]{3,2,1,0:T(8,128)S(1)}, u32[]{:S(2)}, u32[]{:S(2)}) collective-permute-start(f32[2,2,256,256]{3,2,1,0:T(8,128)S(1)} %shard_map.34.own_core), channel_id=1, source_target_pairs={{0,1},{1,0},{2,3},{3,2},{4,5},{5,4},{6,7},{7,6},{8,9},{9,8},{10,11... | collective-permute-start | bytes 3145736 | tf_op jit(solution)/shard_map/ppermute | solution.py:20
  220.0 22.3 %collective-permute-start.31 = (f32[2,2,32,512]{3,2,1,0:T(8,128)S(1)}, f32[2,2,32,512]{3,2,1,0:T(8,128)S(1)}, u32[]{:S(2)}, u32[]{:S(2)}) collective-permute-start(f32[2,2,32,512]{3,2,1,0:T(8,128)S(1)} %get-tuple-element.533), channel_id=1, source_target_pairs={{0,9},{1,8},{2,11},{3,10},{4,13},{5,12},{6,15},{7,14},{8,1},{9,0},... | collective-permute-start | bytes 786440 | tf_op jit(solution)/shard_map/ppermute | solution.py:324
  224.7 28.9 %collective-permute-start.27 = (f32[2,2,32,512]{3,2,1,0:T(8,128)S(1)}, f32[2,2,32,512]{3,2,1,0:T(8,128)S(1)}, u32[]{:S(2)}, u32[]{:S(2)}) collective-permute-start(f32[2,2,32,512]{3,2,1,0:T(8,128)S(1)} %get-tuple-element.503), channel_id=1, source_target_pairs={{0,8},{1,9},{2,10},{3,11},{4,12},{5,13},{6,14},{7,15},{8,0},{9,1},... | collective-permute-start | bytes 786440 | tf_op jit(solution)/shard_map/ppermute | solution.py:324
  224.7 29.0 %collective-permute-start.44 = (f32[2,2,32,512]{3,2,1,0:T(8,128)S(1)}, f32[2,2,32,512]{3,2,1,0:T(8,128)S(1)}, u32[]{:S(2)}, u32[]{:S(2)}) collective-permute-start(f32[2,2,32,512]{3,2,1,0:T(8,128)S(1)} %get-tuple-element.612), channel_id=1, source_target_pairs={{0,3},{1,2},{2,1},{3,0},{4,7},{5,6},{6,5},{7,4},{8,11},{9,10},{10,... | collective-permute-start | bytes 786440 | tf_op jit(solution)/shard_map/ppermute | solution.py:324
  225.3 30.5 %collective-permute-start.18 = (f32[2,2,32,512]{3,2,1,0:T(8,128)S(1)}, f32[2,2,32,512]{3,2,1,0:T(8,128)S(1)}, u32[]{:S(2)}, u32[]{:S(2)}) collective-permute-start(f32[2,2,32,512]{3,2,1,0:T(8,128)S(1)} %get-tuple-element.454), channel_id=1, source_target_pairs={{0,2},{1,3},{2,0},{3,1},{4,6},{5,7},{6,4},{7,5},{8,10},{9,11},{10,... | collective-permute-start | bytes 786440 | tf_op jit(solution)/shard_map/ppermute | solution.py:324
  242.3 23.1 %collective-permute-start.32 = (f32[2,2,32,512]{3,2,1,0:T(8,128)S(1)}, f32[2,2,32,512]{3,2,1,0:T(8,128)S(1)}, u32[]{:S(2)}, u32[]{:S(2)}) collective-permute-start(f32[2,2,32,512]{3,2,1,0:T(8,128)S(1)} %get-tuple-element.534), channel_id=1, source_target_pairs={{0,11},{1,10},{2,9},{3,8},{4,15},{5,14},{6,13},{7,12},{8,3},{9,2},... | collective-permute-start | bytes 786440 | tf_op jit(solution)/shard_map/ppermute | solution.py:324
  253.6 23.1 %collective-permute-start.47 = (f32[2,2,32,512]{3,2,1,0:T(8,128)S(1)}, f32[2,2,32,512]{3,2,1,0:T(8,128)S(1)}, u32[]{:S(2)}, u32[]{:S(2)}) collective-permute-start(f32[2,2,32,512]{3,2,1,0:T(8,128)S(1)} %get-tuple-element.625), channel_id=1, source_target_pairs={{0,10},{1,11},{2,8},{3,9},{4,14},{5,15},{6,12},{7,13},{8,2},{9,3},... | collective-permute-start | bytes 786440 | tf_op jit(solution)/shard_map/ppermute | solution.py:324
  253.7 25.7 %collective-permute-start.45 = (f32[2,2,32,512]{3,2,1,0:T(8,128)S(1)}, f32[2,2,32,512]{3,2,1,0:T(8,128)S(1)}, u32[]{:S(2)}, u32[]{:S(2)}) collective-permute-start(f32[2,2,32,512]{3,2,1,0:T(8,128)S(1)} %get-tuple-element.616), channel_id=1, source_target_pairs={{0,5},{1,4},{2,7},{3,6},{4,1},{5,0},{6,3},{7,2},{8,13},{9,12},{10,... | collective-permute-start | bytes 786440 | tf_op jit(solution)/shard_map/ppermute | solution.py:324
  270.0 18.6 %collective-permute-start.36 = (f32[2,2,32,512]{3,2,1,0:T(8,128)S(1)}, f32[2,2,32,512]{3,2,1,0:T(8,128)S(1)}, u32[]{:S(2)}, u32[]{:S(2)}) collective-permute-start(f32[2,2,32,512]{3,2,1,0:T(8,128)S(1)} %get-tuple-element.542), channel_id=1, source_target_pairs={{0,4},{1,5},{2,6},{3,7},{4,0},{5,1},{6,2},{7,3},{8,12},{9,13},{10,... | collective-permute-start | bytes 786440 | tf_op jit(solution)/shard_map/ppermute | solution.py:324
  279.4 40.4 %collective-permute-start.46 = (f32[2,2,32,512]{3,2,1,0:T(8,128)S(1)}, f32[2,2,32,512]{3,2,1,0:T(8,128)S(1)}, u32[]{:S(2)}, u32[]{:S(2)}) collective-permute-start(f32[2,2,32,512]{3,2,1,0:T(8,128)S(1)} %get-tuple-element.620), channel_id=1, source_target_pairs={{0,7},{1,6},{2,5},{3,4},{4,3},{5,2},{6,1},{7,0},{8,15},{9,14},{10,... | collective-permute-start | bytes 786440 | tf_op jit(solution)/shard_map/ppermute | solution.py:324
  279.4 40.4 %collective-permute-start.34 = (f32[2,2,32,512]{3,2,1,0:T(8,128)S(1)}, f32[2,2,32,512]{3,2,1,0:T(8,128)S(1)}, u32[]{:S(2)}, u32[]{:S(2)}) collective-permute-start(f32[2,2,32,512]{3,2,1,0:T(8,128)S(1)} %get-tuple-element.536), channel_id=1, source_target_pairs={{0,15},{1,14},{2,13},{3,12},{4,11},{5,10},{6,9},{7,8},{8,7},{9,6},... | collective-permute-start | bytes 786440 | tf_op jit(solution)/shard_map/ppermute | solution.py:324
  288.6 31.2 %collective-permute-start.49 = (f32[2,2,32,512]{3,2,1,0:T(8,128)S(1)}, f32[2,2,32,512]{3,2,1,0:T(8,128)S(1)}, u32[]{:S(2)}, u32[]{:S(2)}) collective-permute-start(f32[2,2,32,512]{3,2,1,0:T(8,128)S(1)} %get-tuple-element.633), channel_id=1, source_target_pairs={{0,14},{1,15},{2,12},{3,13},{4,10},{5,11},{6,8},{7,9},{8,6},{9,7},... | collective-permute-start | bytes 786440 | tf_op jit(solution)/shard_map/ppermute | solution.py:324
  303.7 21.4 %collective-permute-start.42 = (f32[2,2,32,512]{3,2,1,0:T(8,128)S(1)}, f32[2,2,32,512]{3,2,1,0:T(8,128)S(1)}, u32[]{:S(2)}, u32[]{:S(2)}) collective-permute-start(f32[2,2,32,512]{3,2,1,0:T(8,128)S(1)} %get-tuple-element.586), channel_id=1, source_target_pairs={{0,6},{1,7},{2,4},{3,5},{4,2},{5,3},{6,0},{7,1},{8,14},{9,15},{10,... | collective-permute-start | bytes 786440 | tf_op jit(solution)/shard_map/ppermute | solution.py:324
  327.7 44.2 %collective-permute-start.54 = (f32[2,2,256,256]{3,2,1,0:T(8,128)S(1)}, f32[2,2,256,256]{3,2,1,0:T(8,128)S(1)}, u32[]{:S(2)}, u32[]{:S(2)}) collective-permute-start(f32[2,2,256,256]{3,2,1,0:T(8,128)S(1)} %shard_map.37.own_core), channel_id=1, source_target_pairs={{0,1},{1,0},{2,3},{3,2},{4,5},{5,4},{6,7},{7,6},{8,9},{9,8},{10,11... | collective-permute-start | bytes 3145736 | tf_op jit(solution)/shard_map/ppermute | solution.py:20
  363.2 26.2 %collective-permute-start.63 = (f32[2,1,32,512]{3,2,1,0:T(8,128)S(1)}, f32[2,1,32,512]{3,2,1,0:T(8,128)S(1)}, u32[]{:S(2)}, u32[]{:S(2)}) collective-permute-start(f32[2,1,32,512]{3,2,1,0:T(8,128)S(1)} %get-tuple-element.694), channel_id=1, source_target_pairs={{0,15},{1,14},{2,13},{3,12},{4,11},{5,10},{6,9},{7,8},{8,7},{9,6},... | collective-permute-start | bytes 393224 | tf_op jit(solution)/shard_map/ppermute | solution.py:324
  365.1 24.3 %collective-permute-start.56 = (f32[2,1,32,512]{3,2,1,0:T(8,128)S(1)}, f32[2,1,32,512]{3,2,1,0:T(8,128)S(1)}, u32[]{:S(2)}, u32[]{:S(2)}) collective-permute-start(f32[2,1,32,512]{3,2,1,0:T(8,128)S(1)} %get-tuple-element.672), channel_id=1, source_target_pairs={{0,7},{1,6},{2,5},{3,4},{4,3},{5,2},{6,1},{7,0},{8,15},{9,14},{10,... | collective-permute-start | bytes 393224 | tf_op jit(solution)/shard_map/ppermute | solution.py:324
  371.9 17.5 %collective-permute-start.64 = (f32[2,1,32,512]{3,2,1,0:T(8,128)S(1)}, f32[2,1,32,512]{3,2,1,0:T(8,128)S(1)}, u32[]{:S(2)}, u32[]{:S(2)}) collective-permute-start(f32[2,1,32,512]{3,2,1,0:T(8,128)S(1)} %get-tuple-element.697), channel_id=1, source_target_pairs={{0,1},{1,0},{2,3},{3,2},{4,5},{5,4},{6,7},{7,6},{8,9},{9,8},{10,11... | collective-permute-start | bytes 393224 | tf_op jit(solution)/shard_map/ppermute | solution.py:324
  396.6 40.4 %collective-permute-start.69 = (f32[1,2,256,256]{3,2,1,0:T(8,128)S(1)}, f32[1,2,256,256]{3,2,1,0:T(8,128)S(1)}, u32[]{:S(2)}, u32[]{:S(2)}) collective-permute-start(f32[1,2,256,256]{3,2,1,0:T(8,128)S(1)} %shard_map.39.own_core), channel_id=1, source_target_pairs={{0,1},{1,0},{2,3},{3,2},{4,5},{5,4},{6,7},{7,6},{8,9},{9,8},{10,11... | collective-permute-start | bytes 1572872 | tf_op jit(solution)/shard_map/ppermute | solution.py:20
  428.3 18.7 %collective-permute-start.79 = (f32[2,1,32,512]{3,2,1,0:T(8,128)S(1)}, f32[2,1,32,512]{3,2,1,0:T(8,128)S(1)}, u32[]{:S(2)}, u32[]{:S(2)}) collective-permute-start(f32[2,1,32,512]{3,2,1,0:T(8,128)S(1)} %get-tuple-element.751), channel_id=1, source_target_pairs={{0,15},{1,14},{2,13},{3,12},{4,11},{5,10},{6,9},{7,8},{8,7},{9,6},... | collective-permute-start | bytes 393224 | tf_op jit(solution)/shard_map/ppermute | solution.py:324
  (35 other events, 378.6 us)
Sparse Core Ops, SparseCore 0:
  464.4 88.0 reduce-scatter.1

commit v3 on v2

v3 whole, which is shorter than its diff:
```python
import functools
import math

import jax
import jax.numpy as jnp
from jax import lax
from jax.experimental import pallas as pl
from jax.experimental.pallas import tpu as pltpu
from jax.sharding import PartitionSpec as P

HIGH = lax.Precision.HIGH
MIB = 1 << 20
ANYWHERE = pl.BlockSpec(memory_space=pl.ANY)
IN_VMEM = pl.BlockSpec(memory_space=pltpu.VMEM)
IN_SMEM = pl.BlockSpec(memory_space=pltpu.SMEM)


def swapped(x, axis):
    return lax.ppermute(x, axis, [(i, i ^ 1) for i in range(lax.axis_size(axis))])


def complex_terms(left_real, left_imag, right_real, right_imag, pattern):
    first = jnp.einsum(pattern, left_real, right_real, precision=HIGH)
    second = jnp.einsum(pattern, left_imag, right_imag, precision=HIGH)
    mixed = jnp.einsum(pattern, left_real + left_imag, right_real + right_imag, precision=HIGH)
    return first, second, mixed


def general(left_factor, right_factor):
    idx_size = lax.axis_size("idx")
    half_size = lax.axis_size("half")
    left = left_factor[0]
    right = right_factor[0]
    _, local_batch, rows, inner = left.shape
    _, batch, inner_part, between = right.shape
    own_rows = rows // (idx_size * half_size)
    half_rows = rows // half_size
    half_cols = between // half_size
    is_lower = lax.axis_index("half") == 0
    scale = 1.0 / math.sqrt(2.0 * batch * between)
    pieces = right.reshape(2, idx_size, local_batch, inner_part, half_size, half_cols)
    split_rows = left.reshape(2, local_batch, idx_size, half_size, own_rows, inner)
    upper_rows = lax.ppermute(split_rows[:, :, :, 1], "half", [(0, 1)])
    other_whole = lax.ppermute(left, "half", [(1, 0)])
    first_left = jnp.where(is_lower, split_rows[:, :, :, 0], upper_rows)
    first_left = first_left.reshape(2, local_batch, half_rows, inner)
    second_left = jnp.where(is_lower, other_whole, left)
    totals = None
    for b in range(local_batch):
        outgoing = jnp.transpose(pieces[:, :, b], (1, 3, 0, 2, 4))
        outgoing = outgoing.reshape(idx_size * half_size, 2, inner_part, half_cols)
        arrived = lax.all_to_all(outgoing, ("idx", "half"), 0, 0, tiled=True)
        arrived = arrived.reshape(idx_size, half_size, 2, inner_part, half_cols)
        factors = jnp.transpose(arrived, (1, 2, 0, 3, 4)).reshape(2, 2, inner, half_cols)
        first, second, mixed = complex_terms(
            factors[0, 0], factors[0, 1], factors[1, 0], factors[1, 1], "kn,ln->kl"
        )
        core = jnp.stack([first - second, mixed - first - second]) * scale
        core = core + swapped(core, "half")
        first, second, mixed = complex_terms(
            first_left[0, b], first_left[1, b], core[0], core[1], "mk,kl->ml"
        )
        terms = complex_terms(
            first - second, mixed - first - second, second_left[0, b], second_left[1, b], "ml,ol->mo"
        )
        totals = terms if totals is None else [t + u for t, u in zip(totals, terms)]
    first, second, mixed = totals
    partial = jnp.stack([first - second, mixed - first - second], axis=1)
    return lax.psum_scatter(partial, "idx", scatter_dimension=0, tiled=True)


def split_float(x):
    high = x.astype(jnp.bfloat16)
    return high, (x - high.astype(jnp.float32)).astype(jnp.bfloat16)


def dot_parts(left, right, dims):
    def dot(a, b):
        return lax.dot_general(a, b, (dims, ((), ())), preferred_element_type=jnp.float32)

    return dot(left[0], right[0]) + (dot(left[0], right[1]) + dot(left[1], right[0]))


def complex_dot(left_real, left_imag, right_real, right_imag, dims):
    first = dot_parts(split_float(left_real), split_float(right_real), dims)
    second = dot_parts(split_float(left_imag), split_float(right_imag), dims)
    mixed = dot_parts(
        split_float(left_real + left_imag), split_float(right_real + right_imag), dims
    )
    return first - second, mixed - first - second


NT = ((1,), (1,))
NN = ((1,), (0,))


def deal_kernel(start, count, half_cols, right, out, sems):
    copies = []
    for half in range(2):
        for plane in range(2):
            source = right.at[plane, :, pl.ds(start, count), :, pl.ds(half * half_cols, half_cols)]
            copies.append(pltpu.make_async_copy(source, out.at[:, half, plane], sems.at[2 * half + plane]))
    for copy in copies:
        copy.start()
    for copy in copies:
        copy.wait()


def core_kernel(count, scale, arrived, core, factors, sems):
    inner = core.shape[2]
    copies = {}
    for b in range(count):
        for part in range(4):
            source = arrived.at[:, part // 2, part % 2, b]
            copies[b, part] = pltpu.make_async_copy(source, factors.at[b, part], sems.at[b, part])
            copies[b, part].start()
    for b in range(count):
        for part in range(4):
            copies[b, part].wait()
        planes = [factors[b, part].reshape(inner, factors.shape[4]) for part in range(4)]
        real, imag = complex_dot(*planes, NT)
        core[b, 0] = real * scale
        core[b, 1] = imag * scale


def amplitude_kernel(start, count, tile, fresh, place, own_core, other_core, own_left, other_left, *refs):
    before = None if fresh else refs[0]
    total, first, second, product, sems, sum_sem = refs[-6:]
    half = place[0]

    def copies(lower, b):
        pairs = (own_left, other_left) if lower else (other_left, own_left)
        side = 0 if lower else 1
        return [
            pltpu.make_async_copy(pairs[0].at[:, start + b, :, side], first.at[b], sems.at[0, b]),
            pltpu.make_async_copy(pairs[1].at[:, start + b], second.at[b], sems.at[1, b]),
        ]

    for lower in (True, False):

        @pl.when(half == (0 if lower else 1))
        def _():
            for b in range(count):
                for copy in copies(lower, b):
                    copy.start()

    if not fresh:
        loading = pltpu.make_async_copy(before, total, sum_sem)
        loading.start()
    _, _, groups, own_rows, inner = first.shape
    rows = groups * own_rows
    columns = second.shape[2] * second.shape[3] * second.shape[4]
    per = second.shape[3] * second.shape[4]
    for b in range(count):
        for copy in copies(True, b):
            copy.wait()
        real, imag = complex_dot(
            first[b, 0].reshape(rows, inner),
            first[b, 1].reshape(rows, inner),
            own_core[b, 0] + other_core[b, 0],
            own_core[b, 1] + other_core[b, 1],
            NN,
        )
        for place_in, part in enumerate((real, imag, real + imag)):
            product[2 * place_in], product[2 * place_in + 1] = split_float(part)
        if b == 0 and not fresh:
            loading.wait()

        def column_tile(step, carry):
            at = pl.multiple_of(step * tile, tile)
            right_real = second[b, 0, pl.ds(step * (tile // per), tile // per)].reshape(tile, inner)
            right_imag = second[b, 1, pl.ds(step * (tile // per), tile // per)].reshape(tile, inner)
            one = dot_parts((product[0], product[1]), split_float(right_real), NT)
            two = dot_parts((product[2], product[3]), split_float(right_imag), NT)
            three = dot_parts((product[4], product[5]), split_float(right_real + right_imag), NT)
            spot = pl.ds(at, tile)
            if fresh and b == 0:
                total[0, :, spot] = one - two
                total[1, :, spot] = three - one - two
            else:
                total[0, :, spot] += one - two
                total[1, :, spot] += three - one - two
            return carry

        lax.fori_loop(0, columns // tile, column_tile, 0)


def chunks_of(count):
    last = min(2, count - 1)
    return [count - last, last]


def overlapped(left_factor, right_factor):
    idx_size = lax.axis_size("idx")
    _, _, local_batch, rows, inner = left_factor.shape
    _, _, batch, inner_part, between = right_factor.shape
    own_rows = rows // (idx_size * 2)
    half_rows = rows // 2
    half_cols = between // 2
    scale = 1.0 / math.sqrt(2.0 * batch * between)
    place = lax.axis_index("half").astype(jnp.int32)[None]
    right = right_factor.reshape(2, idx_size, local_batch, inner_part, between)
    params = pltpu.CompilerParams(vmem_limit_bytes=44 * MIB)
    shape = (2, local_batch, idx_size, 2, own_rows, inner)
    own_left = left_factor.reshape(shape)

    def dealt(start, count):
        return pl.pallas_call(
            functools.partial(deal_kernel, start, count, half_cols),
            out_shape=jax.ShapeDtypeStruct((idx_size, 2, 2, count, inner_part, half_cols), jnp.float32),
            in_specs=[ANYWHERE],
            out_specs=ANYWHERE,
            scratch_shapes=[pltpu.SemaphoreType.DMA((4,))],
            cost_estimate=pl.CostEstimate(
                flops=0, bytes_accessed=32 * idx_size * count * inner_part * half_cols, transcendentals=0
            ),
            compiler_params=params,
        )(right)

    def sent(pieces):
        flat = pieces.reshape(2 * idx_size, *pieces.shape[2:])
        return lax.all_to_all(flat, ("idx", "half"), 0, 0, tiled=True).reshape(pieces.shape)

    def core_of(count, arrived):
        return pl.pallas_call(
            functools.partial(core_kernel, count, scale),
            out_shape=jax.ShapeDtypeStruct((count, 2, inner, inner), jnp.float32),
            in_specs=[ANYWHERE],
            out_specs=IN_VMEM,
            scratch_shapes=[
                pltpu.VMEM((count, 4, idx_size, inner_part, half_cols), jnp.float32),
                pltpu.SemaphoreType.DMA((count, 4)),
            ],
            cost_estimate=pl.CostEstimate(
                flops=18 * count * inner * inner * half_cols,
                bytes_accessed=16 * count * inner * (inner + half_cols),
                transcendentals=0,
            ),
            compiler_params=params,
        )(arrived)

    def added(start, count, core, other_core, other_left, total):
        fresh = total is None
        return pl.pallas_call(
            functools.partial(amplitude_kernel, start, count, 256, fresh),
            out_shape=jax.ShapeDtypeStruct((2, half_rows, rows), jnp.float32),
            in_specs=[IN_SMEM, IN_VMEM, IN_VMEM, ANYWHERE, ANYWHERE] + [ANYWHERE] * (not fresh),
            out_specs=IN_VMEM,
            scratch_shapes=[
                pltpu.VMEM((count, 2, idx_size, own_rows, inner), jnp.float32),
                pltpu.VMEM((count, 2, idx_size, 2, own_rows, inner), jnp.float32),
                pltpu.VMEM((6, half_rows, inner), jnp.bfloat16),
                pltpu.SemaphoreType.DMA((2, count)),
                pltpu.SemaphoreType.DMA,
            ],
            cost_estimate=pl.CostEstimate(
                flops=18 * count * half_rows * inner * (inner + rows),
                bytes_accessed=count * 12 * rows * inner + 16 * half_rows * rows,
                transcendentals=0,
            ),
            compiler_params=params,
        )(place, core, other_core, own_left, other_left, *([] if fresh else [total]))

    many, few = chunks_of(local_batch)
    other_left = swapped(left_factor, "half").reshape(shape)
    arrived = sent(dealt(0, many))
    pieces, other_left = lax.optimization_barrier((dealt(many, few), other_left))
    late = sent(pieces)
    core = core_of(many, arrived)
    total = added(0, many, core, swapped(core, "half"), other_left, None)
    core = core_of(few, late)
    total = added(many, few, core, swapped(core, "half"), other_left, total)

    return lax.psum_scatter(jnp.moveaxis(total, 0, 1), "idx", scatter_dimension=0, tiled=True)


def on_device(left_factor, right_factor):
    idx_size = lax.axis_size("idx")
    rows, inner_part, between = left_factor.shape[3], right_factor.shape[3], right_factor.shape[4]
    aligned = (
        lax.axis_size("half") == 2
        and left_factor.shape[2] > 1
        and idx_size in (2, 4, 8)
        and inner_part % 8 == 0
        and between % 256 == 0
        and rows % 256 == 0
        and rows % (16 * idx_size) == 0
        and 256 % (rows // idx_size) == 0
    )
    return (overlapped if aligned else general)(left_factor, right_factor)


def solution(mesh):
    return jax.shard_map(
        on_device,
        mesh=mesh,
        in_specs=(P("half", "cuts", "idx", None, None), P("half", "cuts", None, "idx", None)),
        out_specs=P(("idx", "half"), "cuts", None),
        check_vma=False,
    )
```

time: 562 us -> 913 us (1.62)
  Pallas kernels: 77.3 us -> 440 us
  starting transfers between devices: 165 us -> 62.5 us
  waiting for transfers between devices: 301 us -> 391 us
    pallas_call x5 -> x2, Pallas kernels: 13.2 us -> 385 us  [dealt(): pl.pallas_call(functools.partial(deal_kernel, start, count, half_cols), o...]
    all_to_all x0 -> x2, waiting for transfers between devices: none -> 266 us  [sent(): lax.all_to_all(flat, ('idx', 'half'), 0, 0, tiled=True)]
    ppermute x75 -> x0, waiting for transfers between devices: 211 us -> none  [overlapped(): pieces[slot] = lax.ppermute(piece, ('idx', 'half'), pairs)]
    ppermute x75 -> x0, starting transfers between devices: 163 us -> none  [overlapped(): pieces[slot] = lax.ppermute(piece, ('idx', 'half'), pairs)]
    all_to_all x0 -> x2, starting transfers between devices: none -> 60.8 us  [sent(): lax.all_to_all(flat, ('idx', 'half'), 0, 0, tiled=True)]
    ppermute x6 -> x3, waiting for transfers between devices: 1.91 us -> 21.9 us  [swapped(): lax.ppermute(x, axis, [(i, i ^ 1) for i in range(lax.axis_size(axis))])]
    reduce_scatter x1, waiting for transfers between devices: 88.3 us -> 103 us  [overlapped(): lax.psum_scatter(jnp.moveaxis(total, 0, 1), 'idx', scatter_dimension=0, t...]
    pallas_call x5 -> x2, Pallas kernels: 50.1 us -> 43.2 us  [added(): pl.pallas_call(functools.partial(amplitude_kernel, start, count, 256, fre...]
  transfers between devices with their start and end apart: 82 -> 6, of which waited for: 41 -> 4; matrix products, arithmetic and copies ran while one was open for 0% -> 0% of each run, Pallas kernels for 11% -> 5%
where the time goes in v3:
time: 913 us
  Pallas kernels  440 us (48%)
  waiting for transfers between devices  391 us (43%)
  starting transfers between devices  62.5 us (7%)
  between operations  13.5 us (1%)
    pallas_call x2, Pallas kernels, dealt(): pl.pallas_call(functools.partial(deal_kernel, start, count, half_cols), o...  385 us
    all_to_all x2, waiting for transfers between devices, sent(): lax.all_to_all(flat, ('idx', 'half'), 0, 0, tiled=True)  266 us
    reduce_scatter x1, waiting for transfers between devices, overlapped(): lax.psum_scatter(jnp.moveaxis(total, 0, 1), 'idx', scatter_dimension=0, t...  103 us
    all_to_all x2, starting transfers between devices, sent(): lax.all_to_all(flat, ('idx', 'half'), 0, 0, tiled=True)  60.8 us
    pallas_call x2, Pallas kernels, added(): pl.pallas_call(functools.partial(amplitude_kernel, start, count, 256, fre...  43.2 us
    ppermute x3, waiting for transfers between devices, swapped(): lax.ppermute(x, axis, [(i, i ^ 1) for i in range(lax.axis_size(axis))])  21.9 us
  transfers between devices with their start and end apart: 6, of which 4 were waited for; matrix products, arithmetic and copies ran while one was open for 0% of the time, Pallas kernels for 5%

profile of v3, /device:TPU:0, one launch (start us, length us, event | category | flops | bytes accessed | tf_op | source)
XLA Modules:
  0.0 912.7 jit_solution(816064728006799200)
XLA Ops:
  6.5 382.3 %shard_map.30 = f32[8,2,2,6,32,512]{5,4,3,2,1,0:T(8,128)} custom-call(f32[2,8,8,32,1024]{4,3,2,1,0:T(8,128)} %bitcast.11), custom_call_target="tpu_custom_call" | custom-call | bytes 25165824 | tf_op jit(solution)/shard_map/pallas_call | solution.py:208
  388.8 7.4 all-to-all-start.1
  396.3 0.4 collective-permute-start
  396.6 2.2 shard_map.28
  398.9 0.0 copy-start
  398.9 1.9 copy-done
  400.8 21.9 %collective-permute-done = f32[1,2,8,1024,256]{4,3,2,1,0:T(8,128)} collective-permute-done((f32[1,2,8,1024,256]{4,3,2,1,0:T(8,128)}, f32[1,2,8,1024,256]{4,3,2,1,0:T(8,128)}, u32[]{:S(2)}, u32[]{:S(2)}) %collective-permute-start) | collective-permute-done | bytes 16777248 | tf_op jit(solution)/shard_map/ppermute | solution.py:19
  422.7 197.3 %all-to-all-done.1 = f32[16,2,6,32,512]{4,3,2,1,0:T(8,128)} async-done(((f32[16,2,6,32,512]{4,3,2,1,0:T(8,128)}), f32[16,2,6,32,512]{4,3,2,1,0:T(8,128)}, u32[]{:S(2)}, u32[]{:S(2)}) %all-to-all-start.1) | async-done | bytes 12582944 | tf_op jit(solution)/shard_map/all_to_all | solution.py:222
  620.0 53.4 %all-to-all-start = ((f32[16,2,2,32,512]{4,3,2,1,0:T(8,128)}), f32[16,2,2,32,512]{4,3,2,1,0:T(8,128)}, u32[]{:S(2)}, u32[]{:S(2)}) async-start(f32[16,2,2,32,512]{4,3,2,1,0:T(8,128)} %bitcast.9), calls=%async_computation | async-start | bytes 8388608 | tf_op jit(solution)/shard_map/all_to_all | solution.py:222
  673.4 0.0 reduce-scatter.2.cloned.1.call-start
  673.5 8.2 shard_map.31.own_core
  681.6 0.4 collective-permute-start.2
  682.1 69.0 %all-to-all-done = f32[16,2,2,32,512]{4,3,2,1,0:T(8,128)} async-done(((f32[16,2,2,32,512]{4,3,2,1,0:T(8,128)}), f32[16,2,2,32,512]{4,3,2,1,0:T(8,128)}, u32[]{:S(2)}, u32[]{:S(2)}) %all-to-all-start) | async-done | bytes 4194336 | tf_op jit(solution)/shard_map/all_to_all | solution.py:222
  751.1 3.7 shard_map.29.own_core
  754.8 0.8 collective-permute-start.1
  755.7 0.0 collective-permute-done.2.other_core
  755.7 31.5 %shard_map.32.refs_0_ = f32[2,512,1024]{2,1,0:T(8,128)} custom-call(s32[1]{0:T(128)} %bitcast.place, f32[6,2,256,256]{3,2,1,0:T(8,128)S(1)} %shard_map.31.own_core, f32[6,2,256,256]{3,2,1,0:T(8,128)} %collective-permute-done.2.other_core, f32[2,8,8,2,64,256]{5,4,3,2,1,0:T(8,128)} %bitcast.14, f32[2,8,8,2,64,256]{5,4,3,2,1,0:T(8,128)} %bitcast.2.other_left), custom_call_target="tpu_custom_call" | custom-call | flops 18119393280 | bytes 27262976 | tf_op jit(solution)/shard_map/pallas_call | solution.py:244
  787.2 0.0 collective-permute-done.1.other_core
  787.2 11.7 %shard_map.33 = f32[2,512,1024]{2,1,0:T(8,128)S(1)} custom-call(s32[1]{0:T(128)} %bitcast.place, f32[2,2,256,256]{3,2,1,0:T(8,128)S(1)} %shard_map.29.own_core, f32[2,2,256,256]{3,2,1,0:T(8,128)S(1)} %collective-permute-done.1.other_core, f32[2,8,8,2,64,256]{5,4,3,2,1,0:T(8,128)} %bitcast.15, f32[2,8,8,2,64,256]{5,4,3,2,1,0:T(8,128)} %bitcast.2.other_left, ...), custom_call_target="tpu_custom_call" | custom-call | flops 6039797760 | bytes 14680064 | tf_op jit(solution)/shard_map/pallas_call | solution.py:244
  798.9 0.0 copy-start.1
  798.9 1.9 copy-done.1
  800.9 0.0 reduce-scatter.2.cloned.1.call-update
  800.9 102.8 %reduce-scatter.2.cloned.1.call-done = f32[64,2,1024]{2,0,1:T(8,128)} async-done(((f32[512,2,1024]{2,0,1:T(8,128)}), f32[64,2,1024]{2,0,1:T(8,128)}) %reduce-scatter.2.cloned.1.call-update) | async-done | bytes 524304 | tf_op jit(solution)/shard_map/reduce_scatter | solution.py:274
  903.6 2.2 copy.3
Async XLA Ops:
  388.8 231.2 %all-to-all-start.1 = ((f32[16,2,6,32,512]{4,3,2,1,0:T(8,128)}), f32[16,2,6,32,512]{4,3,2,1,0:T(8,128)}, u32[]{:S(2)}, u32[]{:S(2)}) async-start(f32[16,2,6,32,512]{4,3,2,1,0:T(8,128)} %bitcast.13), calls=%async_computation.1 | async-start | bytes 25165824 | tf_op jit(solution)/shard_map/all_to_all | solution.py:222
  396.3 26.5 %collective-permute-start = (f32[1,2,8,1024,256]{4,3,2,1,0:T(8,128)}, f32[1,2,8,1024,256]{4,3,2,1,0:T(8,128)}, u32[]{:S(2)}, u32[]{:S(2)}) collective-permute-start(f32[1,2,8,1024,256]{4,3,2,1,0:T(8,128)} %param.2), channel_id=1, source_target_pairs={{0,1},{1,0},{2,3},{3,2},{4,5},{5,4},{6,7},{7,6},{8,9},{9,8},{10,11... | collective-permute-start | bytes 50331656 | tf_op jit(solution)/shard_map/ppermute | solution.py:19
  398.9 1.9 copy-start
  620.0 131.1 %all-to-all-start = ((f32[16,2,2,32,512]{4,3,2,1,0:T(8,128)}), f32[16,2,2,32,512]{4,3,2,1,0:T(8,128)}, u32[]{:S(2)}, u32[]{:S(2)}) async-start(f32[16,2,2,32,512]{4,3,2,1,0:T(8,128)} %bitcast.9), calls=%async_computation | async-start | bytes 8388608 | tf_op jit(solution)/shard_map/all_to_all | solution.py:222
  673.4 230.2 %reduce-scatter.2.cloned.1.call-start = ((), (), s32[]{:S(2)}) async-start(), calls=%async_computation.3 | async-start | bytes 4718592 | tf_op jit(solution)/shard_map/reduce_scatter | solution.py:274
  681.6 74.0 %collective-permute-start.2 = (f32[6,2,256,256]{3,2,1,0:T(8,128)S(1)}, f32[6,2,256,256]{3,2,1,0:T(8,128)}, u32[]{:S(2)}, u32[]{:S(2)}) collective-permute-start(f32[6,2,256,256]{3,2,1,0:T(8,128)S(1)} %shard_map.31.own_core), channel_id=1, source_target_pairs={{0,1},{1,0},{2,3},{3,2},{4,5},{5,4},{6,7},{7,6},{8,9},{9,8},{10,11... | collective-permute-start | bytes 9437192 | tf_op jit(solution)/shard_map/ppermute | solution.py:19
  754.8 32.4 %collective-permute-start.1 = (f32[2,2,256,256]{3,2,1,0:T(8,128)S(1)}, f32[2,2,256,256]{3,2,1,0:T(8,128)S(1)}, u32[]{:S(2)}, u32[]{:S(2)}) collective-permute-start(f32[2,2,256,256]{3,2,1,0:T(8,128)S(1)} %shard_map.29.own_core), channel_id=1, source_target_pairs={{0,1},{1,0},{2,3},{3,2},{4,5},{5,4},{6,7},{7,6},{8,9},{9,8},{10,11... | collective-permute-start | bytes 3145736 | tf_op jit(solution)/shard_map/ppermute | solution.py:19
  798.9 1.9 copy-start.1
Sparse Core Ops, SparseCore 0:
  801.0 102.5 reduce-scatter.1

commit v4 on v3

--- a/solution.py
+++ b/solution.py
@@ -94,16 +94,9 @@
 NN = ((1,), (0,))
 
 
-def deal_kernel(start, count, half_cols, right, out, sems):
-    copies = []
+def deal_kernel(half_cols, right, out):
     for half in range(2):
-        for plane in range(2):
-            source = right.at[plane, :, pl.ds(start, count), :, pl.ds(half * half_cols, half_cols)]
-            copies.append(pltpu.make_async_copy(source, out.at[:, half, plane], sems.at[2 * half + plane]))
-    for copy in copies:
-        copy.start()
-    for copy in copies:
-        copy.wait()
+        out[0, half] = right[:, 0, :, :, half * half_cols : (half + 1) * half_cols]
 
 
 def core_kernel(count, scale, arrived, core, factors, sems):
@@ -186,8 +179,7 @@
 
 
 def chunks_of(count):
-    last = min(2, count - 1)
-    return [count - last, last]
+    return count - 1, 1
 
 
 def overlapped(left_factor, right_factor):
@@ -206,11 +198,11 @@
 
     def dealt(start, count):
         return pl.pallas_call(
-            functools.partial(deal_kernel, start, count, half_cols),
+            functools.partial(deal_kernel, half_cols),
+            grid=(idx_size,),
             out_shape=jax.ShapeDtypeStruct((idx_size, 2, 2, count, inner_part, half_cols), jnp.float32),
-            in_specs=[ANYWHERE],
-            out_specs=ANYWHERE,
-            scratch_shapes=[pltpu.SemaphoreType.DMA((4,))],
+            in_specs=[pl.BlockSpec((2, 1, count, inner_part, between), lambda i: (0, i, start // count, 0, 0))],
+            out_specs=pl.BlockSpec((1, 2, 2, count, inner_part, half_cols), lambda i: (i, 0, 0, 0, 0, 0)),
             cost_estimate=pl.CostEstimate(
                 flops=0, bytes_accessed=32 * idx_size * count * inner_part * half_cols, transcendentals=0
             ),
@@ -268,6 +260,7 @@
     late = sent(pieces)
     core = core_of(many, arrived)
     total = added(0, many, core, swapped(core, "half"), other_left, None)
+    late, total = lax.optimization_barrier((late, total))
     core = core_of(few, late)
     total = added(many, few, core, swapped(core, "half"), other_left, total)
 

time: 913 us -> 524 us (0.57)
  Pallas kernels: 440 us -> 73.4 us
  waiting for transfers between devices: 391 us -> 360 us
    pallas_call x2, Pallas kernels: 385 us -> 18.2 us  [dealt(): pl.pallas_call(functools.partial(deal_kernel, half_cols), grid=(idx_size,...]
    ppermute x3, waiting for transfers between devices: 21.9 us -> 1.54 us  [swapped(): lax.ppermute(x, axis, [(i, i ^ 1) for i in range(lax.axis_size(axis))])]
  transfers between devices with their start and end apart: 6 -> 6, of which waited for: 4 -> 4; matrix products, arithmetic and copies ran while one was open for 0% -> 0% of each run, Pallas kernels for 5% -> 10%
where the time goes in v4:
time: 524 us
  waiting for transfers between devices  360 us (69%)
  Pallas kernels  73.4 us (14%)
  starting transfers between devices  70.8 us (14%)
  between operations  13.5 us (3%)
  local copies, waits for them, and re-layouts  6.37 us (1%)
    all_to_all x2, waiting for transfers between devices, sent(): lax.all_to_all(flat, ('idx', 'half'), 0, 0, tiled=True)  264 us
    reduce_scatter x1, waiting for transfers between devices, overlapped(): lax.psum_scatter(jnp.moveaxis(total, 0, 1), 'idx', scatter_dimension=0, t...  94.2 us
    all_to_all x2, starting transfers between devices, sent(): lax.all_to_all(flat, ('idx', 'half'), 0, 0, tiled=True)  68.7 us
    pallas_call x2, Pallas kernels, added(): pl.pallas_call(functools.partial(amplitude_kernel, start, count, 256, fre...  43.3 us
    pallas_call x2, Pallas kernels, dealt(): pl.pallas_call(functools.partial(deal_kernel, half_cols), grid=(idx_size,...  18.2 us
    pallas_call x2, Pallas kernels, core_of(): pl.pallas_call(functools.partial(core_kernel, count, scale), out_shape=ja...  12 us
  transfers between devices with their start and end apart: 6, of which 4 were waited for; matrix products, arithmetic and copies ran while one was open for 0% of the time, Pallas kernels for 10%

profile of v4, /device:TPU:0, one launch (start us, length us, event | category | flops | bytes accessed | tf_op | source)
XLA Modules:
  0.0 523.7 jit_solution(17641846264187074627)
XLA Ops:
  6.5 12.5 %shard_map.29 = f32[8,2,2,7,32,512]{5,4,3,2,1,0:T(8,128)} custom-call(f32[2,8,8,32,1024]{4,3,2,1,0:T(8,128)} %bitcast.13), custom_call_target="tpu_custom_call" | custom-call | bytes 29360128 | tf_op jit(solution)/shard_map/pallas_call | solution.py:200
  19.1 7.4 %all-to-all-start.1 = ((f32[16,2,7,32,512]{4,3,2,1,0:T(8,128)}), f32[16,2,7,32,512]{4,3,2,1,0:T(8,128)}, u32[]{:S(2)}, u32[]{:S(2)}) async-start(f32[16,2,7,32,512]{4,3,2,1,0:T(8,128)} %bitcast.15), calls=%async_computation.1 | async-start | bytes 29360128 | tf_op jit(solution)/shard_map/all_to_all | solution.py:214
  26.5 0.4 collective-permute-start
  26.9 259.9 %all-to-all-done.1 = f32[16,2,7,32,512]{4,3,2,1,0:T(8,128)} async-done(((f32[16,2,7,32,512]{4,3,2,1,0:T(8,128)}), f32[16,2,7,32,512]{4,3,2,1,0:T(8,128)}, u32[]{:S(2)}, u32[]{:S(2)}) %all-to-all-start.1) | async-done | bytes 14680096 | tf_op jit(solution)/shard_map/all_to_all | solution.py:214
  286.7 10.9 %shard_map.30.own_core = f32[7,2,256,256]{3,2,1,0:T(8,128)} custom-call(f32[8,2,2,7,32,512]{5,4,3,2,1,0:T(8,128)} %bitcast.7.arrived), custom_call_target="tpu_custom_call" | custom-call | flops 4227858432 | bytes 22020096 | tf_op jit(solution)/shard_map/pallas_call | solution.py:217
  297.6 0.8 collective-permute-start.1
  298.5 5.7 %shard_map.28 = f32[8,2,2,1,32,512]{5,4,3,2,1,0:T(8,128)} custom-call(f32[2,8,8,32,1024]{4,3,2,1,0:T(8,128)} %bitcast.14), custom_call_target="tpu_custom_call" | custom-call | bytes 4194304 | tf_op jit(solution)/shard_map/pallas_call | solution.py:200
  304.1 0.0 collective-permute-done
  304.1 61.3 %all-to-all-start = ((f32[16,2,1,32,512]{4,3,1,2,0:T(8,128)}), f32[16,2,1,32,512]{4,3,1,2,0:T(8,128)S(1)}, u32[]{:S(2)}, u32[]{:S(2)}) async-start(f32[16,2,1,32,512]{4,3,1,2,0:T(8,128)} %bitcast.4), calls=%async_computation | async-start | bytes 4194304 | tf_op jit(solution)/shard_map/all_to_all | solution.py:214
  365.4 0.0 reduce-scatter.2.cloned.1.call-start
  365.5 0.0 collective-permute-done.1.other_core
  365.5 37.1 %shard_map.31.refs_0_ = f32[2,512,1024]{2,1,0:T(8,128)} custom-call(s32[1]{0:T(128)} %bitcast.place, f32[7,2,256,256]{3,2,1,0:T(8,128)} %shard_map.30.own_core, f32[7,2,256,256]{3,2,1,0:T(8,128)} %collective-permute-done.1.other_core, f32[2,8,8,2,64,256]{5,4,3,2,1,0:T(8,128)} %bitcast.16, f32[2,8,8,2,64,256]{5,4,3,2,1,0:T(8,128)} %bitcast.2.other_left), custom_call_target="tpu_custom_call" | custom-call | flops 21139292160 | bytes 30408704 | tf_op jit(solution)/shard_map/pallas_call | solution.py:236
  402.6 4.0 all-to-all-done
  406.5 1.1 shard_map.32.own_core
  407.6 0.8 collective-permute-start.2
  408.5 1.5 collective-permute-done.2.other_core
  410.0 0.0 copy-start.1
  410.0 2.2 copy-done.1
  412.2 6.2 %shard_map.33 = f32[2,512,1024]{2,1,0:T(8,128)S(1)} custom-call(s32[1]{0:T(128)} %bitcast.place, f32[1,2,256,256]{3,2,1,0:T(8,128)S(1)} %shard_map.32.own_core, f32[1,2,256,256]{3,2,1,0:T(8,128)S(1)} %collective-permute-done.2.other_core, f32[2,8,8,2,64,256]{5,4,3,2,1,0:T(8,128)} %bitcast.17, f32[2,8,8,2,64,256]{5,4,3,2,1,0:T(8,128)} %bitcast.2.other_left, ...), custom_call_target="tpu_custom_call" | custom-call | flops 3019898880 | bytes 11534336 | tf_op jit(solution)/shard_map/pallas_call | solution.py:236
  418.4 0.0 copy-start
  418.4 1.9 copy-done
  420.3 0.0 reduce-scatter.2.cloned.1.call-update
  420.4 94.2 %reduce-scatter.2.cloned.1.call-done = f32[64,2,1024]{2,0,1:T(8,128)} async-done(((f32[512,2,1024]{2,0,1:T(8,128)}), f32[64,2,1024]{2,0,1:T(8,128)}) %reduce-scatter.2.cloned.1.call-update) | async-done | bytes 524304 | tf_op jit(solution)/shard_map/reduce_scatter | solution.py:267
  514.6 2.2 copy.5
Async XLA Ops:
  19.1 267.7 %all-to-all-start.1 = ((f32[16,2,7,32,512]{4,3,2,1,0:T(8,128)}), f32[16,2,7,32,512]{4,3,2,1,0:T(8,128)}, u32[]{:S(2)}, u32[]{:S(2)}) async-start(f32[16,2,7,32,512]{4,3,2,1,0:T(8,128)} %bitcast.15), calls=%async_computation.1 | async-start | bytes 29360128 | tf_op jit(solution)/shard_map/all_to_all | solution.py:214
  26.5 277.6 %collective-permute-start = (f32[1,2,8,1024,256]{4,3,2,1,0:T(8,128)}, f32[1,2,8,1024,256]{4,3,2,1,0:T(8,128)}, u32[]{:S(2)}, u32[]{:S(2)}) collective-permute-start(f32[1,2,8,1024,256]{4,3,2,1,0:T(8,128)} %param.2), channel_id=1, source_target_pairs={{0,1},{1,0},{2,3},{3,2},{4,5},{5,4},{6,7},{7,6},{8,9},{9,8},{10,11... | collective-permute-start | bytes 50331656 | tf_op jit(solution)/shard_map/ppermute | solution.py:19
  297.6 67.9 %collective-permute-start.1 = (f32[7,2,256,256]{3,2,1,0:T(8,128)}, f32[7,2,256,256]{3,2,1,0:T(8,128)}, u32[]{:S(2)}, u32[]{:S(2)}) collective-permute-start(f32[7,2,256,256]{3,2,1,0:T(8,128)} %shard_map.30.own_core), channel_id=1, source_target_pairs={{0,1},{1,0},{2,3},{3,2},{4,5},{5,4},{6,7},{7,6},{8,9},{9,8},{10,11... | collective-permute-start | bytes 11010056 | tf_op jit(solution)/shard_map/ppermute | solution.py:19
  304.1 102.4 %all-to-all-start = ((f32[16,2,1,32,512]{4,3,1,2,0:T(8,128)}), f32[16,2,1,32,512]{4,3,1,2,0:T(8,128)S(1)}, u32[]{:S(2)}, u32[]{:S(2)}) async-start(f32[16,2,1,32,512]{4,3,1,2,0:T(8,128)} %bitcast.4), calls=%async_computation | async-start | bytes 4194304 | tf_op jit(solution)/shard_map/all_to_all | solution.py:214
  365.4 149.2 %reduce-scatter.2.cloned.1.call-start = ((), (), s32[]{:S(2)}) async-start(), calls=%async_computation.3 | async-start | bytes 4718592 | tf_op jit(solution)/shard_map/reduce_scatter | solution.py:267
  407.6 2.4 collective-permute-start.2
  410.0 2.2 copy-start.1
  418.4 1.9 copy-start
Sparse Core Ops, SparseCore 0:
  420.5 94.0 reduce-scatter.1

commit v5 on v4

--- a/solution.py
+++ b/solution.py
@@ -90,6 +90,7 @@
     return first - second, mixed - first - second
 
 
+BRIEF = pl.CostEstimate(flops=0, bytes_accessed=1024, transcendentals=0)
 NT = ((1,), (1,))
 NN = ((1,), (0,))
 
@@ -203,9 +204,7 @@
             out_shape=jax.ShapeDtypeStruct((idx_size, 2, 2, count, inner_part, half_cols), jnp.float32),
             in_specs=[pl.BlockSpec((2, 1, count, inner_part, between), lambda i: (0, i, start // count, 0, 0))],
             out_specs=pl.BlockSpec((1, 2, 2, count, inner_part, half_cols), lambda i: (i, 0, 0, 0, 0, 0)),
-            cost_estimate=pl.CostEstimate(
-                flops=0, bytes_accessed=32 * idx_size * count * inner_part * half_cols, transcendentals=0
-            ),
+            cost_estimate=BRIEF,
             compiler_params=params,
         )(right)
 
@@ -223,11 +222,7 @@
                 pltpu.VMEM((count, 4, idx_size, inner_part, half_cols), jnp.float32),
                 pltpu.SemaphoreType.DMA((count, 4)),
             ],
-            cost_estimate=pl.CostEstimate(
-                flops=18 * count * inner * inner * half_cols,
-                bytes_accessed=16 * count * inner * (inner + half_cols),
-                transcendentals=0,
-            ),
+            cost_estimate=BRIEF,
             compiler_params=params,
         )(arrived)
 
@@ -245,19 +240,16 @@
                 pltpu.SemaphoreType.DMA((2, count)),
                 pltpu.SemaphoreType.DMA,
             ],
-            cost_estimate=pl.CostEstimate(
-                flops=18 * count * half_rows * inner * (inner + rows),
-                bytes_accessed=count * 12 * rows * inner + 16 * half_rows * rows,
-                transcendentals=0,
-            ),
+            cost_estimate=BRIEF,
             compiler_params=params,
         )(place, core, other_core, own_left, other_left, *([] if fresh else [total]))
 
     many, few = chunks_of(local_batch)
     other_left = swapped(left_factor, "half").reshape(shape)
     arrived = sent(dealt(0, many))
-    pieces, other_left = lax.optimization_barrier((dealt(many, few), other_left))
+    pieces = dealt(many, few)
     late = sent(pieces)
+    arrived, pieces = lax.optimization_barrier((arrived, pieces))
     core = core_of(many, arrived)
     total = added(0, many, core, swapped(core, "half"), other_left, None)
     late, total = lax.optimization_barrier((late, total))

time: 524 us -> 516 us (0.985)
  waiting for transfers between devices: 360 us -> 352 us
    all_to_all x2, waiting for transfers between devices: 264 us -> 254 us  [sent(): lax.all_to_all(flat, ('idx', 'half'), 0, 0, tiled=True)]
    ppermute x3, waiting for transfers between devices: 1.54 us -> 7.91 us  [swapped(): lax.ppermute(x, axis, [(i, i ^ 1) for i in range(lax.axis_size(axis))])]
where the time goes in v5:
time: 516 us; the launch traced here: 515 us
  waiting for transfers between devices  352 us (68%)
  Pallas kernels  73.4 us (14%)
  starting transfers between devices  70.5 us (14%)
  between operations  13.5 us (3%)
  local copies, waits for them, and re-layouts  6.37 us (1%)
    all_to_all x2, waiting for transfers between devices, sent(): lax.all_to_all(flat, ('idx', 'half'), 0, 0, tiled=True)  254 us
    reduce_scatter x1, waiting for transfers between devices, overlapped(): lax.psum_scatter(jnp.moveaxis(total, 0, 1), 'idx', scatter_dimension=0, t...  89.5 us
    all_to_all x2, starting transfers between devices, sent(): lax.all_to_all(flat, ('idx', 'half'), 0, 0, tiled=True)  69.2 us
    pallas_call x2, Pallas kernels, added(): pl.pallas_call(functools.partial(amplitude_kernel, start, count, 256, fre...  43.2 us
    pallas_call x2, Pallas kernels, dealt(): pl.pallas_call(functools.partial(deal_kernel, half_cols), grid=(idx_size,...  18.2 us
    pallas_call x2, Pallas kernels, core_of(): pl.pallas_call(functools.partial(core_kernel, count, scale), out_shape=ja...  12 us
  transfers between devices with their start and end apart: 6, of which 4 were waited for; matrix products, arithmetic and copies ran while one was open for 0% of the time, Pallas kernels for 10%

profile of v5, /device:TPU:0, one launch (start us, length us, event | category | flops | bytes accessed | tf_op | source)
XLA Modules:
  0.0 515.4 jit_solution(11354504084305550619)
XLA Ops:
  6.5 12.5 %shard_map.29 = f32[8,2,2,7,32,512]{5,4,3,2,1,0:T(8,128)} custom-call(f32[2,8,8,32,1024]{4,3,2,1,0:T(8,128)} %bitcast.13), custom_call_target="tpu_custom_call" | custom-call | bytes 1024 | tf_op jit(solution)/shard_map/pallas_call | solution.py:201
  19.1 7.4 %all-to-all-start.1 = ((f32[16,2,7,32,512]{4,3,2,1,0:T(8,128)}), f32[16,2,7,32,512]{4,3,2,1,0:T(8,128)}, u32[]{:S(2)}, u32[]{:S(2)}) async-start(f32[16,2,7,32,512]{4,3,2,1,0:T(8,128)} %bitcast.17), calls=%async_computation.1 | async-start | bytes 29360128 | tf_op jit(solution)/shard_map/all_to_all | solution.py:213
  26.5 0.4 collective-permute-start.1
  26.9 5.6 %shard_map.28 = f32[8,2,2,1,32,512]{5,4,3,2,1,0:T(8,128)} custom-call(f32[2,8,8,32,1024]{4,3,2,1,0:T(8,128)} %bitcast.14), custom_call_target="tpu_custom_call" | custom-call | bytes 1024 | tf_op jit(solution)/shard_map/pallas_call | solution.py:201
  32.5 254.2 %all-to-all-done.1 = f32[16,2,7,32,512]{4,3,2,1,0:T(8,128)} async-done(((f32[16,2,7,32,512]{4,3,2,1,0:T(8,128)}), f32[16,2,7,32,512]{4,3,2,1,0:T(8,128)}, u32[]{:S(2)}, u32[]{:S(2)}) %all-to-all-start.1) | async-done | bytes 14680096 | tf_op jit(solution)/shard_map/all_to_all | solution.py:213
  286.7 61.8 %all-to-all-start = ((f32[16,2,1,32,512]{4,3,1,2,0:T(8,128)}), f32[16,2,1,32,512]{4,3,1,2,0:T(8,128)S(1)}, u32[]{:S(2)}, u32[]{:S(2)}) async-start(f32[16,2,1,32,512]{4,3,1,2,0:T(8,128)} %bitcast.3), calls=%async_computation | async-start | bytes 4194304 | tf_op jit(solution)/shard_map/all_to_all | solution.py:213
  348.5 0.0 reduce-scatter.2.cloned.1.call-start
  348.6 10.9 %shard_map.30.own_core = f32[7,2,256,256]{3,2,1,0:T(8,128)} custom-call(f32[8,2,2,7,32,512]{5,4,3,2,1,0:T(8,128)} %bitcast.6.arrived), custom_call_target="tpu_custom_call" | custom-call | bytes 1024 | tf_op jit(solution)/shard_map/pallas_call | solution.py:216
  359.5 0.5 collective-permute-start
  359.9 0.0 collective-permute-done.1
  359.9 6.4 %collective-permute-done.other_core = f32[7,2,256,256]{3,2,1,0:T(8,128)} collective-permute-done((f32[7,2,256,256]{3,2,1,0:T(8,128)}, f32[7,2,256,256]{3,2,1,0:T(8,128)}, u32[]{:S(2)}, u32[]{:S(2)}) %collective-permute-start) | collective-permute-done | bytes 3670048 | tf_op jit(solution)/shard_map/ppermute | solution.py:19
  366.3 37.0 %shard_map.31.refs_0_ = f32[2,512,1024]{2,1,0:T(8,128)} custom-call(s32[1]{0:T(128)} %bitcast.place, f32[7,2,256,256]{3,2,1,0:T(8,128)} %shard_map.30.own_core, f32[7,2,256,256]{3,2,1,0:T(8,128)} %collective-permute-done.other_core, f32[2,8,8,2,64,256]{5,4,3,2,1,0:T(8,128)} %bitcast.15, f32[2,8,8,2,64,256]{5,4,3,2,1,0:T(8,128)} %bitcast.8.other_left), custom_call_target="tpu_custom_call" | custom-call | bytes 1024 | tf_op jit(solution)/shard_map/pallas_call | solution.py:231
  403.4 0.0 all-to-all-done
  403.4 1.1 shard_map.32.own_core
  404.5 0.4 collective-permute-start.2
  404.9 1.5 collective-permute-done.2.other_core
  406.4 0.0 copy-start
  406.4 2.2 copy-done
  408.6 6.2 %shard_map.33 = f32[2,512,1024]{2,1,0:T(8,128)S(1)} custom-call(s32[1]{0:T(128)} %bitcast.place, f32[1,2,256,256]{3,2,1,0:T(8,128)S(1)} %shard_map.32.own_core, f32[1,2,256,256]{3,2,1,0:T(8,128)S(1)} %collective-permute-done.2.other_core, f32[2,8,8,2,64,256]{5,4,3,2,1,0:T(8,128)} %bitcast.16, f32[2,8,8,2,64,256]{5,4,3,2,1,0:T(8,128)} %bitcast.8.other_left, ...), custom_call_target="tpu_custom_call" | custom-call | bytes 1024 | tf_op jit(solution)/shard_map/pallas_call | solution.py:231
  414.8 0.0 copy-start.1
  414.8 1.9 copy-done.1
  416.8 0.0 reduce-scatter.2.cloned.1.call-update
  416.8 89.5 %reduce-scatter.2.cloned.1.call-done = f32[64,2,1024]{2,0,1:T(8,128)} async-done(((f32[512,2,1024]{2,0,1:T(8,128)}), f32[64,2,1024]{2,0,1:T(8,128)}) %reduce-scatter.2.cloned.1.call-update) | async-done | bytes 524304 | tf_op jit(solution)/shard_map/reduce_scatter | solution.py:259
  506.4 2.2 copy.5
Async XLA Ops:
  19.1 267.7 %all-to-all-start.1 = ((f32[16,2,7,32,512]{4,3,2,1,0:T(8,128)}), f32[16,2,7,32,512]{4,3,2,1,0:T(8,128)}, u32[]{:S(2)}, u32[]{:S(2)}) async-start(f32[16,2,7,32,512]{4,3,2,1,0:T(8,128)} %bitcast.17), calls=%async_computation.1 | async-start | bytes 29360128 | tf_op jit(solution)/shard_map/all_to_all | solution.py:213
  26.5 333.5 %collective-permute-start.1 = (f32[1,2,8,1024,256]{4,3,2,1,0:T(8,128)}, f32[1,2,8,1024,256]{4,3,2,1,0:T(8,128)}, u32[]{:S(2)}, u32[]{:S(2)}) collective-permute-start(f32[1,2,8,1024,256]{4,3,2,1,0:T(8,128)} %param.2), channel_id=1, source_target_pairs={{0,1},{1,0},{2,3},{3,2},{4,5},{5,4},{6,7},{7,6},{8,9},{9,8},{10,11... | collective-permute-start | bytes 50331656 | tf_op jit(solution)/shard_map/ppermute | solution.py:19
  286.7 116.6 %all-to-all-start = ((f32[16,2,1,32,512]{4,3,1,2,0:T(8,128)}), f32[16,2,1,32,512]{4,3,1,2,0:T(8,128)S(1)}, u32[]{:S(2)}, u32[]{:S(2)}) async-start(f32[16,2,1,32,512]{4,3,1,2,0:T(8,128)} %bitcast.3), calls=%async_computation | async-start | bytes 4194304 | tf_op jit(solution)/shard_map/all_to_all | solution.py:213
  348.5 157.8 %reduce-scatter.2.cloned.1.call-start = ((), (), s32[]{:S(2)}) async-start(), calls=%async_computation.3 | async-start | bytes 4718592 | tf_op jit(solution)/shard_map/reduce_scatter | solution.py:259
  359.5 6.8 %collective-permute-start = (f32[7,2,256,256]{3,2,1,0:T(8,128)}, f32[7,2,256,256]{3,2,1,0:T(8,128)}, u32[]{:S(2)}, u32[]{:S(2)}) collective-permute-start(f32[7,2,256,256]{3,2,1,0:T(8,128)} %shard_map.30.own_core), channel_id=1, source_target_pairs={{0,1},{1,0},{2,3},{3,2},{4,5},{5,4},{6,7},{7,6},{8,9},{9,8},{10,11... | collective-permute-start | bytes 11010056 | tf_op jit(solution)/shard_map/ppermute | solution.py:19
  404.5 2.0 collective-permute-start.2
  406.4 2.2 copy-start
  414.8 1.9 copy-start.1
Sparse Core Ops, SparseCore 0:
  416.9 89.3 reduce-scatter.1

commit v6 on v5

--- a/solution.py
+++ b/solution.py
@@ -74,19 +74,33 @@
     return high, (x - high.astype(jnp.float32)).astype(jnp.bfloat16)
 
 
-def dot_parts(left, right, dims):
-    def dot(a, b):
-        return lax.dot_general(a, b, (dims, ((), ())), preferred_element_type=jnp.float32)
-
-    return dot(left[0], right[0]) + (dot(left[0], right[1]) + dot(left[1], right[0]))
+def stacked(parts, axis):
+    return jnp.concatenate(parts, axis=axis)
+
+
+def left_stack(x, axis):
+    high, low = split_float(x)
+    return stacked([high, high, low], axis)
+
+
+def right_stack(x, axis):
+    high, low = split_float(x)
+    return stacked([high, low, high], axis)
+
+
+def dot_stacks(left, right, dims):
+    return lax.dot_general(left, right, (dims, ((), ())), preferred_element_type=jnp.float32)
 
 
 def complex_dot(left_real, left_imag, right_real, right_imag, dims):
-    first = dot_parts(split_float(left_real), split_float(right_real), dims)
-    second = dot_parts(split_float(left_imag), split_float(right_imag), dims)
-    mixed = dot_parts(
-        split_float(left_real + left_imag), split_float(right_real + right_imag), dims
-    )
+    left_axis, right_axis = dims[0][0], dims[1][0]
+
+    def term(left, right):
+        return dot_stacks(left_stack(left, left_axis), right_stack(right, right_axis), dims)
+
+    first = term(left_real, right_real)
+    second = term(left_imag, right_imag)
+    mixed = term(left_real + left_imag, right_real + right_imag)
     return first - second, mixed - first - second
 
 
@@ -117,37 +131,54 @@
         core[b, 1] = imag * scale
 
 
-def amplitude_kernel(start, count, tile, fresh, place, own_core, other_core, own_left, other_left, *refs):
-    before = None if fresh else refs[0]
-    total, first, second, product, sems, sum_sem = refs[-6:]
-    half = place[0]
-
-    def copies(lower, b):
-        pairs = (own_left, other_left) if lower else (other_left, own_left)
-        side = 0 if lower else 1
-        return [
-            pltpu.make_async_copy(pairs[0].at[:, start + b, :, side], first.at[b], sems.at[0, b]),
-            pltpu.make_async_copy(pairs[1].at[:, start + b], second.at[b], sems.at[1, b]),
-        ]
+def row_slots(idx_size):
+    return list(range(0, idx_size, 2)) + list(range(1, idx_size, 2))
+
+
+def amplitude_kernel(start, count, columns, store, n_before, n_out, place, own_core, other_core, *refs):
+    own_split, other_split, own_flat, other_flat = refs[:4]
+    before = refs[4 : 4 + n_before]
+    outs = refs[4 + n_before : 4 + n_before + n_out]
+    first, second, product, sems, *more = refs[4 + n_before + n_out :]
+    half, idx = place[0], place[1]
+    low, high = columns
+    _, _, groups, own_rows, inner = first.shape
+    rows = groups * own_rows
+
+    def first_copy(lower, b, position, slot):
+        source = own_split if lower else other_split
+        return pltpu.make_async_copy(
+            source.at[:, start + b, idx ^ slot, 0 if lower else 1], first.at[b, :, position], sems.at[0, b]
+        )
+
+    def second_copy(lower, b):
+        source = other_flat if lower else own_flat
+        return pltpu.make_async_copy(
+            source.at[:, start + b, low:high], second.at[b], sems.at[1, b]
+        )
 
     for lower in (True, False):
 
         @pl.when(half == (0 if lower else 1))
         def _():
             for b in range(count):
-                for copy in copies(lower, b):
-                    copy.start()
-
-    if not fresh:
-        loading = pltpu.make_async_copy(before, total, sum_sem)
+                for position, slot in enumerate(row_slots(groups)):
+                    first_copy(lower, b, position, slot).start()
+                second_copy(lower, b).start()
+
+    if n_before:
+        held, held_sem = more
+        loading = pltpu.make_async_copy(before[0], held, held_sem)
         loading.start()
-    _, _, groups, own_rows, inner = first.shape
-    rows = groups * own_rows
-    columns = second.shape[2] * second.shape[3] * second.shape[4]
-    per = second.shape[3] * second.shape[4]
-    for b in range(count):
-        for copy in copies(True, b):
-            copy.wait()
+    else:
+        held = None
+        for out in outs:
+            out[...] = jnp.zeros_like(out)
+
+    def one_value(b, carry):
+        whole = own_split.at[:, start + b, :, 0]
+        pltpu.make_async_copy(whole, first.at[b], sems.at[0, b]).wait()
+        second_copy(True, b).wait()
         real, imag = complex_dot(
             first[b, 0].reshape(rows, inner),
             first[b, 1].reshape(rows, inner),
@@ -155,28 +186,51 @@
             own_core[b, 1] + other_core[b, 1],
             NN,
         )
-        for place_in, part in enumerate((real, imag, real + imag)):
-            product[2 * place_in], product[2 * place_in + 1] = split_float(part)
-        if b == 0 and not fresh:
+        for part, value in enumerate((real, imag, real + imag)):
+            product[part] = left_stack(value, 1)
+        if n_before:
             loading.wait()
-
-        def column_tile(step, carry):
-            at = pl.multiple_of(step * tile, tile)
-            right_real = second[b, 0, pl.ds(step * (tile // per), tile // per)].reshape(tile, inner)
-            right_imag = second[b, 1, pl.ds(step * (tile // per), tile // per)].reshape(tile, inner)
-            one = dot_parts((product[0], product[1]), split_float(right_real), NT)
-            two = dot_parts((product[2], product[3]), split_float(right_imag), NT)
-            three = dot_parts((product[4], product[5]), split_float(right_real + right_imag), NT)
-            spot = pl.ds(at, tile)
-            if fresh and b == 0:
-                total[0, :, spot] = one - two
-                total[1, :, spot] = three - one - two
-            else:
-                total[0, :, spot] += one - two
-                total[1, :, spot] += three - one - two
-            return carry
-
-        lax.fori_loop(0, columns // tile, column_tile, 0)
+        at = 0
+        while at < high - low:
+            wide = min(256, high - low - at)
+            right_real, right_imag = second[b, 0, at : at + wide], second[b, 1, at : at + wide]
+            one = dot_stacks(product[0], right_stack(right_real, 1), NT)
+            two = dot_stacks(product[1], right_stack(right_imag, 1), NT)
+            three = dot_stacks(product[2], right_stack(right_real + right_imag, 1), NT)
+            store(outs, held, at, wide, one - two, three - one - two)
+            at += wide
+        return carry
+
+    if count == 1:
+        one_value(0, 0)
+    else:
+        lax.fori_loop(0, count, one_value, 0)
+
+
+def add_running(cut, outs, held, at, wide, real, imag):
+    for out, low, high in ((outs[0], 0, cut), (outs[1], cut, 1 << 30)):
+        left, right = max(at, low), min(at + wide, high)
+        if left < right:
+            for plane, value in enumerate((real, imag)):
+                out[plane, :, left - low : right - low] += value[:, left - at : right - at]
+
+
+def put_near(outs, held, at, wide, real, imag):
+    rows = outs[0].shape[1]
+    for plane, value in enumerate((real, imag)):
+        value = value + held[plane, :, at : at + wide]
+        for bit in range(2):
+            outs[bit][plane, :, at : at + wide] = value[bit * rows : (bit + 1) * rows]
+
+
+def put_far(outs, held, at, wide, real, imag):
+    own_rows = outs[0].shape[2]
+    for plane, value in enumerate((real, imag)):
+        value = value + held[plane, :, at : at + wide]
+        for bit in range(2):
+            for far, out in enumerate(outs):
+                row = (bit * len(outs) + far) * own_rows
+                out[plane, bit, :, at : at + wide] = value[row : row + own_rows]
 
 
 def chunks_of(count):
@@ -191,7 +245,9 @@
     half_rows = rows // 2
     half_cols = between // 2
     scale = 1.0 / math.sqrt(2.0 * batch * between)
-    place = lax.axis_index("half").astype(jnp.int32)[None]
+    place = jnp.stack([lax.axis_index("half"), lax.axis_index("idx")]).astype(jnp.int32)
+    depth = idx_size // 2
+    cut = rows * 5 // 8 // 128 * 128
     right = right_factor.reshape(2, idx_size, local_batch, inner_part, between)
     params = pltpu.CompilerParams(vmem_limit_bytes=44 * MIB)
     shape = (2, local_batch, idx_size, 2, own_rows, inner)
@@ -226,23 +282,32 @@
             compiler_params=params,
         )(arrived)
 
-    def added(start, count, core, other_core, other_left, total):
-        fresh = total is None
+    def added(start, count, columns, store, core, other_core, other_left, before, shapes):
+        low, high = columns
+        flat = (2, local_batch, rows, inner)
+        scratch = [
+            pltpu.VMEM((count, 2, idx_size, own_rows, inner), jnp.float32),
+            pltpu.VMEM((count, 2, high - low, inner), jnp.float32),
+            pltpu.VMEM((3, half_rows, 3 * inner), jnp.bfloat16),
+            pltpu.SemaphoreType.DMA((2, count)),
+        ]
+        if before:
+            scratch += [pltpu.VMEM(before[0].shape, jnp.float32), pltpu.SemaphoreType.DMA]
         return pl.pallas_call(
-            functools.partial(amplitude_kernel, start, count, 256, fresh),
-            out_shape=jax.ShapeDtypeStruct((2, half_rows, rows), jnp.float32),
-            in_specs=[IN_SMEM, IN_VMEM, IN_VMEM, ANYWHERE, ANYWHERE] + [ANYWHERE] * (not fresh),
-            out_specs=IN_VMEM,
-            scratch_shapes=[
-                pltpu.VMEM((count, 2, idx_size, own_rows, inner), jnp.float32),
-                pltpu.VMEM((count, 2, idx_size, 2, own_rows, inner), jnp.float32),
-                pltpu.VMEM((6, half_rows, inner), jnp.bfloat16),
-                pltpu.SemaphoreType.DMA((2, count)),
-                pltpu.SemaphoreType.DMA,
-            ],
+            functools.partial(amplitude_kernel, start, count, columns, store, len(before), len(shapes)),
+            out_shape=[jax.ShapeDtypeStruct(shape, jnp.float32) for shape in shapes],
+            in_specs=[IN_SMEM, IN_VMEM, IN_VMEM] + [ANYWHERE] * (4 + len(before)),
+            out_specs=[IN_VMEM] * len(shapes),
+            scratch_shapes=scratch,
             cost_estimate=BRIEF,
             compiler_params=params,
-        )(place, core, other_core, own_left, other_left, *([] if fresh else [total]))
+        )(
+            place, core, other_core, own_left, other_left,
+            own_left.reshape(flat), other_left.reshape(flat), *before,
+        )
+
+    def hop(x, mask):
+        return lax.ppermute(x, "idx", [(i, i ^ mask) for i in range(idx_size)])
 
     many, few = chunks_of(local_batch)
     other_left = swapped(left_factor, "half").reshape(shape)
@@ -251,12 +316,30 @@
     late = sent(pieces)
     arrived, pieces = lax.optimization_barrier((arrived, pieces))
     core = core_of(many, arrived)
-    total = added(0, many, core, swapped(core, "half"), other_left, None)
-    late, total = lax.optimization_barrier((late, total))
+    sums = added(
+        0, many, (0, rows), functools.partial(add_running, cut), core, swapped(core, "half"), other_left, [],
+        [(2, half_rows, cut), (2, half_rows, rows - cut)],
+    )
+    late, sums = lax.optimization_barrier((late, sums))
     core = core_of(few, late)
-    total = added(many, few, core, swapped(core, "half"), other_left, total)
-
-    return lax.psum_scatter(jnp.moveaxis(total, 0, 1), "idx", scatter_dimension=0, tiled=True)
+    other_core = swapped(core, "half")
+    near = added(
+        many, few, (0, cut), put_near, core, other_core, other_left, [sums[0]],
+        [(2, half_rows // 2, cut)] * 2,
+    )
+    far = added(
+        many, few, (cut, rows), put_far, core, other_core, other_left, [sums[1]],
+        [(2, 2, own_rows, rows - cut)] * depth,
+    )
+    near_sum = (near[0] + hop(near[1], 1)).reshape(2, depth, own_rows, cut)
+    far_sum = far[0]
+    for d in range(1, depth):
+        far_sum = far_sum + hop(far[d], 2 * d)
+    near_out = near_sum[:, 0]
+    for d in range(1, depth):
+        near_out = near_out + hop(near_sum[:, d], 2 * d)
+    far_out = far_sum[:, 0] + hop(far_sum[:, 1], 1)
+    return jnp.moveaxis(jnp.concatenate([near_out, far_out], axis=2), 0, 1)
 
 
 def on_device(left_factor, right_factor):

time: 516 us -> 476 us (0.922)
  waiting for transfers between devices: 352 us -> 312 us
  starting transfers between devices: 70.5 us -> 87.7 us
  between operations: 13.5 us -> 0.14 us
    reduce_scatter x1 -> x0, waiting for transfers between devices: 89.5 us -> none  [overlapped(): lax.psum_scatter(jnp.moveaxis(total, 0, 1), 'idx', scatter_dimension=0, t...]
    ppermute x0 -> x8, waiting for transfers between devices: none -> 49.6 us  [hop(): return lax.ppermute(x, 'idx', [(i, i ^ mask) for i in range(idx_size)])]
    ppermute x0 -> x8, starting transfers between devices: none -> 17.3 us  [hop(): return lax.ppermute(x, 'idx', [(i, i ^ mask) for i in range(idx_size)])]
    pallas_call x2 -> x3, Pallas kernels: 43.2 us -> 38.8 us  [added(): pl.pallas_call(functools.partial(amplitude_kernel, start, count, columns,...]
  transfers between devices with their start and end apart: 6 -> 13, of which waited for: 4 -> 7; matrix products, arithmetic and copies ran while one was open for 0% -> 0% of each run, Pallas kernels for 10% -> 10%
where the time goes in v6:
time: 476 us; the launch traced here: 474 us
  waiting for transfers between devices  312 us (66%)
  starting transfers between devices  87.7 us (18%)
  Pallas kernels  68.7 us (14%)
    all_to_all x2, waiting for transfers between devices, sent(): lax.all_to_all(flat, ('idx', 'half'), 0, 0, tiled=True)  254 us
    all_to_all x2, starting transfers between devices, sent(): lax.all_to_all(flat, ('idx', 'half'), 0, 0, tiled=True)  69.2 us
    ppermute x8, waiting for transfers between devices, hop(): return lax.ppermute(x, 'idx', [(i, i ^ mask) for i in range(idx_size)])  49.6 us
    pallas_call x3, Pallas kernels, added(): pl.pallas_call(functools.partial(amplitude_kernel, start, count, columns,...  38.8 us
    pallas_call x2, Pallas kernels, dealt(): pl.pallas_call(functools.partial(deal_kernel, half_cols), grid=(idx_size,...  18.2 us
    ppermute x8, starting transfers between devices, hop(): return lax.ppermute(x, 'idx', [(i, i ^ mask) for i in range(idx_size)])  17.3 us
    pallas_call x2, Pallas kernels, core_of(): pl.pallas_call(functools.partial(core_kernel, count, scale), out_shape=ja...  11.6 us
  transfers between devices with their start and end apart: 13, of which 7 were waited for; matrix products, arithmetic and copies ran while one was open for 0% of the time, Pallas kernels for 10%

profile of v6, /device:TPU:0, one launch (start us, length us, event | category | flops | bytes accessed | tf_op | source)
XLA Modules:
  0.0 473.6 jit_solution(9956570279470468705)
XLA Ops:
  0.0 12.5 %shard_map.29 = f32[8,2,2,7,32,512]{5,4,3,2,1,0:T(8,128)} custom-call(f32[2,8,8,32,1024]{4,3,2,1,0:T(8,128)} %bitcast.48), custom_call_target="tpu_custom_call" | custom-call | bytes 1024 | tf_op jit(solution)/shard_map/pallas_call | solution.py:257
  12.5 7.4 %all-to-all-start.1 = ((f32[16,2,7,32,512]{4,3,2,1,0:T(8,128)}), f32[16,2,7,32,512]{4,3,2,1,0:T(8,128)}, u32[]{:S(2)}, u32[]{:S(2)}) async-start(f32[16,2,7,32,512]{4,3,2,1,0:T(8,128)} %bitcast.50), calls=%async_computation.1 | async-start | bytes 29360128 | tf_op jit(solution)/shard_map/all_to_all | solution.py:269
  20.0 0.4 collective-permute-start.1
  20.3 5.7 %shard_map.28 = f32[8,2,2,1,32,512]{5,4,3,2,1,0:T(8,128)} custom-call(f32[2,8,8,32,1024]{4,3,2,1,0:T(8,128)} %bitcast.49), custom_call_target="tpu_custom_call" | custom-call | bytes 1024 | tf_op jit(solution)/shard_map/pallas_call | solution.py:257
  26.0 254.2 %all-to-all-done.1 = f32[16,2,7,32,512]{4,3,2,1,0:T(8,128)} async-done(((f32[16,2,7,32,512]{4,3,2,1,0:T(8,128)}), f32[16,2,7,32,512]{4,3,2,1,0:T(8,128)}, u32[]{:S(2)}, u32[]{:S(2)}) %all-to-all-start.1) | async-done | bytes 14680096 | tf_op jit(solution)/shard_map/all_to_all | solution.py:269
  280.2 61.8 %all-to-all-start = ((f32[16,2,1,32,512]{4,3,1,2,0:T(8,128)}), f32[16,2,1,32,512]{4,3,1,2,0:T(8,128)S(1)}, u32[]{:S(2)}, u32[]{:S(2)}) async-start(f32[16,2,1,32,512]{4,3,1,2,0:T(8,128)} %bitcast.4), calls=%async_computation | async-start | bytes 4194304 | tf_op jit(solution)/shard_map/all_to_all | solution.py:269
  342.0 10.6 %shard_map.30.own_core = f32[7,2,256,256]{3,2,1,0:T(8,128)} custom-call(f32[8,2,2,7,32,512]{5,4,3,2,1,0:T(8,128)} %bitcast.7.arrived), custom_call_target="tpu_custom_call" | custom-call | bytes 1024 | tf_op jit(solution)/shard_map/pallas_call | solution.py:272
  352.6 0.5 collective-permute-start
  353.1 0.1 pad_add_fusion.place
  353.1 0.0 collective-permute-done.1
  353.2 6.3 %collective-permute-done.other_core = f32[7,2,256,256]{3,2,1,0:T(8,128)} collective-permute-done((f32[7,2,256,256]{3,2,1,0:T(8,128)}, f32[7,2,256,256]{3,2,1,0:T(8,128)}, u32[]{:S(2)}, u32[]{:S(2)}) %collective-permute-start) | collective-permute-done | bytes 3670048 | tf_op jit(solution)/shard_map/ppermute | solution.py:19
  359.5 28.7 %shard_map.31 = (f32[2,512,640]{2,1,0:T(8,128)S(1)}, f32[2,512,384]{2,1,0:T(8,128)S(1)}) custom-call(s32[2]{0:T(128)S(1)} %pad_add_fusion.place, f32[7,2,256,256]{3,2,1,0:T(8,128)} %shard_map.30.own_core, f32[7,2,256,256]{3,2,1,0:T(8,128)} %collective-permute-done.other_core, f32[2,8,8,2,64,256]{5,4,3,2,1,0:T(8,128)} %bitcast.42, ...), custom_call_target="tpu_custom_call" | custom-call | bytes 1024 | tf_op jit(solution)/shard_map/pallas_call | solution.py:296
  388.2 0.0 copy-start
  388.2 1.5 copy-done
  389.7 1.1 copy-done.2
  390.8 0.0 all-to-all-done
  390.9 1.0 shard_map.32.own_core
  391.9 0.0 copy-start.3
  391.9 0.4 collective-permute-start.2
  392.3 1.5 collective-permute-done.2.other_core
  393.9 0.0 copy-done.1
  393.9 5.7 %shard_map.33 = (f32[2,256,640]{2,1,0:T(8,128)S(1)}, f32[2,256,640]{2,1,0:T(8,128)S(1)}) custom-call(s32[2]{0:T(128)S(1)} %pad_add_fusion.place, f32[1,2,256,256]{3,2,1,0:T(8,128)S(1)} %shard_map.32.own_core, f32[1,2,256,256]{3,2,1,0:T(8,128)S(1)} %collective-permute-done.2.other_core, f32[2,8,8,2,64,256]{5,4,3,2,1,0:T(8,128)} %bitcast.44, ...), custom_call_target="tpu_custom_call" | custom-call | bytes 1024 | tf_op jit(solution)/shard_map/pallas_call | solution.py:296
  399.5 2.0 collective-permute-start.3
  401.5 4.4 shard_map.34
  405.9 1.5 collective-permute-start.7
  407.5 2.4 collective-permute-start.8
  409.8 0.5 collective-permute-start.9
  410.4 14.2 %collective-permute-done.7 = f32[2,2,64,384]{3,2,1,0:T(8,128)S(1)} collective-permute-done((f32[2,2,64,384]{3,2,1,0:T(8,128)S(1)}, f32[2,2,64,384]{3,2,1,0:T(8,128)S(1)}, u32[]{:S(2)}, u32[]{:S(2)}) %collective-permute-start.7) | collective-permute-done | bytes 393248 | tf_op jit(solution)/shard_map/ppermute | solution.py:310
  424.6 12.7 %collective-permute-done.8 = f32[2,2,64,384]{3,2,1,0:T(8,128)S(1)} collective-permute-done((f32[2,2,64,384]{3,2,1,0:T(8,128)S(1)}, f32[2,2,64,384]{3,2,1,0:T(8,128)S(1)}, u32[]{:S(2)}, u32[]{:S(2)}) %collective-permute-start.8) | collective-permute-done | bytes 393248 | tf_op jit(solution)/shard_map/ppermute | solution.py:310
  437.2 0.0 collective-permute-done.9
  437.3 0.1 add_add_fusion
  437.4 0.6 collective-permute-start.10
  438.0 0.0 collective-permute-done.3
  438.0 0.1 add.24
  438.1 0.1 fusion.4
  438.2 0.3 copy.33
  438.5 7.7 %collective-permute-start.4 = (f32[2,64,640]{2,0,1:T(2,128)S(1)}, f32[2,64,640]{2,0,1:T(2,128)S(1)}, u32[]{:S(2)}, u32[]{:S(2)}) collective-permute-start(f32[2,64,640]{2,0,1:T(2,128)S(1)} %bitcast.52), channel_id=1, source_target_pairs={{0,4},{2,6},{4,0},{6,2},{8,12},{10,14},{12,8},{14,10},{1,5},{3,7},... | collective-permute-start | bytes 983048 | tf_op jit(solution)/shard_map/ppermute | solution.py:310
  446.2 0.3 copy.32
  446.5 1.0 collective-permute-start.5
  447.5 0.3 copy.31
  447.7 1.5 collective-permute-start.6
  449.2 0.0 collective-permute-done.10
  449.3 0.2 copy.15
  449.4 8.5 %collective-permute-done.4 = f32[2,64,640]{2,0,1:T(2,128)S(1)} collective-permute-done((f32[2,64,640]{2,0,1:T(2,128)S(1)}, f32[2,64,640]{2,0,1:T(2,128)S(1)}, u32[]{:S(2)}, u32[]{:S(2)}) %collective-permute-start.4) | collective-permute-done | bytes 327712 | tf_op jit(solution)/shard_map/ppermute | solution.py:310
  457.9 14.2 %collective-permute-done.5 = f32[2,64,640]{2,0,1:T(2,128)S(1)} collective-permute-done((f32[2,64,640]{2,0,1:T(2,128)S(1)}, f32[2,64,640]{2,0,1:T(2,128)S(1)}, u32[]{:S(2)}, u32[]{:S(2)}) %collective-permute-start.5) | collective-permute-done | bytes 327712 | tf_op jit(solution)/shard_map/ppermute | solution.py:310
  472.1 0.0 collective-permute-done.6
  472.1 0.4 fusion.2
  472.6 1.0 maximum_bitcast_fusion
  (5 shorter events, 0.0 us)
Async XLA Ops:
  12.5 267.7 %all-to-all-start.1 = ((f32[16,2,7,32,512]{4,3,2,1,0:T(8,128)}), f32[16,2,7,32,512]{4,3,2,1,0:T(8,128)}, u32[]{:S(2)}, u32[]{:S(2)}) async-start(f32[16,2,7,32,512]{4,3,2,1,0:T(8,128)} %bitcast.50), calls=%async_computation.1 | async-start | bytes 29360128 | tf_op jit(solution)/shard_map/all_to_all | solution.py:269
  20.0 333.2 %collective-permute-start.1 = (f32[1,2,8,1024,256]{4,3,2,1,0:T(8,128)}, f32[1,2,8,1024,256]{4,3,2,1,0:T(8,128)}, u32[]{:S(2)}, u32[]{:S(2)}) collective-permute-start(f32[1,2,8,1024,256]{4,3,2,1,0:T(8,128)} %param.2), channel_id=1, source_target_pairs={{0,1},{1,0},{2,3},{3,2},{4,5},{5,4},{6,7},{7,6},{8,9},{9,8},{10,11... | collective-permute-start | bytes 50331656 | tf_op jit(solution)/shard_map/ppermute | solution.py:19
  280.2 110.6 %all-to-all-start = ((f32[16,2,1,32,512]{4,3,1,2,0:T(8,128)}), f32[16,2,1,32,512]{4,3,1,2,0:T(8,128)S(1)}, u32[]{:S(2)}, u32[]{:S(2)}) async-start(f32[16,2,1,32,512]{4,3,1,2,0:T(8,128)} %bitcast.4), calls=%async_computation | async-start | bytes 4194304 | tf_op jit(solution)/shard_map/all_to_all | solution.py:269
  352.6 6.8 %collective-permute-start = (f32[7,2,256,256]{3,2,1,0:T(8,128)}, f32[7,2,256,256]{3,2,1,0:T(8,128)}, u32[]{:S(2)}, u32[]{:S(2)}) collective-permute-start(f32[7,2,256,256]{3,2,1,0:T(8,128)} %shard_map.30.own_core), channel_id=1, source_target_pairs={{0,1},{1,0},{2,3},{3,2},{4,5},{5,4},{6,7},{7,6},{8,9},{9,8},{10,11... | collective-permute-start | bytes 11010056 | tf_op jit(solution)/shard_map/ppermute | solution.py:19
  388.2 1.5 copy-start
  389.7 1.1 copy-start.2
  390.8 3.0 copy-start.1
  391.9 9.6 %copy-start.3 = (f32[2,512,384]{2,1,0:T(8,128)S(1)}, f32[2,512,384]{2,1,0:T(8,128)}, u32[]{:S(2)}) copy-start(f32[2,512,384]{2,1,0:T(8,128)} %copy-done.2) | copy-start | bytes 4718596
  391.9 2.0 collective-permute-start.2
  399.5 38.5 %collective-permute-start.3 = (f32[2,256,640]{2,1,0:T(8,128)S(1)}, f32[2,256,640]{2,1,0:T(8,128)S(1)}, u32[]{:S(2)}, u32[]{:S(2)}) collective-permute-start(f32[2,256,640]{2,1,0:T(8,128)S(1)} %get-tuple-element.23), channel_id=1, source_target_pairs={{0,2},{2,0},{4,6},{6,4},{8,10},{10,8},{12,14},{14,12},{1,3},{3,1},... | collective-permute-start | bytes 3932168 | tf_op jit(solution)/shard_map/ppermute | solution.py:310
  405.9 18.7 %collective-permute-start.7 = (f32[2,2,64,384]{3,2,1,0:T(8,128)S(1)}, f32[2,2,64,384]{3,2,1,0:T(8,128)S(1)}, u32[]{:S(2)}, u32[]{:S(2)}) collective-permute-start(f32[2,2,64,384]{3,2,1,0:T(8,128)S(1)} %get-tuple-element.26), channel_id=1, source_target_pairs={{0,4},{2,6},{4,0},{6,2},{8,12},{10,14},{12,8},{14,10},{1,5},{3,7},... | collective-permute-start | bytes 1179656 | tf_op jit(solution)/shard_map/ppermute | solution.py:310
  407.5 29.8 %collective-permute-start.8 = (f32[2,2,64,384]{3,2,1,0:T(8,128)S(1)}, f32[2,2,64,384]{3,2,1,0:T(8,128)S(1)}, u32[]{:S(2)}, u32[]{:S(2)}) collective-permute-start(f32[2,2,64,384]{3,2,1,0:T(8,128)S(1)} %get-tuple-element.27), channel_id=1, source_target_pairs={{0,8},{2,10},{4,12},{6,14},{8,0},{10,2},{12,4},{14,6},{1,9},{3,11}... | collective-permute-start | bytes 1179656 | tf_op jit(solution)/shard_map/ppermute | solution.py:310
  409.8 27.4 %collective-permute-start.9 = (f32[2,2,64,384]{3,2,1,0:T(8,128)S(1)}, f32[2,2,64,384]{3,2,1,0:T(8,128)S(1)}, u32[]{:S(2)}, u32[]{:S(2)}) collective-permute-start(f32[2,2,64,384]{3,2,1,0:T(8,128)S(1)} %get-tuple-element.28), channel_id=1, source_target_pairs={{0,12},{2,14},{4,8},{6,10},{8,4},{10,6},{12,0},{14,2},{1,13},{3,15... | collective-permute-start | bytes 1179656 | tf_op jit(solution)/shard_map/ppermute | solution.py:310
  437.4 11.9 %collective-permute-start.10 = (f32[2,64,384]{2,1,0:T(8,128)S(1)}, f32[2,64,384]{2,1,0:T(8,128)S(1)}, u32[]{:S(2)}, u32[]{:S(2)}) collective-permute-start(f32[2,64,384]{2,1,0:T(8,128)S(1)} %slice_bitcast_fusion), channel_id=1, source_target_pairs={{0,2},{2,0},{4,6},{6,4},{8,10},{10,8},{12,14},{14,12},{1,3},{3,1},... | collective-permute-start | bytes 589832 | tf_op jit(solution)/shard_map/ppermute | solution.py:310
  438.5 19.5 %collective-permute-start.4 = (f32[2,64,640]{2,0,1:T(2,128)S(1)}, f32[2,64,640]{2,0,1:T(2,128)S(1)}, u32[]{:S(2)}, u32[]{:S(2)}) collective-permute-start(f32[2,64,640]{2,0,1:T(2,128)S(1)} %bitcast.52), channel_id=1, source_target_pairs={{0,4},{2,6},{4,0},{6,2},{8,12},{10,14},{12,8},{14,10},{1,5},{3,7},... | collective-permute-start | bytes 983048 | tf_op jit(solution)/shard_map/ppermute | solution.py:310
  446.5 25.7 %collective-permute-start.5 = (f32[2,64,640]{2,0,1:T(2,128)S(1)}, f32[2,64,640]{2,0,1:T(2,128)S(1)}, u32[]{:S(2)}, u32[]{:S(2)}) collective-permute-start(f32[2,64,640]{2,0,1:T(2,128)S(1)} %bitcast.53), channel_id=1, source_target_pairs={{0,8},{2,10},{4,12},{6,14},{8,0},{10,2},{12,4},{14,6},{1,9},{3,11}... | collective-permute-start | bytes 983048 | tf_op jit(solution)/shard_map/ppermute | solution.py:310
  447.7 24.4 %collective-permute-start.6 = (f32[2,64,640]{2,0,1:T(2,128)S(1)}, f32[2,64,640]{2,0,1:T(2,128)S(1)}, u32[]{:S(2)}, u32[]{:S(2)}) collective-permute-start(f32[2,64,640]{2,0,1:T(2,128)S(1)} %bitcast.54), channel_id=1, source_target_pairs={{0,12},{2,14},{4,8},{6,10},{8,4},{10,6},{12,0},{14,2},{1,13},{3,15... | collective-permute-start | bytes 983048 | tf_op jit(solution)/shard_map/ppermute | solution.py:310

commit v7 on v6

--- a/solution.py
+++ b/solution.py
@@ -109,9 +109,16 @@
 NN = ((1,), (0,))
 
 
-def deal_kernel(half_cols, right, out):
+def deal_kernel(start, count, half_cols, right, out, sems):
+    copies = []
     for half in range(2):
-        out[0, half] = right[:, 0, :, :, half * half_cols : (half + 1) * half_cols]
+        for plane in range(2):
+            source = right.at[plane, :, pl.ds(start, count), :, pl.ds(half * half_cols, half_cols)]
+            copies.append(pltpu.make_async_copy(source, out.at[:, half, plane], sems.at[2 * half + plane]))
+    for copy in copies:
+        copy.start()
+    for copy in copies:
+        copy.wait()
 
 
 def core_kernel(count, scale, arrived, core, factors, sems):
@@ -131,19 +138,14 @@
         core[b, 1] = imag * scale
 
 
-def row_slots(idx_size):
-    return list(range(0, idx_size, 2)) + list(range(1, idx_size, 2))
-
-
-def amplitude_kernel(start, count, columns, store, n_before, n_out, place, own_core, other_core, *refs):
+def amplitude_kernel(start, count, slots, n_before, n_out, place, own_core, other_core, *refs):
     own_split, other_split, own_flat, other_flat = refs[:4]
     before = refs[4 : 4 + n_before]
     outs = refs[4 + n_before : 4 + n_before + n_out]
-    first, second, product, sems, *more = refs[4 + n_before + n_out :]
+    first, second, product, sems = refs[4 + n_before + n_out :]
     half, idx = place[0], place[1]
-    low, high = columns
     _, _, groups, own_rows, inner = first.shape
-    rows = groups * own_rows
+    rows, columns = groups * own_rows, second.shape[2]
 
     def first_copy(lower, b, position, slot):
         source = own_split if lower else other_split
@@ -153,32 +155,25 @@
 
     def second_copy(lower, b):
         source = other_flat if lower else own_flat
-        return pltpu.make_async_copy(
-            source.at[:, start + b, low:high], second.at[b], sems.at[1, b]
-        )
+        return pltpu.make_async_copy(source.at[:, start + b], second.at[b], sems.at[1, b])
 
     for lower in (True, False):
 
         @pl.when(half == (0 if lower else 1))
         def _():
             for b in range(count):
-                for position, slot in enumerate(row_slots(groups)):
+                for position, slot in enumerate(slots):
                     first_copy(lower, b, position, slot).start()
                 second_copy(lower, b).start()
 
-    if n_before:
-        held, held_sem = more
-        loading = pltpu.make_async_copy(before[0], held, held_sem)
-        loading.start()
-    else:
-        held = None
+    if not n_before:
         for out in outs:
             out[...] = jnp.zeros_like(out)
+    piece = rows // n_out
 
     def one_value(b, carry):
-        whole = own_split.at[:, start + b, :, 0]
+        whole = own_split.at[:, start + b, :groups, 0]
         pltpu.make_async_copy(whole, first.at[b], sems.at[0, b]).wait()
-        second_copy(True, b).wait()
         real, imag = complex_dot(
             first[b, 0].reshape(rows, inner),
             first[b, 1].reshape(rows, inner),
@@ -188,49 +183,28 @@
         )
         for part, value in enumerate((real, imag, real + imag)):
             product[part] = left_stack(value, 1)
-        if n_before:
-            loading.wait()
-        at = 0
-        while at < high - low:
-            wide = min(256, high - low - at)
-            right_real, right_imag = second[b, 0, at : at + wide], second[b, 1, at : at + wide]
+        second_copy(True, b).wait()
+        for at in range(0, columns, 256):
+            spot = slice(at, at + 256)
+            right_real, right_imag = second[b, 0, spot], second[b, 1, spot]
             one = dot_stacks(product[0], right_stack(right_real, 1), NT)
             two = dot_stacks(product[1], right_stack(right_imag, 1), NT)
             three = dot_stacks(product[2], right_stack(right_real + right_imag, 1), NT)
-            store(outs, held, at, wide, one - two, three - one - two)
-            at += wide
+            for plane, value in enumerate((one - two, three - one - two)):
+                if n_before:
+                    value = value + before[0][plane, :, spot]
+                for number, out in enumerate(outs):
+                    part = value[number * piece : (number + 1) * piece]
+                    if n_before:
+                        out[plane, :, spot] = part
+                    else:
+                        out[plane, :, spot] += part
         return carry
 
     if count == 1:
         one_value(0, 0)
     else:
         lax.fori_loop(0, count, one_value, 0)
-
-
-def add_running(cut, outs, held, at, wide, real, imag):
-    for out, low, high in ((outs[0], 0, cut), (outs[1], cut, 1 << 30)):
-        left, right = max(at, low), min(at + wide, high)
-        if left < right:
-            for plane, value in enumerate((real, imag)):
-                out[plane, :, left - low : right - low] += value[:, left - at : right - at]
-
-
-def put_near(outs, held, at, wide, real, imag):
-    rows = outs[0].shape[1]
-    for plane, value in enumerate((real, imag)):
-        value = value + held[plane, :, at : at + wide]
-        for bit in range(2):
-            outs[bit][plane, :, at : at + wide] = value[bit * rows : (bit + 1) * rows]
-
-
-def put_far(outs, held, at, wide, real, imag):
-    own_rows = outs[0].shape[2]
-    for plane, value in enumerate((real, imag)):
-        value = value + held[plane, :, at : at + wide]
-        for bit in range(2):
-            for far, out in enumerate(outs):
-                row = (bit * len(outs) + far) * own_rows
-                out[plane, bit, :, at : at + wide] = value[row : row + own_rows]
 
 
 def chunks_of(count):
@@ -247,7 +221,6 @@
     scale = 1.0 / math.sqrt(2.0 * batch * between)
     place = jnp.stack([lax.axis_index("half"), lax.axis_index("idx")]).astype(jnp.int32)
     depth = idx_size // 2
-    cut = rows * 5 // 8 // 128 * 128
     right = right_factor.reshape(2, idx_size, local_batch, inner_part, between)
     params = pltpu.CompilerParams(vmem_limit_bytes=44 * MIB)
     shape = (2, local_batch, idx_size, 2, own_rows, inner)
@@ -255,13 +228,13 @@
 
     def dealt(start, count):
         return pl.pallas_call(
-            functools.partial(deal_kernel, half_cols),
-            grid=(idx_size,),
+            functools.partial(deal_kernel, start, count, half_cols),
             out_shape=jax.ShapeDtypeStruct((idx_size, 2, 2, count, inner_part, half_cols), jnp.float32),
-            in_specs=[pl.BlockSpec((2, 1, count, inner_part, between), lambda i: (0, i, start // count, 0, 0))],
-            out_specs=pl.BlockSpec((1, 2, 2, count, inner_part, half_cols), lambda i: (i, 0, 0, 0, 0, 0)),
+            in_specs=[ANYWHERE],
+            out_specs=IN_VMEM,
+            scratch_shapes=[pltpu.SemaphoreType.DMA((4,))],
             cost_estimate=BRIEF,
-            compiler_params=params,
+            compiler_params=pltpu.CompilerParams(vmem_limit_bytes=38 * MIB),
         )(right)
 
     def sent(pieces):
@@ -282,23 +255,20 @@
             compiler_params=params,
         )(arrived)
 
-    def added(start, count, columns, store, core, other_core, other_left, before, shapes):
-        low, high = columns
+    def added(start, count, slots, n_out, core, other_core, other_left, before):
         flat = (2, local_batch, rows, inner)
-        scratch = [
-            pltpu.VMEM((count, 2, idx_size, own_rows, inner), jnp.float32),
-            pltpu.VMEM((count, 2, high - low, inner), jnp.float32),
-            pltpu.VMEM((3, half_rows, 3 * inner), jnp.bfloat16),
-            pltpu.SemaphoreType.DMA((2, count)),
-        ]
-        if before:
-            scratch += [pltpu.VMEM(before[0].shape, jnp.float32), pltpu.SemaphoreType.DMA]
+        kept_rows = len(slots) * own_rows
         return pl.pallas_call(
-            functools.partial(amplitude_kernel, start, count, columns, store, len(before), len(shapes)),
-            out_shape=[jax.ShapeDtypeStruct(shape, jnp.float32) for shape in shapes],
-            in_specs=[IN_SMEM, IN_VMEM, IN_VMEM] + [ANYWHERE] * (4 + len(before)),
-            out_specs=[IN_VMEM] * len(shapes),
-            scratch_shapes=scratch,
+            functools.partial(amplitude_kernel, start, count, slots, len(before), n_out),
+            out_shape=[jax.ShapeDtypeStruct((2, kept_rows // n_out, rows), jnp.float32)] * n_out,
+            in_specs=[IN_SMEM, IN_VMEM, IN_VMEM] + [ANYWHERE] * 4 + [IN_VMEM] * len(before),
+            out_specs=[IN_VMEM] * n_out,
+            scratch_shapes=[
+                pltpu.VMEM((count, 2, len(slots), own_rows, inner), jnp.float32),
+                pltpu.VMEM((count, 2, rows, inner), jnp.float32),
+                pltpu.VMEM((3, kept_rows, 3 * inner), jnp.bfloat16),
+                pltpu.SemaphoreType.DMA((2, count)),
+            ],
             cost_estimate=BRIEF,
             compiler_params=params,
         )(
@@ -316,30 +286,22 @@
     late = sent(pieces)
     arrived, pieces = lax.optimization_barrier((arrived, pieces))
     core = core_of(many, arrived)
-    sums = added(
-        0, many, (0, rows), functools.partial(add_running, cut), core, swapped(core, "half"), other_left, [],
-        [(2, half_rows, cut), (2, half_rows, rows - cut)],
-    )
+    odd = list(range(idx_size - 1, 0, -2))
+    even = [slot - 1 for slot in odd]
+    sums = added(0, many, odd + even, 2, core, swapped(core, "half"), other_left, [])
     late, sums = lax.optimization_barrier((late, sums))
     core = core_of(few, late)
     other_core = swapped(core, "half")
-    near = added(
-        many, few, (0, cut), put_near, core, other_core, other_left, [sums[0]],
-        [(2, half_rows // 2, cut)] * 2,
-    )
-    far = added(
-        many, few, (cut, rows), put_far, core, other_core, other_left, [sums[1]],
-        [(2, 2, own_rows, rows - cut)] * depth,
-    )
-    near_sum = (near[0] + hop(near[1], 1)).reshape(2, depth, own_rows, cut)
-    far_sum = far[0]
-    for d in range(1, depth):
-        far_sum = far_sum + hop(far[d], 2 * d)
-    near_out = near_sum[:, 0]
-    for d in range(1, depth):
-        near_out = near_out + hop(near_sum[:, d], 2 * d)
-    far_out = far_sum[:, 0] + hop(far_sum[:, 1], 1)
-    return jnp.moveaxis(jnp.concatenate([near_out, far_out], axis=2), 0, 1)
+    leaving = added(many, few, odd, depth, core, other_core, other_left, [sums[0]])
+    core, leaving = lax.optimization_barrier((core, leaving))
+    staying = added(many, few, even, depth, core, other_core, other_left, [sums[1]])
+    landed = [hop(block, 1) for block in leaving]
+    blocks = [kept + block for kept, block in zip(staying, landed)]
+    arrived = [hop(block, slot) for block, slot in zip(blocks, even) if slot]
+    result = blocks[-1]
+    for block in arrived:
+        result = result + block
+    return jnp.moveaxis(result, 0, 1)
 
 
 def on_device(left_factor, right_factor):

time: 476 us -> 461 us (0.968)
  Pallas kernels: 68.7 us -> 57.4 us
  local copies, waits for them, and re-layouts: 3.67 us -> 8.9 us
    pallas_call x5, Pallas kernels: 57 us -> 45.8 us  [the longest x3 37.5 us: added(): pl.pallas_call(functools.partial(amplitude_kernel, start, count, slots, l...]
    ppermute x8 -> x7, starting transfers between devices: 17.3 us -> 12.7 us  [hop(): return lax.ppermute(x, 'idx', [(i, i ^ mask) for i in range(idx_size)])]
    ppermute x8 -> x7, waiting for transfers between devices: 49.6 us -> 45.6 us  [hop(): return lax.ppermute(x, 'idx', [(i, i ^ mask) for i in range(idx_size)])]
  transfers between devices with their start and end apart: 13 -> 12, of which waited for: 7 -> 8; matrix products, arithmetic and copies ran while one was open for 0% -> 0% of each run, Pallas kernels for 10% -> 10%
where the time goes in v7:
time: 461 us; the launch traced here: 460 us
  waiting for transfers between devices  310 us (67%)
  starting transfers between devices  83.2 us (18%)
  Pallas kernels  57.4 us (12%)
  local copies, waits for them, and re-layouts  8.9 us (2%)
    all_to_all x2, waiting for transfers between devices, sent(): lax.all_to_all(flat, ('idx', 'half'), 0, 0, tiled=True)  257 us
    all_to_all x2, starting transfers between devices, sent(): lax.all_to_all(flat, ('idx', 'half'), 0, 0, tiled=True)  69.2 us
    ppermute x7, waiting for transfers between devices, hop(): return lax.ppermute(x, 'idx', [(i, i ^ mask) for i in range(idx_size)])  45.6 us
    pallas_call x3, Pallas kernels, added(): pl.pallas_call(functools.partial(amplitude_kernel, start, count, slots, l...  37.5 us
    ppermute x7, starting transfers between devices, hop(): return lax.ppermute(x, 'idx', [(i, i ^ mask) for i in range(idx_size)])  12.7 us
    pallas_call x2, Pallas kernels, core_of(): pl.pallas_call(functools.partial(core_kernel, count, scale), out_shape=ja...  11.6 us
  transfers between devices with their start and end apart: 12, of which 8 were waited for; matrix products, arithmetic and copies ran while one was open for 0% of the time, Pallas kernels for 10%

profile of v7, /device:TPU:0, one launch (start us, length us, event | category | flops | bytes accessed | tf_op | source)
XLA Modules:
  0.0 460.4 jit_solution(7320291117495803998)
XLA Ops:
  0.0 5.3 %shard_map.29 = f32[8,2,2,7,32,512]{5,4,3,2,1,0:T(8,128)S(1)} custom-call(f32[2,8,8,32,1024]{4,3,2,1,0:T(8,128)} %bitcast.23), custom_call_target="tpu_custom_call" | custom-call | bytes 1024 | tf_op jit(solution)/shard_map/pallas_call | solution.py:230
  5.4 0.0 copy-start
  5.4 5.1 %copy-done = f32[8,2,2,7,32,512]{5,4,3,2,1,0:T(8,128)} copy-done((f32[8,2,2,7,32,512]{5,4,3,2,1,0:T(8,128)}, f32[8,2,2,7,32,512]{5,4,3,2,1,0:T(8,128)S(1)}, u32[]{:S(2)}) %copy-start) | copy-done | bytes 14680088
  10.4 7.4 %all-to-all-start.1 = ((f32[16,2,7,32,512]{4,3,2,1,0:T(8,128)}), f32[16,2,7,32,512]{4,3,2,1,0:T(8,128)}, u32[]{:S(2)}, u32[]{:S(2)}) async-start(f32[16,2,7,32,512]{4,3,2,1,0:T(8,128)} %bitcast.15), calls=%async_computation.1 | async-start | bytes 29360128 | tf_op jit(solution)/shard_map/all_to_all | solution.py:242
  17.8 0.4 collective-permute-start.1
  18.2 2.9 shard_map.28
  21.1 257.0 %all-to-all-done.1 = f32[16,2,7,32,512]{4,3,2,1,0:T(8,128)} async-done(((f32[16,2,7,32,512]{4,3,2,1,0:T(8,128)}), f32[16,2,7,32,512]{4,3,2,1,0:T(8,128)}, u32[]{:S(2)}, u32[]{:S(2)}) %all-to-all-start.1) | async-done | bytes 14680096 | tf_op jit(solution)/shard_map/all_to_all | solution.py:242
  278.1 61.8 %all-to-all-start = ((f32[16,2,1,32,512]{4,3,1,2,0:T(8,128)}), f32[16,2,1,32,512]{4,3,1,2,0:T(8,128)S(1)}, u32[]{:S(2)}, u32[]{:S(2)}) async-start(f32[16,2,1,32,512]{4,3,1,2,0:T(8,128)} %bitcast.4), calls=%async_computation | async-start | bytes 4194304 | tf_op jit(solution)/shard_map/all_to_all | solution.py:242
  339.9 10.6 %shard_map.30.own_core = f32[7,2,256,256]{3,2,1,0:T(8,128)} custom-call(f32[8,2,2,7,32,512]{5,4,3,2,1,0:T(8,128)} %bitcast.7.arrived), custom_call_target="tpu_custom_call" | custom-call | bytes 1024 | tf_op jit(solution)/shard_map/pallas_call | solution.py:245
  350.5 0.5 collective-permute-start
  350.9 0.1 pad_add_fusion.place
  351.0 0.0 collective-permute-done.1
  351.0 6.3 %collective-permute-done.other_core = f32[7,2,256,256]{3,2,1,0:T(8,128)} collective-permute-done((f32[7,2,256,256]{3,2,1,0:T(8,128)}, f32[7,2,256,256]{3,2,1,0:T(8,128)}, u32[]{:S(2)}, u32[]{:S(2)}) %collective-permute-start) | collective-permute-done | bytes 3670048 | tf_op jit(solution)/shard_map/ppermute | solution.py:19
  357.3 29.7 %shard_map.31 = (f32[2,256,1024]{2,1,0:T(8,128)S(1)}, f32[2,256,1024]{2,1,0:T(8,128)S(1)}) custom-call(s32[2]{0:T(128)S(1)} %pad_add_fusion.place, f32[7,2,256,256]{3,2,1,0:T(8,128)} %shard_map.30.own_core, f32[7,2,256,256]{3,2,1,0:T(8,128)} %collective-permute-done.other_core, f32[2,8,8,2,64,256]{5,4,3,2,1,0:T(8,128)} %bitcast.17, ...), custom_call_target="tpu_custom_call" | custom-call | bytes 1024 | tf_op jit(solution)/shard_map/pallas_call | solution.py:261
  387.1 0.0 copy-start.1
  387.1 1.3 copy-done.1
  388.4 0.0 copy-start.3
  388.4 1.3 copy-done.3
  389.7 0.0 all-to-all-done
  389.7 0.0 copy-start.4
  389.7 1.0 shard_map.32.own_core
  390.7 0.0 copy-start.2
  390.7 0.4 collective-permute-start.2
  391.2 1.5 collective-permute-done.2.other_core
  392.7 0.0 copy-done.4
  392.7 3.9 shard_map.33
  396.6 1.9 collective-permute-start.4
  398.6 0.2 collective-permute-start.6
  398.7 1.9 collective-permute-start.8
  400.6 0.2 collective-permute-start.3
  400.8 0.0 copy-done.2
  400.8 3.9 shard_map.34
  404.7 6.8 %collective-permute-done.4 = f32[2,64,1024]{2,1,0:T(8,128)S(1)} collective-permute-done((f32[2,64,1024]{2,1,0:T(8,128)S(1)}, f32[2,64,1024]{2,1,0:T(8,128)S(1)}, u32[]{:S(2)}, u32[]{:S(2)}) %collective-permute-start.4) | collective-permute-done | bytes 524320 | tf_op jit(solution)/shard_map/ppermute | solution.py:280
  411.4 0.1 add.22
  411.5 3.8 collective-permute-start.5
  415.3 7.4 %collective-permute-done.6 = f32[2,64,1024]{2,1,0:T(8,128)S(1)} collective-permute-done((f32[2,64,1024]{2,1,0:T(8,128)S(1)}, f32[2,64,1024]{2,1,0:T(8,128)S(1)}, u32[]{:S(2)}, u32[]{:S(2)}) %collective-permute-start.6) | collective-permute-done | bytes 524320 | tf_op jit(solution)/shard_map/ppermute | solution.py:280
  422.7 0.1 add.24
  422.7 2.9 collective-permute-start.7
  425.6 8.3 %collective-permute-done.8 = f32[2,64,1024]{2,1,0:T(8,128)S(1)} collective-permute-done((f32[2,64,1024]{2,1,0:T(8,128)S(1)}, f32[2,64,1024]{2,1,0:T(8,128)S(1)}, u32[]{:S(2)}, u32[]{:S(2)}) %collective-permute-start.8) | collective-permute-done | bytes 524320 | tf_op jit(solution)/shard_map/ppermute | solution.py:280
  433.9 0.1 add.26
  434.0 2.0 collective-permute-start.9
  435.9 8.7 %collective-permute-done.3 = f32[2,64,1024]{2,1,0:T(8,128)S(1)} collective-permute-done((f32[2,64,1024]{2,1,0:T(8,128)S(1)}, f32[2,64,1024]{2,1,0:T(8,128)S(1)}, u32[]{:S(2)}, u32[]{:S(2)}) %collective-permute-start.3) | collective-permute-done | bytes 524320 | tf_op jit(solution)/shard_map/ppermute | solution.py:280
  444.6 0.0 collective-permute-done.5
  444.6 14.4 %collective-permute-done.7 = f32[2,64,1024]{2,1,0:T(8,128)S(1)} collective-permute-done((f32[2,64,1024]{2,1,0:T(8,128)S(1)}, f32[2,64,1024]{2,1,0:T(8,128)S(1)}, u32[]{:S(2)}, u32[]{:S(2)}) %collective-permute-start.7) | collective-permute-done | bytes 524320 | tf_op jit(solution)/shard_map/ppermute | solution.py:280
  459.0 0.0 collective-permute-done.9
  459.0 0.2 add_bitcast_fusion
  459.2 1.2 copy.5
Async XLA Ops:
  5.4 5.1 %copy-start = (f32[8,2,2,7,32,512]{5,4,3,2,1,0:T(8,128)}, f32[8,2,2,7,32,512]{5,4,3,2,1,0:T(8,128)S(1)}, u32[]{:S(2)}) copy-start(f32[8,2,2,7,32,512]{5,4,3,2,1,0:T(8,128)S(1)} %shard_map.29) | copy-start | bytes 44040196
  10.4 267.7 %all-to-all-start.1 = ((f32[16,2,7,32,512]{4,3,2,1,0:T(8,128)}), f32[16,2,7,32,512]{4,3,2,1,0:T(8,128)}, u32[]{:S(2)}, u32[]{:S(2)}) async-start(f32[16,2,7,32,512]{4,3,2,1,0:T(8,128)} %bitcast.15), calls=%async_computation.1 | async-start | bytes 29360128 | tf_op jit(solution)/shard_map/all_to_all | solution.py:242
  17.8 333.2 %collective-permute-start.1 = (f32[1,2,8,1024,256]{4,3,2,1,0:T(8,128)}, f32[1,2,8,1024,256]{4,3,2,1,0:T(8,128)}, u32[]{:S(2)}, u32[]{:S(2)}) collective-permute-start(f32[1,2,8,1024,256]{4,3,2,1,0:T(8,128)} %param.2), channel_id=1, source_target_pairs={{0,1},{1,0},{2,3},{3,2},{4,5},{5,4},{6,7},{7,6},{8,9},{9,8},{10,11... | collective-permute-start | bytes 50331656 | tf_op jit(solution)/shard_map/ppermute | solution.py:19
  278.1 111.6 %all-to-all-start = ((f32[16,2,1,32,512]{4,3,1,2,0:T(8,128)}), f32[16,2,1,32,512]{4,3,1,2,0:T(8,128)S(1)}, u32[]{:S(2)}, u32[]{:S(2)}) async-start(f32[16,2,1,32,512]{4,3,1,2,0:T(8,128)} %bitcast.4), calls=%async_computation | async-start | bytes 4194304 | tf_op jit(solution)/shard_map/all_to_all | solution.py:242
  350.5 6.8 %collective-permute-start = (f32[7,2,256,256]{3,2,1,0:T(8,128)}, f32[7,2,256,256]{3,2,1,0:T(8,128)}, u32[]{:S(2)}, u32[]{:S(2)}) collective-permute-start(f32[7,2,256,256]{3,2,1,0:T(8,128)} %shard_map.30.own_core), channel_id=1, source_target_pairs={{0,1},{1,0},{2,3},{3,2},{4,5},{5,4},{6,7},{7,6},{8,9},{9,8},{10,11... | collective-permute-start | bytes 11010056 | tf_op jit(solution)/shard_map/ppermute | solution.py:19
  387.1 1.3 copy-start.1
  388.4 1.3 copy-start.3
  389.7 3.0 copy-start.4
  390.7 10.0 %copy-start.2 = (f32[2,256,1024]{2,1,0:T(8,128)S(1)}, f32[2,256,1024]{2,1,0:T(8,128)}, u32[]{:S(2)}) copy-start(f32[2,256,1024]{2,1,0:T(8,128)} %copy-done.1) | copy-start | bytes 6291460
  390.7 2.0 collective-permute-start.2
  396.6 14.8 %collective-permute-start.4 = (f32[2,64,1024]{2,1,0:T(8,128)S(1)}, f32[2,64,1024]{2,1,0:T(8,128)S(1)}, u32[]{:S(2)}, u32[]{:S(2)}) collective-permute-start(f32[2,64,1024]{2,1,0:T(8,128)S(1)} %get-tuple-element.38), channel_id=1, source_target_pairs={{0,2},{2,0},{4,6},{6,4},{8,10},{10,8},{12,14},{14,12},{1,3},{3,1},... | collective-permute-start | bytes 1572872 | tf_op jit(solution)/shard_map/ppermute | solution.py:280
  398.6 24.1 %collective-permute-start.6 = (f32[2,64,1024]{2,1,0:T(8,128)S(1)}, f32[2,64,1024]{2,1,0:T(8,128)S(1)}, u32[]{:S(2)}, u32[]{:S(2)}) collective-permute-start(f32[2,64,1024]{2,1,0:T(8,128)S(1)} %get-tuple-element.40), channel_id=1, source_target_pairs={{0,2},{2,0},{4,6},{6,4},{8,10},{10,8},{12,14},{14,12},{1,3},{3,1},... | collective-permute-start | bytes 1572872 | tf_op jit(solution)/shard_map/ppermute | solution.py:280
  398.7 35.2 %collective-permute-start.8 = (f32[2,64,1024]{2,1,0:T(8,128)S(1)}, f32[2,64,1024]{2,1,0:T(8,128)S(1)}, u32[]{:S(2)}, u32[]{:S(2)}) collective-permute-start(f32[2,64,1024]{2,1,0:T(8,128)S(1)} %get-tuple-element.42), channel_id=1, source_target_pairs={{0,2},{2,0},{4,6},{6,4},{8,10},{10,8},{12,14},{14,12},{1,3},{3,1},... | collective-permute-start | bytes 1572872 | tf_op jit(solution)/shard_map/ppermute | solution.py:280
  400.6 44.0 %collective-permute-start.3 = (f32[2,64,1024]{2,1,0:T(8,128)S(1)}, f32[2,64,1024]{2,1,0:T(8,128)S(1)}, u32[]{:S(2)}, u32[]{:S(2)}) collective-permute-start(f32[2,64,1024]{2,1,0:T(8,128)S(1)} %get-tuple-element.36), channel_id=1, source_target_pairs={{0,2},{2,0},{4,6},{6,4},{8,10},{10,8},{12,14},{14,12},{1,3},{3,1},... | collective-permute-start | bytes 1572872 | tf_op jit(solution)/shard_map/ppermute | solution.py:280
  411.5 33.1 %collective-permute-start.5 = (f32[2,64,1024]{2,1,0:T(8,128)S(1)}, f32[2,64,1024]{2,1,0:T(8,128)S(1)}, u32[]{:S(2)}, u32[]{:S(2)}) collective-permute-start(f32[2,64,1024]{2,1,0:T(8,128)S(1)} %add.22), channel_id=1, source_target_pairs={{0,12},{2,14},{4,8},{6,10},{8,4},{10,6},{12,0},{14,2},{1,13},{3,15... | collective-permute-start | bytes 1572872 | tf_op jit(solution)/shard_map/ppermute | solution.py:280
  422.7 36.3 %collective-permute-start.7 = (f32[2,64,1024]{2,1,0:T(8,128)S(1)}, f32[2,64,1024]{2,1,0:T(8,128)S(1)}, u32[]{:S(2)}, u32[]{:S(2)}) collective-permute-start(f32[2,64,1024]{2,1,0:T(8,128)S(1)} %add.24), channel_id=1, source_target_pairs={{0,8},{2,10},{4,12},{6,14},{8,0},{10,2},{12,4},{14,6},{1,9},{3,11}... | collective-permute-start | bytes 1572872 | tf_op jit(solution)/shard_map/ppermute | solution.py:280
  434.0 25.0 %collective-permute-start.9 = (f32[2,64,1024]{2,1,0:T(8,128)S(1)}, f32[2,64,1024]{2,1,0:T(8,128)S(1)}, u32[]{:S(2)}, u32[]{:S(2)}) collective-permute-start(f32[2,64,1024]{2,1,0:T(8,128)S(1)} %add.26), channel_id=1, source_target_pairs={{0,4},{2,6},{4,0},{6,2},{8,12},{10,14},{12,8},{14,10},{1,5},{3,7},... | collective-permute-start | bytes 1572872 | tf_op jit(solution)/shard_map/ppermute | solution.py:280

commit v8 on v7

--- a/solution.py
+++ b/solution.py
@@ -10,6 +10,7 @@
 
 HIGH = lax.Precision.HIGH
 MIB = 1 << 20
+PIECES = 2
 ANYWHERE = pl.BlockSpec(memory_space=pl.ANY)
 IN_VMEM = pl.BlockSpec(memory_space=pltpu.VMEM)
 IN_SMEM = pl.BlockSpec(memory_space=pltpu.SMEM)
@@ -223,6 +224,7 @@
     depth = idx_size // 2
     right = right_factor.reshape(2, idx_size, local_batch, inner_part, between)
     params = pltpu.CompilerParams(vmem_limit_bytes=44 * MIB)
+    small = pltpu.CompilerParams(vmem_limit_bytes=20 * MIB)
     shape = (2, local_batch, idx_size, 2, own_rows, inner)
     own_left = left_factor.reshape(shape)
 
@@ -252,7 +254,7 @@
                 pltpu.SemaphoreType.DMA((count, 4)),
             ],
             cost_estimate=BRIEF,
-            compiler_params=params,
+            compiler_params=params if count > 1 else small,
         )(arrived)
 
     def added(start, count, slots, n_out, core, other_core, other_left, before):
@@ -270,7 +272,7 @@
                 pltpu.SemaphoreType.DMA((2, count)),
             ],
             cost_estimate=BRIEF,
-            compiler_params=params,
+            compiler_params=params if count > 1 else small,
         )(
             place, core, other_core, own_left, other_left,
             own_left.reshape(flat), other_left.reshape(flat), *before,
@@ -289,19 +291,23 @@
     odd = list(range(idx_size - 1, 0, -2))
     even = [slot - 1 for slot in odd]
     sums = added(0, many, odd + even, 2, core, swapped(core, "half"), other_left, [])
-    late, sums = lax.optimization_barrier((late, sums))
+    late, _ = lax.optimization_barrier((late, sums[0][0, :8, :128]))
     core = core_of(few, late)
     other_core = swapped(core, "half")
-    leaving = added(many, few, odd, depth, core, other_core, other_left, [sums[0]])
+    leaving = added(many, few, odd, PIECES * depth, core, other_core, other_left, [sums[0]])
     core, leaving = lax.optimization_barrier((core, leaving))
-    staying = added(many, few, even, depth, core, other_core, other_left, [sums[1]])
+    staying = added(many, few, even, PIECES * depth, core, other_core, other_left, [sums[1]])
     landed = [hop(block, 1) for block in leaving]
     blocks = [kept + block for kept, block in zip(staying, landed)]
-    arrived = [hop(block, slot) for block, slot in zip(blocks, even) if slot]
-    result = blocks[-1]
-    for block in arrived:
-        result = result + block
-    return jnp.moveaxis(result, 0, 1)
+    blocks = {even[n // PIECES] // 2: blocks[n : n + PIECES] for n in range(0, PIECES * depth, PIECES)}
+    bit = 1
+    while bit < depth:
+        for d in sorted(blocks, reverse=True):
+            if d & bit:
+                coming = [hop(block, 2 * bit) for block in blocks.pop(d)]
+                blocks[d ^ bit] = [mine + block for mine, block in zip(blocks[d ^ bit], coming)]
+        bit *= 2
+    return jnp.moveaxis(jnp.concatenate(blocks[0], axis=1), 0, 1)
 
 
 def on_device(left_factor, right_factor):
@@ -314,7 +320,7 @@
         and inner_part % 8 == 0
         and between % 256 == 0
         and rows % 256 == 0
-        and rows % (16 * idx_size) == 0
+        and rows % (32 * idx_size) == 0
         and 256 % (rows // idx_size) == 0
     )
     return (overlapped if aligned else general)(left_factor, right_factor)

time: 461 us -> 486 us (1.054)
  starting transfers between devices: 83.2 us -> 114 us
  waiting for transfers between devices: 310 us -> 302 us
    ppermute x7 -> x14, waiting for transfers between devices: 45.6 us -> 15.2 us  [hop(): return lax.ppermute(x, 'idx', [(i, i ^ mask) for i in range(idx_size)])]
    ppermute x7 -> x14, starting transfers between devices: 12.7 us -> 42.9 us  [hop(): return lax.ppermute(x, 'idx', [(i, i ^ mask) for i in range(idx_size)])]
    all_to_all x2, waiting for transfers between devices: 257 us -> 287 us  [sent(): lax.all_to_all(flat, ('idx', 'half'), 0, 0, tiled=True)]
    ppermute x3, waiting for transfers between devices: 7.84 us -> 0.01 us  [swapped(): lax.ppermute(x, axis, [(i, i ^ 1) for i in range(lax.axis_size(axis))])]
    unnamed x10 -> x4, local copies, waits for them, and re-layouts: 7.7 us -> 10.8 us
  transfers between devices with their start and end apart: 12 -> 19, of which waited for: 8 -> 6; matrix products, arithmetic and copies ran while one was open for 0% -> 0% of each run, Pallas kernels for 10% -> 10%
where the time goes in v8:
time: 486 us
  waiting for transfers between devices  302 us (62%)
  starting transfers between devices  114 us (23%)
  Pallas kernels  57.5 us (12%)
  local copies, waits for them, and re-layouts  12 us (2%)
    all_to_all x2, waiting for transfers between devices, sent(): lax.all_to_all(flat, ('idx', 'half'), 0, 0, tiled=True)  287 us
    all_to_all x2, starting transfers between devices, sent(): lax.all_to_all(flat, ('idx', 'half'), 0, 0, tiled=True)  69.2 us
    ppermute x14, starting transfers between devices, hop(): return lax.ppermute(x, 'idx', [(i, i ^ mask) for i in range(idx_size)])  42.9 us
    pallas_call x3, Pallas kernels, added(): pl.pallas_call(functools.partial(amplitude_kernel, start, count, slots, l...  37.6 us
    ppermute x14, waiting for transfers between devices, hop(): return lax.ppermute(x, 'idx', [(i, i ^ mask) for i in range(idx_size)])  15.2 us
    pallas_call x2, Pallas kernels, core_of(): pl.pallas_call(functools.partial(core_kernel, count, scale), out_shape=ja...  11.6 us
    unnamed x4, local copies, waits for them, and re-layouts  10.8 us
  transfers between devices with their start and end apart: 19, of which 6 were waited for; matrix products, arithmetic and copies ran while one was open for 0% of the time, Pallas kernels for 10%

profile of v8, /device:TPU:0, one launch (start us, length us, event | category | flops | bytes accessed | tf_op | source)
XLA Modules:
  0.0 486.0 jit_solution(5197686899998978489)
XLA Ops:
  0.0 5.3 %shard_map.30 = f32[8,2,2,7,32,512]{5,4,3,2,1,0:T(8,128)S(1)} custom-call(f32[2,8,8,32,1024]{4,3,2,1,0:T(8,128)} %bitcast.23), custom_call_target="tpu_custom_call" | custom-call | bytes 1024 | tf_op jit(solution)/shard_map/pallas_call | solution.py:232
  5.4 5.1 %copy-done.1 = f32[8,2,2,7,32,512]{5,4,3,2,1,0:T(8,128)} copy-done((f32[8,2,2,7,32,512]{5,4,3,2,1,0:T(8,128)}, f32[8,2,2,7,32,512]{5,4,3,2,1,0:T(8,128)S(1)}, u32[]{:S(2)}) %copy-start.1) | copy-done | bytes 14680088
  10.4 7.4 %all-to-all-start.1 = ((f32[16,2,7,32,512]{4,3,2,1,0:T(8,128)}), f32[16,2,7,32,512]{4,3,2,1,0:T(8,128)}, u32[]{:S(2)}, u32[]{:S(2)}) async-start(f32[16,2,7,32,512]{4,3,2,1,0:T(8,128)} %bitcast.21), calls=%async_computation.1 | async-start | bytes 29360128 | tf_op jit(solution)/shard_map/all_to_all | solution.py:244
  17.8 0.4 collective-permute-start.1
  18.2 2.9 shard_map.28
  21.1 257.0 %all-to-all-done.1 = f32[16,2,7,32,512]{4,3,2,1,0:T(8,128)} async-done(((f32[16,2,7,32,512]{4,3,2,1,0:T(8,128)}), f32[16,2,7,32,512]{4,3,2,1,0:T(8,128)}, u32[]{:S(2)}, u32[]{:S(2)}) %all-to-all-start.1) | async-done | bytes 14680096 | tf_op jit(solution)/shard_map/all_to_all | solution.py:244
  278.1 61.8 %all-to-all-start = ((f32[16,2,1,32,512]{4,3,1,2,0:T(8,128)}), f32[16,2,1,32,512]{4,3,1,2,0:T(8,128)S(1)}, u32[]{:S(2)}, u32[]{:S(2)}) async-start(f32[16,2,1,32,512]{4,3,1,2,0:T(8,128)} %bitcast.4), calls=%async_computation | async-start | bytes 4194304 | tf_op jit(solution)/shard_map/all_to_all | solution.py:244
  339.9 10.6 %shard_map.31.own_core = f32[7,2,256,256]{3,2,1,0:T(8,128)} custom-call(f32[8,2,2,7,32,512]{5,4,3,2,1,0:T(8,128)} %bitcast.11.arrived), custom_call_target="tpu_custom_call" | custom-call | bytes 1024 | tf_op jit(solution)/shard_map/pallas_call | solution.py:247
  350.5 0.5 collective-permute-start.2
  351.0 30.0 %all-to-all-done = f32[16,2,1,32,512]{4,3,1,2,0:T(8,128)S(1)} async-done(((f32[16,2,1,32,512]{4,3,1,2,0:T(8,128)}), f32[16,2,1,32,512]{4,3,1,2,0:T(8,128)S(1)}, u32[]{:S(2)}, u32[]{:S(2)}) %all-to-all-start) | async-done | bytes 2097184 | tf_op jit(solution)/shard_map/all_to_all | solution.py:244
  381.0 1.0 shard_map.29.own_core
  382.0 0.8 collective-permute-start
  382.8 0.1 pad_add_fusion.place
  382.9 0.0 collective-permute-done.1
  382.9 0.0 collective-permute-done.2.other_core
  382.9 29.8 %shard_map.32 = (f32[2,256,1024]{2,1,0:T(8,128)S(1)}, f32[2,256,1024]{2,1,0:T(8,128)S(1)}) custom-call(s32[2]{0:T(128)S(1)} %pad_add_fusion.place, f32[7,2,256,256]{3,2,1,0:T(8,128)} %shard_map.31.own_core, f32[7,2,256,256]{3,2,1,0:T(8,128)} %collective-permute-done.2.other_core, f32[2,8,8,2,64,256]{5,4,3,2,1,0:T(8,128)} %bitcast.15, ...), custom_call_target="tpu_custom_call" | custom-call | bytes 1024 | tf_op jit(solution)/shard_map/pallas_call | solution.py:263
  412.7 0.0 collective-permute-done.other_core
  412.7 0.0 copy-start
  412.7 5.8 %copy-done = f32[1,2,8,1024,256]{4,3,2,1,0:T(8,128)S(1)} copy-done((f32[1,2,8,1024,256]{4,3,2,1,0:T(8,128)S(1)}, f32[1,2,8,1024,256]{4,3,2,1,0:T(8,128)}, u32[]{:S(2)}) %copy-start) | copy-done | bytes 16777240
  418.5 3.9 shard_map.33
  422.4 3.4 collective-permute-start.7
  425.8 0.1 collective-permute-start.14
  425.9 1.9 collective-permute-start.4
  427.9 0.1 collective-permute-start.6
  427.9 3.9 shard_map.34
  431.9 1.1 collective-permute-done.7
  433.0 5.8 %collective-permute-start.8 = (f32[2,32,1024]{2,1,0:T(8,128)S(1)}, f32[2,32,1024]{2,1,0:T(8,128)S(1)}, u32[]{:S(2)}, u32[]{:S(2)}) collective-permute-start(f32[2,32,1024]{2,1,0:T(8,128)S(1)} %add.46), channel_id=1, source_target_pairs={{0,4},{2,6},{4,0},{6,2},{8,12},{10,14},{12,8},{14,10},{1,5},{3,7},... | collective-permute-start | bytes 786440 | tf_op jit(solution)/shard_map/ppermute | solution.py:282
  438.8 2.1 collective-permute-start.11
  440.8 0.0 collective-permute-done.14
  440.8 0.0 collective-permute-start.13
  440.9 3.3 collective-permute-done.4
  444.2 5.7 %collective-permute-start.15 = (f32[2,32,1024]{2,1,0:T(8,128)S(1)}, f32[2,32,1024]{2,1,0:T(8,128)S(1)}, u32[]{:S(2)}, u32[]{:S(2)}) collective-permute-start(f32[2,32,1024]{2,1,0:T(8,128)S(1)} %add.53), channel_id=1, source_target_pairs={{0,4},{2,6},{4,0},{6,2},{8,12},{10,14},{12,8},{14,10},{1,5},{3,7},... | collective-permute-start | bytes 786440 | tf_op jit(solution)/shard_map/ppermute | solution.py:282
  449.9 0.0 collective-permute-done.6
  450.0 2.1 collective-permute-start.3
  452.1 0.0 collective-permute-done.8
  452.1 5.5 %collective-permute-start.5 = (f32[2,32,1024]{2,1,0:T(8,128)S(1)}, f32[2,32,1024]{2,1,0:T(8,128)S(1)}, u32[]{:S(2)}, u32[]{:S(2)}) collective-permute-start(f32[2,32,1024]{2,1,0:T(8,128)S(1)} %add.43), channel_id=1, source_target_pairs={{0,4},{2,6},{4,0},{6,2},{8,12},{10,14},{12,8},{14,10},{1,5},{3,7},... | collective-permute-start | bytes 786440 | tf_op jit(solution)/shard_map/ppermute | solution.py:282
  457.6 0.0 collective-permute-done.11
  457.6 5.0 %collective-permute-start.9 = (f32[2,32,1024]{2,1,0:T(8,128)S(1)}, f32[2,32,1024]{2,1,0:T(8,128)S(1)}, u32[]{:S(2)}, u32[]{:S(2)}) collective-permute-start(f32[2,32,1024]{2,1,0:T(8,128)S(1)} %add_add_fusion.2), channel_id=1, source_target_pairs={{0,8},{2,10},{4,12},{6,14},{8,0},{10,2},{12,4},{14,6},{1,9},{3,11}... | collective-permute-start | bytes 786440 | tf_op jit(solution)/shard_map/ppermute | solution.py:282
  462.7 0.0 collective-permute-done.13
  462.7 0.4 collective-permute-start.10
  463.1 0.0 collective-permute-done.15
  463.1 5.7 %collective-permute-start.12 = (f32[2,32,1024]{2,1,0:T(8,128)S(1)}, f32[2,32,1024]{2,1,0:T(8,128)S(1)}, u32[]{:S(2)}, u32[]{:S(2)}) collective-permute-start(f32[2,32,1024]{2,1,0:T(8,128)S(1)} %add.50), channel_id=1, source_target_pairs={{0,4},{2,6},{4,0},{6,2},{8,12},{10,14},{12,8},{14,10},{1,5},{3,7},... | collective-permute-start | bytes 786440 | tf_op jit(solution)/shard_map/ppermute | solution.py:282
  468.9 5.0 %collective-permute-start.16 = (f32[2,32,1024]{2,1,0:T(8,128)S(1)}, f32[2,32,1024]{2,1,0:T(8,128)S(1)}, u32[]{:S(2)}, u32[]{:S(2)}) collective-permute-start(f32[2,32,1024]{2,1,0:T(8,128)S(1)} %add_add_fusion), channel_id=1, source_target_pairs={{0,8},{2,10},{4,12},{6,14},{8,0},{10,2},{12,4},{14,6},{1,9},{3,11}... | collective-permute-start | bytes 786440 | tf_op jit(solution)/shard_map/ppermute | solution.py:282
  473.9 0.1 add_add_fusion.3
  474.0 4.6 collective-permute-done.12
  478.6 6.1 %collective-permute-done.16 = f32[2,32,1024]{2,1,0:T(8,128)S(1)} collective-permute-done((f32[2,32,1024]{2,1,0:T(8,128)S(1)}, f32[2,32,1024]{2,1,0:T(8,128)S(1)}, u32[]{:S(2)}, u32[]{:S(2)}) %collective-permute-start.16) | collective-permute-done | bytes 262176 | tf_op jit(solution)/shard_map/ppermute | solution.py:282
  484.7 0.1 add_add_fusion.1
  484.8 1.2 copy.5
  (12 shorter events, 0.3 us)
Async XLA Ops:
  5.4 5.1 %copy-start.1 = (f32[8,2,2,7,32,512]{5,4,3,2,1,0:T(8,128)}, f32[8,2,2,7,32,512]{5,4,3,2,1,0:T(8,128)S(1)}, u32[]{:S(2)}) copy-start(f32[8,2,2,7,32,512]{5,4,3,2,1,0:T(8,128)S(1)} %shard_map.30) | copy-start | bytes 44040196
  10.4 267.7 %all-to-all-start.1 = ((f32[16,2,7,32,512]{4,3,2,1,0:T(8,128)}), f32[16,2,7,32,512]{4,3,2,1,0:T(8,128)}, u32[]{:S(2)}, u32[]{:S(2)}) async-start(f32[16,2,7,32,512]{4,3,2,1,0:T(8,128)} %bitcast.21), calls=%async_computation.1 | async-start | bytes 29360128 | tf_op jit(solution)/shard_map/all_to_all | solution.py:244
  17.8 365.1 %collective-permute-start.1 = (f32[1,2,8,1024,256]{4,3,2,1,0:T(8,128)}, f32[1,2,8,1024,256]{4,3,2,1,0:T(8,128)}, u32[]{:S(2)}, u32[]{:S(2)}) collective-permute-start(f32[1,2,8,1024,256]{4,3,2,1,0:T(8,128)} %param.2), channel_id=1, source_target_pairs={{0,1},{1,0},{2,3},{3,2},{4,5},{5,4},{6,7},{7,6},{8,9},{9,8},{10,11... | collective-permute-start | bytes 50331656 | tf_op jit(solution)/shard_map/ppermute | solution.py:20
  278.1 102.9 %all-to-all-start = ((f32[16,2,1,32,512]{4,3,1,2,0:T(8,128)}), f32[16,2,1,32,512]{4,3,1,2,0:T(8,128)S(1)}, u32[]{:S(2)}, u32[]{:S(2)}) async-start(f32[16,2,1,32,512]{4,3,1,2,0:T(8,128)} %bitcast.4), calls=%async_computation | async-start | bytes 4194304 | tf_op jit(solution)/shard_map/all_to_all | solution.py:244
  350.5 32.4 %collective-permute-start.2 = (f32[7,2,256,256]{3,2,1,0:T(8,128)}, f32[7,2,256,256]{3,2,1,0:T(8,128)}, u32[]{:S(2)}, u32[]{:S(2)}) collective-permute-start(f32[7,2,256,256]{3,2,1,0:T(8,128)} %shard_map.31.own_core), channel_id=1, source_target_pairs={{0,1},{1,0},{2,3},{3,2},{4,5},{5,4},{6,7},{7,6},{8,9},{9,8},{10,11... | collective-permute-start | bytes 11010056 | tf_op jit(solution)/shard_map/ppermute | solution.py:20
  382.0 30.7 %collective-permute-start = (f32[1,2,256,256]{3,2,1,0:T(8,128)S(1)}, f32[1,2,256,256]{3,2,1,0:T(8,128)S(1)}, u32[]{:S(2)}, u32[]{:S(2)}) collective-permute-start(f32[1,2,256,256]{3,2,1,0:T(8,128)S(1)} %shard_map.29.own_core), channel_id=1, source_target_pairs={{0,1},{1,0},{2,3},{3,2},{4,5},{5,4},{6,7},{7,6},{8,9},{9,8},{10,11... | collective-permute-start | bytes 1572872 | tf_op jit(solution)/shard_map/ppermute | solution.py:20
  412.7 5.8 %copy-start = (f32[1,2,8,1024,256]{4,3,2,1,0:T(8,128)S(1)}, f32[1,2,8,1024,256]{4,3,2,1,0:T(8,128)}, u32[]{:S(2)}) copy-start(f32[1,2,8,1024,256]{4,3,2,1,0:T(8,128)} %param.2) | copy-start | bytes 50331652
  422.4 10.6 %collective-permute-start.7 = (f32[2,32,1024]{2,1,0:T(8,128)S(1)}, f32[2,32,1024]{2,1,0:T(8,128)S(1)}, u32[]{:S(2)}, u32[]{:S(2)}) collective-permute-start(f32[2,32,1024]{2,1,0:T(8,128)S(1)} %get-tuple-element.52), channel_id=1, source_target_pairs={{0,2},{2,0},{4,6},{6,4},{8,10},{10,8},{12,14},{14,12},{1,3},{3,1},... | collective-permute-start | bytes 786440 | tf_op jit(solution)/shard_map/ppermute | solution.py:282
  425.8 15.0 %collective-permute-start.14 = (f32[2,32,1024]{2,1,0:T(8,128)S(1)}, f32[2,32,1024]{2,1,0:T(8,128)S(1)}, u32[]{:S(2)}, u32[]{:S(2)}) collective-permute-start(f32[2,32,1024]{2,1,0:T(8,128)S(1)} %get-tuple-element.60), channel_id=1, source_target_pairs={{0,2},{2,0},{4,6},{6,4},{8,10},{10,8},{12,14},{14,12},{1,3},{3,1},... | collective-permute-start | bytes 786440 | tf_op jit(solution)/shard_map/ppermute | solution.py:282
  425.9 18.3 %collective-permute-start.4 = (f32[2,32,1024]{2,1,0:T(8,128)S(1)}, f32[2,32,1024]{2,1,0:T(8,128)S(1)}, u32[]{:S(2)}, u32[]{:S(2)}) collective-permute-start(f32[2,32,1024]{2,1,0:T(8,128)S(1)} %get-tuple-element.48), channel_id=1, source_target_pairs={{0,2},{2,0},{4,6},{6,4},{8,10},{10,8},{12,14},{14,12},{1,3},{3,1},... | collective-permute-start | bytes 786440 | tf_op jit(solution)/shard_map/ppermute | solution.py:282
  427.9 22.1 %collective-permute-start.6 = (f32[2,32,1024]{2,1,0:T(8,128)S(1)}, f32[2,32,1024]{2,1,0:T(8,128)S(1)}, u32[]{:S(2)}, u32[]{:S(2)}) collective-permute-start(f32[2,32,1024]{2,1,0:T(8,128)S(1)} %get-tuple-element.50), channel_id=1, source_target_pairs={{0,2},{2,0},{4,6},{6,4},{8,10},{10,8},{12,14},{14,12},{1,3},{3,1},... | collective-permute-start | bytes 786440 | tf_op jit(solution)/shard_map/ppermute | solution.py:282
  433.0 19.1 %collective-permute-start.8 = (f32[2,32,1024]{2,1,0:T(8,128)S(1)}, f32[2,32,1024]{2,1,0:T(8,128)S(1)}, u32[]{:S(2)}, u32[]{:S(2)}) collective-permute-start(f32[2,32,1024]{2,1,0:T(8,128)S(1)} %add.46), channel_id=1, source_target_pairs={{0,4},{2,6},{4,0},{6,2},{8,12},{10,14},{12,8},{14,10},{1,5},{3,7},... | collective-permute-start | bytes 786440 | tf_op jit(solution)/shard_map/ppermute | solution.py:282
  438.8 18.9 %collective-permute-start.11 = (f32[2,32,1024]{2,1,0:T(8,128)S(1)}, f32[2,32,1024]{2,1,0:T(8,128)S(1)}, u32[]{:S(2)}, u32[]{:S(2)}) collective-permute-start(f32[2,32,1024]{2,1,0:T(8,128)S(1)} %get-tuple-element.56), channel_id=1, source_target_pairs={{0,2},{2,0},{4,6},{6,4},{8,10},{10,8},{12,14},{14,12},{1,3},{3,1},... | collective-permute-start | bytes 786440 | tf_op jit(solution)/shard_map/ppermute | solution.py:282
  440.8 21.9 %collective-permute-start.13 = (f32[2,32,1024]{2,1,0:T(8,128)S(1)}, f32[2,32,1024]{2,1,0:T(8,128)S(1)}, u32[]{:S(2)}, u32[]{:S(2)}) collective-permute-start(f32[2,32,1024]{2,1,0:T(8,128)S(1)} %get-tuple-element.58), channel_id=1, source_target_pairs={{0,2},{2,0},{4,6},{6,4},{8,10},{10,8},{12,14},{14,12},{1,3},{3,1},... | collective-permute-start | bytes 786440 | tf_op jit(solution)/shard_map/ppermute | solution.py:282
  444.2 18.9 %collective-permute-start.15 = (f32[2,32,1024]{2,1,0:T(8,128)S(1)}, f32[2,32,1024]{2,1,0:T(8,128)S(1)}, u32[]{:S(2)}, u32[]{:S(2)}) collective-permute-start(f32[2,32,1024]{2,1,0:T(8,128)S(1)} %add.53), channel_id=1, source_target_pairs={{0,4},{2,6},{4,0},{6,2},{8,12},{10,14},{12,8},{14,10},{1,5},{3,7},... | collective-permute-start | bytes 786440 | tf_op jit(solution)/shard_map/ppermute | solution.py:282
  450.0 18.9 %collective-permute-start.3 = (f32[2,32,1024]{2,1,0:T(8,128)S(1)}, f32[2,32,1024]{2,1,0:T(8,128)S(1)}, u32[]{:S(2)}, u32[]{:S(2)}) collective-permute-start(f32[2,32,1024]{2,1,0:T(8,128)S(1)} %get-tuple-element.46), channel_id=1, source_target_pairs={{0,2},{2,0},{4,6},{6,4},{8,10},{10,8},{12,14},{14,12},{1,3},{3,1},... | collective-permute-start | bytes 786440 | tf_op jit(solution)/shard_map/ppermute | solution.py:282
  452.1 21.9 %collective-permute-start.5 = (f32[2,32,1024]{2,1,0:T(8,128)S(1)}, f32[2,32,1024]{2,1,0:T(8,128)S(1)}, u32[]{:S(2)}, u32[]{:S(2)}) collective-permute-start(f32[2,32,1024]{2,1,0:T(8,128)S(1)} %add.43), channel_id=1, source_target_pairs={{0,4},{2,6},{4,0},{6,2},{8,12},{10,14},{12,8},{14,10},{1,5},{3,7},... | collective-permute-start | bytes 786440 | tf_op jit(solution)/shard_map/ppermute | solution.py:282
  457.6 16.3 %collective-permute-start.9 = (f32[2,32,1024]{2,1,0:T(8,128)S(1)}, f32[2,32,1024]{2,1,0:T(8,128)S(1)}, u32[]{:S(2)}, u32[]{:S(2)}) collective-permute-start(f32[2,32,1024]{2,1,0:T(8,128)S(1)} %add_add_fusion.2), channel_id=1, source_target_pairs={{0,8},{2,10},{4,12},{6,14},{8,0},{10,2},{12,4},{14,6},{1,9},{3,11}... | collective-permute-start | bytes 786440 | tf_op jit(solution)/shard_map/ppermute | solution.py:282
  462.7 11.3 %collective-permute-start.10 = (f32[2,32,1024]{2,1,0:T(8,128)S(1)}, f32[2,32,1024]{2,1,0:T(8,128)S(1)}, u32[]{:S(2)}, u32[]{:S(2)}) collective-permute-start(f32[2,32,1024]{2,1,0:T(8,128)S(1)} %get-tuple-element.54), channel_id=1, source_target_pairs={{0,2},{2,0},{4,6},{6,4},{8,10},{10,8},{12,14},{14,12},{1,3},{3,1},... | collective-permute-start | bytes 786440 | tf_op jit(solution)/shard_map/ppermute | solution.py:282
  463.1 15.5 %collective-permute-start.12 = (f32[2,32,1024]{2,1,0:T(8,128)S(1)}, f32[2,32,1024]{2,1,0:T(8,128)S(1)}, u32[]{:S(2)}, u32[]{:S(2)}) collective-permute-start(f32[2,32,1024]{2,1,0:T(8,128)S(1)} %add.50), channel_id=1, source_target_pairs={{0,4},{2,6},{4,0},{6,2},{8,12},{10,14},{12,8},{14,10},{1,5},{3,7},... | collective-permute-start | bytes 786440 | tf_op jit(solution)/shard_map/ppermute | solution.py:282
  468.9 15.9 %collective-permute-start.16 = (f32[2,32,1024]{2,1,0:T(8,128)S(1)}, f32[2,32,1024]{2,1,0:T(8,128)S(1)}, u32[]{:S(2)}, u32[]{:S(2)}) collective-permute-start(f32[2,32,1024]{2,1,0:T(8,128)S(1)} %add_add_fusion), channel_id=1, source_target_pairs={{0,8},{2,10},{4,12},{6,14},{8,0},{10,2},{12,4},{14,6},{1,9},{3,11}... | collective-permute-start | bytes 786440 | tf_op jit(solution)/shard_map/ppermute | solution.py:282

commit v9 on v8

--- a/solution.py
+++ b/solution.py
@@ -11,6 +11,7 @@
 HIGH = lax.Precision.HIGH
 MIB = 1 << 20
 PIECES = 2
+WINDOW = 4
 ANYWHERE = pl.BlockSpec(memory_space=pl.ANY)
 IN_VMEM = pl.BlockSpec(memory_space=pltpu.VMEM)
 IN_SMEM = pl.BlockSpec(memory_space=pltpu.SMEM)
@@ -122,7 +123,8 @@
         copy.wait()
 
 
-def core_kernel(count, scale, arrived, core, factors, sems):
+def core_kernel(count, scale, arrived, *refs):
+    core, factors, sems = refs[-3:]
     inner = core.shape[2]
     copies = {}
     for b in range(count):
@@ -143,7 +145,7 @@
     own_split, other_split, own_flat, other_flat = refs[:4]
     before = refs[4 : 4 + n_before]
     outs = refs[4 + n_before : 4 + n_before + n_out]
-    first, second, product, sems = refs[4 + n_before + n_out :]
+    first, second, product, sems, *more = refs[4 + n_before + n_out :]
     half, idx = place[0], place[1]
     _, _, groups, own_rows, inner = first.shape
     rows, columns = groups * own_rows, second.shape[2]
@@ -167,7 +169,11 @@
                     first_copy(lower, b, position, slot).start()
                 second_copy(lower, b).start()
 
-    if not n_before:
+    if n_before:
+        held, held_sem = more
+        loading = pltpu.make_async_copy(before[0], held, held_sem)
+        loading.start()
+    else:
         for out in outs:
             out[...] = jnp.zeros_like(out)
     piece = rows // n_out
@@ -185,6 +191,8 @@
         for part, value in enumerate((real, imag, real + imag)):
             product[part] = left_stack(value, 1)
         second_copy(True, b).wait()
+        if n_before:
+            loading.wait()
         for at in range(0, columns, 256):
             spot = slice(at, at + 256)
             right_real, right_imag = second[b, 0, spot], second[b, 1, spot]
@@ -193,7 +201,7 @@
             three = dot_stacks(product[2], right_stack(right_real + right_imag, 1), NT)
             for plane, value in enumerate((one - two, three - one - two)):
                 if n_before:
-                    value = value + before[0][plane, :, spot]
+                    value = value + held[plane, :, spot]
                 for number, out in enumerate(outs):
                     part = value[number * piece : (number + 1) * piece]
                     if n_before:
@@ -224,7 +232,6 @@
     depth = idx_size // 2
     right = right_factor.reshape(2, idx_size, local_batch, inner_part, between)
     params = pltpu.CompilerParams(vmem_limit_bytes=44 * MIB)
-    small = pltpu.CompilerParams(vmem_limit_bytes=20 * MIB)
     shape = (2, local_batch, idx_size, 2, own_rows, inner)
     own_left = left_factor.reshape(shape)
 
@@ -243,19 +250,19 @@
         flat = pieces.reshape(2 * idx_size, *pieces.shape[2:])
         return lax.all_to_all(flat, ("idx", "half"), 0, 0, tiled=True).reshape(pieces.shape)
 
-    def core_of(count, arrived):
+    def core_of(count, arrived, after=()):
         return pl.pallas_call(
             functools.partial(core_kernel, count, scale),
             out_shape=jax.ShapeDtypeStruct((count, 2, inner, inner), jnp.float32),
-            in_specs=[ANYWHERE],
+            in_specs=[ANYWHERE] + [IN_VMEM] * len(after),
             out_specs=IN_VMEM,
             scratch_shapes=[
                 pltpu.VMEM((count, 4, idx_size, inner_part, half_cols), jnp.float32),
                 pltpu.SemaphoreType.DMA((count, 4)),
             ],
             cost_estimate=BRIEF,
-            compiler_params=params if count > 1 else small,
-        )(arrived)
+            compiler_params=params,
+        )(arrived, *after)
 
     def added(start, count, slots, n_out, core, other_core, other_left, before):
         flat = (2, local_batch, rows, inner)
@@ -263,16 +270,18 @@
         return pl.pallas_call(
             functools.partial(amplitude_kernel, start, count, slots, len(before), n_out),
             out_shape=[jax.ShapeDtypeStruct((2, kept_rows // n_out, rows), jnp.float32)] * n_out,
-            in_specs=[IN_SMEM, IN_VMEM, IN_VMEM] + [ANYWHERE] * 4 + [IN_VMEM] * len(before),
+            in_specs=[IN_SMEM, IN_VMEM, IN_VMEM] + [ANYWHERE] * (4 + len(before)),
             out_specs=[IN_VMEM] * n_out,
             scratch_shapes=[
                 pltpu.VMEM((count, 2, len(slots), own_rows, inner), jnp.float32),
                 pltpu.VMEM((count, 2, rows, inner), jnp.float32),
                 pltpu.VMEM((3, kept_rows, 3 * inner), jnp.bfloat16),
                 pltpu.SemaphoreType.DMA((2, count)),
-            ],
+            ]
+            + [pltpu.VMEM(part.shape, jnp.float32) for part in before]
+            + [pltpu.SemaphoreType.DMA] * len(before),
             cost_estimate=BRIEF,
-            compiler_params=params if count > 1 else small,
+            compiler_params=params,
         )(
             place, core, other_core, own_left, other_left,
             own_left.reshape(flat), other_left.reshape(flat), *before,
@@ -291,21 +300,29 @@
     odd = list(range(idx_size - 1, 0, -2))
     even = [slot - 1 for slot in odd]
     sums = added(0, many, odd + even, 2, core, swapped(core, "half"), other_left, [])
-    late, _ = lax.optimization_barrier((late, sums[0][0, :8, :128]))
-    core = core_of(few, late)
+    core = core_of(few, late, (sums[0][0, :8, :128],))
     other_core = swapped(core, "half")
     leaving = added(many, few, odd, PIECES * depth, core, other_core, other_left, [sums[0]])
     core, leaving = lax.optimization_barrier((core, leaving))
-    staying = added(many, few, even, PIECES * depth, core, other_core, other_left, [sums[1]])
-    landed = [hop(block, 1) for block in leaving]
-    blocks = [kept + block for kept, block in zip(staying, landed)]
-    blocks = {even[n // PIECES] // 2: blocks[n : n + PIECES] for n in range(0, PIECES * depth, PIECES)}
-    bit = 1
+    staying = list(added(many, few, even, PIECES * depth, core, other_core, other_left, [sums[1]]))
+    mine, coming = [], {}
+    for n, block in enumerate(leaving):
+        if n >= WINDOW:
+            block, mine[n - WINDOW] = lax.optimization_barrier((block, mine[n - WINDOW]))
+        if n - WINDOW - 2 in coming:
+            block, coming[n - WINDOW - 2] = lax.optimization_barrier((block, coming[n - WINDOW - 2]))
+        mine.append(staying[n] + hop(block, 1))
+        if even[n // PIECES] // 2 % 2:
+            coming[n] = hop(mine[n], 2)
+    for n, block in coming.items():
+        target = n + PIECES
+        mine[target] = mine[target] + block
+    blocks = {even[n // PIECES] // 2: mine[n : n + PIECES] for n in range(0, PIECES * depth, PIECES)}
+    bit = 2
     while bit < depth:
-        for d in sorted(blocks, reverse=True):
-            if d & bit:
-                coming = [hop(block, 2 * bit) for block in blocks.pop(d)]
-                blocks[d ^ bit] = [mine + block for mine, block in zip(blocks[d ^ bit], coming)]
+        for d in range(bit, depth, 2 * bit):
+            arriving = [hop(block, 2 * bit) for block in blocks[d]]
+            blocks[d - bit] = [block + new for block, new in zip(blocks[d - bit], arriving)]
         bit *= 2
     return jnp.moveaxis(jnp.concatenate(blocks[0], axis=1), 0, 1)
 

time: 486 us -> 451 us (0.928)
  starting transfers between devices: 114 us -> 93.9 us
  waiting for transfers between devices: 302 us -> 290 us
    all_to_all x2, waiting for transfers between devices: 287 us -> 257 us  [sent(): lax.all_to_all(flat, ('idx', 'half'), 0, 0, tiled=True)]
    ppermute x14, starting transfers between devices: 42.9 us -> 23.4 us  [hop(): return lax.ppermute(x, 'idx', [(i, i ^ mask) for i in range(idx_size)])]
    ppermute x14, waiting for transfers between devices: 15.2 us -> 24.7 us  [hop(): return lax.ppermute(x, 'idx', [(i, i ^ mask) for i in range(idx_size)])]
    ppermute x3, waiting for transfers between devices: 0.01 us -> 7.84 us  [swapped(): lax.ppermute(x, axis, [(i, i ^ 1) for i in range(lax.axis_size(axis))])]
    unnamed x4 -> x10, local copies, waits for them, and re-layouts: 10.8 us -> 7.71 us
  transfers between devices with their start and end apart: 19 -> 19, of which waited for: 6 -> 11; matrix products, arithmetic and copies ran while one was open for 0% -> 0% of each run, Pallas kernels for 10% -> 10%
where the time goes in v9:
time: 451 us; the launch traced here: 450 us
  waiting for transfers between devices  290 us (64%)
  starting transfers between devices  93.9 us (21%)
  Pallas kernels  57.4 us (13%)
  local copies, waits for them, and re-layouts  8.91 us (2%)
    all_to_all x2, waiting for transfers between devices, sent(): lax.all_to_all(flat, ('idx', 'half'), 0, 0, tiled=True)  257 us
    all_to_all x2, starting transfers between devices, sent(): lax.all_to_all(flat, ('idx', 'half'), 0, 0, tiled=True)  69.2 us
    pallas_call x3, Pallas kernels, added(): pl.pallas_call(functools.partial(amplitude_kernel, start, count, slots, l...  37.5 us
    ppermute x14, waiting for transfers between devices, hop(): return lax.ppermute(x, 'idx', [(i, i ^ mask) for i in range(idx_size)])  24.7 us
    ppermute x14, starting transfers between devices, hop(): return lax.ppermute(x, 'idx', [(i, i ^ mask) for i in range(idx_size)])  23.4 us
    pallas_call x2, Pallas kernels, core_of(): pl.pallas_call(functools.partial(core_kernel, count, scale), out_shape=ja...  11.6 us
  transfers between devices with their start and end apart: 19, of which 11 were waited for; matrix products, arithmetic and copies ran while one was open for 0% of the time, Pallas kernels for 10%

profile of v9, /device:TPU:0, one launch (start us, length us, event | category | flops | bytes accessed | tf_op | source)
XLA Modules:
  0.0 450.4 jit_solution(10040332367697013070)
XLA Ops:
  0.0 5.3 %shard_map.29 = f32[8,2,2,7,32,512]{5,4,3,2,1,0:T(8,128)S(1)} custom-call(f32[2,8,8,32,1024]{4,3,2,1,0:T(8,128)} %bitcast.25), custom_call_target="tpu_custom_call" | custom-call | bytes 1024 | tf_op jit(solution)/shard_map/pallas_call | solution.py:239
  5.4 5.1 %copy-done = f32[8,2,2,7,32,512]{5,4,3,2,1,0:T(8,128)} copy-done((f32[8,2,2,7,32,512]{5,4,3,2,1,0:T(8,128)}, f32[8,2,2,7,32,512]{5,4,3,2,1,0:T(8,128)S(1)}, u32[]{:S(2)}) %copy-start) | copy-done | bytes 14680088
  10.4 7.4 %all-to-all-start.1 = ((f32[16,2,7,32,512]{4,3,2,1,0:T(8,128)}), f32[16,2,7,32,512]{4,3,2,1,0:T(8,128)}, u32[]{:S(2)}, u32[]{:S(2)}) async-start(f32[16,2,7,32,512]{4,3,2,1,0:T(8,128)} %bitcast.17), calls=%async_computation.1 | async-start | bytes 29360128 | tf_op jit(solution)/shard_map/all_to_all | solution.py:251
  17.8 0.4 collective-permute-start.1
  18.2 2.9 shard_map.28
  21.1 257.0 %all-to-all-done.1 = f32[16,2,7,32,512]{4,3,2,1,0:T(8,128)} async-done(((f32[16,2,7,32,512]{4,3,2,1,0:T(8,128)}), f32[16,2,7,32,512]{4,3,2,1,0:T(8,128)}, u32[]{:S(2)}, u32[]{:S(2)}) %all-to-all-start.1) | async-done | bytes 14680096 | tf_op jit(solution)/shard_map/all_to_all | solution.py:251
  278.1 61.8 %all-to-all-start = ((f32[16,2,1,32,512]{4,3,1,2,0:T(8,128)}), f32[16,2,1,32,512]{4,3,1,2,0:T(8,128)S(1)}, u32[]{:S(2)}, u32[]{:S(2)}) async-start(f32[16,2,1,32,512]{4,3,1,2,0:T(8,128)} %bitcast.4), calls=%async_computation | async-start | bytes 4194304 | tf_op jit(solution)/shard_map/all_to_all | solution.py:251
  339.9 10.6 %shard_map.30.own_core = f32[7,2,256,256]{3,2,1,0:T(8,128)} custom-call(f32[8,2,2,7,32,512]{5,4,3,2,1,0:T(8,128)} %bitcast.7.arrived), custom_call_target="tpu_custom_call" | custom-call | bytes 1024 | tf_op jit(solution)/shard_map/pallas_call | solution.py:254
  350.5 0.5 collective-permute-start
  351.0 0.1 pad_add_fusion.place
  351.1 0.0 collective-permute-done.1
  351.1 6.3 %collective-permute-done.other_core = f32[7,2,256,256]{3,2,1,0:T(8,128)} collective-permute-done((f32[7,2,256,256]{3,2,1,0:T(8,128)}, f32[7,2,256,256]{3,2,1,0:T(8,128)}, u32[]{:S(2)}, u32[]{:S(2)}) %collective-permute-start) | collective-permute-done | bytes 3670048 | tf_op jit(solution)/shard_map/ppermute | solution.py:21
  357.4 29.7 %shard_map.31 = (f32[2,256,1024]{2,1,0:T(8,128)S(1)}, f32[2,256,1024]{2,1,0:T(8,128)S(1)}) custom-call(s32[2]{0:T(128)S(1)} %pad_add_fusion.place, f32[7,2,256,256]{3,2,1,0:T(8,128)} %shard_map.30.own_core, f32[7,2,256,256]{3,2,1,0:T(8,128)} %collective-permute-done.other_core, f32[2,8,8,2,64,256]{5,4,3,2,1,0:T(8,128)} %bitcast.19, ...), custom_call_target="tpu_custom_call" | custom-call | bytes 1024 | tf_op jit(solution)/shard_map/pallas_call | solution.py:270
  387.1 1.3 copy-done.3
  388.5 1.3 copy-done.1
  389.8 0.0 all-to-all-done
  389.8 1.0 shard_map.32.own_core
  390.8 0.4 collective-permute-start.2
  391.3 1.5 collective-permute-done.2.other_core
  392.8 3.9 shard_map.33
  396.7 1.9 collective-permute-start.4
  398.6 0.2 collective-permute-start.11
  398.8 3.9 shard_map.34
  402.7 3.2 collective-permute-done.4
  405.9 1.9 collective-permute-start.7
  407.9 0.2 collective-permute-start.3
  408.0 1.9 collective-permute-start.5
  409.9 1.5 collective-permute-start.10
  411.4 0.1 collective-permute-done.11
  411.6 1.9 collective-permute-start.14
  413.5 3.6 collective-permute-done.7
  417.1 1.9 collective-permute-start.12
  419.1 3.7 collective-permute-done.3
  422.8 1.9 collective-permute-start.8
  424.7 0.0 collective-permute-done.5
  424.7 2.4 collective-permute-start.9
  427.2 1.2 collective-permute-done.10
  428.4 1.9 collective-permute-start.6
  430.3 3.7 collective-permute-done.14
  434.0 2.0 collective-permute-start.15
  436.0 0.0 collective-permute-done.12
  436.0 2.4 collective-permute-start.16
  438.5 1.5 collective-permute-start.13
  439.9 0.1 add_add_fusion.1
  440.0 7.0 %collective-permute-done.15 = f32[2,32,1024]{2,1,0:T(8,128)S(1)} collective-permute-done((f32[2,32,1024]{2,1,0:T(8,128)S(1)}, f32[2,32,1024]{2,1,0:T(8,128)S(1)}, u32[]{:S(2)}, u32[]{:S(2)}) %collective-permute-start.15) | collective-permute-done | bytes 262176 | tf_op jit(solution)/shard_map/ppermute | solution.py:291
  447.0 2.1 collective-permute-done.16
  449.1 0.1 add_add_fusion
  449.2 1.2 copy.5
  (21 shorter events, 0.3 us)
Async XLA Ops:
  5.4 5.1 %copy-start = (f32[8,2,2,7,32,512]{5,4,3,2,1,0:T(8,128)}, f32[8,2,2,7,32,512]{5,4,3,2,1,0:T(8,128)S(1)}, u32[]{:S(2)}) copy-start(f32[8,2,2,7,32,512]{5,4,3,2,1,0:T(8,128)S(1)} %shard_map.29) | copy-start | bytes 44040196
  10.4 267.7 %all-to-all-start.1 = ((f32[16,2,7,32,512]{4,3,2,1,0:T(8,128)}), f32[16,2,7,32,512]{4,3,2,1,0:T(8,128)}, u32[]{:S(2)}, u32[]{:S(2)}) async-start(f32[16,2,7,32,512]{4,3,2,1,0:T(8,128)} %bitcast.17), calls=%async_computation.1 | async-start | bytes 29360128 | tf_op jit(solution)/shard_map/all_to_all | solution.py:251
  17.8 333.2 %collective-permute-start.1 = (f32[1,2,8,1024,256]{4,3,2,1,0:T(8,128)}, f32[1,2,8,1024,256]{4,3,2,1,0:T(8,128)}, u32[]{:S(2)}, u32[]{:S(2)}) collective-permute-start(f32[1,2,8,1024,256]{4,3,2,1,0:T(8,128)} %param.2), channel_id=1, source_target_pairs={{0,1},{1,0},{2,3},{3,2},{4,5},{5,4},{6,7},{7,6},{8,9},{9,8},{10,11... | collective-permute-start | bytes 50331656 | tf_op jit(solution)/shard_map/ppermute | solution.py:21
  278.1 111.7 %all-to-all-start = ((f32[16,2,1,32,512]{4,3,1,2,0:T(8,128)}), f32[16,2,1,32,512]{4,3,1,2,0:T(8,128)S(1)}, u32[]{:S(2)}, u32[]{:S(2)}) async-start(f32[16,2,1,32,512]{4,3,1,2,0:T(8,128)} %bitcast.4), calls=%async_computation | async-start | bytes 4194304 | tf_op jit(solution)/shard_map/all_to_all | solution.py:251
  350.5 6.9 %collective-permute-start = (f32[7,2,256,256]{3,2,1,0:T(8,128)}, f32[7,2,256,256]{3,2,1,0:T(8,128)}, u32[]{:S(2)}, u32[]{:S(2)}) collective-permute-start(f32[7,2,256,256]{3,2,1,0:T(8,128)} %shard_map.30.own_core), channel_id=1, source_target_pairs={{0,1},{1,0},{2,3},{3,2},{4,5},{5,4},{6,7},{7,6},{8,9},{9,8},{10,11... | collective-permute-start | bytes 11010056 | tf_op jit(solution)/shard_map/ppermute | solution.py:21
  387.1 1.3 copy-start.3
  388.5 1.3 copy-start.1
  389.8 3.0 copy-start.2
  390.8 8.0 %copy-start.4 = (f32[2,256,1024]{2,1,0:T(8,128)S(1)}, f32[2,256,1024]{2,1,0:T(8,128)}, u32[]{:S(2)}) copy-start(f32[2,256,1024]{2,1,0:T(8,128)} %copy-done.3) | copy-start | bytes 6291460
  390.8 2.0 collective-permute-start.2
  396.7 9.2 %collective-permute-start.4 = (f32[2,32,1024]{2,1,0:T(8,128)S(1)}, f32[2,32,1024]{2,1,0:T(8,128)S(1)}, u32[]{:S(2)}, u32[]{:S(2)}) collective-permute-start(f32[2,32,1024]{2,1,0:T(8,128)S(1)} %get-tuple-element.61), channel_id=1, source_target_pairs={{0,2},{2,0},{4,6},{6,4},{8,10},{10,8},{12,14},{14,12},{1,3},{3,1},... | collective-permute-start | bytes 786440 | tf_op jit(solution)/shard_map/ppermute | solution.py:291
  398.6 12.9 %collective-permute-start.11 = (f32[2,32,1024]{2,1,0:T(8,128)S(1)}, f32[2,32,1024]{2,1,0:T(8,128)S(1)}, u32[]{:S(2)}, u32[]{:S(2)}) collective-permute-start(f32[2,32,1024]{2,1,0:T(8,128)S(1)} %get-tuple-element.74), channel_id=1, source_target_pairs={{0,2},{2,0},{4,6},{6,4},{8,10},{10,8},{12,14},{14,12},{1,3},{3,1},... | collective-permute-start | bytes 786440 | tf_op jit(solution)/shard_map/ppermute | solution.py:291
  405.9 11.2 %collective-permute-start.7 = (f32[2,32,1024]{2,1,0:T(8,128)S(1)}, f32[2,32,1024]{2,1,0:T(8,128)S(1)}, u32[]{:S(2)}, u32[]{:S(2)}) collective-permute-start(f32[2,32,1024]{2,1,0:T(8,128)S(1)} %get-tuple-element.65), channel_id=1, source_target_pairs={{0,2},{2,0},{4,6},{6,4},{8,10},{10,8},{12,14},{14,12},{1,3},{3,1},... | collective-permute-start | bytes 786440 | tf_op jit(solution)/shard_map/ppermute | solution.py:291
  407.9 14.9 %collective-permute-start.3 = (f32[2,32,1024]{2,1,0:T(8,128)S(1)}, f32[2,32,1024]{2,1,0:T(8,128)S(1)}, u32[]{:S(2)}, u32[]{:S(2)}) collective-permute-start(f32[2,32,1024]{2,1,0:T(8,128)S(1)} %get-tuple-element.58), channel_id=1, source_target_pairs={{0,2},{2,0},{4,6},{6,4},{8,10},{10,8},{12,14},{14,12},{1,3},{3,1},... | collective-permute-start | bytes 786440 | tf_op jit(solution)/shard_map/ppermute | solution.py:291
  408.0 16.7 %collective-permute-start.5 = (f32[2,32,1024]{2,1,0:T(8,128)S(1)}, f32[2,32,1024]{2,1,0:T(8,128)S(1)}, u32[]{:S(2)}, u32[]{:S(2)}) collective-permute-start(f32[2,32,1024]{2,1,0:T(8,128)S(1)} %add.43), channel_id=1, source_target_pairs={{0,4},{2,6},{4,0},{6,2},{8,12},{10,14},{12,8},{14,10},{1,5},{3,7},... | collective-permute-start | bytes 786440 | tf_op jit(solution)/shard_map/ppermute | solution.py:291
  409.9 18.5 %collective-permute-start.10 = (f32[2,32,1024]{2,1,0:T(8,128)S(1)}, f32[2,32,1024]{2,1,0:T(8,128)S(1)}, u32[]{:S(2)}, u32[]{:S(2)}) collective-permute-start(f32[2,32,1024]{2,1,0:T(8,128)S(1)} %get-tuple-element.71), channel_id=1, source_target_pairs={{0,2},{2,0},{4,6},{6,4},{8,10},{10,8},{12,14},{14,12},{1,3},{3,1},... | collective-permute-start | bytes 786440 | tf_op jit(solution)/shard_map/ppermute | solution.py:291
  411.6 22.4 %collective-permute-start.14 = (f32[2,32,1024]{2,1,0:T(8,128)S(1)}, f32[2,32,1024]{2,1,0:T(8,128)S(1)}, u32[]{:S(2)}, u32[]{:S(2)}) collective-permute-start(f32[2,32,1024]{2,1,0:T(8,128)S(1)} %get-tuple-element.78), channel_id=1, source_target_pairs={{0,2},{2,0},{4,6},{6,4},{8,10},{10,8},{12,14},{14,12},{1,3},{3,1},... | collective-permute-start | bytes 786440 | tf_op jit(solution)/shard_map/ppermute | solution.py:291
  417.1 18.9 %collective-permute-start.12 = (f32[2,32,1024]{2,1,0:T(8,128)S(1)}, f32[2,32,1024]{2,1,0:T(8,128)S(1)}, u32[]{:S(2)}, u32[]{:S(2)}) collective-permute-start(f32[2,32,1024]{2,1,0:T(8,128)S(1)} %add.50), channel_id=1, source_target_pairs={{0,4},{2,6},{4,0},{6,2},{8,12},{10,14},{12,8},{14,10},{1,5},{3,7},... | collective-permute-start | bytes 786440 | tf_op jit(solution)/shard_map/ppermute | solution.py:291
  422.8 15.7 %collective-permute-start.8 = (f32[2,32,1024]{2,1,0:T(8,128)S(1)}, f32[2,32,1024]{2,1,0:T(8,128)S(1)}, u32[]{:S(2)}, u32[]{:S(2)}) collective-permute-start(f32[2,32,1024]{2,1,0:T(8,128)S(1)} %add.45), channel_id=1, source_target_pairs={{0,4},{2,6},{4,0},{6,2},{8,12},{10,14},{12,8},{14,10},{1,5},{3,7},... | collective-permute-start | bytes 786440 | tf_op jit(solution)/shard_map/ppermute | solution.py:291
  424.7 15.2 %collective-permute-start.9 = (f32[2,32,1024]{2,1,0:T(8,128)S(1)}, f32[2,32,1024]{2,1,0:T(8,128)S(1)}, u32[]{:S(2)}, u32[]{:S(2)}) collective-permute-start(f32[2,32,1024]{2,1,0:T(8,128)S(1)} %add.47), channel_id=1, source_target_pairs={{0,8},{2,10},{4,12},{6,14},{8,0},{10,2},{12,4},{14,6},{1,9},{3,11}... | collective-permute-start | bytes 786440 | tf_op jit(solution)/shard_map/ppermute | solution.py:291
  428.4 11.6 %collective-permute-start.6 = (f32[2,32,1024]{2,1,0:T(8,128)S(1)}, f32[2,32,1024]{2,1,0:T(8,128)S(1)}, u32[]{:S(2)}, u32[]{:S(2)}) collective-permute-start(f32[2,32,1024]{2,1,0:T(8,128)S(1)} %get-tuple-element.62), channel_id=1, source_target_pairs={{0,2},{2,0},{4,6},{6,4},{8,10},{10,8},{12,14},{14,12},{1,3},{3,1},... | collective-permute-start | bytes 786440 | tf_op jit(solution)/shard_map/ppermute | solution.py:291
  434.0 13.0 %collective-permute-start.15 = (f32[2,32,1024]{2,1,0:T(8,128)S(1)}, f32[2,32,1024]{2,1,0:T(8,128)S(1)}, u32[]{:S(2)}, u32[]{:S(2)}) collective-permute-start(f32[2,32,1024]{2,1,0:T(8,128)S(1)} %add.52), channel_id=1, source_target_pairs={{0,4},{2,6},{4,0},{6,2},{8,12},{10,14},{12,8},{14,10},{1,5},{3,7},... | collective-permute-start | bytes 786440 | tf_op jit(solution)/shard_map/ppermute | solution.py:291
  436.0 13.1 %collective-permute-start.16 = (f32[2,32,1024]{2,1,0:T(8,128)S(1)}, f32[2,32,1024]{2,1,0:T(8,128)S(1)}, u32[]{:S(2)}, u32[]{:S(2)}) collective-permute-start(f32[2,32,1024]{2,1,0:T(8,128)S(1)} %add.54), channel_id=1, source_target_pairs={{0,8},{2,10},{4,12},{6,14},{8,0},{10,2},{12,4},{14,6},{1,9},{3,11}... | collective-permute-start | bytes 786440 | tf_op jit(solution)/shard_map/ppermute | solution.py:291
  438.5 10.6 %collective-permute-start.13 = (f32[2,32,1024]{2,1,0:T(8,128)S(1)}, f32[2,32,1024]{2,1,0:T(8,128)S(1)}, u32[]{:S(2)}, u32[]{:S(2)}) collective-permute-start(f32[2,32,1024]{2,1,0:T(8,128)S(1)} %get-tuple-element.75), channel_id=1, source_target_pairs={{0,2},{2,0},{4,6},{6,4},{8,10},{10,8},{12,14},{14,12},{1,3},{3,1},... | collective-permute-start | bytes 786440 | tf_op jit(solution)/shard_map/ppermute | solution.py:291

commit v10 on v9

--- a/solution.py
+++ b/solution.py
@@ -141,7 +141,8 @@
         core[b, 1] = imag * scale
 
 
-def amplitude_kernel(start, count, slots, n_before, n_out, place, own_core, other_core, *refs):
+def amplitude_kernel(start, count, slots, n_before, sizes, place, own_core, other_core, *refs):
+    n_out = len(sizes)
     own_split, other_split, own_flat, other_flat = refs[:4]
     before = refs[4 : 4 + n_before]
     outs = refs[4 + n_before : 4 + n_before + n_out]
@@ -176,7 +177,7 @@
     else:
         for out in outs:
             out[...] = jnp.zeros_like(out)
-    piece = rows // n_out
+    offsets = [sum(sizes[:n]) for n in range(n_out)]
 
     def one_value(b, carry):
         whole = own_split.at[:, start + b, :groups, 0]
@@ -203,7 +204,7 @@
                 if n_before:
                     value = value + held[plane, :, spot]
                 for number, out in enumerate(outs):
-                    part = value[number * piece : (number + 1) * piece]
+                    part = value[offsets[number] : offsets[number] + sizes[number]]
                     if n_before:
                         out[plane, :, spot] = part
                     else:
@@ -264,14 +265,14 @@
             compiler_params=params,
         )(arrived, *after)
 
-    def added(start, count, slots, n_out, core, other_core, other_left, before):
+    def added(start, count, slots, sizes, core, other_core, other_left, before):
         flat = (2, local_batch, rows, inner)
         kept_rows = len(slots) * own_rows
         return pl.pallas_call(
-            functools.partial(amplitude_kernel, start, count, slots, len(before), n_out),
-            out_shape=[jax.ShapeDtypeStruct((2, kept_rows // n_out, rows), jnp.float32)] * n_out,
+            functools.partial(amplitude_kernel, start, count, slots, len(before), sizes),
+            out_shape=[jax.ShapeDtypeStruct((2, size, rows), jnp.float32) for size in sizes],
             in_specs=[IN_SMEM, IN_VMEM, IN_VMEM] + [ANYWHERE] * (4 + len(before)),
-            out_specs=[IN_VMEM] * n_out,
+            out_specs=[IN_VMEM] * len(sizes),
             scratch_shapes=[
                 pltpu.VMEM((count, 2, len(slots), own_rows, inner), jnp.float32),
                 pltpu.VMEM((count, 2, rows, inner), jnp.float32),
@@ -299,32 +300,50 @@
     core = core_of(many, arrived)
     odd = list(range(idx_size - 1, 0, -2))
     even = [slot - 1 for slot in odd]
-    sums = added(0, many, odd + even, 2, core, swapped(core, "half"), other_left, [])
+    sums = added(0, many, odd + even, [half_rows // 2] * 2, core, swapped(core, "half"), other_left, [])
     core = core_of(few, late, (sums[0][0, :8, :128],))
     other_core = swapped(core, "half")
-    leaving = added(many, few, odd, PIECES * depth, core, other_core, other_left, [sums[0]])
+    sizes = [own_rows * 3 // 8] * PIECES + [own_rows // 4]
+    stride = len(sizes)
+    leaving = added(many, few, odd, sizes * depth, core, other_core, other_left, [sums[0]])
     core, leaving = lax.optimization_barrier((core, leaving))
-    staying = list(added(many, few, even, PIECES * depth, core, other_core, other_left, [sums[1]]))
+    staying = added(many, few, even, sizes * depth, core, other_core, other_left, [sums[1]])
+    far_of = [slot // 2 for slot in even]
+
+    def halved(parts, bit):
+        while bit < depth:
+            for d in range(bit, depth, 2 * bit):
+                parts[d - bit] = parts[d - bit] + hop(parts[d], 2 * bit)
+            bit *= 2
+        return parts[0]
+
+    last_leaving = halved({d: leaving[at * stride + PIECES] for at, d in enumerate(far_of)}, 1)
+    last_staying = halved({d: staying[at * stride + PIECES] for at, d in enumerate(far_of)}, 1)
+    last_coming = None
     mine, coming = [], {}
-    for n, block in enumerate(leaving):
+    count = PIECES * depth
+    for n in range(count):
+        at, part = n // PIECES, n % PIECES
+        block = leaving[at * stride + part]
         if n >= WINDOW:
             block, mine[n - WINDOW] = lax.optimization_barrier((block, mine[n - WINDOW]))
         if n - WINDOW - 2 in coming:
             block, coming[n - WINDOW - 2] = lax.optimization_barrier((block, coming[n - WINDOW - 2]))
-        mine.append(staying[n] + hop(block, 1))
-        if even[n // PIECES] // 2 % 2:
+        if n == count - 1:
+            block, last_leaving = lax.optimization_barrier((block, last_leaving))
+            last_coming = hop(last_leaving, 1)
+        mine.append(staying[at * stride + part] + hop(block, 1))
+        if far_of[at] % 2:
             coming[n] = hop(mine[n], 2)
     for n, block in coming.items():
         target = n + PIECES
         mine[target] = mine[target] + block
-    blocks = {even[n // PIECES] // 2: mine[n : n + PIECES] for n in range(0, PIECES * depth, PIECES)}
-    bit = 2
-    while bit < depth:
-        for d in range(bit, depth, 2 * bit):
-            arriving = [hop(block, 2 * bit) for block in blocks[d]]
-            blocks[d - bit] = [block + new for block, new in zip(blocks[d - bit], arriving)]
-        bit *= 2
-    return jnp.moveaxis(jnp.concatenate(blocks[0], axis=1), 0, 1)
+    parts = [
+        halved({d: mine[at * PIECES + part] for at, d in enumerate(far_of) if d % 2 == 0}, 2)
+        for part in range(PIECES)
+    ]
+    result = jnp.concatenate(parts + [last_staying + last_coming], axis=1)
+    return jnp.moveaxis(result, 0, 1)
 
 
 def on_device(left_factor, right_factor):
@@ -337,7 +356,7 @@
         and inner_part % 8 == 0
         and between % 256 == 0
         and rows % 256 == 0
-        and rows % (32 * idx_size) == 0
+        and rows % (128 * idx_size) == 0
         and 256 % (rows // idx_size) == 0
     )
     return (overlapped if aligned else general)(left_factor, right_factor)

time: 451 us -> 452 us (level)
  starting transfers between devices: 93.9 us -> 104 us
  waiting for transfers between devices: 290 us -> 281 us
    ppermute x14 -> x21, starting transfers between devices: 23.4 us -> 33.3 us  [hop(): return lax.ppermute(x, 'idx', [(i, i ^ mask) for i in range(idx_size)])]
    ppermute x14 -> x21, waiting for transfers between devices: 24.7 us -> 16.4 us  [hop(): return lax.ppermute(x, 'idx', [(i, i ^ mask) for i in range(idx_size)])]
  transfers between devices with their start and end apart: 19 -> 26, of which waited for: 11 -> 11; matrix products, arithmetic and copies ran while one was open for 0% -> 0% of each run, Pallas kernels for 10% -> 10%
where the time goes in v10:
time: 452 us
  waiting for transfers between devices  281 us (62%)
  starting transfers between devices  104 us (23%)
  Pallas kernels  57.4 us (13%)
  local copies, waits for them, and re-layouts  8.95 us (2%)
    all_to_all x2, waiting for transfers between devices, sent(): lax.all_to_all(flat, ('idx', 'half'), 0, 0, tiled=True)  257 us
    all_to_all x2, starting transfers between devices, sent(): lax.all_to_all(flat, ('idx', 'half'), 0, 0, tiled=True)  69.2 us
    pallas_call x3, Pallas kernels, added(): pl.pallas_call(functools.partial(amplitude_kernel, start, count, slots, l...  37.5 us
    ppermute x21, starting transfers between devices, hop(): return lax.ppermute(x, 'idx', [(i, i ^ mask) for i in range(idx_size)])  33.3 us
    ppermute x21, waiting for transfers between devices, hop(): return lax.ppermute(x, 'idx', [(i, i ^ mask) for i in range(idx_size)])  16.4 us
    pallas_call x2, Pallas kernels, core_of(): pl.pallas_call(functools.partial(core_kernel, count, scale), out_shape=ja...  11.7 us
  transfers between devices with their start and end apart: 26, of which 11 were waited for; matrix products, arithmetic and copies ran while one was open for 0% of the time, Pallas kernels for 10%

profile of v10, /device:TPU:0, one launch (start us, length us, event | category | flops | bytes accessed | tf_op | source)
XLA Modules:
  0.0 452.1 jit_solution(17606762038916955674)
XLA Ops:
  0.0 5.3 %shard_map.29 = f32[8,2,2,7,32,512]{5,4,3,2,1,0:T(8,128)S(1)} custom-call(f32[2,8,8,32,1024]{4,3,2,1,0:T(8,128)} %bitcast.25), custom_call_target="tpu_custom_call" | custom-call | bytes 1024 | tf_op jit(solution)/shard_map/pallas_call | solution.py:240
  5.4 5.1 %copy-done = f32[8,2,2,7,32,512]{5,4,3,2,1,0:T(8,128)} copy-done((f32[8,2,2,7,32,512]{5,4,3,2,1,0:T(8,128)}, f32[8,2,2,7,32,512]{5,4,3,2,1,0:T(8,128)S(1)}, u32[]{:S(2)}) %copy-start) | copy-done | bytes 14680088
  10.4 7.4 %all-to-all-start.1 = ((f32[16,2,7,32,512]{4,3,2,1,0:T(8,128)}), f32[16,2,7,32,512]{4,3,2,1,0:T(8,128)}, u32[]{:S(2)}, u32[]{:S(2)}) async-start(f32[16,2,7,32,512]{4,3,2,1,0:T(8,128)} %bitcast.17), calls=%async_computation.1 | async-start | bytes 29360128 | tf_op jit(solution)/shard_map/all_to_all | solution.py:252
  17.9 0.4 collective-permute-start.1
  18.2 2.9 shard_map.28
  21.1 257.0 %all-to-all-done.1 = f32[16,2,7,32,512]{4,3,2,1,0:T(8,128)} async-done(((f32[16,2,7,32,512]{4,3,2,1,0:T(8,128)}), f32[16,2,7,32,512]{4,3,2,1,0:T(8,128)}, u32[]{:S(2)}, u32[]{:S(2)}) %all-to-all-start.1) | async-done | bytes 14680096 | tf_op jit(solution)/shard_map/all_to_all | solution.py:252
  278.1 61.8 %all-to-all-start = ((f32[16,2,1,32,512]{4,3,1,2,0:T(8,128)}), f32[16,2,1,32,512]{4,3,1,2,0:T(8,128)S(1)}, u32[]{:S(2)}, u32[]{:S(2)}) async-start(f32[16,2,1,32,512]{4,3,1,2,0:T(8,128)} %bitcast.4), calls=%async_computation | async-start | bytes 4194304 | tf_op jit(solution)/shard_map/all_to_all | solution.py:252
  339.9 10.6 %shard_map.30.own_core = f32[7,2,256,256]{3,2,1,0:T(8,128)} custom-call(f32[8,2,2,7,32,512]{5,4,3,2,1,0:T(8,128)} %bitcast.7.arrived), custom_call_target="tpu_custom_call" | custom-call | bytes 1024 | tf_op jit(solution)/shard_map/pallas_call | solution.py:255
  350.5 0.5 collective-permute-start
  351.1 6.3 %collective-permute-done.other_core = f32[7,2,256,256]{3,2,1,0:T(8,128)} collective-permute-done((f32[7,2,256,256]{3,2,1,0:T(8,128)}, f32[7,2,256,256]{3,2,1,0:T(8,128)}, u32[]{:S(2)}, u32[]{:S(2)}) %collective-permute-start) | collective-permute-done | bytes 3670048 | tf_op jit(solution)/shard_map/ppermute | solution.py:21
  357.4 29.7 %shard_map.31 = (f32[2,256,1024]{2,1,0:T(8,128)S(1)}, f32[2,256,1024]{2,1,0:T(8,128)S(1)}) custom-call(s32[2]{0:T(128)S(1)} %pad_add_fusion.place, f32[7,2,256,256]{3,2,1,0:T(8,128)} %shard_map.30.own_core, f32[7,2,256,256]{3,2,1,0:T(8,128)} %collective-permute-done.other_core, f32[2,8,8,2,64,256]{5,4,3,2,1,0:T(8,128)} %bitcast.19, ...), custom_call_target="tpu_custom_call" | custom-call | bytes 1024 | tf_op jit(solution)/shard_map/pallas_call | solution.py:271
  387.2 1.3 copy-done.3
  388.5 1.3 copy-done.1
  389.8 1.0 shard_map.32.own_core
  390.9 0.4 collective-permute-start.2
  391.3 1.5 collective-permute-done.2.other_core
  392.8 3.9 shard_map.33
  396.8 1.9 collective-permute-start.14
  398.7 3.9 shard_map.34
  402.6 0.2 collective-permute-start.21
  402.8 1.9 collective-permute-start.4
  404.7 0.2 collective-permute-start.11
  404.9 1.9 collective-permute-start.10
  406.7 1.5 collective-permute-start.13
  408.2 2.4 collective-permute-start.15
  410.7 2.0 collective-permute-start.3
  412.7 2.2 collective-permute-done.11
  414.8 1.9 collective-permute-start.5
  416.8 2.3 collective-permute-done.10
  419.1 1.9 collective-permute-start.12
  421.0 1.5 collective-permute-start.7
  422.5 0.6 collective-permute-start.17
  423.1 1.6 collective-permute-done.12
  424.7 1.9 collective-permute-start.20
  426.6 2.4 collective-permute-start.22
  429.0 1.5 collective-permute-start.23
  430.5 0.6 collective-permute-start.8
  431.2 0.7 collective-permute-done.17
  431.9 3.5 collective-permute-start.9
  435.4 1.3 collective-permute-start.6
  436.7 0.8 collective-permute-start.18
  437.5 1.8 collective-permute-start.19
  439.3 3.3 collective-permute-done.8
  442.7 1.9 collective-permute-start.16
  444.5 0.9 collective-permute-done.9
  445.5 3.0 collective-permute-done.18
  448.5 2.3 collective-permute-done.19
  450.9 1.2 copy.5
  (39 shorter events, 0.5 us)
Async XLA Ops:
  5.4 5.1 %copy-start = (f32[8,2,2,7,32,512]{5,4,3,2,1,0:T(8,128)}, f32[8,2,2,7,32,512]{5,4,3,2,1,0:T(8,128)S(1)}, u32[]{:S(2)}) copy-start(f32[8,2,2,7,32,512]{5,4,3,2,1,0:T(8,128)S(1)} %shard_map.29) | copy-start | bytes 44040196
  10.4 267.7 %all-to-all-start.1 = ((f32[16,2,7,32,512]{4,3,2,1,0:T(8,128)}), f32[16,2,7,32,512]{4,3,2,1,0:T(8,128)}, u32[]{:S(2)}, u32[]{:S(2)}) async-start(f32[16,2,7,32,512]{4,3,2,1,0:T(8,128)} %bitcast.17), calls=%async_computation.1 | async-start | bytes 29360128 | tf_op jit(solution)/shard_map/all_to_all | solution.py:252
  17.9 333.2 %collective-permute-start.1 = (f32[1,2,8,1024,256]{4,3,2,1,0:T(8,128)}, f32[1,2,8,1024,256]{4,3,2,1,0:T(8,128)}, u32[]{:S(2)}, u32[]{:S(2)}) collective-permute-start(f32[1,2,8,1024,256]{4,3,2,1,0:T(8,128)} %param.2), channel_id=1, source_target_pairs={{0,1},{1,0},{2,3},{3,2},{4,5},{5,4},{6,7},{7,6},{8,9},{9,8},{10,11... | collective-permute-start | bytes 50331656 | tf_op jit(solution)/shard_map/ppermute | solution.py:21
  278.1 111.7 %all-to-all-start = ((f32[16,2,1,32,512]{4,3,1,2,0:T(8,128)}), f32[16,2,1,32,512]{4,3,1,2,0:T(8,128)S(1)}, u32[]{:S(2)}, u32[]{:S(2)}) async-start(f32[16,2,1,32,512]{4,3,1,2,0:T(8,128)} %bitcast.4), calls=%async_computation | async-start | bytes 4194304 | tf_op jit(solution)/shard_map/all_to_all | solution.py:252
  350.5 6.9 %collective-permute-start = (f32[7,2,256,256]{3,2,1,0:T(8,128)}, f32[7,2,256,256]{3,2,1,0:T(8,128)}, u32[]{:S(2)}, u32[]{:S(2)}) collective-permute-start(f32[7,2,256,256]{3,2,1,0:T(8,128)} %shard_map.30.own_core), channel_id=1, source_target_pairs={{0,1},{1,0},{2,3},{3,2},{4,5},{5,4},{6,7},{7,6},{8,9},{9,8},{10,11... | collective-permute-start | bytes 11010056 | tf_op jit(solution)/shard_map/ppermute | solution.py:21
  387.1 1.3 copy-start.3
  388.5 1.3 copy-start.1
  389.8 3.0 copy-start.2
  390.8 7.8 %copy-start.4 = (f32[2,256,1024]{2,1,0:T(8,128)S(1)}, f32[2,256,1024]{2,1,0:T(8,128)}, u32[]{:S(2)}) copy-start(f32[2,256,1024]{2,1,0:T(8,128)} %copy-done.3) | copy-start | bytes 6291460
  390.9 2.0 collective-permute-start.2
  396.8 10.0 %collective-permute-start.14 = (f32[2,16,1024]{2,1,0:T(8,128)S(1)}, f32[2,16,1024]{2,1,0:T(8,128)S(1)}, u32[]{:S(2)}, u32[]{:S(2)}) collective-permute-start(f32[2,16,1024]{2,1,0:T(8,128)S(1)} %get-tuple-element.97), channel_id=1, source_target_pairs={{0,4},{2,6},{4,0},{6,2},{8,12},{10,14},{12,8},{14,10},{1,5},{3,7},... | collective-permute-start | bytes 393224 | tf_op jit(solution)/shard_map/ppermute | solution.py:292
  402.6 5.6 %collective-permute-start.21 = (f32[2,16,1024]{2,1,0:T(8,128)S(1)}, f32[2,16,1024]{2,1,0:T(8,128)S(1)}, u32[]{:S(2)}, u32[]{:S(2)}) collective-permute-start(f32[2,16,1024]{2,1,0:T(8,128)S(1)} %get-tuple-element.107), channel_id=1, source_target_pairs={{0,4},{2,6},{4,0},{6,2},{8,12},{10,14},{12,8},{14,10},{1,5},{3,7},... | collective-permute-start | bytes 393224 | tf_op jit(solution)/shard_map/ppermute | solution.py:292
  402.8 7.8 %collective-permute-start.4 = (f32[2,24,1024]{2,1,0:T(8,128)S(1)}, f32[2,24,1024]{2,1,0:T(8,128)S(1)}, u32[]{:S(2)}, u32[]{:S(2)}) collective-permute-start(f32[2,24,1024]{2,1,0:T(8,128)S(1)} %get-tuple-element.79), channel_id=1, source_target_pairs={{0,2},{2,0},{4,6},{6,4},{8,10},{10,8},{12,14},{14,12},{1,3},{3,1},... | collective-permute-start | bytes 589832 | tf_op jit(solution)/shard_map/ppermute | solution.py:292
  404.7 10.2 %collective-permute-start.11 = (f32[2,24,1024]{2,1,0:T(8,128)S(1)}, f32[2,24,1024]{2,1,0:T(8,128)S(1)}, u32[]{:S(2)}, u32[]{:S(2)}) collective-permute-start(f32[2,24,1024]{2,1,0:T(8,128)S(1)} %get-tuple-element.92), channel_id=1, source_target_pairs={{0,2},{2,0},{4,6},{6,4},{8,10},{10,8},{12,14},{14,12},{1,3},{3,1},... | collective-permute-start | bytes 589832 | tf_op jit(solution)/shard_map/ppermute | solution.py:292
  404.9 14.2 %collective-permute-start.10 = (f32[2,24,1024]{2,1,0:T(8,128)S(1)}, f32[2,24,1024]{2,1,0:T(8,128)S(1)}, u32[]{:S(2)}, u32[]{:S(2)}) collective-permute-start(f32[2,24,1024]{2,1,0:T(8,128)S(1)} %get-tuple-element.89), channel_id=1, source_target_pairs={{0,2},{2,0},{4,6},{6,4},{8,10},{10,8},{12,14},{14,12},{1,3},{3,1},... | collective-permute-start | bytes 589832 | tf_op jit(solution)/shard_map/ppermute | solution.py:292
  406.7 14.2 %collective-permute-start.13 = (f32[2,16,1024]{2,1,0:T(8,128)S(1)}, f32[2,16,1024]{2,1,0:T(8,128)S(1)}, u32[]{:S(2)}, u32[]{:S(2)}) collective-permute-start(f32[2,16,1024]{2,1,0:T(8,128)S(1)} %get-tuple-element.95), channel_id=1, source_target_pairs={{0,4},{2,6},{4,0},{6,2},{8,12},{10,14},{12,8},{14,10},{1,5},{3,7},... | collective-permute-start | bytes 393224 | tf_op jit(solution)/shard_map/ppermute | solution.py:292
  408.2 14.3 %collective-permute-start.15 = (f32[2,16,1024]{2,1,0:T(8,128)S(1)}, f32[2,16,1024]{2,1,0:T(8,128)S(1)}, u32[]{:S(2)}, u32[]{:S(2)}) collective-permute-start(f32[2,16,1024]{2,1,0:T(8,128)S(1)} %add.73), channel_id=1, source_target_pairs={{0,8},{2,10},{4,12},{6,14},{8,0},{10,2},{12,4},{14,6},{1,9},{3,11}... | collective-permute-start | bytes 393224 | tf_op jit(solution)/shard_map/ppermute | solution.py:292
  410.7 15.9 %collective-permute-start.3 = (f32[2,24,1024]{2,1,0:T(8,128)S(1)}, f32[2,24,1024]{2,1,0:T(8,128)S(1)}, u32[]{:S(2)}, u32[]{:S(2)}) collective-permute-start(f32[2,24,1024]{2,1,0:T(8,128)S(1)} %get-tuple-element.76), channel_id=1, source_target_pairs={{0,2},{2,0},{4,6},{6,4},{8,10},{10,8},{12,14},{14,12},{1,3},{3,1},... | collective-permute-start | bytes 589832 | tf_op jit(solution)/shard_map/ppermute | solution.py:292
  414.8 15.7 %collective-permute-start.5 = (f32[2,24,1024]{2,1,0:T(8,128)S(1)}, f32[2,24,1024]{2,1,0:T(8,128)S(1)}, u32[]{:S(2)}, u32[]{:S(2)}) collective-permute-start(f32[2,24,1024]{2,1,0:T(8,128)S(1)} %add.64), channel_id=1, source_target_pairs={{0,4},{2,6},{4,0},{6,2},{8,12},{10,14},{12,8},{14,10},{1,5},{3,7},... | collective-permute-start | bytes 589832 | tf_op jit(solution)/shard_map/ppermute | solution.py:292
  419.1 5.7 %collective-permute-start.12 = (f32[2,24,1024]{2,1,0:T(8,128)S(1)}, f32[2,24,1024]{2,1,0:T(8,128)S(1)}, u32[]{:S(2)}, u32[]{:S(2)}) collective-permute-start(f32[2,24,1024]{2,1,0:T(8,128)S(1)} %add.71), channel_id=1, source_target_pairs={{0,4},{2,6},{4,0},{6,2},{8,12},{10,14},{12,8},{14,10},{1,5},{3,7},... | collective-permute-start | bytes 589832 | tf_op jit(solution)/shard_map/ppermute | solution.py:292
  421.0 8.0 %collective-permute-start.7 = (f32[2,24,1024]{2,1,0:T(8,128)S(1)}, f32[2,24,1024]{2,1,0:T(8,128)S(1)}, u32[]{:S(2)}, u32[]{:S(2)}) collective-permute-start(f32[2,24,1024]{2,1,0:T(8,128)S(1)} %get-tuple-element.83), channel_id=1, source_target_pairs={{0,2},{2,0},{4,6},{6,4},{8,10},{10,8},{12,14},{14,12},{1,3},{3,1},... | collective-permute-start | bytes 589832 | tf_op jit(solution)/shard_map/ppermute | solution.py:292
  422.5 9.4 %collective-permute-start.17 = (f32[2,24,1024]{2,1,0:T(8,128)S(1)}, f32[2,24,1024]{2,1,0:T(8,128)S(1)}, u32[]{:S(2)}, u32[]{:S(2)}) collective-permute-start(f32[2,24,1024]{2,1,0:T(8,128)S(1)} %get-tuple-element.101), channel_id=1, source_target_pairs={{0,2},{2,0},{4,6},{6,4},{8,10},{10,8},{12,14},{14,12},{1,3},{3,1},... | collective-permute-start | bytes 589832 | tf_op jit(solution)/shard_map/ppermute | solution.py:292
  424.7 10.7 %collective-permute-start.20 = (f32[2,16,1024]{2,1,0:T(8,128)S(1)}, f32[2,16,1024]{2,1,0:T(8,128)S(1)}, u32[]{:S(2)}, u32[]{:S(2)}) collective-permute-start(f32[2,16,1024]{2,1,0:T(8,128)S(1)} %get-tuple-element.105), channel_id=1, source_target_pairs={{0,4},{2,6},{4,0},{6,2},{8,12},{10,14},{12,8},{14,10},{1,5},{3,7},... | collective-permute-start | bytes 393224 | tf_op jit(solution)/shard_map/ppermute | solution.py:292
  426.6 10.1 %collective-permute-start.22 = (f32[2,16,1024]{2,1,0:T(8,128)S(1)}, f32[2,16,1024]{2,1,0:T(8,128)S(1)}, u32[]{:S(2)}, u32[]{:S(2)}) collective-permute-start(f32[2,16,1024]{2,1,0:T(8,128)S(1)} %add.81), channel_id=1, source_target_pairs={{0,8},{2,10},{4,12},{6,14},{8,0},{10,2},{12,4},{14,6},{1,9},{3,11}... | collective-permute-start | bytes 393224 | tf_op jit(solution)/shard_map/ppermute | solution.py:292
  429.0 8.5 %collective-permute-start.23 = (f32[2,16,1024]{2,1,0:T(8,128)S(1)}, f32[2,16,1024]{2,1,0:T(8,128)S(1)}, u32[]{:S(2)}, u32[]{:S(2)}) collective-permute-start(f32[2,16,1024]{2,1,0:T(8,128)S(1)} %add_add_fusion.3), channel_id=1, source_target_pairs={{0,2},{2,0},{4,6},{6,4},{8,10},{10,8},{12,14},{14,12},{1,3},{3,1},... | collective-permute-start | bytes 393224 | tf_op jit(solution)/shard_map/ppermute | solution.py:292
  430.5 12.1 %collective-permute-start.8 = (f32[2,24,1024]{2,1,0:T(8,128)S(1)}, f32[2,24,1024]{2,1,0:T(8,128)S(1)}, u32[]{:S(2)}, u32[]{:S(2)}) collective-permute-start(f32[2,24,1024]{2,1,0:T(8,128)S(1)} %add.66), channel_id=1, source_target_pairs={{0,4},{2,6},{4,0},{6,2},{8,12},{10,14},{12,8},{14,10},{1,5},{3,7},... | collective-permute-start | bytes 589832 | tf_op jit(solution)/shard_map/ppermute | solution.py:292
  431.9 13.5 %collective-permute-start.9 = (f32[2,24,1024]{2,1,0:T(8,128)S(1)}, f32[2,24,1024]{2,1,0:T(8,128)S(1)}, u32[]{:S(2)}, u32[]{:S(2)}) collective-permute-start(f32[2,24,1024]{2,1,0:T(8,128)S(1)} %add.68), channel_id=1, source_target_pairs={{0,8},{2,10},{4,12},{6,14},{8,0},{10,2},{12,4},{14,6},{1,9},{3,11}... | collective-permute-start | bytes 589832 | tf_op jit(solution)/shard_map/ppermute | solution.py:292
  435.4 10.0 %collective-permute-start.6 = (f32[2,24,1024]{2,1,0:T(8,128)S(1)}, f32[2,24,1024]{2,1,0:T(8,128)S(1)}, u32[]{:S(2)}, u32[]{:S(2)}) collective-permute-start(f32[2,24,1024]{2,1,0:T(8,128)S(1)} %get-tuple-element.80), channel_id=1, source_target_pairs={{0,2},{2,0},{4,6},{6,4},{8,10},{10,8},{12,14},{14,12},{1,3},{3,1},... | collective-permute-start | bytes 589832 | tf_op jit(solution)/shard_map/ppermute | solution.py:292
  436.7 11.8 %collective-permute-start.18 = (f32[2,24,1024]{2,1,0:T(8,128)S(1)}, f32[2,24,1024]{2,1,0:T(8,128)S(1)}, u32[]{:S(2)}, u32[]{:S(2)}) collective-permute-start(f32[2,24,1024]{2,1,0:T(8,128)S(1)} %add.76), channel_id=1, source_target_pairs={{0,4},{2,6},{4,0},{6,2},{8,12},{10,14},{12,8},{14,10},{1,5},{3,7},... | collective-permute-start | bytes 589832 | tf_op jit(solution)/shard_map/ppermute | solution.py:292
  437.5 13.3 %collective-permute-start.19 = (f32[2,24,1024]{2,1,0:T(8,128)S(1)}, f32[2,24,1024]{2,1,0:T(8,128)S(1)}, u32[]{:S(2)}, u32[]{:S(2)}) collective-permute-start(f32[2,24,1024]{2,1,0:T(8,128)S(1)} %add.78), channel_id=1, source_target_pairs={{0,8},{2,10},{4,12},{6,14},{8,0},{10,2},{12,4},{14,6},{1,9},{3,11}... | collective-permute-start | bytes 589832 | tf_op jit(solution)/shard_map/ppermute | solution.py:292
  442.7 8.1 %collective-permute-start.16 = (f32[2,24,1024]{2,1,0:T(8,128)S(1)}, f32[2,24,1024]{2,1,0:T(8,128)S(1)}, u32[]{:S(2)}, u32[]{:S(2)}) collective-permute-start(f32[2,24,1024]{2,1,0:T(8,128)S(1)} %get-tuple-element.98), channel_id=1, source_target_pairs={{0,2},{2,0},{4,6},{6,4},{8,10},{10,8},{12,14},{14,12},{1,3},{3,1},... | collective-permute-start | bytes 589832 | tf_op jit(solution)/shard_map/ppermute | solution.py:292

commit v11 on v9

--- a/solution.py
+++ b/solution.py
@@ -13,6 +13,7 @@
 PIECES = 2
 WINDOW = 4
 ANYWHERE = pl.BlockSpec(memory_space=pl.ANY)
+IN_HBM = pl.BlockSpec(memory_space=pltpu.HBM)
 IN_VMEM = pl.BlockSpec(memory_space=pltpu.VMEM)
 IN_SMEM = pl.BlockSpec(memory_space=pltpu.SMEM)
 
@@ -111,25 +112,31 @@
 NN = ((1,), (0,))
 
 
-def deal_kernel(start, count, half_cols, right, out, sems):
-    copies = []
-    for half in range(2):
-        for plane in range(2):
-            source = right.at[plane, :, pl.ds(start, count), :, pl.ds(half * half_cols, half_cols)]
-            copies.append(pltpu.make_async_copy(source, out.at[:, half, plane], sems.at[2 * half + plane]))
-    for copy in copies:
-        copy.start()
-    for copy in copies:
+def deal_kernel(start, count, half_cols, right, out, held, in_sems, out_sems):
+    incoming, leaving = [], []
+    for to in range(out.shape[0]):
+        for part in range(4):
+            column = part // 2 * half_cols
+            source = right.at[part % 2, to, start : start + count, :, column : column + half_cols]
+            target = held.at[to, part // 2, part % 2]
+            incoming.append(pltpu.make_async_copy(source, target, in_sems.at[to, part]))
+            incoming[-1].start()
+    for to in range(out.shape[0]):
+        for part in range(4):
+            incoming[4 * to + part].wait()
+        leaving.append(pltpu.make_async_copy(held.at[to], out.at[to], out_sems.at[to]))
+        leaving[-1].start()
+    for copy in leaving:
         copy.wait()
 
 
-def core_kernel(count, scale, arrived, *refs):
+def core_kernel(start, count, scale, arrived, *refs):
     core, factors, sems = refs[-3:]
     inner = core.shape[2]
     copies = {}
     for b in range(count):
         for part in range(4):
-            source = arrived.at[:, part // 2, part % 2, b]
+            source = arrived.at[:, part // 2, part % 2, start + b]
             copies[b, part] = pltpu.make_async_copy(source, factors.at[b, part], sems.at[b, part])
             copies[b, part].start()
     for b in range(count):
@@ -141,7 +148,9 @@
         core[b, 1] = imag * scale
 
 
-def amplitude_kernel(start, count, slots, n_before, n_out, place, own_core, other_core, *refs):
+def amplitude_kernel(start, n_cores, slots, n_before, n_out, place, *refs):
+    own_cores, other_cores, refs = refs[:n_cores], refs[n_cores : 2 * n_cores], refs[2 * n_cores :]
+    count = sum(core.shape[0] for core in own_cores)
     own_split, other_split, own_flat, other_flat = refs[:4]
     before = refs[4 : 4 + n_before]
     outs = refs[4 + n_before : 4 + n_before + n_out]
@@ -178,14 +187,15 @@
             out[...] = jnp.zeros_like(out)
     piece = rows // n_out
 
-    def one_value(b, carry):
+    def one_value(own_core, other_core, first_b, at_b, carry):
+        b = first_b + at_b
         whole = own_split.at[:, start + b, :groups, 0]
         pltpu.make_async_copy(whole, first.at[b], sems.at[0, b]).wait()
         real, imag = complex_dot(
             first[b, 0].reshape(rows, inner),
             first[b, 1].reshape(rows, inner),
-            own_core[b, 0] + other_core[b, 0],
-            own_core[b, 1] + other_core[b, 1],
+            own_core[at_b, 0] + other_core[at_b, 0],
+            own_core[at_b, 1] + other_core[at_b, 1],
             NN,
         )
         for part, value in enumerate((real, imag, real + imag)):
@@ -210,10 +220,14 @@
                         out[plane, :, spot] += part
         return carry
 
-    if count == 1:
-        one_value(0, 0)
-    else:
-        lax.fori_loop(0, count, one_value, 0)
+    first_b = 0
+    for own_core, other_core in zip(own_cores, other_cores):
+        values = functools.partial(one_value, own_core, other_core, first_b)
+        if own_core.shape[0] == 1:
+            values(0, 0)
+        else:
+            lax.fori_loop(0, own_core.shape[0], values, 0)
+        first_b += own_core.shape[0]
 
 
 def chunks_of(count):
@@ -236,23 +250,28 @@
     own_left = left_factor.reshape(shape)
 
     def dealt(start, count):
+        laid = (idx_size, 2, 2, count, inner_part, half_cols)
         return pl.pallas_call(
             functools.partial(deal_kernel, start, count, half_cols),
-            out_shape=jax.ShapeDtypeStruct((idx_size, 2, 2, count, inner_part, half_cols), jnp.float32),
+            out_shape=jax.ShapeDtypeStruct(laid, jnp.float32),
             in_specs=[ANYWHERE],
-            out_specs=IN_VMEM,
-            scratch_shapes=[pltpu.SemaphoreType.DMA((4,))],
+            out_specs=IN_HBM,
+            scratch_shapes=[
+                pltpu.VMEM(laid, jnp.float32),
+                pltpu.SemaphoreType.DMA((idx_size, 4)),
+                pltpu.SemaphoreType.DMA((idx_size,)),
+            ],
             cost_estimate=BRIEF,
-            compiler_params=pltpu.CompilerParams(vmem_limit_bytes=38 * MIB),
+            compiler_params=params,
         )(right)
 
     def sent(pieces):
         flat = pieces.reshape(2 * idx_size, *pieces.shape[2:])
         return lax.all_to_all(flat, ("idx", "half"), 0, 0, tiled=True).reshape(pieces.shape)
 
-    def core_of(count, arrived, after=()):
+    def core_of(start, count, arrived, after=()):
         return pl.pallas_call(
-            functools.partial(core_kernel, count, scale),
+            functools.partial(core_kernel, start, count, scale),
             out_shape=jax.ShapeDtypeStruct((count, 2, inner, inner), jnp.float32),
             in_specs=[ANYWHERE] + [IN_VMEM] * len(after),
             out_specs=IN_VMEM,
@@ -264,13 +283,13 @@
             compiler_params=params,
         )(arrived, *after)
 
-    def added(start, count, slots, n_out, core, other_core, other_left, before):
+    def added(start, count, slots, n_out, cores, other_cores, other_left, before):
         flat = (2, local_batch, rows, inner)
         kept_rows = len(slots) * own_rows
         return pl.pallas_call(
-            functools.partial(amplitude_kernel, start, count, slots, len(before), n_out),
+            functools.partial(amplitude_kernel, start, len(cores), slots, len(before), n_out),
             out_shape=[jax.ShapeDtypeStruct((2, kept_rows // n_out, rows), jnp.float32)] * n_out,
-            in_specs=[IN_SMEM, IN_VMEM, IN_VMEM] + [ANYWHERE] * (4 + len(before)),
+            in_specs=[IN_SMEM] + [IN_VMEM] * (2 * len(cores)) + [ANYWHERE] * (4 + len(before)),
             out_specs=[IN_VMEM] * n_out,
             scratch_shapes=[
                 pltpu.VMEM((count, 2, len(slots), own_rows, inner), jnp.float32),
@@ -283,7 +302,7 @@
             cost_estimate=BRIEF,
             compiler_params=params,
         )(
-            place, core, other_core, own_left, other_left,
+            place, *cores, *other_cores, own_left, other_left,
             own_left.reshape(flat), other_left.reshape(flat), *before,
         )
 
@@ -296,15 +315,20 @@
     pieces = dealt(many, few)
     late = sent(pieces)
     arrived, pieces = lax.optimization_barrier((arrived, pieces))
-    core = core_of(many, arrived)
+    share = (many + 1) // 2
+    cores = [core_of(0, share, arrived)]
+    swaps = [swapped(cores[0], "half")]
+    if many > share:
+        cores.append(core_of(share, many - share, arrived))
+        swaps.append(swapped(cores[1], "half"))
     odd = list(range(idx_size - 1, 0, -2))
     even = [slot - 1 for slot in odd]
-    sums = added(0, many, odd + even, 2, core, swapped(core, "half"), other_left, [])
-    core = core_of(few, late, (sums[0][0, :8, :128],))
+    sums = added(0, many, odd + even, 2, cores, swaps, other_left, [])
+    core = core_of(0, few, late, (sums[0][0, :8, :128],))
     other_core = swapped(core, "half")
-    leaving = added(many, few, odd, PIECES * depth, core, other_core, other_left, [sums[0]])
+    leaving = added(many, few, odd, PIECES * depth, [core], [other_core], other_left, [sums[0]])
     core, leaving = lax.optimization_barrier((core, leaving))
-    staying = list(added(many, few, even, PIECES * depth, core, other_core, other_left, [sums[1]]))
+    staying = list(added(many, few, even, PIECES * depth, [core], [other_core], other_left, [sums[1]]))
     mine, coming = [], {}
     for n, block in enumerate(leaving):
         if n >= WINDOW:

time: 451 us -> 451 us (level)
  Pallas kernels: 57.4 us -> 65.1 us
  local copies, waits for them, and re-layouts: 8.91 us -> 3.85 us
    pallas_call x2, Pallas kernels: 8.24 us -> 13.4 us  [dealt(): pl.pallas_call(functools.partial(deal_kernel, start, count, half_cols), o...]
    unnamed x10 -> x8, local copies, waits for them, and re-layouts: 7.71 us -> 2.65 us
    pallas_call x5 -> x6, Pallas kernels: 49.2 us -> 51.7 us  [the longest x3 37.9 us: added(): pl.pallas_call(functools.partial(amplitude_kernel, start, len(cores), slo...]
  transfers between devices with their start and end apart: 19 -> 20, of which waited for: 11 -> 11; matrix products, arithmetic and copies ran while one was open for 0% -> 0% of each run, Pallas kernels for 10% -> 11%
where the time goes in v11:
time: 451 us
  waiting for transfers between devices  289 us (64%)
  starting transfers between devices  92.5 us (21%)
  Pallas kernels  65.1 us (14%)
    all_to_all x2, waiting for transfers between devices, sent(): lax.all_to_all(flat, ('idx', 'half'), 0, 0, tiled=True)  257 us
    all_to_all x2, starting transfers between devices, sent(): lax.all_to_all(flat, ('idx', 'half'), 0, 0, tiled=True)  69.2 us
    pallas_call x3, Pallas kernels, added(): pl.pallas_call(functools.partial(amplitude_kernel, start, len(cores), slo...  37.9 us
    ppermute x14, waiting for transfers between devices, hop(): return lax.ppermute(x, 'idx', [(i, i ^ mask) for i in range(idx_size)])  26.2 us
    ppermute x14, starting transfers between devices, hop(): return lax.ppermute(x, 'idx', [(i, i ^ mask) for i in range(idx_size)])  22.1 us
    pallas_call x3, Pallas kernels, core_of(): pl.pallas_call(functools.partial(core_kernel, start, count, scale), out_s...  13.8 us
    pallas_call x2, Pallas kernels, dealt(): pl.pallas_call(functools.partial(deal_kernel, start, count, half_cols), o...  13.4 us
  transfers between devices with their start and end apart: 20, of which 11 were waited for; matrix products, arithmetic and copies ran while one was open for 0% of the time, Pallas kernels for 11%

profile of v11, /device:TPU:0, one launch (start us, length us, event | category | flops | bytes accessed | tf_op | source)
XLA Modules:
  0.0 450.9 jit_solution(258945477216245991)
XLA Ops:
  0.0 10.7 %shard_map.29 = f32[8,2,2,7,32,512]{5,4,3,2,1,0:T(8,128)} custom-call(f32[2,8,8,32,1024]{4,3,2,1,0:T(8,128)} %bitcast.24), custom_call_target="tpu_custom_call" | custom-call | bytes 1024 | tf_op jit(solution)/shard_map/pallas_call | solution.py:254
  10.7 7.4 %all-to-all-start.1 = ((f32[16,2,7,32,512]{4,3,2,1,0:T(8,128)}), f32[16,2,7,32,512]{4,3,2,1,0:T(8,128)}, u32[]{:S(2)}, u32[]{:S(2)}) async-start(f32[16,2,7,32,512]{4,3,2,1,0:T(8,128)} %bitcast.26), calls=%async_computation.1 | async-start | bytes 29360128 | tf_op jit(solution)/shard_map/all_to_all | solution.py:270
  18.1 0.4 collective-permute-start.2
  18.5 2.7 shard_map.28
  21.2 257.2 %all-to-all-done.1 = f32[16,2,7,32,512]{4,3,2,1,0:T(8,128)} async-done(((f32[16,2,7,32,512]{4,3,2,1,0:T(8,128)}), f32[16,2,7,32,512]{4,3,2,1,0:T(8,128)}, u32[]{:S(2)}, u32[]{:S(2)}) %all-to-all-start.1) | async-done | bytes 14680096 | tf_op jit(solution)/shard_map/all_to_all | solution.py:270
  278.4 61.8 %all-to-all-start = ((f32[16,2,1,32,512]{4,3,1,2,0:T(8,128)}), f32[16,2,1,32,512]{4,3,1,2,0:T(8,128)S(1)}, u32[]{:S(2)}, u32[]{:S(2)}) async-start(f32[16,2,1,32,512]{4,3,1,2,0:T(8,128)} %bitcast.4), calls=%async_computation | async-start | bytes 4194304 | tf_op jit(solution)/shard_map/all_to_all | solution.py:270
  340.2 7.1 %shard_map.30.refs_0_ = f32[4,2,256,256]{3,2,1,0:T(8,128)} custom-call(f32[8,2,2,7,32,512]{5,4,3,2,1,0:T(8,128)} %bitcast.7.arrived), custom_call_target="tpu_custom_call" | custom-call | bytes 1024 | tf_op jit(solution)/shard_map/pallas_call | solution.py:273
  347.3 0.5 collective-permute-start
  347.8 5.7 %shard_map.31.refs_1_ = f32[3,2,256,256]{3,2,1,0:T(8,128)} custom-call(f32[8,2,2,7,32,512]{5,4,3,2,1,0:T(8,128)} %bitcast.7.arrived), custom_call_target="tpu_custom_call" | custom-call | bytes 1024 | tf_op jit(solution)/shard_map/pallas_call | solution.py:273
  353.5 0.2 collective-permute-start.1
  353.7 0.1 pad_add_fusion.place
  353.7 0.0 collective-permute-done.2
  353.7 3.6 collective-permute-done.1.refs_3_
  357.3 0.0 collective-permute-done.refs_2_
  357.3 30.1 %shard_map.32 = (f32[2,256,1024]{2,1,0:T(8,128)S(1)}, f32[2,256,1024]{2,1,0:T(8,128)S(1)}) custom-call(s32[2]{0:T(128)S(1)} %pad_add_fusion.place, f32[4,2,256,256]{3,2,1,0:T(8,128)} %shard_map.30.refs_0_, f32[3,2,256,256]{3,2,1,0:T(8,128)} %shard_map.31.refs_1_, f32[4,2,256,256]{3,2,1,0:T(8,128)} %collective-permute-done.refs_2_, ...), custom_call_target="tpu_custom_call" | custom-call | bytes 1024 | tf_op jit(solution)/shard_map/pallas_call | solution.py:289
  387.4 1.3 copy-done.2
  388.7 1.3 copy-done
  390.1 1.0 shard_map.33.refs_0_
  391.1 0.2 collective-permute-start.3
  391.3 1.8 collective-permute-done.3.refs_1_
  393.1 3.9 shard_map.34
  397.0 1.7 collective-permute-start.5
  398.7 0.3 collective-permute-start.12
  399.1 3.9 shard_map.35
  403.0 3.2 collective-permute-done.5
  406.2 1.7 collective-permute-start.8
  407.9 0.4 collective-permute-start.4
  408.3 1.7 collective-permute-start.6
  410.0 1.5 collective-permute-start.11
  411.4 0.4 collective-permute-done.12
  411.8 1.7 collective-permute-start.15
  413.6 3.8 collective-permute-done.8
  417.4 1.7 collective-permute-start.13
  419.1 3.9 collective-permute-done.4
  423.0 1.7 collective-permute-start.9
  424.8 2.4 collective-permute-start.10
  427.2 1.4 collective-permute-done.11
  428.6 1.7 collective-permute-start.7
  430.3 3.9 collective-permute-done.15
  434.3 1.7 collective-permute-start.16
  436.1 2.4 collective-permute-start.17
  438.5 1.5 collective-permute-start.14
  440.0 0.0 collective-permute-done.7
  440.0 0.1 add_add_fusion.1
  440.1 7.1 %collective-permute-done.16 = f32[2,32,1024]{2,1,0:T(8,128)S(1)} collective-permute-done((f32[2,32,1024]{2,1,0:T(8,128)S(1)}, f32[2,32,1024]{2,1,0:T(8,128)S(1)}, u32[]{:S(2)}, u32[]{:S(2)}) %collective-permute-start.16) | collective-permute-done | bytes 262176 | tf_op jit(solution)/shard_map/ppermute | solution.py:310
  447.2 2.4 collective-permute-done.17
  449.6 0.1 add_add_fusion
  449.7 1.2 copy.5
  (22 shorter events, 0.3 us)
Async XLA Ops:
  10.7 267.7 %all-to-all-start.1 = ((f32[16,2,7,32,512]{4,3,2,1,0:T(8,128)}), f32[16,2,7,32,512]{4,3,2,1,0:T(8,128)}, u32[]{:S(2)}, u32[]{:S(2)}) async-start(f32[16,2,7,32,512]{4,3,2,1,0:T(8,128)} %bitcast.26), calls=%async_computation.1 | async-start | bytes 29360128 | tf_op jit(solution)/shard_map/all_to_all | solution.py:270
  18.1 335.6 %collective-permute-start.2 = (f32[1,2,8,1024,256]{4,3,2,1,0:T(8,128)}, f32[1,2,8,1024,256]{4,3,2,1,0:T(8,128)}, u32[]{:S(2)}, u32[]{:S(2)}) collective-permute-start(f32[1,2,8,1024,256]{4,3,2,1,0:T(8,128)} %param.2), channel_id=1, source_target_pairs={{0,1},{1,0},{2,3},{3,2},{4,5},{5,4},{6,7},{7,6},{8,9},{9,8},{10,11... | collective-permute-start | bytes 50331656 | tf_op jit(solution)/shard_map/ppermute | solution.py:22
  278.4 111.7 %all-to-all-start = ((f32[16,2,1,32,512]{4,3,1,2,0:T(8,128)}), f32[16,2,1,32,512]{4,3,1,2,0:T(8,128)S(1)}, u32[]{:S(2)}, u32[]{:S(2)}) async-start(f32[16,2,1,32,512]{4,3,1,2,0:T(8,128)} %bitcast.4), calls=%async_computation | async-start | bytes 4194304 | tf_op jit(solution)/shard_map/all_to_all | solution.py:270
  347.3 10.0 %collective-permute-start = (f32[4,2,256,256]{3,2,1,0:T(8,128)}, f32[4,2,256,256]{3,2,1,0:T(8,128)}, u32[]{:S(2)}, u32[]{:S(2)}) collective-permute-start(f32[4,2,256,256]{3,2,1,0:T(8,128)} %shard_map.30.refs_0_), channel_id=1, source_target_pairs={{0,1},{1,0},{2,3},{3,2},{4,5},{5,4},{6,7},{7,6},{8,9},{9,8},{10,11... | collective-permute-start | bytes 6291464 | tf_op jit(solution)/shard_map/ppermute | solution.py:22
  353.5 3.8 collective-permute-start.1
  387.4 1.3 copy-start.2
  388.7 1.3 copy-start
  390.1 3.0 copy-start.1
  391.1 8.0 %copy-start.3 = (f32[2,256,1024]{2,1,0:T(8,128)S(1)}, f32[2,256,1024]{2,1,0:T(8,128)}, u32[]{:S(2)}) copy-start(f32[2,256,1024]{2,1,0:T(8,128)} %copy-done.2) | copy-start | bytes 6291460
  391.1 2.0 collective-permute-start.3
  397.0 9.2 %collective-permute-start.5 = (f32[2,32,1024]{2,1,0:T(8,128)S(1)}, f32[2,32,1024]{2,1,0:T(8,128)S(1)}, u32[]{:S(2)}, u32[]{:S(2)}) collective-permute-start(f32[2,32,1024]{2,1,0:T(8,128)S(1)} %get-tuple-element.61), channel_id=1, source_target_pairs={{0,2},{2,0},{4,6},{6,4},{8,10},{10,8},{12,14},{14,12},{1,3},{3,1},... | collective-permute-start | bytes 786440 | tf_op jit(solution)/shard_map/ppermute | solution.py:310
  398.7 13.1 %collective-permute-start.12 = (f32[2,32,1024]{2,1,0:T(8,128)S(1)}, f32[2,32,1024]{2,1,0:T(8,128)S(1)}, u32[]{:S(2)}, u32[]{:S(2)}) collective-permute-start(f32[2,32,1024]{2,1,0:T(8,128)S(1)} %get-tuple-element.74), channel_id=1, source_target_pairs={{0,2},{2,0},{4,6},{6,4},{8,10},{10,8},{12,14},{14,12},{1,3},{3,1},... | collective-permute-start | bytes 786440 | tf_op jit(solution)/shard_map/ppermute | solution.py:310
  406.2 11.2 %collective-permute-start.8 = (f32[2,32,1024]{2,1,0:T(8,128)S(1)}, f32[2,32,1024]{2,1,0:T(8,128)S(1)}, u32[]{:S(2)}, u32[]{:S(2)}) collective-permute-start(f32[2,32,1024]{2,1,0:T(8,128)S(1)} %get-tuple-element.65), channel_id=1, source_target_pairs={{0,2},{2,0},{4,6},{6,4},{8,10},{10,8},{12,14},{14,12},{1,3},{3,1},... | collective-permute-start | bytes 786440 | tf_op jit(solution)/shard_map/ppermute | solution.py:310
  407.9 15.1 %collective-permute-start.4 = (f32[2,32,1024]{2,1,0:T(8,128)S(1)}, f32[2,32,1024]{2,1,0:T(8,128)S(1)}, u32[]{:S(2)}, u32[]{:S(2)}) collective-permute-start(f32[2,32,1024]{2,1,0:T(8,128)S(1)} %get-tuple-element.58), channel_id=1, source_target_pairs={{0,2},{2,0},{4,6},{6,4},{8,10},{10,8},{12,14},{14,12},{1,3},{3,1},... | collective-permute-start | bytes 786440 | tf_op jit(solution)/shard_map/ppermute | solution.py:310
  408.3 16.4 %collective-permute-start.6 = (f32[2,32,1024]{2,1,0:T(8,128)S(1)}, f32[2,32,1024]{2,1,0:T(8,128)S(1)}, u32[]{:S(2)}, u32[]{:S(2)}) collective-permute-start(f32[2,32,1024]{2,1,0:T(8,128)S(1)} %add.43), channel_id=1, source_target_pairs={{0,4},{2,6},{4,0},{6,2},{8,12},{10,14},{12,8},{14,10},{1,5},{3,7},... | collective-permute-start | bytes 786440 | tf_op jit(solution)/shard_map/ppermute | solution.py:310
  410.0 18.7 %collective-permute-start.11 = (f32[2,32,1024]{2,1,0:T(8,128)S(1)}, f32[2,32,1024]{2,1,0:T(8,128)S(1)}, u32[]{:S(2)}, u32[]{:S(2)}) collective-permute-start(f32[2,32,1024]{2,1,0:T(8,128)S(1)} %get-tuple-element.71), channel_id=1, source_target_pairs={{0,2},{2,0},{4,6},{6,4},{8,10},{10,8},{12,14},{14,12},{1,3},{3,1},... | collective-permute-start | bytes 786440 | tf_op jit(solution)/shard_map/ppermute | solution.py:310
  411.8 22.4 %collective-permute-start.15 = (f32[2,32,1024]{2,1,0:T(8,128)S(1)}, f32[2,32,1024]{2,1,0:T(8,128)S(1)}, u32[]{:S(2)}, u32[]{:S(2)}) collective-permute-start(f32[2,32,1024]{2,1,0:T(8,128)S(1)} %get-tuple-element.78), channel_id=1, source_target_pairs={{0,2},{2,0},{4,6},{6,4},{8,10},{10,8},{12,14},{14,12},{1,3},{3,1},... | collective-permute-start | bytes 786440 | tf_op jit(solution)/shard_map/ppermute | solution.py:310
  417.4 18.6 %collective-permute-start.13 = (f32[2,32,1024]{2,1,0:T(8,128)S(1)}, f32[2,32,1024]{2,1,0:T(8,128)S(1)}, u32[]{:S(2)}, u32[]{:S(2)}) collective-permute-start(f32[2,32,1024]{2,1,0:T(8,128)S(1)} %add.50), channel_id=1, source_target_pairs={{0,4},{2,6},{4,0},{6,2},{8,12},{10,14},{12,8},{14,10},{1,5},{3,7},... | collective-permute-start | bytes 786440 | tf_op jit(solution)/shard_map/ppermute | solution.py:310
  423.0 15.5 %collective-permute-start.9 = (f32[2,32,1024]{2,1,0:T(8,128)S(1)}, f32[2,32,1024]{2,1,0:T(8,128)S(1)}, u32[]{:S(2)}, u32[]{:S(2)}) collective-permute-start(f32[2,32,1024]{2,1,0:T(8,128)S(1)} %add.45), channel_id=1, source_target_pairs={{0,4},{2,6},{4,0},{6,2},{8,12},{10,14},{12,8},{14,10},{1,5},{3,7},... | collective-permute-start | bytes 786440 | tf_op jit(solution)/shard_map/ppermute | solution.py:310
  424.8 15.2 %collective-permute-start.10 = (f32[2,32,1024]{2,1,0:T(8,128)S(1)}, f32[2,32,1024]{2,1,0:T(8,128)S(1)}, u32[]{:S(2)}, u32[]{:S(2)}) collective-permute-start(f32[2,32,1024]{2,1,0:T(8,128)S(1)} %add.47), channel_id=1, source_target_pairs={{0,8},{2,10},{4,12},{6,14},{8,0},{10,2},{12,4},{14,6},{1,9},{3,11}... | collective-permute-start | bytes 786440 | tf_op jit(solution)/shard_map/ppermute | solution.py:310
  428.6 11.3 %collective-permute-start.7 = (f32[2,32,1024]{2,1,0:T(8,128)S(1)}, f32[2,32,1024]{2,1,0:T(8,128)S(1)}, u32[]{:S(2)}, u32[]{:S(2)}) collective-permute-start(f32[2,32,1024]{2,1,0:T(8,128)S(1)} %get-tuple-element.62), channel_id=1, source_target_pairs={{0,2},{2,0},{4,6},{6,4},{8,10},{10,8},{12,14},{14,12},{1,3},{3,1},... | collective-permute-start | bytes 786440 | tf_op jit(solution)/shard_map/ppermute | solution.py:310
  434.3 12.9 %collective-permute-start.16 = (f32[2,32,1024]{2,1,0:T(8,128)S(1)}, f32[2,32,1024]{2,1,0:T(8,128)S(1)}, u32[]{:S(2)}, u32[]{:S(2)}) collective-permute-start(f32[2,32,1024]{2,1,0:T(8,128)S(1)} %add.52), channel_id=1, source_target_pairs={{0,4},{2,6},{4,0},{6,2},{8,12},{10,14},{12,8},{14,10},{1,5},{3,7},... | collective-permute-start | bytes 786440 | tf_op jit(solution)/shard_map/ppermute | solution.py:310
  436.1 13.5 %collective-permute-start.17 = (f32[2,32,1024]{2,1,0:T(8,128)S(1)}, f32[2,32,1024]{2,1,0:T(8,128)S(1)}, u32[]{:S(2)}, u32[]{:S(2)}) collective-permute-start(f32[2,32,1024]{2,1,0:T(8,128)S(1)} %add.54), channel_id=1, source_target_pairs={{0,8},{2,10},{4,12},{6,14},{8,0},{10,2},{12,4},{14,6},{1,9},{3,11}... | collective-permute-start | bytes 786440 | tf_op jit(solution)/shard_map/ppermute | solution.py:310
  438.5 11.1 %collective-permute-start.14 = (f32[2,32,1024]{2,1,0:T(8,128)S(1)}, f32[2,32,1024]{2,1,0:T(8,128)S(1)}, u32[]{:S(2)}, u32[]{:S(2)}) collective-permute-start(f32[2,32,1024]{2,1,0:T(8,128)S(1)} %get-tuple-element.75), channel_id=1, source_target_pairs={{0,2},{2,0},{4,6},{6,4},{8,10},{10,8},{12,14},{14,12},{1,3},{3,1},... | collective-permute-start | bytes 786440 | tf_op jit(solution)/shard_map/ppermute | solution.py:310

commit v12 on v9

--- a/solution.py
+++ b/solution.py
@@ -11,7 +11,7 @@
 HIGH = lax.Precision.HIGH
 MIB = 1 << 20
 PIECES = 2
-WINDOW = 4
+WINDOW = 3
 ANYWHERE = pl.BlockSpec(memory_space=pl.ANY)
 IN_VMEM = pl.BlockSpec(memory_space=pltpu.VMEM)
 IN_SMEM = pl.BlockSpec(memory_space=pltpu.SMEM)
@@ -309,8 +309,8 @@
     for n, block in enumerate(leaving):
         if n >= WINDOW:
             block, mine[n - WINDOW] = lax.optimization_barrier((block, mine[n - WINDOW]))
-        if n - WINDOW - 2 in coming:
-            block, coming[n - WINDOW - 2] = lax.optimization_barrier((block, coming[n - WINDOW - 2]))
+        if n - 3 * PIECES in coming:
+            block, coming[n - 3 * PIECES] = lax.optimization_barrier((block, coming[n - 3 * PIECES]))
         mine.append(staying[n] + hop(block, 1))
         if even[n // PIECES] // 2 % 2:
             coming[n] = hop(mine[n], 2)

time: 451 us -> 452 us (level)
  no operation moved by 1% of the time
where the time goes in v12:
time: 452 us
  waiting for transfers between devices  289 us (64%)
  starting transfers between devices  95.3 us (21%)
  Pallas kernels  57.4 us (13%)
  local copies, waits for them, and re-layouts  8.91 us (2%)
    all_to_all x2, waiting for transfers between devices, sent(): lax.all_to_all(flat, ('idx', 'half'), 0, 0, tiled=True)  257 us
    all_to_all x2, starting transfers between devices, sent(): lax.all_to_all(flat, ('idx', 'half'), 0, 0, tiled=True)  69.2 us
    pallas_call x3, Pallas kernels, added(): pl.pallas_call(functools.partial(amplitude_kernel, start, count, slots, l...  37.5 us
    ppermute x14, starting transfers between devices, hop(): return lax.ppermute(x, 'idx', [(i, i ^ mask) for i in range(idx_size)])  24.8 us
    ppermute x14, waiting for transfers between devices, hop(): return lax.ppermute(x, 'idx', [(i, i ^ mask) for i in range(idx_size)])  24.6 us
    pallas_call x2, Pallas kernels, core_of(): pl.pallas_call(functools.partial(core_kernel, count, scale), out_shape=ja...  11.6 us
  transfers between devices with their start and end apart: 19, of which 11 were waited for; matrix products, arithmetic and copies ran while one was open for 0% of the time, Pallas kernels for 10%

profile of v12, /device:TPU:0, one launch (start us, length us, event | category | flops | bytes accessed | tf_op | source)
XLA Modules:
  0.0 451.8 jit_solution(8552470407404382526)
XLA Ops:
  0.0 5.3 %shard_map.29 = f32[8,2,2,7,32,512]{5,4,3,2,1,0:T(8,128)S(1)} custom-call(f32[2,8,8,32,1024]{4,3,2,1,0:T(8,128)} %bitcast.25), custom_call_target="tpu_custom_call" | custom-call | bytes 1024 | tf_op jit(solution)/shard_map/pallas_call | solution.py:239
  5.4 5.1 %copy-done = f32[8,2,2,7,32,512]{5,4,3,2,1,0:T(8,128)} copy-done((f32[8,2,2,7,32,512]{5,4,3,2,1,0:T(8,128)}, f32[8,2,2,7,32,512]{5,4,3,2,1,0:T(8,128)S(1)}, u32[]{:S(2)}) %copy-start) | copy-done | bytes 14680088
  10.4 7.4 %all-to-all-start.1 = ((f32[16,2,7,32,512]{4,3,2,1,0:T(8,128)}), f32[16,2,7,32,512]{4,3,2,1,0:T(8,128)}, u32[]{:S(2)}, u32[]{:S(2)}) async-start(f32[16,2,7,32,512]{4,3,2,1,0:T(8,128)} %bitcast.17), calls=%async_computation.1 | async-start | bytes 29360128 | tf_op jit(solution)/shard_map/all_to_all | solution.py:251
  17.8 0.4 collective-permute-start.1
  18.2 2.9 shard_map.28
  21.1 257.0 %all-to-all-done.1 = f32[16,2,7,32,512]{4,3,2,1,0:T(8,128)} async-done(((f32[16,2,7,32,512]{4,3,2,1,0:T(8,128)}), f32[16,2,7,32,512]{4,3,2,1,0:T(8,128)}, u32[]{:S(2)}, u32[]{:S(2)}) %all-to-all-start.1) | async-done | bytes 14680096 | tf_op jit(solution)/shard_map/all_to_all | solution.py:251
  278.1 61.8 %all-to-all-start = ((f32[16,2,1,32,512]{4,3,1,2,0:T(8,128)}), f32[16,2,1,32,512]{4,3,1,2,0:T(8,128)S(1)}, u32[]{:S(2)}, u32[]{:S(2)}) async-start(f32[16,2,1,32,512]{4,3,1,2,0:T(8,128)} %bitcast.4), calls=%async_computation | async-start | bytes 4194304 | tf_op jit(solution)/shard_map/all_to_all | solution.py:251
  339.9 10.6 %shard_map.30.own_core = f32[7,2,256,256]{3,2,1,0:T(8,128)} custom-call(f32[8,2,2,7,32,512]{5,4,3,2,1,0:T(8,128)} %bitcast.7.arrived), custom_call_target="tpu_custom_call" | custom-call | bytes 1024 | tf_op jit(solution)/shard_map/pallas_call | solution.py:254
  350.5 0.5 collective-permute-start
  351.0 0.1 pad_add_fusion.place
  351.1 0.0 collective-permute-done.1
  351.1 6.3 %collective-permute-done.other_core = f32[7,2,256,256]{3,2,1,0:T(8,128)} collective-permute-done((f32[7,2,256,256]{3,2,1,0:T(8,128)}, f32[7,2,256,256]{3,2,1,0:T(8,128)}, u32[]{:S(2)}, u32[]{:S(2)}) %collective-permute-start) | collective-permute-done | bytes 3670048 | tf_op jit(solution)/shard_map/ppermute | solution.py:21
  357.4 29.7 %shard_map.31 = (f32[2,256,1024]{2,1,0:T(8,128)S(1)}, f32[2,256,1024]{2,1,0:T(8,128)S(1)}) custom-call(s32[2]{0:T(128)S(1)} %pad_add_fusion.place, f32[7,2,256,256]{3,2,1,0:T(8,128)} %shard_map.30.own_core, f32[7,2,256,256]{3,2,1,0:T(8,128)} %collective-permute-done.other_core, f32[2,8,8,2,64,256]{5,4,3,2,1,0:T(8,128)} %bitcast.19, ...), custom_call_target="tpu_custom_call" | custom-call | bytes 1024 | tf_op jit(solution)/shard_map/pallas_call | solution.py:270
  387.1 1.3 copy-done.3
  388.5 1.3 copy-done.1
  389.8 0.0 all-to-all-done
  389.8 1.0 shard_map.32.own_core
  390.8 0.4 collective-permute-start.2
  391.3 1.5 collective-permute-done.2.other_core
  392.8 3.9 shard_map.33
  396.7 1.9 collective-permute-start.3
  398.6 0.2 collective-permute-start.7
  398.8 1.8 collective-permute-start.10
  400.7 3.9 shard_map.34
  404.6 1.3 collective-permute-done.3
  405.9 1.9 collective-permute-start.4
  407.9 1.5 collective-permute-start.5
  409.4 2.2 collective-permute-done.7
  411.6 1.9 collective-permute-start.8
  413.5 3.6 collective-permute-done.10
  417.2 1.9 collective-permute-start.14
  419.1 1.5 collective-permute-start.12
  420.6 2.2 collective-permute-done.4
  422.8 0.0 collective-permute-done.5
  422.8 2.8 collective-permute-start.11
  425.7 1.5 collective-permute-start.6
  427.2 1.2 collective-permute-done.8
  428.4 2.0 collective-permute-start.9
  430.4 3.6 collective-permute-done.14
  434.0 2.0 collective-permute-start.15
  436.0 0.0 collective-permute-done.12
  436.0 2.4 collective-permute-start.16
  438.5 1.5 collective-permute-start.13
  439.9 6.9 %collective-permute-done.9 = f32[2,32,1024]{2,1,0:T(8,128)S(1)} collective-permute-done((f32[2,32,1024]{2,1,0:T(8,128)S(1)}, f32[2,32,1024]{2,1,0:T(8,128)S(1)}, u32[]{:S(2)}, u32[]{:S(2)}) %collective-permute-start.9) | collective-permute-done | bytes 262176 | tf_op jit(solution)/shard_map/ppermute | solution.py:291
  446.8 0.1 add_add_fusion.1
  446.9 3.5 collective-permute-done.15
  450.4 0.1 add_add_fusion
  450.6 1.2 copy.5
  (21 shorter events, 0.3 us)
Async XLA Ops:
  5.4 5.1 %copy-start = (f32[8,2,2,7,32,512]{5,4,3,2,1,0:T(8,128)}, f32[8,2,2,7,32,512]{5,4,3,2,1,0:T(8,128)S(1)}, u32[]{:S(2)}) copy-start(f32[8,2,2,7,32,512]{5,4,3,2,1,0:T(8,128)S(1)} %shard_map.29) | copy-start | bytes 44040196
  10.4 267.7 %all-to-all-start.1 = ((f32[16,2,7,32,512]{4,3,2,1,0:T(8,128)}), f32[16,2,7,32,512]{4,3,2,1,0:T(8,128)}, u32[]{:S(2)}, u32[]{:S(2)}) async-start(f32[16,2,7,32,512]{4,3,2,1,0:T(8,128)} %bitcast.17), calls=%async_computation.1 | async-start | bytes 29360128 | tf_op jit(solution)/shard_map/all_to_all | solution.py:251
  17.8 333.2 %collective-permute-start.1 = (f32[1,2,8,1024,256]{4,3,2,1,0:T(8,128)}, f32[1,2,8,1024,256]{4,3,2,1,0:T(8,128)}, u32[]{:S(2)}, u32[]{:S(2)}) collective-permute-start(f32[1,2,8,1024,256]{4,3,2,1,0:T(8,128)} %param.2), channel_id=1, source_target_pairs={{0,1},{1,0},{2,3},{3,2},{4,5},{5,4},{6,7},{7,6},{8,9},{9,8},{10,11... | collective-permute-start | bytes 50331656 | tf_op jit(solution)/shard_map/ppermute | solution.py:21
  278.1 111.7 %all-to-all-start = ((f32[16,2,1,32,512]{4,3,1,2,0:T(8,128)}), f32[16,2,1,32,512]{4,3,1,2,0:T(8,128)S(1)}, u32[]{:S(2)}, u32[]{:S(2)}) async-start(f32[16,2,1,32,512]{4,3,1,2,0:T(8,128)} %bitcast.4), calls=%async_computation | async-start | bytes 4194304 | tf_op jit(solution)/shard_map/all_to_all | solution.py:251
  350.5 6.9 %collective-permute-start = (f32[7,2,256,256]{3,2,1,0:T(8,128)}, f32[7,2,256,256]{3,2,1,0:T(8,128)}, u32[]{:S(2)}, u32[]{:S(2)}) collective-permute-start(f32[7,2,256,256]{3,2,1,0:T(8,128)} %shard_map.30.own_core), channel_id=1, source_target_pairs={{0,1},{1,0},{2,3},{3,2},{4,5},{5,4},{6,7},{7,6},{8,9},{9,8},{10,11... | collective-permute-start | bytes 11010056 | tf_op jit(solution)/shard_map/ppermute | solution.py:21
  387.1 1.3 copy-start.3
  388.5 1.3 copy-start.1
  389.8 3.0 copy-start.2
  390.8 9.9 %copy-start.4 = (f32[2,256,1024]{2,1,0:T(8,128)S(1)}, f32[2,256,1024]{2,1,0:T(8,128)}, u32[]{:S(2)}) copy-start(f32[2,256,1024]{2,1,0:T(8,128)} %copy-done.3) | copy-start | bytes 6291460
  390.8 2.0 collective-permute-start.2
  396.7 9.2 %collective-permute-start.3 = (f32[2,32,1024]{2,1,0:T(8,128)S(1)}, f32[2,32,1024]{2,1,0:T(8,128)S(1)}, u32[]{:S(2)}, u32[]{:S(2)}) collective-permute-start(f32[2,32,1024]{2,1,0:T(8,128)S(1)} %get-tuple-element.61), channel_id=1, source_target_pairs={{0,2},{2,0},{4,6},{6,4},{8,10},{10,8},{12,14},{14,12},{1,3},{3,1},... | collective-permute-start | bytes 786440 | tf_op jit(solution)/shard_map/ppermute | solution.py:291
  398.6 12.9 %collective-permute-start.7 = (f32[2,32,1024]{2,1,0:T(8,128)S(1)}, f32[2,32,1024]{2,1,0:T(8,128)S(1)}, u32[]{:S(2)}, u32[]{:S(2)}) collective-permute-start(f32[2,32,1024]{2,1,0:T(8,128)S(1)} %get-tuple-element.68), channel_id=1, source_target_pairs={{0,2},{2,0},{4,6},{6,4},{8,10},{10,8},{12,14},{14,12},{1,3},{3,1},... | collective-permute-start | bytes 786440 | tf_op jit(solution)/shard_map/ppermute | solution.py:291
  398.8 18.3 %collective-permute-start.10 = (f32[2,32,1024]{2,1,0:T(8,128)S(1)}, f32[2,32,1024]{2,1,0:T(8,128)S(1)}, u32[]{:S(2)}, u32[]{:S(2)}) collective-permute-start(f32[2,32,1024]{2,1,0:T(8,128)S(1)} %get-tuple-element.72), channel_id=1, source_target_pairs={{0,2},{2,0},{4,6},{6,4},{8,10},{10,8},{12,14},{14,12},{1,3},{3,1},... | collective-permute-start | bytes 786440 | tf_op jit(solution)/shard_map/ppermute | solution.py:291
  405.9 16.8 %collective-permute-start.4 = (f32[2,32,1024]{2,1,0:T(8,128)S(1)}, f32[2,32,1024]{2,1,0:T(8,128)S(1)}, u32[]{:S(2)}, u32[]{:S(2)}) collective-permute-start(f32[2,32,1024]{2,1,0:T(8,128)S(1)} %get-tuple-element.62), channel_id=1, source_target_pairs={{0,2},{2,0},{4,6},{6,4},{8,10},{10,8},{12,14},{14,12},{1,3},{3,1},... | collective-permute-start | bytes 786440 | tf_op jit(solution)/shard_map/ppermute | solution.py:291
  407.9 14.9 %collective-permute-start.5 = (f32[2,32,1024]{2,1,0:T(8,128)S(1)}, f32[2,32,1024]{2,1,0:T(8,128)S(1)}, u32[]{:S(2)}, u32[]{:S(2)}) collective-permute-start(f32[2,32,1024]{2,1,0:T(8,128)S(1)} %add.42), channel_id=1, source_target_pairs={{0,4},{2,6},{4,0},{6,2},{8,12},{10,14},{12,8},{14,10},{1,5},{3,7},... | collective-permute-start | bytes 786440 | tf_op jit(solution)/shard_map/ppermute | solution.py:291
  411.6 16.8 %collective-permute-start.8 = (f32[2,32,1024]{2,1,0:T(8,128)S(1)}, f32[2,32,1024]{2,1,0:T(8,128)S(1)}, u32[]{:S(2)}, u32[]{:S(2)}) collective-permute-start(f32[2,32,1024]{2,1,0:T(8,128)S(1)} %get-tuple-element.69), channel_id=1, source_target_pairs={{0,2},{2,0},{4,6},{6,4},{8,10},{10,8},{12,14},{14,12},{1,3},{3,1},... | collective-permute-start | bytes 786440 | tf_op jit(solution)/shard_map/ppermute | solution.py:291
  417.2 16.8 %collective-permute-start.14 = (f32[2,32,1024]{2,1,0:T(8,128)S(1)}, f32[2,32,1024]{2,1,0:T(8,128)S(1)}, u32[]{:S(2)}, u32[]{:S(2)}) collective-permute-start(f32[2,32,1024]{2,1,0:T(8,128)S(1)} %get-tuple-element.80), channel_id=1, source_target_pairs={{0,2},{2,0},{4,6},{6,4},{8,10},{10,8},{12,14},{14,12},{1,3},{3,1},... | collective-permute-start | bytes 786440 | tf_op jit(solution)/shard_map/ppermute | solution.py:291
  419.1 16.9 %collective-permute-start.12 = (f32[2,32,1024]{2,1,0:T(8,128)S(1)}, f32[2,32,1024]{2,1,0:T(8,128)S(1)}, u32[]{:S(2)}, u32[]{:S(2)}) collective-permute-start(f32[2,32,1024]{2,1,0:T(8,128)S(1)} %add.45), channel_id=1, source_target_pairs={{0,4},{2,6},{4,0},{6,2},{8,12},{10,14},{12,8},{14,10},{1,5},{3,7},... | collective-permute-start | bytes 786440 | tf_op jit(solution)/shard_map/ppermute | solution.py:291
  422.8 15.6 %collective-permute-start.11 = (f32[2,32,1024]{2,1,0:T(8,128)S(1)}, f32[2,32,1024]{2,1,0:T(8,128)S(1)}, u32[]{:S(2)}, u32[]{:S(2)}) collective-permute-start(f32[2,32,1024]{2,1,0:T(8,128)S(1)} %add.49), channel_id=1, source_target_pairs={{0,8},{2,10},{4,12},{6,14},{8,0},{10,2},{12,4},{14,6},{1,9},{3,11}... | collective-permute-start | bytes 786440 | tf_op jit(solution)/shard_map/ppermute | solution.py:291
  425.7 14.2 %collective-permute-start.6 = (f32[2,32,1024]{2,1,0:T(8,128)S(1)}, f32[2,32,1024]{2,1,0:T(8,128)S(1)}, u32[]{:S(2)}, u32[]{:S(2)}) collective-permute-start(f32[2,32,1024]{2,1,0:T(8,128)S(1)} %get-tuple-element.64), channel_id=1, source_target_pairs={{0,2},{2,0},{4,6},{6,4},{8,10},{10,8},{12,14},{14,12},{1,3},{3,1},... | collective-permute-start | bytes 786440 | tf_op jit(solution)/shard_map/ppermute | solution.py:291
  428.4 18.4 %collective-permute-start.9 = (f32[2,32,1024]{2,1,0:T(8,128)S(1)}, f32[2,32,1024]{2,1,0:T(8,128)S(1)}, u32[]{:S(2)}, u32[]{:S(2)}) collective-permute-start(f32[2,32,1024]{2,1,0:T(8,128)S(1)} %add.46), channel_id=1, source_target_pairs={{0,4},{2,6},{4,0},{6,2},{8,12},{10,14},{12,8},{14,10},{1,5},{3,7},... | collective-permute-start | bytes 786440 | tf_op jit(solution)/shard_map/ppermute | solution.py:291
  434.0 16.4 %collective-permute-start.15 = (f32[2,32,1024]{2,1,0:T(8,128)S(1)}, f32[2,32,1024]{2,1,0:T(8,128)S(1)}, u32[]{:S(2)}, u32[]{:S(2)}) collective-permute-start(f32[2,32,1024]{2,1,0:T(8,128)S(1)} %add.52), channel_id=1, source_target_pairs={{0,4},{2,6},{4,0},{6,2},{8,12},{10,14},{12,8},{14,10},{1,5},{3,7},... | collective-permute-start | bytes 786440 | tf_op jit(solution)/shard_map/ppermute | solution.py:291
  436.0 14.4 %collective-permute-start.16 = (f32[2,32,1024]{2,1,0:T(8,128)S(1)}, f32[2,32,1024]{2,1,0:T(8,128)S(1)}, u32[]{:S(2)}, u32[]{:S(2)}) collective-permute-start(f32[2,32,1024]{2,1,0:T(8,128)S(1)} %add.54), channel_id=1, source_target_pairs={{0,8},{2,10},{4,12},{6,14},{8,0},{10,2},{12,4},{14,6},{1,9},{3,11}... | collective-permute-start | bytes 786440 | tf_op jit(solution)/shard_map/ppermute | solution.py:291
  438.5 12.0 %collective-permute-start.13 = (f32[2,32,1024]{2,1,0:T(8,128)S(1)}, f32[2,32,1024]{2,1,0:T(8,128)S(1)}, u32[]{:S(2)}, u32[]{:S(2)}) collective-permute-start(f32[2,32,1024]{2,1,0:T(8,128)S(1)} %get-tuple-element.78), channel_id=1, source_target_pairs={{0,2},{2,0},{4,6},{6,4},{8,10},{10,8},{12,14},{14,12},{1,3},{3,1},... | collective-permute-start | bytes 786440 | tf_op jit(solution)/shard_map/ppermute | solution.py:291

commit v13 on v9

--- a/solution.py
+++ b/solution.py
@@ -13,6 +13,7 @@
 PIECES = 2
 WINDOW = 4
 ANYWHERE = pl.BlockSpec(memory_space=pl.ANY)
+IN_HBM = pl.BlockSpec(memory_space=pltpu.HBM)
 IN_VMEM = pl.BlockSpec(memory_space=pltpu.VMEM)
 IN_SMEM = pl.BlockSpec(memory_space=pltpu.SMEM)
 
@@ -145,7 +146,7 @@
     own_split, other_split, own_flat, other_flat = refs[:4]
     before = refs[4 : 4 + n_before]
     outs = refs[4 + n_before : 4 + n_before + n_out]
-    first, second, product, sems, *more = refs[4 + n_before + n_out :]
+    first, second, product, sems = refs[4 + n_before + n_out :]
     half, idx = place[0], place[1]
     _, _, groups, own_rows, inner = first.shape
     rows, columns = groups * own_rows, second.shape[2]
@@ -169,11 +170,7 @@
                     first_copy(lower, b, position, slot).start()
                 second_copy(lower, b).start()
 
-    if n_before:
-        held, held_sem = more
-        loading = pltpu.make_async_copy(before[0], held, held_sem)
-        loading.start()
-    else:
+    if not n_before:
         for out in outs:
             out[...] = jnp.zeros_like(out)
     piece = rows // n_out
@@ -191,8 +188,6 @@
         for part, value in enumerate((real, imag, real + imag)):
             product[part] = left_stack(value, 1)
         second_copy(True, b).wait()
-        if n_before:
-            loading.wait()
         for at in range(0, columns, 256):
             spot = slice(at, at + 256)
             right_real, right_imag = second[b, 0, spot], second[b, 1, spot]
@@ -201,7 +196,7 @@
             three = dot_stacks(product[2], right_stack(right_real + right_imag, 1), NT)
             for plane, value in enumerate((one - two, three - one - two)):
                 if n_before:
-                    value = value + held[plane, :, spot]
+                    value = value + before[0][plane, :, spot]
                 for number, out in enumerate(outs):
                     part = value[number * piece : (number + 1) * piece]
                     if n_before:
@@ -232,6 +227,7 @@
     depth = idx_size // 2
     right = right_factor.reshape(2, idx_size, local_batch, inner_part, between)
     params = pltpu.CompilerParams(vmem_limit_bytes=44 * MIB)
+    small = pltpu.CompilerParams(vmem_limit_bytes=20 * MIB)
     shape = (2, local_batch, idx_size, 2, own_rows, inner)
     own_left = left_factor.reshape(shape)
 
@@ -261,7 +257,7 @@
                 pltpu.SemaphoreType.DMA((count, 4)),
             ],
             cost_estimate=BRIEF,
-            compiler_params=params,
+            compiler_params=params if count > 1 else small,
         )(arrived, *after)
 
     def added(start, count, slots, n_out, core, other_core, other_left, before):
@@ -270,18 +266,16 @@
         return pl.pallas_call(
             functools.partial(amplitude_kernel, start, count, slots, len(before), n_out),
             out_shape=[jax.ShapeDtypeStruct((2, kept_rows // n_out, rows), jnp.float32)] * n_out,
-            in_specs=[IN_SMEM, IN_VMEM, IN_VMEM] + [ANYWHERE] * (4 + len(before)),
+            in_specs=[IN_SMEM, IN_VMEM, IN_VMEM] + [IN_HBM] * 4 + [IN_VMEM] * len(before),
             out_specs=[IN_VMEM] * n_out,
             scratch_shapes=[
                 pltpu.VMEM((count, 2, len(slots), own_rows, inner), jnp.float32),
                 pltpu.VMEM((count, 2, rows, inner), jnp.float32),
                 pltpu.VMEM((3, kept_rows, 3 * inner), jnp.bfloat16),
                 pltpu.SemaphoreType.DMA((2, count)),
-            ]
-            + [pltpu.VMEM(part.shape, jnp.float32) for part in before]
-            + [pltpu.SemaphoreType.DMA] * len(before),
+            ],
             cost_estimate=BRIEF,
-            compiler_params=params,
+            compiler_params=small if before else params,
         )(
             place, core, other_core, own_left, other_left,
             own_left.reshape(flat), other_left.reshape(flat), *before,

time: 451 us -> 456 us (1.011)
  local copies, waits for them, and re-layouts: 8.91 us -> 14.7 us
    unnamed x10 -> x12, local copies, waits for them, and re-layouts: 7.71 us -> 13.5 us
where the time goes in v13:
time: 456 us
  waiting for transfers between devices  289 us (63%)
  starting transfers between devices  94.1 us (21%)
  Pallas kernels  57.6 us (13%)
  local copies, waits for them, and re-layouts  14.7 us (3%)
    all_to_all x2, waiting for transfers between devices, sent(): lax.all_to_all(flat, ('idx', 'half'), 0, 0, tiled=True)  257 us
    all_to_all x2, starting transfers between devices, sent(): lax.all_to_all(flat, ('idx', 'half'), 0, 0, tiled=True)  69.2 us
    pallas_call x3, Pallas kernels, added(): pl.pallas_call(functools.partial(amplitude_kernel, start, count, slots, l...  37.7 us
    ppermute x14, waiting for transfers between devices, hop(): return lax.ppermute(x, 'idx', [(i, i ^ mask) for i in range(idx_size)])  24.1 us
    ppermute x14, starting transfers between devices, hop(): return lax.ppermute(x, 'idx', [(i, i ^ mask) for i in range(idx_size)])  23.6 us
    unnamed x12, local copies, waits for them, and re-layouts  13.5 us
    pallas_call x2, Pallas kernels, core_of(): pl.pallas_call(functools.partial(core_kernel, count, scale), out_shape=ja...  11.6 us
  transfers between devices with their start and end apart: 19, of which 11 were waited for; matrix products, arithmetic and copies ran while one was open for 0% of the time, Pallas kernels for 10%

profile of v13, /device:TPU:0, one launch (start us, length us, event | category | flops | bytes accessed | tf_op | source)
XLA Modules:
  0.0 455.8 jit_solution(519403732542049558)
XLA Ops:
  0.0 5.3 %shard_map.29 = f32[8,2,2,7,32,512]{5,4,3,2,1,0:T(8,128)S(1)} custom-call(f32[2,8,8,32,1024]{4,3,2,1,0:T(8,128)} %bitcast.25), custom_call_target="tpu_custom_call" | custom-call | bytes 1024 | tf_op jit(solution)/shard_map/pallas_call | solution.py:235
  5.4 5.1 %copy-done.1 = f32[8,2,2,7,32,512]{5,4,3,2,1,0:T(8,128)} copy-done((f32[8,2,2,7,32,512]{5,4,3,2,1,0:T(8,128)}, f32[8,2,2,7,32,512]{5,4,3,2,1,0:T(8,128)S(1)}, u32[]{:S(2)}) %copy-start.1) | copy-done | bytes 14680088
  10.4 7.4 %all-to-all-start.1 = ((f32[16,2,7,32,512]{4,3,2,1,0:T(8,128)}), f32[16,2,7,32,512]{4,3,2,1,0:T(8,128)}, u32[]{:S(2)}, u32[]{:S(2)}) async-start(f32[16,2,7,32,512]{4,3,2,1,0:T(8,128)} %bitcast.23), calls=%async_computation.1 | async-start | bytes 29360128 | tf_op jit(solution)/shard_map/all_to_all | solution.py:247
  17.9 0.4 collective-permute-start.1
  18.2 2.9 shard_map.28
  21.1 257.0 %all-to-all-done.1 = f32[16,2,7,32,512]{4,3,2,1,0:T(8,128)} async-done(((f32[16,2,7,32,512]{4,3,2,1,0:T(8,128)}), f32[16,2,7,32,512]{4,3,2,1,0:T(8,128)}, u32[]{:S(2)}, u32[]{:S(2)}) %all-to-all-start.1) | async-done | bytes 14680096 | tf_op jit(solution)/shard_map/all_to_all | solution.py:247
  278.1 61.8 %all-to-all-start = ((f32[16,2,1,32,512]{4,3,1,2,0:T(8,128)}), f32[16,2,1,32,512]{4,3,1,2,0:T(8,128)S(1)}, u32[]{:S(2)}, u32[]{:S(2)}) async-start(f32[16,2,1,32,512]{4,3,1,2,0:T(8,128)} %bitcast.4), calls=%async_computation | async-start | bytes 4194304 | tf_op jit(solution)/shard_map/all_to_all | solution.py:247
  339.9 10.6 %shard_map.30.own_core = f32[7,2,256,256]{3,2,1,0:T(8,128)} custom-call(f32[8,2,2,7,32,512]{5,4,3,2,1,0:T(8,128)} %bitcast.7.arrived), custom_call_target="tpu_custom_call" | custom-call | bytes 1024 | tf_op jit(solution)/shard_map/pallas_call | solution.py:250
  350.5 0.5 collective-permute-start
  351.0 0.1 pad_add_fusion.place
  351.1 6.3 %collective-permute-done.other_core = f32[7,2,256,256]{3,2,1,0:T(8,128)} collective-permute-done((f32[7,2,256,256]{3,2,1,0:T(8,128)}, f32[7,2,256,256]{3,2,1,0:T(8,128)}, u32[]{:S(2)}, u32[]{:S(2)}) %collective-permute-start) | collective-permute-done | bytes 3670048 | tf_op jit(solution)/shard_map/ppermute | solution.py:22
  357.4 29.7 %shard_map.31 = (f32[2,256,1024]{2,1,0:T(8,128)S(1)}, f32[2,256,1024]{2,1,0:T(8,128)S(1)}) custom-call(s32[2]{0:T(128)S(1)} %pad_add_fusion.place, f32[7,2,256,256]{3,2,1,0:T(8,128)} %shard_map.30.own_core, f32[7,2,256,256]{3,2,1,0:T(8,128)} %collective-permute-done.other_core, f32[2,8,8,2,64,256]{5,4,3,2,1,0:T(8,128)} %bitcast.17, ...), custom_call_target="tpu_custom_call" | custom-call | bytes 1024 | tf_op jit(solution)/shard_map/pallas_call | solution.py:266
  387.1 1.3 copy-done.4
  388.5 1.3 copy-done.2
  389.8 1.0 shard_map.32.own_core
  390.8 0.4 collective-permute-start.2
  391.2 1.5 collective-permute-done.2.other_core
  392.8 5.8 %copy-done = f32[1,2,8,1024,256]{4,3,2,1,0:T(8,128)S(1)} copy-done((f32[1,2,8,1024,256]{4,3,2,1,0:T(8,128)S(1)}, f32[1,2,8,1024,256]{4,3,2,1,0:T(8,128)}, u32[]{:S(2)}) %copy-start) | copy-done | bytes 16777240
  398.5 3.9 shard_map.33
  402.5 1.9 collective-permute-start.4
  404.4 0.1 collective-permute-start.11
  404.6 4.0 shard_map.34
  408.6 3.1 collective-permute-done.4
  411.7 2.0 collective-permute-start.7
  413.7 0.1 collective-permute-start.3
  413.8 1.9 collective-permute-start.5
  415.7 1.5 collective-permute-start.10
  417.2 0.1 collective-permute-done.11
  417.4 2.0 collective-permute-start.14
  419.3 3.6 collective-permute-done.7
  422.9 1.9 collective-permute-start.12
  424.9 3.7 collective-permute-done.3
  428.6 1.9 collective-permute-start.8
  430.5 0.0 collective-permute-done.5
  430.6 2.4 collective-permute-start.9
  433.0 1.2 collective-permute-done.10
  434.2 1.9 collective-permute-start.6
  436.1 3.7 collective-permute-done.14
  439.8 2.0 collective-permute-start.15
  441.8 0.0 collective-permute-done.12
  441.8 2.4 collective-permute-start.16
  444.3 1.5 collective-permute-start.13
  445.8 0.0 collective-permute-done.9
  445.8 0.1 add_add_fusion.1
  445.8 6.5 %collective-permute-done.15 = f32[2,32,1024]{2,1,0:T(8,128)S(1)} collective-permute-done((f32[2,32,1024]{2,1,0:T(8,128)S(1)}, f32[2,32,1024]{2,1,0:T(8,128)S(1)}, u32[]{:S(2)}, u32[]{:S(2)}) %collective-permute-start.15) | collective-permute-done | bytes 262176 | tf_op jit(solution)/shard_map/ppermute | solution.py:285
  452.3 2.2 collective-permute-done.16
  454.5 0.1 add_add_fusion
  454.6 1.2 copy.5
  (23 shorter events, 0.3 us)
Async XLA Ops:
  5.4 5.1 %copy-start.1 = (f32[8,2,2,7,32,512]{5,4,3,2,1,0:T(8,128)}, f32[8,2,2,7,32,512]{5,4,3,2,1,0:T(8,128)S(1)}, u32[]{:S(2)}) copy-start(f32[8,2,2,7,32,512]{5,4,3,2,1,0:T(8,128)S(1)} %shard_map.29) | copy-start | bytes 44040196
  10.4 267.7 %all-to-all-start.1 = ((f32[16,2,7,32,512]{4,3,2,1,0:T(8,128)}), f32[16,2,7,32,512]{4,3,2,1,0:T(8,128)}, u32[]{:S(2)}, u32[]{:S(2)}) async-start(f32[16,2,7,32,512]{4,3,2,1,0:T(8,128)} %bitcast.23), calls=%async_computation.1 | async-start | bytes 29360128 | tf_op jit(solution)/shard_map/all_to_all | solution.py:247
  17.9 333.2 %collective-permute-start.1 = (f32[1,2,8,1024,256]{4,3,2,1,0:T(8,128)}, f32[1,2,8,1024,256]{4,3,2,1,0:T(8,128)}, u32[]{:S(2)}, u32[]{:S(2)}) collective-permute-start(f32[1,2,8,1024,256]{4,3,2,1,0:T(8,128)} %param.2), channel_id=1, source_target_pairs={{0,1},{1,0},{2,3},{3,2},{4,5},{5,4},{6,7},{7,6},{8,9},{9,8},{10,11... | collective-permute-start | bytes 50331656 | tf_op jit(solution)/shard_map/ppermute | solution.py:22
  278.1 111.7 %all-to-all-start = ((f32[16,2,1,32,512]{4,3,1,2,0:T(8,128)}), f32[16,2,1,32,512]{4,3,1,2,0:T(8,128)S(1)}, u32[]{:S(2)}, u32[]{:S(2)}) async-start(f32[16,2,1,32,512]{4,3,1,2,0:T(8,128)} %bitcast.4), calls=%async_computation | async-start | bytes 4194304 | tf_op jit(solution)/shard_map/all_to_all | solution.py:247
  350.5 6.8 %collective-permute-start = (f32[7,2,256,256]{3,2,1,0:T(8,128)}, f32[7,2,256,256]{3,2,1,0:T(8,128)}, u32[]{:S(2)}, u32[]{:S(2)}) collective-permute-start(f32[7,2,256,256]{3,2,1,0:T(8,128)} %shard_map.30.own_core), channel_id=1, source_target_pairs={{0,1},{1,0},{2,3},{3,2},{4,5},{5,4},{6,7},{7,6},{8,9},{9,8},{10,11... | collective-permute-start | bytes 11010056 | tf_op jit(solution)/shard_map/ppermute | solution.py:22
  387.1 1.3 copy-start.4
  388.5 1.3 copy-start.2
  389.8 3.0 copy-start.3
  390.8 2.0 collective-permute-start.2
  392.8 5.8 %copy-start = (f32[1,2,8,1024,256]{4,3,2,1,0:T(8,128)S(1)}, f32[1,2,8,1024,256]{4,3,2,1,0:T(8,128)}, u32[]{:S(2)}) copy-start(f32[1,2,8,1024,256]{4,3,2,1,0:T(8,128)} %param.2) | copy-start | bytes 50331652
  398.5 6.0 %copy-start.5 = (f32[2,256,1024]{2,1,0:T(8,128)S(1)}, f32[2,256,1024]{2,1,0:T(8,128)}, u32[]{:S(2)}) copy-start(f32[2,256,1024]{2,1,0:T(8,128)} %copy-done.4) | copy-start | bytes 6291460
  402.5 9.2 %collective-permute-start.4 = (f32[2,32,1024]{2,1,0:T(8,128)S(1)}, f32[2,32,1024]{2,1,0:T(8,128)S(1)}, u32[]{:S(2)}, u32[]{:S(2)}) collective-permute-start(f32[2,32,1024]{2,1,0:T(8,128)S(1)} %get-tuple-element.61), channel_id=1, source_target_pairs={{0,2},{2,0},{4,6},{6,4},{8,10},{10,8},{12,14},{14,12},{1,3},{3,1},... | collective-permute-start | bytes 786440 | tf_op jit(solution)/shard_map/ppermute | solution.py:285
  404.4 12.9 %collective-permute-start.11 = (f32[2,32,1024]{2,1,0:T(8,128)S(1)}, f32[2,32,1024]{2,1,0:T(8,128)S(1)}, u32[]{:S(2)}, u32[]{:S(2)}) collective-permute-start(f32[2,32,1024]{2,1,0:T(8,128)S(1)} %get-tuple-element.74), channel_id=1, source_target_pairs={{0,2},{2,0},{4,6},{6,4},{8,10},{10,8},{12,14},{14,12},{1,3},{3,1},... | collective-permute-start | bytes 786440 | tf_op jit(solution)/shard_map/ppermute | solution.py:285
  411.7 11.2 %collective-permute-start.7 = (f32[2,32,1024]{2,1,0:T(8,128)S(1)}, f32[2,32,1024]{2,1,0:T(8,128)S(1)}, u32[]{:S(2)}, u32[]{:S(2)}) collective-permute-start(f32[2,32,1024]{2,1,0:T(8,128)S(1)} %get-tuple-element.65), channel_id=1, source_target_pairs={{0,2},{2,0},{4,6},{6,4},{8,10},{10,8},{12,14},{14,12},{1,3},{3,1},... | collective-permute-start | bytes 786440 | tf_op jit(solution)/shard_map/ppermute | solution.py:285
  413.7 14.8 %collective-permute-start.3 = (f32[2,32,1024]{2,1,0:T(8,128)S(1)}, f32[2,32,1024]{2,1,0:T(8,128)S(1)}, u32[]{:S(2)}, u32[]{:S(2)}) collective-permute-start(f32[2,32,1024]{2,1,0:T(8,128)S(1)} %get-tuple-element.58), channel_id=1, source_target_pairs={{0,2},{2,0},{4,6},{6,4},{8,10},{10,8},{12,14},{14,12},{1,3},{3,1},... | collective-permute-start | bytes 786440 | tf_op jit(solution)/shard_map/ppermute | solution.py:285
  413.8 16.7 %collective-permute-start.5 = (f32[2,32,1024]{2,1,0:T(8,128)S(1)}, f32[2,32,1024]{2,1,0:T(8,128)S(1)}, u32[]{:S(2)}, u32[]{:S(2)}) collective-permute-start(f32[2,32,1024]{2,1,0:T(8,128)S(1)} %add.43), channel_id=1, source_target_pairs={{0,4},{2,6},{4,0},{6,2},{8,12},{10,14},{12,8},{14,10},{1,5},{3,7},... | collective-permute-start | bytes 786440 | tf_op jit(solution)/shard_map/ppermute | solution.py:285
  415.7 18.4 %collective-permute-start.10 = (f32[2,32,1024]{2,1,0:T(8,128)S(1)}, f32[2,32,1024]{2,1,0:T(8,128)S(1)}, u32[]{:S(2)}, u32[]{:S(2)}) collective-permute-start(f32[2,32,1024]{2,1,0:T(8,128)S(1)} %get-tuple-element.71), channel_id=1, source_target_pairs={{0,2},{2,0},{4,6},{6,4},{8,10},{10,8},{12,14},{14,12},{1,3},{3,1},... | collective-permute-start | bytes 786440 | tf_op jit(solution)/shard_map/ppermute | solution.py:285
  417.4 22.4 %collective-permute-start.14 = (f32[2,32,1024]{2,1,0:T(8,128)S(1)}, f32[2,32,1024]{2,1,0:T(8,128)S(1)}, u32[]{:S(2)}, u32[]{:S(2)}) collective-permute-start(f32[2,32,1024]{2,1,0:T(8,128)S(1)} %get-tuple-element.78), channel_id=1, source_target_pairs={{0,2},{2,0},{4,6},{6,4},{8,10},{10,8},{12,14},{14,12},{1,3},{3,1},... | collective-permute-start | bytes 786440 | tf_op jit(solution)/shard_map/ppermute | solution.py:285
  422.9 18.9 %collective-permute-start.12 = (f32[2,32,1024]{2,1,0:T(8,128)S(1)}, f32[2,32,1024]{2,1,0:T(8,128)S(1)}, u32[]{:S(2)}, u32[]{:S(2)}) collective-permute-start(f32[2,32,1024]{2,1,0:T(8,128)S(1)} %add.50), channel_id=1, source_target_pairs={{0,4},{2,6},{4,0},{6,2},{8,12},{10,14},{12,8},{14,10},{1,5},{3,7},... | collective-permute-start | bytes 786440 | tf_op jit(solution)/shard_map/ppermute | solution.py:285
  428.6 15.7 %collective-permute-start.8 = (f32[2,32,1024]{2,1,0:T(8,128)S(1)}, f32[2,32,1024]{2,1,0:T(8,128)S(1)}, u32[]{:S(2)}, u32[]{:S(2)}) collective-permute-start(f32[2,32,1024]{2,1,0:T(8,128)S(1)} %add.45), channel_id=1, source_target_pairs={{0,4},{2,6},{4,0},{6,2},{8,12},{10,14},{12,8},{14,10},{1,5},{3,7},... | collective-permute-start | bytes 786440 | tf_op jit(solution)/shard_map/ppermute | solution.py:285
  430.6 15.2 %collective-permute-start.9 = (f32[2,32,1024]{2,1,0:T(8,128)S(1)}, f32[2,32,1024]{2,1,0:T(8,128)S(1)}, u32[]{:S(2)}, u32[]{:S(2)}) collective-permute-start(f32[2,32,1024]{2,1,0:T(8,128)S(1)} %add.47), channel_id=1, source_target_pairs={{0,8},{2,10},{4,12},{6,14},{8,0},{10,2},{12,4},{14,6},{1,9},{3,11}... | collective-permute-start | bytes 786440 | tf_op jit(solution)/shard_map/ppermute | solution.py:285
  434.2 11.6 %collective-permute-start.6 = (f32[2,32,1024]{2,1,0:T(8,128)S(1)}, f32[2,32,1024]{2,1,0:T(8,128)S(1)}, u32[]{:S(2)}, u32[]{:S(2)}) collective-permute-start(f32[2,32,1024]{2,1,0:T(8,128)S(1)} %get-tuple-element.62), channel_id=1, source_target_pairs={{0,2},{2,0},{4,6},{6,4},{8,10},{10,8},{12,14},{14,12},{1,3},{3,1},... | collective-permute-start | bytes 786440 | tf_op jit(solution)/shard_map/ppermute | solution.py:285
  439.8 12.5 %collective-permute-start.15 = (f32[2,32,1024]{2,1,0:T(8,128)S(1)}, f32[2,32,1024]{2,1,0:T(8,128)S(1)}, u32[]{:S(2)}, u32[]{:S(2)}) collective-permute-start(f32[2,32,1024]{2,1,0:T(8,128)S(1)} %add.52), channel_id=1, source_target_pairs={{0,4},{2,6},{4,0},{6,2},{8,12},{10,14},{12,8},{14,10},{1,5},{3,7},... | collective-permute-start | bytes 786440 | tf_op jit(solution)/shard_map/ppermute | solution.py:285
  441.8 12.7 %collective-permute-start.16 = (f32[2,32,1024]{2,1,0:T(8,128)S(1)}, f32[2,32,1024]{2,1,0:T(8,128)S(1)}, u32[]{:S(2)}, u32[]{:S(2)}) collective-permute-start(f32[2,32,1024]{2,1,0:T(8,128)S(1)} %add.54), channel_id=1, source_target_pairs={{0,8},{2,10},{4,12},{6,14},{8,0},{10,2},{12,4},{14,6},{1,9},{3,11}... | collective-permute-start | bytes 786440 | tf_op jit(solution)/shard_map/ppermute | solution.py:285
  444.3 10.2 %collective-permute-start.13 = (f32[2,32,1024]{2,1,0:T(8,128)S(1)}, f32[2,32,1024]{2,1,0:T(8,128)S(1)}, u32[]{:S(2)}, u32[]{:S(2)}) collective-permute-start(f32[2,32,1024]{2,1,0:T(8,128)S(1)} %get-tuple-element.75), channel_id=1, source_target_pairs={{0,2},{2,0},{4,6},{6,4},{8,10},{10,8},{12,14},{14,12},{1,3},{3,1},... | collective-permute-start | bytes 786440 | tf_op jit(solution)/shard_map/ppermute | solution.py:285

commit v14 on v9

--- a/solution.py
+++ b/solution.py
@@ -145,7 +145,11 @@
     own_split, other_split, own_flat, other_flat = refs[:4]
     before = refs[4 : 4 + n_before]
     outs = refs[4 + n_before : 4 + n_before + n_out]
-    first, second, product, sems, *more = refs[4 + n_before + n_out :]
+    rest = refs[4 + n_before + n_out :]
+    if not n_before:
+        rest[0][...] = jnp.zeros_like(rest[0])
+        rest = rest[1:]
+    first, second, product, sems, *more = rest
     half, idx = place[0], place[1]
     _, _, groups, own_rows, inner = first.shape
     rows, columns = groups * own_rows, second.shape[2]
@@ -269,9 +273,10 @@
         kept_rows = len(slots) * own_rows
         return pl.pallas_call(
             functools.partial(amplitude_kernel, start, count, slots, len(before), n_out),
-            out_shape=[jax.ShapeDtypeStruct((2, kept_rows // n_out, rows), jnp.float32)] * n_out,
+            out_shape=[jax.ShapeDtypeStruct((2, kept_rows // n_out, rows), jnp.float32)] * n_out
+            + [jax.ShapeDtypeStruct((8, 128), jnp.float32)] * (not before),
             in_specs=[IN_SMEM, IN_VMEM, IN_VMEM] + [ANYWHERE] * (4 + len(before)),
-            out_specs=[IN_VMEM] * n_out,
+            out_specs=[IN_VMEM] * (n_out + (not before)),
             scratch_shapes=[
                 pltpu.VMEM((count, 2, len(slots), own_rows, inner), jnp.float32),
                 pltpu.VMEM((count, 2, rows, inner), jnp.float32),
@@ -300,7 +305,7 @@
     odd = list(range(idx_size - 1, 0, -2))
     even = [slot - 1 for slot in odd]
     sums = added(0, many, odd + even, 2, core, swapped(core, "half"), other_left, [])
-    core = core_of(few, late, (sums[0][0, :8, :128],))
+    core = core_of(few, late, (sums[2],))
     other_core = swapped(core, "half")
     leaving = added(many, few, odd, PIECES * depth, core, other_core, other_left, [sums[0]])
     core, leaving = lax.optimization_barrier((core, leaving))

time: 451 us -> 451 us (level)
  no operation moved by 1% of the time
where the time goes in v14:
time: 451 us; the launch traced here: 450 us
  waiting for transfers between devices  290 us (64%)
  starting transfers between devices  93.9 us (21%)
  Pallas kernels  57.5 us (13%)
  local copies, waits for them, and re-layouts  8.91 us (2%)
    all_to_all x2, waiting for transfers between devices, sent(): lax.all_to_all(flat, ('idx', 'half'), 0, 0, tiled=True)  257 us
    all_to_all x2, starting transfers between devices, sent(): lax.all_to_all(flat, ('idx', 'half'), 0, 0, tiled=True)  69.2 us
    pallas_call x3, Pallas kernels, added(): pl.pallas_call(functools.partial(amplitude_kernel, start, count, slots, l...  37.6 us
    ppermute x14, waiting for transfers between devices, hop(): return lax.ppermute(x, 'idx', [(i, i ^ mask) for i in range(idx_size)])  24.7 us
    ppermute x14, starting transfers between devices, hop(): return lax.ppermute(x, 'idx', [(i, i ^ mask) for i in range(idx_size)])  23.4 us
    pallas_call x2, Pallas kernels, core_of(): pl.pallas_call(functools.partial(core_kernel, count, scale), out_shape=ja...  11.6 us
  transfers between devices with their start and end apart: 19, of which 11 were waited for; matrix products, arithmetic and copies ran while one was open for 0% of the time, Pallas kernels for 10%

profile of v14, /device:TPU:0, one launch (start us, length us, event | category | flops | bytes accessed | tf_op | source)
XLA Modules:
  0.0 450.5 jit_solution(5155632865828669912)
XLA Ops:
  0.0 5.3 %shard_map.29 = f32[8,2,2,7,32,512]{5,4,3,2,1,0:T(8,128)S(1)} custom-call(f32[2,8,8,32,1024]{4,3,2,1,0:T(8,128)} %bitcast.23), custom_call_target="tpu_custom_call" | custom-call | bytes 1024 | tf_op jit(solution)/shard_map/pallas_call | solution.py:243
  5.4 5.1 %copy-done = f32[8,2,2,7,32,512]{5,4,3,2,1,0:T(8,128)} copy-done((f32[8,2,2,7,32,512]{5,4,3,2,1,0:T(8,128)}, f32[8,2,2,7,32,512]{5,4,3,2,1,0:T(8,128)S(1)}, u32[]{:S(2)}) %copy-start) | copy-done | bytes 14680088
  10.4 7.4 %all-to-all-start.1 = ((f32[16,2,7,32,512]{4,3,2,1,0:T(8,128)}), f32[16,2,7,32,512]{4,3,2,1,0:T(8,128)}, u32[]{:S(2)}, u32[]{:S(2)}) async-start(f32[16,2,7,32,512]{4,3,2,1,0:T(8,128)} %bitcast.15), calls=%async_computation.1 | async-start | bytes 29360128 | tf_op jit(solution)/shard_map/all_to_all | solution.py:255
  17.8 0.4 collective-permute-start.1
  18.2 2.9 shard_map.28
  21.1 257.0 %all-to-all-done.1 = f32[16,2,7,32,512]{4,3,2,1,0:T(8,128)} async-done(((f32[16,2,7,32,512]{4,3,2,1,0:T(8,128)}), f32[16,2,7,32,512]{4,3,2,1,0:T(8,128)}, u32[]{:S(2)}, u32[]{:S(2)}) %all-to-all-start.1) | async-done | bytes 14680096 | tf_op jit(solution)/shard_map/all_to_all | solution.py:255
  278.1 61.8 %all-to-all-start = ((f32[16,2,1,32,512]{4,3,1,2,0:T(8,128)}), f32[16,2,1,32,512]{4,3,1,2,0:T(8,128)S(1)}, u32[]{:S(2)}, u32[]{:S(2)}) async-start(f32[16,2,1,32,512]{4,3,1,2,0:T(8,128)} %bitcast.4), calls=%async_computation | async-start | bytes 4194304 | tf_op jit(solution)/shard_map/all_to_all | solution.py:255
  339.9 10.6 %shard_map.30.own_core = f32[7,2,256,256]{3,2,1,0:T(8,128)} custom-call(f32[8,2,2,7,32,512]{5,4,3,2,1,0:T(8,128)} %bitcast.7.arrived), custom_call_target="tpu_custom_call" | custom-call | bytes 1024 | tf_op jit(solution)/shard_map/pallas_call | solution.py:258
  350.5 0.5 collective-permute-start
  351.0 0.1 pad_add_fusion.place
  351.1 0.0 collective-permute-done.1
  351.1 6.3 %collective-permute-done.other_core = f32[7,2,256,256]{3,2,1,0:T(8,128)} collective-permute-done((f32[7,2,256,256]{3,2,1,0:T(8,128)}, f32[7,2,256,256]{3,2,1,0:T(8,128)}, u32[]{:S(2)}, u32[]{:S(2)}) %collective-permute-start) | collective-permute-done | bytes 3670048 | tf_op jit(solution)/shard_map/ppermute | solution.py:21
  357.4 29.7 %shard_map.31 = (f32[2,256,1024]{2,1,0:T(8,128)S(1)}, f32[2,256,1024]{2,1,0:T(8,128)S(1)}, f32[8,128]{1,0:T(8,128)S(1)}) custom-call(s32[2]{0:T(128)S(1)} %pad_add_fusion.place, f32[7,2,256,256]{3,2,1,0:T(8,128)} %shard_map.30.own_core, f32[7,2,256,256]{3,2,1,0:T(8,128)} %collective-permute-done.other_core, f32[2,8,8,2,64,256]{5,4,3,2,1,0:T(8,128)} %bitcast.17, ...), custom_call_target="tpu_custom_call" | custom-call | bytes 1024 | tf_op jit(solution)/shard_map/pallas_call | solution.py:274
  387.1 1.3 copy-done.1
  388.5 1.3 copy-done.3
  389.8 0.0 all-to-all-done
  389.8 1.0 shard_map.32.own_core
  390.8 0.4 collective-permute-start.2
  391.2 1.5 collective-permute-done.2.other_core
  392.8 4.0 shard_map.33
  396.8 1.9 collective-permute-start.4
  398.7 0.2 collective-permute-start.11
  398.9 3.9 shard_map.34
  402.8 3.2 collective-permute-done.4
  406.0 1.9 collective-permute-start.7
  407.9 0.1 collective-permute-start.3
  408.1 1.9 collective-permute-start.5
  410.0 1.5 collective-permute-start.10
  411.4 0.1 collective-permute-done.11
  411.6 1.9 collective-permute-start.14
  413.6 3.6 collective-permute-done.7
  417.2 1.9 collective-permute-start.12
  419.1 3.7 collective-permute-done.3
  422.8 1.9 collective-permute-start.8
  424.8 2.4 collective-permute-start.9
  427.2 1.2 collective-permute-done.10
  428.4 1.9 collective-permute-start.6
  430.3 3.7 collective-permute-done.14
  434.1 2.0 collective-permute-start.15
  436.1 2.4 collective-permute-start.16
  438.5 0.0 collective-permute-done.8
  438.5 1.5 collective-permute-start.13
  440.0 0.0 collective-permute-done.9
  440.0 0.1 add_add_fusion.1
  440.1 7.0 %collective-permute-done.15 = f32[2,32,1024]{2,1,0:T(8,128)S(1)} collective-permute-done((f32[2,32,1024]{2,1,0:T(8,128)S(1)}, f32[2,32,1024]{2,1,0:T(8,128)S(1)}, u32[]{:S(2)}, u32[]{:S(2)}) %collective-permute-start.15) | collective-permute-done | bytes 262176 | tf_op jit(solution)/shard_map/ppermute | solution.py:296
  447.0 2.1 collective-permute-done.16
  449.2 0.1 add_add_fusion
  449.3 1.2 copy.5
  (20 shorter events, 0.3 us)
Async XLA Ops:
  5.4 5.1 %copy-start = (f32[8,2,2,7,32,512]{5,4,3,2,1,0:T(8,128)}, f32[8,2,2,7,32,512]{5,4,3,2,1,0:T(8,128)S(1)}, u32[]{:S(2)}) copy-start(f32[8,2,2,7,32,512]{5,4,3,2,1,0:T(8,128)S(1)} %shard_map.29) | copy-start | bytes 44040196
  10.4 267.7 %all-to-all-start.1 = ((f32[16,2,7,32,512]{4,3,2,1,0:T(8,128)}), f32[16,2,7,32,512]{4,3,2,1,0:T(8,128)}, u32[]{:S(2)}, u32[]{:S(2)}) async-start(f32[16,2,7,32,512]{4,3,2,1,0:T(8,128)} %bitcast.15), calls=%async_computation.1 | async-start | bytes 29360128 | tf_op jit(solution)/shard_map/all_to_all | solution.py:255
  17.8 333.2 %collective-permute-start.1 = (f32[1,2,8,1024,256]{4,3,2,1,0:T(8,128)}, f32[1,2,8,1024,256]{4,3,2,1,0:T(8,128)}, u32[]{:S(2)}, u32[]{:S(2)}) collective-permute-start(f32[1,2,8,1024,256]{4,3,2,1,0:T(8,128)} %param.2), channel_id=1, source_target_pairs={{0,1},{1,0},{2,3},{3,2},{4,5},{5,4},{6,7},{7,6},{8,9},{9,8},{10,11... | collective-permute-start | bytes 50331656 | tf_op jit(solution)/shard_map/ppermute | solution.py:21
  278.1 111.7 %all-to-all-start = ((f32[16,2,1,32,512]{4,3,1,2,0:T(8,128)}), f32[16,2,1,32,512]{4,3,1,2,0:T(8,128)S(1)}, u32[]{:S(2)}, u32[]{:S(2)}) async-start(f32[16,2,1,32,512]{4,3,1,2,0:T(8,128)} %bitcast.4), calls=%async_computation | async-start | bytes 4194304 | tf_op jit(solution)/shard_map/all_to_all | solution.py:255
  350.5 6.9 %collective-permute-start = (f32[7,2,256,256]{3,2,1,0:T(8,128)}, f32[7,2,256,256]{3,2,1,0:T(8,128)}, u32[]{:S(2)}, u32[]{:S(2)}) collective-permute-start(f32[7,2,256,256]{3,2,1,0:T(8,128)} %shard_map.30.own_core), channel_id=1, source_target_pairs={{0,1},{1,0},{2,3},{3,2},{4,5},{5,4},{6,7},{7,6},{8,9},{9,8},{10,11... | collective-permute-start | bytes 11010056 | tf_op jit(solution)/shard_map/ppermute | solution.py:21
  387.1 1.3 copy-start.1
  388.5 1.3 copy-start.3
  389.8 3.0 copy-start.4
  390.8 2.0 collective-permute-start.2
  392.8 6.1 %copy-start.2 = (f32[2,256,1024]{2,1,0:T(8,128)S(1)}, f32[2,256,1024]{2,1,0:T(8,128)}, u32[]{:S(2)}) copy-start(f32[2,256,1024]{2,1,0:T(8,128)} %copy-done.1) | copy-start | bytes 6291460
  396.8 9.2 %collective-permute-start.4 = (f32[2,32,1024]{2,1,0:T(8,128)S(1)}, f32[2,32,1024]{2,1,0:T(8,128)S(1)}, u32[]{:S(2)}, u32[]{:S(2)}) collective-permute-start(f32[2,32,1024]{2,1,0:T(8,128)S(1)} %get-tuple-element.63), channel_id=1, source_target_pairs={{0,2},{2,0},{4,6},{6,4},{8,10},{10,8},{12,14},{14,12},{1,3},{3,1},... | collective-permute-start | bytes 786440 | tf_op jit(solution)/shard_map/ppermute | solution.py:296
  398.7 12.9 %collective-permute-start.11 = (f32[2,32,1024]{2,1,0:T(8,128)S(1)}, f32[2,32,1024]{2,1,0:T(8,128)S(1)}, u32[]{:S(2)}, u32[]{:S(2)}) collective-permute-start(f32[2,32,1024]{2,1,0:T(8,128)S(1)} %get-tuple-element.76), channel_id=1, source_target_pairs={{0,2},{2,0},{4,6},{6,4},{8,10},{10,8},{12,14},{14,12},{1,3},{3,1},... | collective-permute-start | bytes 786440 | tf_op jit(solution)/shard_map/ppermute | solution.py:296
  406.0 11.2 %collective-permute-start.7 = (f32[2,32,1024]{2,1,0:T(8,128)S(1)}, f32[2,32,1024]{2,1,0:T(8,128)S(1)}, u32[]{:S(2)}, u32[]{:S(2)}) collective-permute-start(f32[2,32,1024]{2,1,0:T(8,128)S(1)} %get-tuple-element.67), channel_id=1, source_target_pairs={{0,2},{2,0},{4,6},{6,4},{8,10},{10,8},{12,14},{14,12},{1,3},{3,1},... | collective-permute-start | bytes 786440 | tf_op jit(solution)/shard_map/ppermute | solution.py:296
  407.9 14.9 %collective-permute-start.3 = (f32[2,32,1024]{2,1,0:T(8,128)S(1)}, f32[2,32,1024]{2,1,0:T(8,128)S(1)}, u32[]{:S(2)}, u32[]{:S(2)}) collective-permute-start(f32[2,32,1024]{2,1,0:T(8,128)S(1)} %get-tuple-element.60), channel_id=1, source_target_pairs={{0,2},{2,0},{4,6},{6,4},{8,10},{10,8},{12,14},{14,12},{1,3},{3,1},... | collective-permute-start | bytes 786440 | tf_op jit(solution)/shard_map/ppermute | solution.py:296
  408.1 16.7 %collective-permute-start.5 = (f32[2,32,1024]{2,1,0:T(8,128)S(1)}, f32[2,32,1024]{2,1,0:T(8,128)S(1)}, u32[]{:S(2)}, u32[]{:S(2)}) collective-permute-start(f32[2,32,1024]{2,1,0:T(8,128)S(1)} %add.43), channel_id=1, source_target_pairs={{0,4},{2,6},{4,0},{6,2},{8,12},{10,14},{12,8},{14,10},{1,5},{3,7},... | collective-permute-start | bytes 786440 | tf_op jit(solution)/shard_map/ppermute | solution.py:296
  410.0 18.5 %collective-permute-start.10 = (f32[2,32,1024]{2,1,0:T(8,128)S(1)}, f32[2,32,1024]{2,1,0:T(8,128)S(1)}, u32[]{:S(2)}, u32[]{:S(2)}) collective-permute-start(f32[2,32,1024]{2,1,0:T(8,128)S(1)} %get-tuple-element.73), channel_id=1, source_target_pairs={{0,2},{2,0},{4,6},{6,4},{8,10},{10,8},{12,14},{14,12},{1,3},{3,1},... | collective-permute-start | bytes 786440 | tf_op jit(solution)/shard_map/ppermute | solution.py:296
  411.6 22.4 %collective-permute-start.14 = (f32[2,32,1024]{2,1,0:T(8,128)S(1)}, f32[2,32,1024]{2,1,0:T(8,128)S(1)}, u32[]{:S(2)}, u32[]{:S(2)}) collective-permute-start(f32[2,32,1024]{2,1,0:T(8,128)S(1)} %get-tuple-element.80), channel_id=1, source_target_pairs={{0,2},{2,0},{4,6},{6,4},{8,10},{10,8},{12,14},{14,12},{1,3},{3,1},... | collective-permute-start | bytes 786440 | tf_op jit(solution)/shard_map/ppermute | solution.py:296
  417.2 18.9 %collective-permute-start.12 = (f32[2,32,1024]{2,1,0:T(8,128)S(1)}, f32[2,32,1024]{2,1,0:T(8,128)S(1)}, u32[]{:S(2)}, u32[]{:S(2)}) collective-permute-start(f32[2,32,1024]{2,1,0:T(8,128)S(1)} %add.50), channel_id=1, source_target_pairs={{0,4},{2,6},{4,0},{6,2},{8,12},{10,14},{12,8},{14,10},{1,5},{3,7},... | collective-permute-start | bytes 786440 | tf_op jit(solution)/shard_map/ppermute | solution.py:296
  422.8 15.7 %collective-permute-start.8 = (f32[2,32,1024]{2,1,0:T(8,128)S(1)}, f32[2,32,1024]{2,1,0:T(8,128)S(1)}, u32[]{:S(2)}, u32[]{:S(2)}) collective-permute-start(f32[2,32,1024]{2,1,0:T(8,128)S(1)} %add.45), channel_id=1, source_target_pairs={{0,4},{2,6},{4,0},{6,2},{8,12},{10,14},{12,8},{14,10},{1,5},{3,7},... | collective-permute-start | bytes 786440 | tf_op jit(solution)/shard_map/ppermute | solution.py:296
  424.8 15.2 %collective-permute-start.9 = (f32[2,32,1024]{2,1,0:T(8,128)S(1)}, f32[2,32,1024]{2,1,0:T(8,128)S(1)}, u32[]{:S(2)}, u32[]{:S(2)}) collective-permute-start(f32[2,32,1024]{2,1,0:T(8,128)S(1)} %add.47), channel_id=1, source_target_pairs={{0,8},{2,10},{4,12},{6,14},{8,0},{10,2},{12,4},{14,6},{1,9},{3,11}... | collective-permute-start | bytes 786440 | tf_op jit(solution)/shard_map/ppermute | solution.py:296
  428.4 11.6 %collective-permute-start.6 = (f32[2,32,1024]{2,1,0:T(8,128)S(1)}, f32[2,32,1024]{2,1,0:T(8,128)S(1)}, u32[]{:S(2)}, u32[]{:S(2)}) collective-permute-start(f32[2,32,1024]{2,1,0:T(8,128)S(1)} %get-tuple-element.64), channel_id=1, source_target_pairs={{0,2},{2,0},{4,6},{6,4},{8,10},{10,8},{12,14},{14,12},{1,3},{3,1},... | collective-permute-start | bytes 786440 | tf_op jit(solution)/shard_map/ppermute | solution.py:296
  434.1 13.0 %collective-permute-start.15 = (f32[2,32,1024]{2,1,0:T(8,128)S(1)}, f32[2,32,1024]{2,1,0:T(8,128)S(1)}, u32[]{:S(2)}, u32[]{:S(2)}) collective-permute-start(f32[2,32,1024]{2,1,0:T(8,128)S(1)} %add.52), channel_id=1, source_target_pairs={{0,4},{2,6},{4,0},{6,2},{8,12},{10,14},{12,8},{14,10},{1,5},{3,7},... | collective-permute-start | bytes 786440 | tf_op jit(solution)/shard_map/ppermute | solution.py:296
  436.1 13.1 %collective-permute-start.16 = (f32[2,32,1024]{2,1,0:T(8,128)S(1)}, f32[2,32,1024]{2,1,0:T(8,128)S(1)}, u32[]{:S(2)}, u32[]{:S(2)}) collective-permute-start(f32[2,32,1024]{2,1,0:T(8,128)S(1)} %add.54), channel_id=1, source_target_pairs={{0,8},{2,10},{4,12},{6,14},{8,0},{10,2},{12,4},{14,6},{1,9},{3,11}... | collective-permute-start | bytes 786440 | tf_op jit(solution)/shard_map/ppermute | solution.py:296
  438.5 10.6 %collective-permute-start.13 = (f32[2,32,1024]{2,1,0:T(8,128)S(1)}, f32[2,32,1024]{2,1,0:T(8,128)S(1)}, u32[]{:S(2)}, u32[]{:S(2)}) collective-permute-start(f32[2,32,1024]{2,1,0:T(8,128)S(1)} %get-tuple-element.77), channel_id=1, source_target_pairs={{0,2},{2,0},{4,6},{6,4},{8,10},{10,8},{12,14},{14,12},{1,3},{3,1},... | collective-permute-start | bytes 786440 | tf_op jit(solution)/shard_map/ppermute | solution.py:296

commit v15 on v9

--- a/solution.py
+++ b/solution.py
@@ -299,12 +299,19 @@
     core = core_of(many, arrived)
     odd = list(range(idx_size - 1, 0, -2))
     even = [slot - 1 for slot in odd]
-    sums = added(0, many, odd + even, 2, core, swapped(core, "half"), other_left, [])
+    groups = 2 if depth % 2 == 0 else 1
+    sums = added(0, many, odd + even, 2 * groups, core, swapped(core, "half"), other_left, [])
     core = core_of(few, late, (sums[0][0, :8, :128],))
     other_core = swapped(core, "half")
-    leaving = added(many, few, odd, PIECES * depth, core, other_core, other_left, [sums[0]])
-    core, leaving = lax.optimization_barrier((core, leaving))
-    staying = list(added(many, few, even, PIECES * depth, core, other_core, other_left, [sums[1]]))
+    formed = []
+    per = depth // groups
+    for number, kept in enumerate(sums):
+        slots = (odd + even)[number * per : (number + 1) * per]
+        formed.append(added(many, few, slots, PIECES * per, core, other_core, other_left, [kept]))
+        if number + 1 < len(sums):
+            core, formed[-1] = lax.optimization_barrier((core, formed[-1]))
+    flat = [block for part in formed for block in part]
+    leaving, staying = flat[: PIECES * depth], flat[PIECES * depth :]
     mine, coming = [], {}
     for n, block in enumerate(leaving):
         if n >= WINDOW:

time: 451 us -> 451 us (level)
  Pallas kernels: 57.4 us -> 65.7 us
  waiting for transfers between devices: 290 us -> 284 us
    pallas_call x3 -> x5, Pallas kernels: 37.5 us -> 45.8 us  [added(): pl.pallas_call(functools.partial(amplitude_kernel, start, count, slots, l...]
    ppermute x14, waiting for transfers between devices: 24.7 us -> 19 us  [hop(): return lax.ppermute(x, 'idx', [(i, i ^ mask) for i in range(idx_size)])]
  transfers between devices with their start and end apart: 19 -> 19, of which waited for: 11 -> 9; matrix products, arithmetic and copies ran while one was open for 0% -> 0% of each run, Pallas kernels for 10% -> 12%
where the time goes in v15:
time: 451 us
  waiting for transfers between devices  284 us (63%)
  starting transfers between devices  91.5 us (20%)
  Pallas kernels  65.7 us (15%)
  local copies, waits for them, and re-layouts  9.23 us (2%)
    all_to_all x2, waiting for transfers between devices, sent(): lax.all_to_all(flat, ('idx', 'half'), 0, 0, tiled=True)  257 us
    all_to_all x2, starting transfers between devices, sent(): lax.all_to_all(flat, ('idx', 'half'), 0, 0, tiled=True)  69.2 us
    pallas_call x5, Pallas kernels, added(): pl.pallas_call(functools.partial(amplitude_kernel, start, count, slots, l...  45.8 us
    ppermute x14, starting transfers between devices, hop(): return lax.ppermute(x, 'idx', [(i, i ^ mask) for i in range(idx_size)])  21 us
    ppermute x14, waiting for transfers between devices, hop(): return lax.ppermute(x, 'idx', [(i, i ^ mask) for i in range(idx_size)])  19 us
    pallas_call x2, Pallas kernels, core_of(): pl.pallas_call(functools.partial(core_kernel, count, scale), out_shape=ja...  11.6 us
  transfers between devices with their start and end apart: 19, of which 9 were waited for; matrix products, arithmetic and copies ran while one was open for 0% of the time, Pallas kernels for 12%

profile of v15, /device:TPU:0, one launch (start us, length us, event | category | flops | bytes accessed | tf_op | source)
XLA Modules:
  0.0 450.9 jit_solution(3540716545127599606)
XLA Ops:
  0.0 5.3 %shard_map.29 = f32[8,2,2,7,32,512]{5,4,3,2,1,0:T(8,128)S(1)} custom-call(f32[2,8,8,32,1024]{4,3,2,1,0:T(8,128)} %bitcast.29), custom_call_target="tpu_custom_call" | custom-call | bytes 1024 | tf_op jit(solution)/shard_map/pallas_call | solution.py:239
  5.4 5.1 %copy-done = f32[8,2,2,7,32,512]{5,4,3,2,1,0:T(8,128)} copy-done((f32[8,2,2,7,32,512]{5,4,3,2,1,0:T(8,128)}, f32[8,2,2,7,32,512]{5,4,3,2,1,0:T(8,128)S(1)}, u32[]{:S(2)}) %copy-start) | copy-done | bytes 14680088
  10.4 7.4 %all-to-all-start.1 = ((f32[16,2,7,32,512]{4,3,2,1,0:T(8,128)}), f32[16,2,7,32,512]{4,3,2,1,0:T(8,128)}, u32[]{:S(2)}, u32[]{:S(2)}) async-start(f32[16,2,7,32,512]{4,3,2,1,0:T(8,128)} %bitcast.17), calls=%async_computation.1 | async-start | bytes 29360128 | tf_op jit(solution)/shard_map/all_to_all | solution.py:251
  17.9 0.4 collective-permute-start.1
  18.2 2.9 shard_map.28
  21.1 257.0 %all-to-all-done.1 = f32[16,2,7,32,512]{4,3,2,1,0:T(8,128)} async-done(((f32[16,2,7,32,512]{4,3,2,1,0:T(8,128)}), f32[16,2,7,32,512]{4,3,2,1,0:T(8,128)}, u32[]{:S(2)}, u32[]{:S(2)}) %all-to-all-start.1) | async-done | bytes 14680096 | tf_op jit(solution)/shard_map/all_to_all | solution.py:251
  278.1 61.8 %all-to-all-start = ((f32[16,2,1,32,512]{4,3,1,2,0:T(8,128)}), f32[16,2,1,32,512]{4,3,1,2,0:T(8,128)S(1)}, u32[]{:S(2)}, u32[]{:S(2)}) async-start(f32[16,2,1,32,512]{4,3,1,2,0:T(8,128)} %bitcast.4), calls=%async_computation | async-start | bytes 4194304 | tf_op jit(solution)/shard_map/all_to_all | solution.py:251
  339.9 10.6 %shard_map.30.own_core = f32[7,2,256,256]{3,2,1,0:T(8,128)} custom-call(f32[8,2,2,7,32,512]{5,4,3,2,1,0:T(8,128)} %bitcast.7.arrived), custom_call_target="tpu_custom_call" | custom-call | bytes 1024 | tf_op jit(solution)/shard_map/pallas_call | solution.py:254
  350.5 0.5 collective-permute-start
  351.0 0.1 pad_add_fusion.place
  351.1 6.3 %collective-permute-done.other_core = f32[7,2,256,256]{3,2,1,0:T(8,128)} collective-permute-done((f32[7,2,256,256]{3,2,1,0:T(8,128)}, f32[7,2,256,256]{3,2,1,0:T(8,128)}, u32[]{:S(2)}, u32[]{:S(2)}) %collective-permute-start) | collective-permute-done | bytes 3670048 | tf_op jit(solution)/shard_map/ppermute | solution.py:21
  357.4 29.7 %shard_map.31 = (f32[2,128,1024]{2,1,0:T(8,128)S(1)}, f32[2,128,1024]{2,1,0:T(8,128)S(1)}, f32[2,128,1024]{2,1,0:T(8,128)S(1)}, f32[2,128,1024]{2,1,0:T(8,128)S(1)}) custom-call(s32[2]{0:T(128)S(1)} %pad_add_fusion.place, f32[7,2,256,256]{3,2,1,0:T(8,128)} %shard_map.30.own_core, f32[7,2,256,256]{3,2,1,0:T(8,128)} %collective-permute-done.other_core, ...), custom_call_target="tpu_custom_call" | custom-call | bytes 1024 | tf_op jit(solution)/shard_map/pallas_call | solution.py:270
  387.2 1.0 copy-done.1
  388.1 1.0 copy-done.3
  389.1 1.0 copy-done.5
  390.1 0.0 all-to-all-done
  390.1 1.0 shard_map.32.own_core
  391.1 0.4 collective-permute-start.2
  391.6 1.5 collective-permute-done.2.other_core
  393.1 4.0 shard_map.33
  397.1 1.9 collective-permute-start.4
  399.1 4.0 shard_map.34
  403.1 0.2 collective-permute-start.11
  403.3 4.0 shard_map.35
  407.4 0.0 collective-permute-done.4
  407.4 1.9 collective-permute-start.7
  409.3 0.2 collective-permute-start.3
  409.5 1.9 collective-permute-start.5
  411.4 1.5 collective-permute-start.10
  412.9 1.1 collective-permute-start.14
  413.9 4.0 collective-permute-done.7
  418.0 1.5 collective-permute-start.12
  419.4 4.0 shard_map.36
  423.5 0.1 collective-permute-done.3
  423.6 1.5 collective-permute-start.8
  425.1 2.4 collective-permute-start.9
  427.6 1.6 collective-permute-done.10
  429.2 1.5 collective-permute-start.6
  430.7 4.1 collective-permute-done.14
  434.9 1.5 collective-permute-start.15
  436.4 0.0 collective-permute-done.12
  436.4 2.4 collective-permute-start.16
  438.9 1.5 collective-permute-start.13
  440.4 0.1 add_add_fusion.1
  440.4 6.7 %collective-permute-done.15 = f32[2,32,1024]{2,1,0:T(8,128)S(1)} collective-permute-done((f32[2,32,1024]{2,1,0:T(8,128)S(1)}, f32[2,32,1024]{2,1,0:T(8,128)S(1)}, u32[]{:S(2)}, u32[]{:S(2)}) %collective-permute-start.15) | collective-permute-done | bytes 262176 | tf_op jit(solution)/shard_map/ppermute | solution.py:291
  447.1 2.4 collective-permute-done.16
  449.6 0.1 add_add_fusion
  449.7 1.2 copy.5
  (27 shorter events, 0.4 us)
Async XLA Ops:
  5.4 5.1 %copy-start = (f32[8,2,2,7,32,512]{5,4,3,2,1,0:T(8,128)}, f32[8,2,2,7,32,512]{5,4,3,2,1,0:T(8,128)S(1)}, u32[]{:S(2)}) copy-start(f32[8,2,2,7,32,512]{5,4,3,2,1,0:T(8,128)S(1)} %shard_map.29) | copy-start | bytes 44040196
  10.4 267.7 %all-to-all-start.1 = ((f32[16,2,7,32,512]{4,3,2,1,0:T(8,128)}), f32[16,2,7,32,512]{4,3,2,1,0:T(8,128)}, u32[]{:S(2)}, u32[]{:S(2)}) async-start(f32[16,2,7,32,512]{4,3,2,1,0:T(8,128)} %bitcast.17), calls=%async_computation.1 | async-start | bytes 29360128 | tf_op jit(solution)/shard_map/all_to_all | solution.py:251
  17.9 333.2 %collective-permute-start.1 = (f32[1,2,8,1024,256]{4,3,2,1,0:T(8,128)}, f32[1,2,8,1024,256]{4,3,2,1,0:T(8,128)}, u32[]{:S(2)}, u32[]{:S(2)}) collective-permute-start(f32[1,2,8,1024,256]{4,3,2,1,0:T(8,128)} %param.2), channel_id=1, source_target_pairs={{0,1},{1,0},{2,3},{3,2},{4,5},{5,4},{6,7},{7,6},{8,9},{9,8},{10,11... | collective-permute-start | bytes 50331656 | tf_op jit(solution)/shard_map/ppermute | solution.py:21
  278.1 112.0 %all-to-all-start = ((f32[16,2,1,32,512]{4,3,1,2,0:T(8,128)}), f32[16,2,1,32,512]{4,3,1,2,0:T(8,128)S(1)}, u32[]{:S(2)}, u32[]{:S(2)}) async-start(f32[16,2,1,32,512]{4,3,1,2,0:T(8,128)} %bitcast.4), calls=%async_computation | async-start | bytes 4194304 | tf_op jit(solution)/shard_map/all_to_all | solution.py:251
  350.5 6.9 %collective-permute-start = (f32[7,2,256,256]{3,2,1,0:T(8,128)}, f32[7,2,256,256]{3,2,1,0:T(8,128)}, u32[]{:S(2)}, u32[]{:S(2)}) collective-permute-start(f32[7,2,256,256]{3,2,1,0:T(8,128)} %shard_map.30.own_core), channel_id=1, source_target_pairs={{0,1},{1,0},{2,3},{3,2},{4,5},{5,4},{6,7},{7,6},{8,9},{9,8},{10,11... | collective-permute-start | bytes 11010056 | tf_op jit(solution)/shard_map/ppermute | solution.py:21
  387.1 1.0 copy-start.1
  388.1 1.0 copy-start.3
  389.1 1.0 copy-start.5
  391.1 7.9 %copy-start.6 = (f32[2,128,1024]{2,1,0:T(8,128)S(1)}, f32[2,128,1024]{2,1,0:T(8,128)}, u32[]{:S(2)}) copy-start(f32[2,128,1024]{2,1,0:T(8,128)} %copy-done.5) | copy-start | bytes 3145732
  391.1 2.0 collective-permute-start.2
  397.1 10.2 %collective-permute-start.4 = (f32[2,32,1024]{2,1,0:T(8,128)S(1)}, f32[2,32,1024]{2,1,0:T(8,128)S(1)}, u32[]{:S(2)}, u32[]{:S(2)}) collective-permute-start(f32[2,32,1024]{2,1,0:T(8,128)S(1)} %get-tuple-element.77), channel_id=1, source_target_pairs={{0,2},{2,0},{4,6},{6,4},{8,10},{10,8},{12,14},{14,12},{1,3},{3,1},... | collective-permute-start | bytes 786440 | tf_op jit(solution)/shard_map/ppermute | solution.py:291
  399.1 4.3 copy-start.4
  403.1 9.7 %collective-permute-start.11 = (f32[2,32,1024]{2,1,0:T(8,128)S(1)}, f32[2,32,1024]{2,1,0:T(8,128)S(1)}, u32[]{:S(2)}, u32[]{:S(2)}) collective-permute-start(f32[2,32,1024]{2,1,0:T(8,128)S(1)} %get-tuple-element.90), channel_id=1, source_target_pairs={{0,2},{2,0},{4,6},{6,4},{8,10},{10,8},{12,14},{14,12},{1,3},{3,1},... | collective-permute-start | bytes 786440 | tf_op jit(solution)/shard_map/ppermute | solution.py:291
  403.3 16.1 %copy-start.2 = (f32[2,128,1024]{2,1,0:T(8,128)S(1)}, f32[2,128,1024]{2,1,0:T(8,128)}, u32[]{:S(2)}) copy-start(f32[2,128,1024]{2,1,0:T(8,128)} %copy-done.1) | copy-start | bytes 3145732
  407.4 10.5 %collective-permute-start.7 = (f32[2,32,1024]{2,1,0:T(8,128)S(1)}, f32[2,32,1024]{2,1,0:T(8,128)S(1)}, u32[]{:S(2)}, u32[]{:S(2)}) collective-permute-start(f32[2,32,1024]{2,1,0:T(8,128)S(1)} %get-tuple-element.81), channel_id=1, source_target_pairs={{0,2},{2,0},{4,6},{6,4},{8,10},{10,8},{12,14},{14,12},{1,3},{3,1},... | collective-permute-start | bytes 786440 | tf_op jit(solution)/shard_map/ppermute | solution.py:291
  409.3 14.3 %collective-permute-start.3 = (f32[2,32,1024]{2,1,0:T(8,128)S(1)}, f32[2,32,1024]{2,1,0:T(8,128)S(1)}, u32[]{:S(2)}, u32[]{:S(2)}) collective-permute-start(f32[2,32,1024]{2,1,0:T(8,128)S(1)} %get-tuple-element.74), channel_id=1, source_target_pairs={{0,2},{2,0},{4,6},{6,4},{8,10},{10,8},{12,14},{14,12},{1,3},{3,1},... | collective-permute-start | bytes 786440 | tf_op jit(solution)/shard_map/ppermute | solution.py:291
  409.5 15.6 %collective-permute-start.5 = (f32[2,32,1024]{2,1,0:T(8,128)S(1)}, f32[2,32,1024]{2,1,0:T(8,128)S(1)}, u32[]{:S(2)}, u32[]{:S(2)}) collective-permute-start(f32[2,32,1024]{2,1,0:T(8,128)S(1)} %add.43), channel_id=1, source_target_pairs={{0,4},{2,6},{4,0},{6,2},{8,12},{10,14},{12,8},{14,10},{1,5},{3,7},... | collective-permute-start | bytes 786440 | tf_op jit(solution)/shard_map/ppermute | solution.py:291
  411.4 17.8 %collective-permute-start.10 = (f32[2,32,1024]{2,1,0:T(8,128)S(1)}, f32[2,32,1024]{2,1,0:T(8,128)S(1)}, u32[]{:S(2)}, u32[]{:S(2)}) collective-permute-start(f32[2,32,1024]{2,1,0:T(8,128)S(1)} %get-tuple-element.87), channel_id=1, source_target_pairs={{0,2},{2,0},{4,6},{6,4},{8,10},{10,8},{12,14},{14,12},{1,3},{3,1},... | collective-permute-start | bytes 786440 | tf_op jit(solution)/shard_map/ppermute | solution.py:291
  412.9 21.9 %collective-permute-start.14 = (f32[2,32,1024]{2,1,0:T(8,128)S(1)}, f32[2,32,1024]{2,1,0:T(8,128)S(1)}, u32[]{:S(2)}, u32[]{:S(2)}) collective-permute-start(f32[2,32,1024]{2,1,0:T(8,128)S(1)} %get-tuple-element.94), channel_id=1, source_target_pairs={{0,2},{2,0},{4,6},{6,4},{8,10},{10,8},{12,14},{14,12},{1,3},{3,1},... | collective-permute-start | bytes 786440 | tf_op jit(solution)/shard_map/ppermute | solution.py:291
  418.0 18.4 %collective-permute-start.12 = (f32[2,32,1024]{2,1,0:T(8,128)S(1)}, f32[2,32,1024]{2,1,0:T(8,128)S(1)}, u32[]{:S(2)}, u32[]{:S(2)}) collective-permute-start(f32[2,32,1024]{2,1,0:T(8,128)S(1)} %add.50), channel_id=1, source_target_pairs={{0,4},{2,6},{4,0},{6,2},{8,12},{10,14},{12,8},{14,10},{1,5},{3,7},... | collective-permute-start | bytes 786440 | tf_op jit(solution)/shard_map/ppermute | solution.py:291
  423.6 15.3 %collective-permute-start.8 = (f32[2,32,1024]{2,1,0:T(8,128)S(1)}, f32[2,32,1024]{2,1,0:T(8,128)S(1)}, u32[]{:S(2)}, u32[]{:S(2)}) collective-permute-start(f32[2,32,1024]{2,1,0:T(8,128)S(1)} %add.45), channel_id=1, source_target_pairs={{0,4},{2,6},{4,0},{6,2},{8,12},{10,14},{12,8},{14,10},{1,5},{3,7},... | collective-permute-start | bytes 786440 | tf_op jit(solution)/shard_map/ppermute | solution.py:291
  425.1 15.2 %collective-permute-start.9 = (f32[2,32,1024]{2,1,0:T(8,128)S(1)}, f32[2,32,1024]{2,1,0:T(8,128)S(1)}, u32[]{:S(2)}, u32[]{:S(2)}) collective-permute-start(f32[2,32,1024]{2,1,0:T(8,128)S(1)} %add.47), channel_id=1, source_target_pairs={{0,8},{2,10},{4,12},{6,14},{8,0},{10,2},{12,4},{14,6},{1,9},{3,11}... | collective-permute-start | bytes 786440 | tf_op jit(solution)/shard_map/ppermute | solution.py:291
  429.2 11.2 %collective-permute-start.6 = (f32[2,32,1024]{2,1,0:T(8,128)S(1)}, f32[2,32,1024]{2,1,0:T(8,128)S(1)}, u32[]{:S(2)}, u32[]{:S(2)}) collective-permute-start(f32[2,32,1024]{2,1,0:T(8,128)S(1)} %get-tuple-element.78), channel_id=1, source_target_pairs={{0,2},{2,0},{4,6},{6,4},{8,10},{10,8},{12,14},{14,12},{1,3},{3,1},... | collective-permute-start | bytes 786440 | tf_op jit(solution)/shard_map/ppermute | solution.py:291
  434.9 12.3 %collective-permute-start.15 = (f32[2,32,1024]{2,1,0:T(8,128)S(1)}, f32[2,32,1024]{2,1,0:T(8,128)S(1)}, u32[]{:S(2)}, u32[]{:S(2)}) collective-permute-start(f32[2,32,1024]{2,1,0:T(8,128)S(1)} %add.52), channel_id=1, source_target_pairs={{0,4},{2,6},{4,0},{6,2},{8,12},{10,14},{12,8},{14,10},{1,5},{3,7},... | collective-permute-start | bytes 786440 | tf_op jit(solution)/shard_map/ppermute | solution.py:291
  436.4 13.1 %collective-permute-start.16 = (f32[2,32,1024]{2,1,0:T(8,128)S(1)}, f32[2,32,1024]{2,1,0:T(8,128)S(1)}, u32[]{:S(2)}, u32[]{:S(2)}) collective-permute-start(f32[2,32,1024]{2,1,0:T(8,128)S(1)} %add.54), channel_id=1, source_target_pairs={{0,8},{2,10},{4,12},{6,14},{8,0},{10,2},{12,4},{14,6},{1,9},{3,11}... | collective-permute-start | bytes 786440 | tf_op jit(solution)/shard_map/ppermute | solution.py:291
  438.9 10.7 %collective-permute-start.13 = (f32[2,32,1024]{2,1,0:T(8,128)S(1)}, f32[2,32,1024]{2,1,0:T(8,128)S(1)}, u32[]{:S(2)}, u32[]{:S(2)}) collective-permute-start(f32[2,32,1024]{2,1,0:T(8,128)S(1)} %get-tuple-element.91), channel_id=1, source_target_pairs={{0,2},{2,0},{4,6},{6,4},{8,10},{10,8},{12,14},{14,12},{1,3},{3,1},... | collective-permute-start | bytes 786440 | tf_op jit(solution)/shard_map/ppermute | solution.py:291
